TPU v7x, 256 devices: a whole 4x4x8 slice. The times are simulated.
256 devices in a mesh: tm: 8 (over x, core), space: 32 (over y, z).
Axes of the slice: x: 4, y: 4, z: 8, core: 2. Of those that a mesh axis runs over, the one named last changes fastest.
Arguments:
- guess: float32 [8, 16, 2048, 128], P('tm', None, 'space'), may hold values from -6 to 6
- coeffs: bfloat16 [128, 128, 128], replicated, may hold values from -0.1875 to 0.1875
- coef_index: int32 [2048, 8], P('space'), may hold values from 0 to 127
- neighbours: int32 [2048, 7], P('space'), may hold values from 0 to 127
- send_lists: int32 [128, 16], P('space'), may hold values from -1 to 63, as said below
- mixing: float32 [16, 16], replicated, may hold values from -1.5 to 1.5
Outputs:
- finals: float32 [8, 16, 2048, 128], P('tm', None, 'space')
Inputs may be any that keep to these rules, and one draw needn't show every extreme that they name: `send_lists`: in each row the live local block indices come first and -1 marks the empty slots after them; every row has 4 or more live slots; row 0 is full.
All inputs are finite; a program needn't handle non-finite values.
Results may differ from a plain program's by a relative error of at most 0.00065.
Values may be sent and summed in bfloat16 or wider, within the bound.
No kernel may reach another device: no remote copies, remote signals or barrier semaphores. Data moves between devices by JAX's collectives and lax.ppermute only.
A program may use at most 128 MiB of HBM per device.

v0:
```python
import math

import jax
import jax.numpy as jnp
from jax import lax
from jax.sharding import PartitionSpec as P

SWEEPS = 2


step_size = 0.3
root_six = math.sqrt(6.0)
node_times = ((4.0 - root_six) / 10.0, (4.0 + root_six) / 10.0, 1.0)
radau_rows = (
    (
        (88.0 - 7.0 * root_six) / 360.0,
        (296.0 - 169.0 * root_six) / 1800.0,
        (-2.0 + 3.0 * root_six) / 225.0,
    ),
    (
        (296.0 + 169.0 * root_six) / 1800.0,
        (88.0 + 7.0 * root_six) / 360.0,
        (-2.0 - 3.0 * root_six) / 225.0,
    ),
    ((16.0 - root_six) / 36.0, (16.0 + root_six) / 36.0, 1.0 / 9.0),
)
node_gaps = (node_times[0], node_times[1] - node_times[0], node_times[2] - node_times[1])
node_integrals = (
    radau_rows[0],
    tuple((radau_rows[1][j] - radau_rows[0][j] for j in range(3))),
    tuple((radau_rows[2][j] - radau_rows[1][j] for j in range(3))),
)


def shifted(block, axis, distance):
    devices = range(lax.axis_size(axis))
    route = [(i - distance, i) for i in devices if i - distance in devices]
    return lax.ppermute(block, axis, route)


def pack_rows(blocks, rows):
    live = rows >= 0
    taken = blocks[:, jnp.maximum(rows, 0), :]
    return jnp.where(live[None, :, None], taken, jnp.zeros((), blocks.dtype))


def exchange_rim(packed):
    near_parts = [None, None]
    far_parts = [None, None]
    for slot, offset in ((0, 1), (1, -1)):
        both = jnp.stack([packed[slot], packed[slot + 2]])
        moved = shifted(both, "space", offset)
        near_parts[slot] = moved[0]
        far_parts[slot] = shifted(moved[1], "space", offset)
    return near_parts + far_parts


def per_device(guess, coeffs, coef_index, neighbours, send_lists, mixing):
    first = guess[0]
    species, nblocks, cells = first.shape
    stack = coeffs[coef_index]
    own_rows = lax.broadcasted_iota(jnp.int32, (nblocks, 1), 0)
    columns = jnp.concatenate([own_rows, neighbours], axis=1)

    def operate(field):
        rounded = field.astype(jnp.bfloat16)
        packed = [pack_rows(rounded, send_lists[slot]) for slot in range(4)]
        received = exchange_rim(packed)
        extended = jnp.concatenate([rounded] + received, axis=1)
        picked = extended[:, columns, :]
        linear = jnp.einsum("sbtc,btcd->sbd", picked, stack, preferred_element_type=jnp.float32)
        reaction = jnp.dot(
            mixing, jnp.tanh(field).reshape(species, -1), precision=lax.Precision.HIGHEST
        ).reshape(field.shape)
        return linear + reaction

    forces = [operate(first)] * 4
    ending = first
    leading = lax.axis_index("tm") == 0
    for sweep in range(SWEEPS):
        incoming = shifted(ending, "tm", 1)
        start = jnp.where(leading, first, incoming)
        f_current = operate(start)
        current = start
        new_forces = [f_current]
        for node in range(3):
            quad = (
                node_integrals[node][0] * forces[1]
                + node_integrals[node][1] * forces[2]
                + node_integrals[node][2] * forces[3]
            )
            current = current + step_size * (node_gaps[node] * (f_current - forces[node]) + quad)
            if node < 2 or sweep + 1 < SWEEPS:
                f_current = operate(current)
                new_forces.append(f_current)
        forces = new_forces
        ending = current
    return ending[None]


def solution(mesh):
    placed = (
        P("tm", None, "space", None),
        P(),
        P("space", None),
        P("space", None),
        P("space", None),
        P(),
    )
    return jax.shard_map(
        per_device,
        mesh=mesh,
        in_specs=placed,
        out_specs=P("tm", None, "space", None),
        check_vma=False,
    )
```

profile of v0, /device:TPU:8, one launch (start us, length us, event | category | flops | bytes accessed | tf_op | source)
XLA Modules:
  0.0 294.4 jit_solution(15402211881912596568)
XLA Ops:
  0.0 1.4 copy.104
  1.4 1.8 collective-permute-start
  3.2 1.4 constant_dynamic-update-slice_fusion.9
  7.5 16.2 %gather_fusion = bf16[512,128,128]{2,1,0:T(8,128)(2,1)} fusion(bf16[128,128,128]{2,1,0:T(8,128)(2,1)} %param.7, s32[1024]{0:T(1024)S(1)} %pad_clamp_fusion), kind=kCustom, calls=%fused_computation | custom fusion | bytes 33556480 | tf_op jit(solution)/shard_map/gather | solution.py:61
  23.8 1.6 fusion.40
  29.8 3.8 %collective-permute-start.5 = (bf16[2,16,16,128]{3,1,2,0:T(8,128)(2,1)S(1)}, bf16[2,16,16,128]{3,1,2,0:T(8,128)(2,1)S(1)}, u32[]{:S(2)}, u32[]{:S(2)}) collective-permute-start(bf16[2,16,16,128]{3,1,2,0:T(8,128)(2,1)S(1)} %pad_maximum_fusion.2), channel_id=1, source_target_pairs={{0,1},{1,2},{2,3},{3,4},{4,5},{5,6},{6,7},{7,8},{8,9},{9,10},{10,1... | collective-permute-start | bytes 393224 | tf_op jit(solution)/shard_map/ppermute | solution.py:38
  33.7 3.8 %collective-permute-start.1 = (bf16[2,16,16,128]{3,1,2,0:T(8,128)(2,1)S(1)}, bf16[2,16,16,128]{3,1,2,0:T(8,128)(2,1)S(1)}, u32[]{:S(2)}, u32[]{:S(2)}) collective-permute-start(bf16[2,16,16,128]{3,1,2,0:T(8,128)(2,1)S(1)} %pad_maximum_fusion), channel_id=1, source_target_pairs={{0,1},{1,2},{2,3},{3,4},{4,5},{5,6},{6,7},{7,8},{8,9},{9,10},{10,1... | collective-permute-start | bytes 393224 | tf_op jit(solution)/shard_map/ppermute | solution.py:38
  37.7 4.1 %collective-permute-start.6 = (bf16[2,16,16,128]{3,1,2,0:T(8,128)(2,1)S(1)}, bf16[2,16,16,128]{3,1,2,0:T(8,128)(2,1)S(1)}, u32[]{:S(2)}, u32[]{:S(2)}) collective-permute-start(bf16[2,16,16,128]{3,1,2,0:T(8,128)(2,1)S(1)} %pad_maximum_fusion.3), channel_id=1, source_target_pairs={{1,0},{2,1},{3,2},{4,3},{5,4},{6,5},{7,6},{8,7},{9,8},{10,9},{11,1... | collective-permute-start | bytes 393224 | tf_op jit(solution)/shard_map/ppermute | solution.py:38
  41.9 3.6 %collective-permute-start.2 = (bf16[2,16,16,128]{3,1,2,0:T(8,128)(2,1)S(1)}, bf16[2,16,16,128]{3,1,2,0:T(8,128)(2,1)S(1)}, u32[]{:S(2)}, u32[]{:S(2)}) collective-permute-start(bf16[2,16,16,128]{3,1,2,0:T(8,128)(2,1)S(1)} %pad_maximum_fusion.1), channel_id=1, source_target_pairs={{1,0},{2,1},{3,2},{4,3},{5,4},{6,5},{7,6},{8,7},{9,8},{10,9},{11,1... | collective-permute-start | bytes 393224 | tf_op jit(solution)/shard_map/ppermute | solution.py:38
  45.5 1.4 convolution_bitcast_fusion.14
  46.9 2.2 collective-permute-start.7
  49.1 2.7 collective-permute-start.3
  51.9 5.2 %collective-permute-start.8 = (bf16[16,16,128]{2,0,1:T(8,128)(2,1)S(1)}, bf16[16,16,128]{2,0,1:T(8,128)(2,1)S(1)}, u32[]{:S(2)}, u32[]{:S(2)}) collective-permute-start(bf16[16,16,128]{2,0,1:T(8,128)(2,1)S(1)} %slice_bitcast_fusion.24), channel_id=1, source_target_pairs={{1,0},{2,1},{3,2},{4,3},{5,4},{6,5},{7,6},{8,7},{9,8},{10,9},{11,1... | collective-permute-start | bytes 196616 | tf_op jit(solution)/shard_map/ppermute | solution.py:38
  57.1 3.6 %collective-permute-start.4 = (bf16[16,16,128]{2,0,1:T(8,128)(2,1)S(1)}, bf16[16,16,128]{2,0,1:T(8,128)(2,1)S(1)}, u32[]{:S(2)}, u32[]{:S(2)}) collective-permute-start(bf16[16,16,128]{2,0,1:T(8,128)(2,1)S(1)} %slice_bitcast_fusion.28), channel_id=1, source_target_pairs={{1,0},{2,1},{3,2},{4,3},{5,4},{6,5},{7,6},{8,7},{9,8},{10,9},{11,1... | collective-permute-start | bytes 196616 | tf_op jit(solution)/shard_map/ppermute | solution.py:38
  63.9 2.2 gather_fusion.5
  66.2 2.7 gather_fusion.10
  68.9 8.8 %fusion.1 = f32[16,64,128]{2,0,1:T(8,128)S(1)} fusion(f32[16,64,128]{2,0,1:T(8,128)} %fusion.40, bf16[16,64,8,128]{3,0,2,1:T(8,128)(2,1)} %bitcast.497, bf16[64,8,128,128]{3,2,1,0:T(8,128)(2,1)} %bitcast.484), kind=kOutput, calls=%fused_computation.57 | convolution fusion | flops 268566528 | bytes 19922944 | tf_op jit(solution)/shard_map/sbtc,btcd->sbd/dot_general | solution.py:71
  77.8 7.2 %fusion = f32[16,64,128]{2,0,1:T(8,128)S(1)} fusion(bf16[16,64,8,128]{3,0,2,1:T(8,128)(2,1)S(1)} %bitcast.495, bf16[64,8,128,128]{3,2,1,0:T(8,128)(2,1)} %bitcast.485, f32[2,64,8,128]{3,2,1,0:T(8,128)S(1)} %copy-done.15), kind=kOutput, calls=%fused_computation.56 | convolution fusion | flops 268566528 | bytes 19922944 | tf_op jit(solution)/shard_map/sbtc,btcd->sbd/dot_general | solution.py:71
  89.4 1.9 collective-permute-start.9
  91.3 6.2 %collective-permute-start.10 = (bf16[2,16,16,128]{3,1,2,0:T(8,128)(2,1)S(1)}, bf16[2,16,16,128]{3,1,2,0:T(8,128)(2,1)S(1)}, u32[]{:S(2)}, u32[]{:S(2)}) collective-permute-start(bf16[2,16,16,128]{3,1,2,0:T(8,128)(2,1)S(1)} %pad_maximum_fusion.5), channel_id=1, source_target_pairs={{1,0},{2,1},{3,2},{4,3},{5,4},{6,5},{7,6},{8,7},{9,8},{10,9},{11,1... | collective-permute-start | bytes 393224 | tf_op jit(solution)/shard_map/ppermute | solution.py:38
  97.5 1.4 convolution_bitcast_fusion.13
  98.9 1.9 collective-permute-start.11
  100.9 6.0 %collective-permute-start.12 = (bf16[16,16,128]{2,0,1:T(8,128)(2,1)S(1)}, bf16[16,16,128]{2,0,1:T(8,128)(2,1)S(1)}, u32[]{:S(2)}, u32[]{:S(2)}) collective-permute-start(bf16[16,16,128]{2,0,1:T(8,128)(2,1)S(1)} %slice_bitcast_fusion.20), channel_id=1, source_target_pairs={{1,0},{2,1},{3,2},{4,3},{5,4},{6,5},{7,6},{8,7},{9,8},{10,9},{11,1... | collective-permute-start | bytes 196616 | tf_op jit(solution)/shard_map/ppermute | solution.py:38
  107.2 1.6 collective-permute-done.12
  108.8 2.0 gather_fusion.15
  110.9 7.3 %fusion.2 = f32[16,64,128]{2,0,1:T(8,128)S(1)} fusion(bf16[16,64,8,128]{3,0,2,1:T(8,128)(2,1)S(1)} %bitcast.498, bf16[64,8,128,128]{3,2,1,0:T(8,128)(2,1)} %bitcast.486, f32[2,64,8,128]{3,2,1,0:T(8,128)} %convolution_bitcast_fusion.13), kind=kOutput, calls=%fused_computation.58 | convolution fusion | flops 268566528 | bytes 19922944 | tf_op jit(solution)/shard_map/sbtc,btcd->sbd/dot_general | solution.py:71
  121.2 1.9 collective-permute-start.13
  123.1 6.4 %collective-permute-start.14 = (bf16[2,16,16,128]{3,1,2,0:T(8,128)(2,1)S(1)}, bf16[2,16,16,128]{3,1,2,0:T(8,128)(2,1)S(1)}, u32[]{:S(2)}, u32[]{:S(2)}) collective-permute-start(bf16[2,16,16,128]{3,1,2,0:T(8,128)(2,1)S(1)} %pad_maximum_fusion.7), channel_id=1, source_target_pairs={{1,0},{2,1},{3,2},{4,3},{5,4},{6,5},{7,6},{8,7},{9,8},{10,9},{11,1... | collective-permute-start | bytes 393224 | tf_op jit(solution)/shard_map/ppermute | solution.py:38
  130.5 1.9 collective-permute-start.15
  132.4 6.0 %collective-permute-start.16 = (bf16[16,16,128]{2,0,1:T(8,128)(2,1)S(1)}, bf16[16,16,128]{2,0,1:T(8,128)(2,1)S(1)}, u32[]{:S(2)}, u32[]{:S(2)}) collective-permute-start(bf16[16,16,128]{2,0,1:T(8,128)(2,1)S(1)} %slice_bitcast_fusion.16), channel_id=1, source_target_pairs={{1,0},{2,1},{3,2},{4,3},{5,4},{6,5},{7,6},{8,7},{9,8},{10,9},{11,1... | collective-permute-start | bytes 196616 | tf_op jit(solution)/shard_map/ppermute | solution.py:38
  138.8 1.6 collective-permute-done.16
  140.4 2.7 gather_fusion.20
  143.1 8.8 %fusion.3 = f32[16,64,128]{2,0,1:T(8,128)S(1)} fusion(bf16[16,64,8,128]{3,0,2,1:T(8,128)(2,1)} %bitcast.499, bf16[64,8,128,128]{3,2,1,0:T(8,128)(2,1)} %bitcast.487, f32[2,64,8,128]{3,2,1,0:T(8,128)S(1)} %convolution_bitcast_fusion.12), kind=kOutput, calls=%fused_computation.59 | convolution fusion | flops 268566528 | bytes 19922944 | tf_op jit(solution)/shard_map/sbtc,btcd->sbd/dot_general | solution.py:71
  152.8 2.1 collective-permute-start.17
  161.7 1.3 gather_fusion.24
  168.9 1.9 collective-permute-start.18
  170.9 2.4 collective-permute-start.22
  175.2 5.9 %collective-permute-start.19 = (bf16[2,16,16,128]{3,1,2,0:T(8,128)(2,1)S(1)}, bf16[2,16,16,128]{3,1,2,0:T(8,128)(2,1)S(1)}, u32[]{:S(2)}, u32[]{:S(2)}) collective-permute-start(bf16[2,16,16,128]{3,1,2,0:T(8,128)(2,1)S(1)} %pad_maximum_fusion.9), channel_id=1, source_target_pairs={{1,0},{2,1},{3,2},{4,3},{5,4},{6,5},{7,6},{8,7},{9,8},{10,9},{11,1... | collective-permute-start | bytes 393224 | tf_op jit(solution)/shard_map/ppermute | solution.py:38
  181.1 3.9 %collective-permute-start.23 = (bf16[2,16,16,128]{3,1,2,0:T(8,128)(2,1)S(1)}, bf16[2,16,16,128]{3,1,2,0:T(8,128)(2,1)S(1)}, u32[]{:S(2)}, u32[]{:S(2)}) collective-permute-start(bf16[2,16,16,128]{3,1,2,0:T(8,128)(2,1)S(1)} %pad_maximum_fusion.11), channel_id=1, source_target_pairs={{1,0},{2,1},{3,2},{4,3},{5,4},{6,5},{7,6},{8,7},{9,8},{10,9},{11,1... | collective-permute-start | bytes 393224 | tf_op jit(solution)/shard_map/ppermute | solution.py:38
  185.0 1.4 convolution_bitcast_fusion.11
  186.4 1.9 collective-permute-start.20
  188.4 1.9 collective-permute-start.24
  190.4 6.0 %collective-permute-start.21 = (bf16[16,16,128]{2,0,1:T(8,128)(2,1)S(1)}, bf16[16,16,128]{2,0,1:T(8,128)(2,1)S(1)}, u32[]{:S(2)}, u32[]{:S(2)}) collective-permute-start(bf16[16,16,128]{2,0,1:T(8,128)(2,1)S(1)} %slice_bitcast_fusion.12), channel_id=1, source_target_pairs={{1,0},{2,1},{3,2},{4,3},{5,4},{6,5},{7,6},{8,7},{9,8},{10,9},{11,1... | collective-permute-start | bytes 196616 | tf_op jit(solution)/shard_map/ppermute | solution.py:38
  196.4 4.1 %collective-permute-start.25 = (bf16[16,16,128]{2,0,1:T(8,128)(2,1)S(1)}, bf16[16,16,128]{2,0,1:T(8,128)(2,1)S(1)}, u32[]{:S(2)}, u32[]{:S(2)}) collective-permute-start(bf16[16,16,128]{2,0,1:T(8,128)(2,1)S(1)} %slice_bitcast_fusion.8), channel_id=1, source_target_pairs={{1,0},{2,1},{3,2},{4,3},{5,4},{6,5},{7,6},{8,7},{9,8},{10,9},{11,1... | collective-permute-start | bytes 196616 | tf_op jit(solution)/shard_map/ppermute | solution.py:38
  200.7 1.9 collective-permute-done.25
  202.6 2.7 gather_fusion.30
  205.3 2.8 gather_fusion.25
  208.1 8.9 %fusion.10 = f32[16,64,128]{2,0,1:T(8,128)S(1)} fusion(bf16[16,64,8,128]{3,0,2,1:T(8,128)(2,1)} %bitcast.496, bf16[64,8,128,128]{3,2,1,0:T(8,128)(2,1)} %bitcast.488, f32[2,64,8,128]{3,2,1,0:T(8,128)S(1)} %convolution_bitcast_fusion.10), kind=kOutput, calls=%fused_computation.66 | convolution fusion | flops 268566528 | bytes 19922944 | tf_op jit(solution)/shard_map/sbtc,btcd->sbd/dot_general | solution.py:71
  217.1 7.2 %constant_dynamic-update-slice_fusion.34 = (bf16[16,128,128]{2,0,1:T(8,128)(2,1)S(1)}, bf16[16,64,128]{2,0,1:T(8,128)(2,1)S(1)}, f32[16,64,128]{2,0,1:T(8,128)S(1)}) fusion(f32[16,64,128]{2,0,1:T(8,128)S(1)} %copy-done.9, f32[16,64,128]{2,0,1:T(8,128)S(1)} %fusion.10, f32[16,64,128]{2,0,1:T(8,128)S(1)} %fusion.3, f32[16,64,128]{2,0,1:T(8,128)S(1)} %fusion.2, ...), kind=kOutput, calls=%fused_computation.167 | convolution fusion | flops 270008320 | bytes 23068672 | tf_op jit(solution)/shard_map/sbtc,btcd->sbd/dot_general | solution.py:71
  227.5 1.9 collective-permute-start.26
  229.4 6.0 %collective-permute-start.27 = (bf16[2,16,16,128]{3,1,2,0:T(8,128)(2,1)S(1)}, bf16[2,16,16,128]{3,1,2,0:T(8,128)(2,1)S(1)}, u32[]{:S(2)}, u32[]{:S(2)}) collective-permute-start(bf16[2,16,16,128]{3,1,2,0:T(8,128)(2,1)S(1)} %pad_maximum_fusion.13), channel_id=1, source_target_pairs={{1,0},{2,1},{3,2},{4,3},{5,4},{6,5},{7,6},{8,7},{9,8},{10,9},{11,1... | collective-permute-start | bytes 393224 | tf_op jit(solution)/shard_map/ppermute | solution.py:38
  235.5 1.4 convolution_bitcast_fusion.9
  237.8 1.9 collective-permute-start.28
  239.7 6.0 %collective-permute-start.29 = (bf16[16,16,128]{2,0,1:T(8,128)(2,1)S(1)}, bf16[16,16,128]{2,0,1:T(8,128)(2,1)S(1)}, u32[]{:S(2)}, u32[]{:S(2)}) collective-permute-start(bf16[16,16,128]{2,0,1:T(8,128)(2,1)S(1)} %slice_bitcast_fusion.4), channel_id=1, source_target_pairs={{1,0},{2,1},{3,2},{4,3},{5,4},{6,5},{7,6},{8,7},{9,8},{10,9},{11,1... | collective-permute-start | bytes 196616 | tf_op jit(solution)/shard_map/ppermute | solution.py:38
  246.0 1.6 collective-permute-done.29
  247.6 2.7 gather_fusion.35
  250.3 9.0 %constant_dynamic-update-slice_fusion.39 = (bf16[16,128,128]{2,0,1:T(8,128)(2,1)S(1)}, bf16[16,64,128]{2,0,1:T(8,128)(2,1)S(1)}, f32[16,64,128]{2,0,1:T(8,128)S(1)}) fusion(f32[16,64,128]{2,0,1:T(8,128)S(1)} %get-tuple-element.55, f32[16,64,128]{2,0,1:T(8,128)S(1)} %fusion.10, f32[16,64,128]{2,0,1:T(8,128)S(1)} %fusion.3, f32[16,64,128]{2,0,1:T(8,128)S(1)} %fusion.2, ...), kind=kOutput, calls=%fused_computation.172 | convolution fusion | flops 270008320 | bytes 22544384 | tf_op jit(solution)/shard_map/sbtc,btcd->sbd/dot_general | solution.py:71
  262.6 1.9 collective-permute-start.30
  264.5 6.4 %collective-permute-start.31 = (bf16[2,16,16,128]{3,1,2,0:T(8,128)(2,1)S(1)}, bf16[2,16,16,128]{3,1,2,0:T(8,128)(2,1)S(1)}, u32[]{:S(2)}, u32[]{:S(2)}) collective-permute-start(bf16[2,16,16,128]{3,1,2,0:T(8,128)(2,1)S(1)} %pad_maximum_fusion.15), channel_id=1, source_target_pairs={{1,0},{2,1},{3,2},{4,3},{5,4},{6,5},{7,6},{8,7},{9,8},{10,9},{11,1... | collective-permute-start | bytes 393224 | tf_op jit(solution)/shard_map/ppermute | solution.py:38
  271.9 1.9 collective-permute-start.32
  273.8 6.3 %collective-permute-start.33 = (bf16[16,16,128]{2,0,1:T(8,128)(2,1)S(1)}, bf16[16,16,128]{2,0,1:T(8,128)(2,1)S(1)}, u32[]{:S(2)}, u32[]{:S(2)}) collective-permute-start(bf16[16,16,128]{2,0,1:T(8,128)(2,1)S(1)} %slice_bitcast_fusion), channel_id=1, source_target_pairs={{1,0},{2,1},{3,2},{4,3},{5,4},{6,5},{7,6},{8,7},{9,8},{10,9},{11,1... | collective-permute-start | bytes 196616 | tf_op jit(solution)/shard_map/ppermute | solution.py:38
  280.2 1.6 collective-permute-done.33
  281.8 2.7 gather_fusion.40
  284.5 9.0 %fusion.23 = f32[1,16,64,128]{3,1,2,0:T(8,128)S(1)} fusion(f32[16,64,128]{2,0,1:T(8,128)S(1)} %get-tuple-element.56, f32[16,64,128]{2,0,1:T(8,128)S(1)} %fusion.3, bf16[16,64,8,128]{3,0,2,1:T(8,128)(2,1)} %bitcast.493, bf16[64,8,128,128]{3,2,1,0:T(8,128)(2,1)} %bitcast.491, f32[2,64,8,128]{3,2,1,0:T(8,128)S(1)} %convolution_bitcast_fusion.8, ...), kind=kOutput, calls=%fused_computation.79 | convolution fusion | flops 269877248 | bytes 22020096 | tf_op jit(solution)/shard_map/sbtc,btcd->sbd/dot_general | solution.py:71
  (234 shorter events, 44.6 us)
Async XLA Ops:
  0.0 23.8 %copy-start = (f32[16,16]{1,0:T(8,128)S(1)}, f32[16,16]{1,0:T(8,128)}, u32[]{:S(2)}) copy-start(f32[16,16]{1,0:T(8,128)} %param.11) | copy-start | bytes 3076
  0.0 5.1 %copy-start.1 = (f32[1,16,64,128]{3,2,1,0:T(8,128)S(1)}, f32[1,16,64,128]{3,2,1,0:T(8,128)}, u32[]{:S(2)}) copy-start(f32[1,16,64,128]{3,2,1,0:T(8,128)} %param.6) | copy-start | bytes 1572868
  0.0 4.6 %copy-start.26 = (s32[4,16]{1,0:T(4,128)S(1)}, s32[4,16]{1,0:T(4,128)}, u32[]{:S(2)}) copy-start(s32[4,16]{1,0:T(4,128)} %param.10) | copy-start | bytes 772
  0.0 4.6 %copy-start.27 = (s32[64,8]{0,1:T(8,128)S(1)}, s32[64,8]{0,1:T(8,128)}, u32[]{:S(2)}) copy-start(s32[64,8]{0,1:T(8,128)} %param.8) | copy-start | bytes 6148
  0.0 4.8 %copy-start.28 = (s32[64,7]{0,1:T(8,128)S(1)}, s32[64,7]{0,1:T(8,128)}, u32[]{:S(2)}) copy-start(s32[64,7]{0,1:T(8,128)} %param.9) | copy-start | bytes 5380
  1.4 24.0 %collective-permute-start = (f32[16,64,128]{2,0,1:T(8,128)S(1)}, f32[16,64,128]{2,0,1:T(8,128)S(1)}, u32[]{:S(2)}, u32[]{:S(2)}) collective-permute-start(f32[16,64,128]{2,0,1:T(8,128)S(1)} %bitcast.501), channel_id=1, source_target_pairs={{0,32},{32,64},{64,96},{96,128},{128,160},{160,192},{192,224},{1,3... | collective-permute-start | bytes 1572872 | tf_op jit(solution)/shard_map/ppermute | solution.py:38
  5.1 113.9 %copy-start.22 = (s32[1024]{0:T(1024)}, s32[1024]{0:T(1024)S(1)}, u32[]{:S(2)}) copy-start(s32[1024]{0:T(1024)S(1)} %get-tuple-element.58) | copy-start | bytes 12292
  5.1 150.9 %copy-start.23 = (s32[1024]{0:T(1024)}, s32[1024]{0:T(1024)S(1)}, u32[]{:S(2)}) copy-start(s32[1024]{0:T(1024)S(1)} %get-tuple-element.57) | copy-start | bytes 12292
  5.1 114.5 %copy-start.25 = (s32[1024]{0:T(1024)}, s32[1024]{0:T(1024)S(1)}, u32[]{:S(2)}) copy-start(s32[1024]{0:T(1024)S(1)} %get-tuple-element.59) | copy-start | bytes 12292
  5.1 115.1 %copy-start.24 = (s32[1024]{0:T(1024)}, s32[1024]{0:T(1024)S(1)}, u32[]{:S(2)}) copy-start(s32[1024]{0:T(1024)S(1)} %get-tuple-element.60) | copy-start | bytes 12292
  23.7 97.0 %copy-start.20 = (pred[16]{0:T(512)(128)(4,1)}, pred[16]{0:T(512)(128)(4,1)S(1)}, u32[]{:S(2)}) copy-start(pred[16]{0:T(512)(128)(4,1)S(1)} %get-tuple-element.34) | copy-start | bytes 52
  23.8 97.1 %copy-start.18 = (pred[16]{0:T(512)(128)(4,1)}, pred[16]{0:T(512)(128)(4,1)S(1)}, u32[]{:S(2)}) copy-start(pred[16]{0:T(512)(128)(4,1)S(1)} %get-tuple-element.31) | copy-start | bytes 52
  23.8 97.2 %copy-start.16 = (pred[16]{0:T(512)(128)(4,1)}, pred[16]{0:T(512)(128)(4,1)S(1)}, u32[]{:S(2)}) copy-start(pred[16]{0:T(512)(128)(4,1)S(1)} %get-tuple-element.33) | copy-start | bytes 52
  25.7 0.8 copy-start.10
  29.8 17.1 %collective-permute-start.5 = (bf16[2,16,16,128]{3,1,2,0:T(8,128)(2,1)S(1)}, bf16[2,16,16,128]{3,1,2,0:T(8,128)(2,1)S(1)}, u32[]{:S(2)}, u32[]{:S(2)}) collective-permute-start(bf16[2,16,16,128]{3,1,2,0:T(8,128)(2,1)S(1)} %pad_maximum_fusion.2), channel_id=1, source_target_pairs={{0,1},{1,2},{2,3},{3,4},{4,5},{5,6},{6,7},{7,8},{8,9},{9,10},{10,1... | collective-permute-start | bytes 393224 | tf_op jit(solution)/shard_map/ppermute | solution.py:38
  33.7 15.4 %collective-permute-start.1 = (bf16[2,16,16,128]{3,1,2,0:T(8,128)(2,1)S(1)}, bf16[2,16,16,128]{3,1,2,0:T(8,128)(2,1)S(1)}, u32[]{:S(2)}, u32[]{:S(2)}) collective-permute-start(bf16[2,16,16,128]{3,1,2,0:T(8,128)(2,1)S(1)} %pad_maximum_fusion), channel_id=1, source_target_pairs={{0,1},{1,2},{2,3},{3,4},{4,5},{5,6},{6,7},{7,8},{8,9},{9,10},{10,1... | collective-permute-start | bytes 393224 | tf_op jit(solution)/shard_map/ppermute | solution.py:38
  37.7 14.2 %collective-permute-start.6 = (bf16[2,16,16,128]{3,1,2,0:T(8,128)(2,1)S(1)}, bf16[2,16,16,128]{3,1,2,0:T(8,128)(2,1)S(1)}, u32[]{:S(2)}, u32[]{:S(2)}) collective-permute-start(bf16[2,16,16,128]{3,1,2,0:T(8,128)(2,1)S(1)} %pad_maximum_fusion.3), channel_id=1, source_target_pairs={{1,0},{2,1},{3,2},{4,3},{5,4},{6,5},{7,6},{8,7},{9,8},{10,9},{11,1... | collective-permute-start | bytes 393224 | tf_op jit(solution)/shard_map/ppermute | solution.py:38
  41.9 15.3 %collective-permute-start.2 = (bf16[2,16,16,128]{3,1,2,0:T(8,128)(2,1)S(1)}, bf16[2,16,16,128]{3,1,2,0:T(8,128)(2,1)S(1)}, u32[]{:S(2)}, u32[]{:S(2)}) collective-permute-start(bf16[2,16,16,128]{3,1,2,0:T(8,128)(2,1)S(1)} %pad_maximum_fusion.1), channel_id=1, source_target_pairs={{1,0},{2,1},{3,2},{4,3},{5,4},{6,5},{7,6},{8,7},{9,8},{10,9},{11,1... | collective-permute-start | bytes 393224 | tf_op jit(solution)/shard_map/ppermute | solution.py:38
  46.9 19.3 %collective-permute-start.7 = (bf16[16,16,128]{2,0,1:T(8,128)(2,1)S(1)}, bf16[16,16,128]{2,0,1:T(8,128)(2,1)S(1)}, u32[]{:S(2)}, u32[]{:S(2)}) collective-permute-start(bf16[16,16,128]{2,0,1:T(8,128)(2,1)S(1)} %slice_bitcast_fusion.25), channel_id=1, source_target_pairs={{0,1},{1,2},{2,3},{3,4},{4,5},{5,6},{6,7},{7,8},{8,9},{9,10},{10,1... | collective-permute-start | bytes 196616 | tf_op jit(solution)/shard_map/ppermute | solution.py:38
  49.1 12.9 %collective-permute-start.3 = (bf16[16,16,128]{2,0,1:T(8,128)(2,1)S(1)}, bf16[16,16,128]{2,0,1:T(8,128)(2,1)S(1)}, u32[]{:S(2)}, u32[]{:S(2)}) collective-permute-start(bf16[16,16,128]{2,0,1:T(8,128)(2,1)S(1)} %slice_bitcast_fusion.29), channel_id=1, source_target_pairs={{0,1},{1,2},{2,3},{3,4},{4,5},{5,6},{6,7},{7,8},{8,9},{9,10},{10,1... | collective-permute-start | bytes 196616 | tf_op jit(solution)/shard_map/ppermute | solution.py:38
  51.9 14.3 %collective-permute-start.8 = (bf16[16,16,128]{2,0,1:T(8,128)(2,1)S(1)}, bf16[16,16,128]{2,0,1:T(8,128)(2,1)S(1)}, u32[]{:S(2)}, u32[]{:S(2)}) collective-permute-start(bf16[16,16,128]{2,0,1:T(8,128)(2,1)S(1)} %slice_bitcast_fusion.24), channel_id=1, source_target_pairs={{1,0},{2,1},{3,2},{4,3},{5,4},{6,5},{7,6},{8,7},{9,8},{10,9},{11,1... | collective-permute-start | bytes 196616 | tf_op jit(solution)/shard_map/ppermute | solution.py:38
  57.1 6.2 %collective-permute-start.4 = (bf16[16,16,128]{2,0,1:T(8,128)(2,1)S(1)}, bf16[16,16,128]{2,0,1:T(8,128)(2,1)S(1)}, u32[]{:S(2)}, u32[]{:S(2)}) collective-permute-start(bf16[16,16,128]{2,0,1:T(8,128)(2,1)S(1)} %slice_bitcast_fusion.28), channel_id=1, source_target_pairs={{1,0},{2,1},{3,2},{4,3},{5,4},{6,5},{7,6},{8,7},{9,8},{10,9},{11,1... | collective-permute-start | bytes 196616 | tf_op jit(solution)/shard_map/ppermute | solution.py:38
  68.9 8.8 %copy-start.15 = (f32[2,64,8,128]{3,2,1,0:T(8,128)S(1)}, f32[2,64,8,128]{3,2,1,0:T(8,128)}, u32[]{:S(2)}) copy-start(f32[2,64,8,128]{3,2,1,0:T(8,128)} %convolution_bitcast_fusion.14) | copy-start | bytes 1572868
  77.7 7.3 %copy-start.3 = (f32[16,64,128]{2,0,1:T(8,128)}, f32[16,64,128]{2,0,1:T(8,128)S(1)}, u32[]{:S(2)}) copy-start(f32[16,64,128]{2,0,1:T(8,128)S(1)} %fusion.1) | copy-start | bytes 1572868
  77.7 7.3 %copy-start.11 = (f32[16,64,128]{2,0,1:T(8,128)S(1)}, f32[16,64,128]{2,0,1:T(8,128)}, u32[]{:S(2)}) copy-start(f32[16,64,128]{2,0,1:T(8,128)} %copy-done.10) | copy-start | bytes 1572868
  85.0 0.8 copy-start.6
  85.8 0.8 copy-start.12
  89.4 9.6 %collective-permute-start.9 = (bf16[2,16,16,128]{3,1,2,0:T(8,128)(2,1)S(1)}, bf16[2,16,16,128]{3,1,2,0:T(8,128)(2,1)S(1)}, u32[]{:S(2)}, u32[]{:S(2)}) collective-permute-start(bf16[2,16,16,128]{3,1,2,0:T(8,128)(2,1)S(1)} %pad_maximum_fusion.4), channel_id=1, source_target_pairs={{0,1},{1,2},{2,3},{3,4},{4,5},{5,6},{6,7},{7,8},{8,9},{9,10},{10,1... | collective-permute-start | bytes 393224 | tf_op jit(solution)/shard_map/ppermute | solution.py:38
  91.3 9.5 %collective-permute-start.10 = (bf16[2,16,16,128]{3,1,2,0:T(8,128)(2,1)S(1)}, bf16[2,16,16,128]{3,1,2,0:T(8,128)(2,1)S(1)}, u32[]{:S(2)}, u32[]{:S(2)}) collective-permute-start(bf16[2,16,16,128]{3,1,2,0:T(8,128)(2,1)S(1)} %pad_maximum_fusion.5), channel_id=1, source_target_pairs={{1,0},{2,1},{3,2},{4,3},{5,4},{6,5},{7,6},{8,7},{9,8},{10,9},{11,1... | collective-permute-start | bytes 393224 | tf_op jit(solution)/shard_map/ppermute | solution.py:38
  98.9 8.3 %collective-permute-start.11 = (bf16[16,16,128]{2,0,1:T(8,128)(2,1)S(1)}, bf16[16,16,128]{2,0,1:T(8,128)(2,1)S(1)}, u32[]{:S(2)}, u32[]{:S(2)}) collective-permute-start(bf16[16,16,128]{2,0,1:T(8,128)(2,1)S(1)} %slice_bitcast_fusion.21), channel_id=1, source_target_pairs={{0,1},{1,2},{2,3},{3,4},{4,5},{5,6},{6,7},{7,8},{8,9},{9,10},{10,1... | collective-permute-start | bytes 196616 | tf_op jit(solution)/shard_map/ppermute | solution.py:38
  100.9 7.9 %collective-permute-start.12 = (bf16[16,16,128]{2,0,1:T(8,128)(2,1)S(1)}, bf16[16,16,128]{2,0,1:T(8,128)(2,1)S(1)}, u32[]{:S(2)}, u32[]{:S(2)}) collective-permute-start(bf16[16,16,128]{2,0,1:T(8,128)(2,1)S(1)} %slice_bitcast_fusion.20), channel_id=1, source_target_pairs={{1,0},{2,1},{3,2},{4,3},{5,4},{6,5},{7,6},{8,7},{9,8},{10,9},{11,1... | collective-permute-start | bytes 196616 | tf_op jit(solution)/shard_map/ppermute | solution.py:38
  110.9 7.3 %copy-start.4 = (f32[16,64,128]{2,0,1:T(8,128)S(1)}, f32[16,64,128]{2,0,1:T(8,128)}, u32[]{:S(2)}) copy-start(f32[16,64,128]{2,0,1:T(8,128)} %copy-done.3) | copy-start | bytes 1572868
  110.9 7.3 %copy-start.13 = (f32[16,64,128]{2,0,1:T(8,128)S(1)}, f32[16,64,128]{2,0,1:T(8,128)}, u32[]{:S(2)}) copy-start(f32[16,64,128]{2,0,1:T(8,128)} %copy-done.12) | copy-start | bytes 1572868
  121.2 9.3 %collective-permute-start.13 = (bf16[2,16,16,128]{3,1,2,0:T(8,128)(2,1)S(1)}, bf16[2,16,16,128]{3,1,2,0:T(8,128)(2,1)S(1)}, u32[]{:S(2)}, u32[]{:S(2)}) collective-permute-start(bf16[2,16,16,128]{3,1,2,0:T(8,128)(2,1)S(1)} %pad_maximum_fusion.6), channel_id=1, source_target_pairs={{0,1},{1,2},{2,3},{3,4},{4,5},{5,6},{6,7},{7,8},{8,9},{9,10},{10,1... | collective-permute-start | bytes 393224 | tf_op jit(solution)/shard_map/ppermute | solution.py:38
  123.1 9.3 %collective-permute-start.14 = (bf16[2,16,16,128]{3,1,2,0:T(8,128)(2,1)S(1)}, bf16[2,16,16,128]{3,1,2,0:T(8,128)(2,1)S(1)}, u32[]{:S(2)}, u32[]{:S(2)}) collective-permute-start(bf16[2,16,16,128]{3,1,2,0:T(8,128)(2,1)S(1)} %pad_maximum_fusion.7), channel_id=1, source_target_pairs={{1,0},{2,1},{3,2},{4,3},{5,4},{6,5},{7,6},{8,7},{9,8},{10,9},{11,1... | collective-permute-start | bytes 393224 | tf_op jit(solution)/shard_map/ppermute | solution.py:38
  130.5 8.3 %collective-permute-start.15 = (bf16[16,16,128]{2,0,1:T(8,128)(2,1)S(1)}, bf16[16,16,128]{2,0,1:T(8,128)(2,1)S(1)}, u32[]{:S(2)}, u32[]{:S(2)}) collective-permute-start(bf16[16,16,128]{2,0,1:T(8,128)(2,1)S(1)} %slice_bitcast_fusion.17), channel_id=1, source_target_pairs={{0,1},{1,2},{2,3},{3,4},{4,5},{5,6},{6,7},{7,8},{8,9},{9,10},{10,1... | collective-permute-start | bytes 196616 | tf_op jit(solution)/shard_map/ppermute | solution.py:38
  132.4 7.9 %collective-permute-start.16 = (bf16[16,16,128]{2,0,1:T(8,128)(2,1)S(1)}, bf16[16,16,128]{2,0,1:T(8,128)(2,1)S(1)}, u32[]{:S(2)}, u32[]{:S(2)}) collective-permute-start(bf16[16,16,128]{2,0,1:T(8,128)(2,1)S(1)} %slice_bitcast_fusion.16), channel_id=1, source_target_pairs={{1,0},{2,1},{3,2},{4,3},{5,4},{6,5},{7,6},{8,7},{9,8},{10,9},{11,1... | collective-permute-start | bytes 196616 | tf_op jit(solution)/shard_map/ppermute | solution.py:38
  143.1 8.8 %copy-start.5 = (f32[16,64,128]{2,0,1:T(8,128)S(1)}, f32[16,64,128]{2,0,1:T(8,128)}, u32[]{:S(2)}) copy-start(f32[16,64,128]{2,0,1:T(8,128)} %copy-done.3) | copy-start | bytes 1572868
  152.8 7.7 %collective-permute-start.17 = (f32[16,64,128]{2,0,1:T(8,128)}, f32[16,64,128]{2,0,1:T(8,128)}, u32[]{:S(2)}, u32[]{:S(2)}) collective-permute-start(f32[16,64,128]{2,0,1:T(8,128)} %get-tuple-element.10), channel_id=1, source_target_pairs={{0,32},{32,64},{64,96},{96,128},{128,160},{160,192},{192,224},{1,3... | collective-permute-start | bytes 1572872 | tf_op jit(solution)/shard_map/ppermute | solution.py:38
  160.9 0.8 copy-start.8
  168.9 17.5 %collective-permute-start.18 = (bf16[2,16,16,128]{3,1,2,0:T(8,128)(2,1)S(1)}, bf16[2,16,16,128]{3,1,2,0:T(8,128)(2,1)S(1)}, u32[]{:S(2)}, u32[]{:S(2)}) collective-permute-start(bf16[2,16,16,128]{3,1,2,0:T(8,128)(2,1)S(1)} %pad_maximum_fusion.8), channel_id=1, source_target_pairs={{0,1},{1,2},{2,3},{3,4},{4,5},{5,6},{6,7},{7,8},{8,9},{9,10},{10,1... | collective-permute-start | bytes 393224 | tf_op jit(solution)/shard_map/ppermute | solution.py:38
  170.9 17.5 %collective-permute-start.22 = (bf16[2,16,16,128]{3,1,2,0:T(8,128)(2,1)S(1)}, bf16[2,16,16,128]{3,1,2,0:T(8,128)(2,1)S(1)}, u32[]{:S(2)}, u32[]{:S(2)}) collective-permute-start(bf16[2,16,16,128]{3,1,2,0:T(8,128)(2,1)S(1)} %pad_maximum_fusion.10), channel_id=1, source_target_pairs={{0,1},{1,2},{2,3},{3,4},{4,5},{5,6},{6,7},{7,8},{8,9},{9,10},{10,1... | collective-permute-start | bytes 393224 | tf_op jit(solution)/shard_map/ppermute | solution.py:38
  175.2 15.2 %collective-permute-start.19 = (bf16[2,16,16,128]{3,1,2,0:T(8,128)(2,1)S(1)}, bf16[2,16,16,128]{3,1,2,0:T(8,128)(2,1)S(1)}, u32[]{:S(2)}, u32[]{:S(2)}) collective-permute-start(bf16[2,16,16,128]{3,1,2,0:T(8,128)(2,1)S(1)} %pad_maximum_fusion.9), channel_id=1, source_target_pairs={{1,0},{2,1},{3,2},{4,3},{5,4},{6,5},{7,6},{8,7},{9,8},{10,9},{11,1... | collective-permute-start | bytes 393224 | tf_op jit(solution)/shard_map/ppermute | solution.py:38
  181.1 15.3 %collective-permute-start.23 = (bf16[2,16,16,128]{3,1,2,0:T(8,128)(2,1)S(1)}, bf16[2,16,16,128]{3,1,2,0:T(8,128)(2,1)S(1)}, u32[]{:S(2)}, u32[]{:S(2)}) collective-permute-start(bf16[2,16,16,128]{3,1,2,0:T(8,128)(2,1)S(1)} %pad_maximum_fusion.11), channel_id=1, source_target_pairs={{1,0},{2,1},{3,2},{4,3},{5,4},{6,5},{7,6},{8,7},{9,8},{10,9},{11,1... | collective-permute-start | bytes 393224 | tf_op jit(solution)/shard_map/ppermute | solution.py:38
  186.4 18.9 %collective-permute-start.20 = (bf16[16,16,128]{2,0,1:T(8,128)(2,1)S(1)}, bf16[16,16,128]{2,0,1:T(8,128)(2,1)S(1)}, u32[]{:S(2)}, u32[]{:S(2)}) collective-permute-start(bf16[16,16,128]{2,0,1:T(8,128)(2,1)S(1)} %slice_bitcast_fusion.13), channel_id=1, source_target_pairs={{0,1},{1,2},{2,3},{3,4},{4,5},{5,6},{6,7},{7,8},{8,9},{9,10},{10,1... | collective-permute-start | bytes 196616 | tf_op jit(solution)/shard_map/ppermute | solution.py:38
  188.4 12.2 %collective-permute-start.24 = (bf16[16,16,128]{2,0,1:T(8,128)(2,1)S(1)}, bf16[16,16,128]{2,0,1:T(8,128)(2,1)S(1)}, u32[]{:S(2)}, u32[]{:S(2)}) collective-permute-start(bf16[16,16,128]{2,0,1:T(8,128)(2,1)S(1)} %slice_bitcast_fusion.9), channel_id=1, source_target_pairs={{0,1},{1,2},{2,3},{3,4},{4,5},{5,6},{6,7},{7,8},{8,9},{9,10},{10,1... | collective-permute-start | bytes 196616 | tf_op jit(solution)/shard_map/ppermute | solution.py:38
  190.4 15.0 %collective-permute-start.21 = (bf16[16,16,128]{2,0,1:T(8,128)(2,1)S(1)}, bf16[16,16,128]{2,0,1:T(8,128)(2,1)S(1)}, u32[]{:S(2)}, u32[]{:S(2)}) collective-permute-start(bf16[16,16,128]{2,0,1:T(8,128)(2,1)S(1)} %slice_bitcast_fusion.12), channel_id=1, source_target_pairs={{1,0},{2,1},{3,2},{4,3},{5,4},{6,5},{7,6},{8,7},{9,8},{10,9},{11,1... | collective-permute-start | bytes 196616 | tf_op jit(solution)/shard_map/ppermute | solution.py:38
  196.4 6.2 %collective-permute-start.25 = (bf16[16,16,128]{2,0,1:T(8,128)(2,1)S(1)}, bf16[16,16,128]{2,0,1:T(8,128)(2,1)S(1)}, u32[]{:S(2)}, u32[]{:S(2)}) collective-permute-start(bf16[16,16,128]{2,0,1:T(8,128)(2,1)S(1)} %slice_bitcast_fusion.8), channel_id=1, source_target_pairs={{1,0},{2,1},{3,2},{4,3},{5,4},{6,5},{7,6},{8,7},{9,8},{10,9},{11,1... | collective-permute-start | bytes 196616 | tf_op jit(solution)/shard_map/ppermute | solution.py:38
  208.1 8.9 %copy-start.2 = (bf16[512,16,128]{2,1,0:T(8,128)(2,1)S(1)}, bf16[512,16,128]{2,1,0:T(8,128)(2,1)}, u32[]{:S(2)}) copy-start(bf16[512,16,128]{2,1,0:T(8,128)(2,1)} %gather_fusion.25) | copy-start | bytes 6291460
  208.1 8.9 %copy-start.7 = (f32[16,64,128]{2,0,1:T(8,128)S(1)}, f32[16,64,128]{2,0,1:T(8,128)}, u32[]{:S(2)}) copy-start(f32[16,64,128]{2,0,1:T(8,128)} %copy-done.6) | copy-start | bytes 1572868
  208.1 8.9 %copy-start.9 = (f32[16,64,128]{2,0,1:T(8,128)S(1)}, f32[16,64,128]{2,0,1:T(8,128)}, u32[]{:S(2)}) copy-start(f32[16,64,128]{2,0,1:T(8,128)} %copy-done.8) | copy-start | bytes 1572868
  208.1 8.9 %copy-start.14 = (f32[2,64,8,128]{3,2,1,0:T(8,128)S(1)}, f32[2,64,8,128]{3,2,1,0:T(8,128)}, u32[]{:S(2)}) copy-start(f32[2,64,8,128]{3,2,1,0:T(8,128)} %convolution_bitcast_fusion.11) | copy-start | bytes 1572868
  217.0 10.0 %copy-start.21 = (pred[16]{0:T(512)(128)(4,1)S(1)}, pred[16]{0:T(512)(128)(4,1)}, u32[]{:S(2)}) copy-start(pred[16]{0:T(512)(128)(4,1)} %copy-done.20) | copy-start | bytes 52
  217.1 10.1 %copy-start.19 = (pred[16]{0:T(512)(128)(4,1)S(1)}, pred[16]{0:T(512)(128)(4,1)}, u32[]{:S(2)}) copy-start(pred[16]{0:T(512)(128)(4,1)} %copy-done.18) | copy-start | bytes 52
  217.1 10.2 %copy-start.17 = (pred[16]{0:T(512)(128)(4,1)S(1)}, pred[16]{0:T(512)(128)(4,1)}, u32[]{:S(2)}) copy-start(pred[16]{0:T(512)(128)(4,1)} %copy-done.16) | copy-start | bytes 52
  227.5 10.3 %collective-permute-start.26 = (bf16[2,16,16,128]{3,1,2,0:T(8,128)(2,1)S(1)}, bf16[2,16,16,128]{3,1,2,0:T(8,128)(2,1)S(1)}, u32[]{:S(2)}, u32[]{:S(2)}) collective-permute-start(bf16[2,16,16,128]{3,1,2,0:T(8,128)(2,1)S(1)} %pad_maximum_fusion.12), channel_id=1, source_target_pairs={{0,1},{1,2},{2,3},{3,4},{4,5},{5,6},{6,7},{7,8},{8,9},{9,10},{10,1... | collective-permute-start | bytes 393224 | tf_op jit(solution)/shard_map/ppermute | solution.py:38
  229.4 10.3 %collective-permute-start.27 = (bf16[2,16,16,128]{3,1,2,0:T(8,128)(2,1)S(1)}, bf16[2,16,16,128]{3,1,2,0:T(8,128)(2,1)S(1)}, u32[]{:S(2)}, u32[]{:S(2)}) collective-permute-start(bf16[2,16,16,128]{3,1,2,0:T(8,128)(2,1)S(1)} %pad_maximum_fusion.13), channel_id=1, source_target_pairs={{1,0},{2,1},{3,2},{4,3},{5,4},{6,5},{7,6},{8,7},{9,8},{10,9},{11,1... | collective-permute-start | bytes 393224 | tf_op jit(solution)/shard_map/ppermute | solution.py:38
  237.8 8.3 %collective-permute-start.28 = (bf16[16,16,128]{2,0,1:T(8,128)(2,1)S(1)}, bf16[16,16,128]{2,0,1:T(8,128)(2,1)S(1)}, u32[]{:S(2)}, u32[]{:S(2)}) collective-permute-start(bf16[16,16,128]{2,0,1:T(8,128)(2,1)S(1)} %slice_bitcast_fusion.5), channel_id=1, source_target_pairs={{0,1},{1,2},{2,3},{3,4},{4,5},{5,6},{6,7},{7,8},{8,9},{9,10},{10,1... | collective-permute-start | bytes 196616 | tf_op jit(solution)/shard_map/ppermute | solution.py:38
  239.7 7.9 %collective-permute-start.29 = (bf16[16,16,128]{2,0,1:T(8,128)(2,1)S(1)}, bf16[16,16,128]{2,0,1:T(8,128)(2,1)S(1)}, u32[]{:S(2)}, u32[]{:S(2)}) collective-permute-start(bf16[16,16,128]{2,0,1:T(8,128)(2,1)S(1)} %slice_bitcast_fusion.4), channel_id=1, source_target_pairs={{1,0},{2,1},{3,2},{4,3},{5,4},{6,5},{7,6},{8,7},{9,8},{10,9},{11,1... | collective-permute-start | bytes 196616 | tf_op jit(solution)/shard_map/ppermute | solution.py:38
  262.6 9.3 %collective-permute-start.30 = (bf16[2,16,16,128]{3,1,2,0:T(8,128)(2,1)S(1)}, bf16[2,16,16,128]{3,1,2,0:T(8,128)(2,1)S(1)}, u32[]{:S(2)}, u32[]{:S(2)}) collective-permute-start(bf16[2,16,16,128]{3,1,2,0:T(8,128)(2,1)S(1)} %pad_maximum_fusion.14), channel_id=1, source_target_pairs={{0,1},{1,2},{2,3},{3,4},{4,5},{5,6},{6,7},{7,8},{8,9},{9,10},{10,1... | collective-permute-start | bytes 393224 | tf_op jit(solution)/shard_map/ppermute | solution.py:38
  264.5 9.3 %collective-permute-start.31 = (bf16[2,16,16,128]{3,1,2,0:T(8,128)(2,1)S(1)}, bf16[2,16,16,128]{3,1,2,0:T(8,128)(2,1)S(1)}, u32[]{:S(2)}, u32[]{:S(2)}) collective-permute-start(bf16[2,16,16,128]{3,1,2,0:T(8,128)(2,1)S(1)} %pad_maximum_fusion.15), channel_id=1, source_target_pairs={{1,0},{2,1},{3,2},{4,3},{5,4},{6,5},{7,6},{8,7},{9,8},{10,9},{11,1... | collective-permute-start | bytes 393224 | tf_op jit(solution)/shard_map/ppermute | solution.py:38
  271.9 8.3 %collective-permute-start.32 = (bf16[16,16,128]{2,0,1:T(8,128)(2,1)S(1)}, bf16[16,16,128]{2,0,1:T(8,128)(2,1)S(1)}, u32[]{:S(2)}, u32[]{:S(2)}) collective-permute-start(bf16[16,16,128]{2,0,1:T(8,128)(2,1)S(1)} %slice_bitcast_fusion.1), channel_id=1, source_target_pairs={{0,1},{1,2},{2,3},{3,4},{4,5},{5,6},{6,7},{7,8},{8,9},{9,10},{10,1... | collective-permute-start | bytes 196616 | tf_op jit(solution)/shard_map/ppermute | solution.py:38
  273.8 7.9 %collective-permute-start.33 = (bf16[16,16,128]{2,0,1:T(8,128)(2,1)S(1)}, bf16[16,16,128]{2,0,1:T(8,128)(2,1)S(1)}, u32[]{:S(2)}, u32[]{:S(2)}) collective-permute-start(bf16[16,16,128]{2,0,1:T(8,128)(2,1)S(1)} %slice_bitcast_fusion), channel_id=1, source_target_pairs={{1,0},{2,1},{3,2},{4,3},{5,4},{6,5},{7,6},{8,7},{9,8},{10,9},{11,1... | collective-permute-start | bytes 196616 | tf_op jit(solution)/shard_map/ppermute | solution.py:38
where the time goes:
time: 299 us; the launch traced here: 294 us
  starting transfers between devices  126 us (42%)
  matrix products  75.1 us (25%)
  local copies, waits for them, and re-layouts  70.9 us (24%)
  waiting for transfers between devices  11.3 us (4%)
  other arithmetic  9.76 us (3%)
    ppermute x34, starting transfers between devices, shifted(): return lax.ppermute(block, axis, route)  126 us
    dot_general x8, matrix products, operate(): jnp.einsum('sbtc,btcd->sbd', picked, stack, preferred_element_type=jnp.fl...  66.2 us
    gather x32, local copies, waits for them, and re-layouts, pack_rows(): taken = blocks[:, jnp.maximum(rows, 0), :]  23.8 us
    gather x8, local copies, waits for them, and re-layouts, operate(): picked = extended[:, columns, :]  20.6 us
    gather x1, local copies, waits for them, and re-layouts, per_device(): stack = coeffs[coef_index]  16.2 us
    ppermute x34, waiting for transfers between devices, shifted(): return lax.ppermute(block, axis, route)  11.3 us
    dot_general x8, matrix products, operate(): jnp.dot(mixing, jnp.tanh(field).reshape(species, -1), precision=lax.Preci...  8.92 us
    unnamed x84, local copies, waits for them, and re-layouts  8.09 us
  transfers between devices with their start and end apart: 34, of which 12 were waited for; matrix products, arithmetic and copies ran while one was open for 15% of the time, Pallas kernels for 0%

commit v1 on v0

v1 whole, which is shorter than its diff:
```python
import functools
import math

import jax
import jax.numpy as jnp
from jax import lax
from jax.experimental import pallas as pl
from jax.experimental.pallas import tpu as pltpu
from jax.sharding import PartitionSpec as P

SWEEPS = 2

step_size = 0.3
root_six = math.sqrt(6.0)
node_times = ((4.0 - root_six) / 10.0, (4.0 + root_six) / 10.0, 1.0)
radau_rows = (
    (
        (88.0 - 7.0 * root_six) / 360.0,
        (296.0 - 169.0 * root_six) / 1800.0,
        (-2.0 + 3.0 * root_six) / 225.0,
    ),
    (
        (296.0 + 169.0 * root_six) / 1800.0,
        (88.0 + 7.0 * root_six) / 360.0,
        (-2.0 - 3.0 * root_six) / 225.0,
    ),
    ((16.0 - root_six) / 36.0, (16.0 + root_six) / 36.0, 1.0 / 9.0),
)
node_gaps = (node_times[0], node_times[1] - node_times[0], node_times[2] - node_times[1])
node_integrals = (
    radau_rows[0],
    tuple((radau_rows[1][j] - radau_rows[0][j] for j in range(3))),
    tuple((radau_rows[2][j] - radau_rows[1][j] for j in range(3))),
)

f32 = jnp.float32
bf16 = jnp.bfloat16
VMEM = pl.BlockSpec(memory_space=pltpu.VMEM)
SMEM = pl.BlockSpec(memory_space=pltpu.SMEM)
PARAMS = pltpu.CompilerParams(vmem_limit_bytes=32 * 1024 * 1024)
UNROLL = 16


def pairing(slices, parts, distance, late):
    route = []
    for a in range(slices):
        for p in range(parts):
            ahead = ((p // distance) % 2 == 0) != late
            q = p + distance if ahead else p - distance
            b, q = (a, q) if 0 <= q < parts else (a ^ 1, p)
            route.append((a * parts + p, b * parts + q))
    return route


def swap(block, distance, late):
    route = pairing(lax.axis_size("tm"), lax.axis_size("space"), distance, late)
    return lax.ppermute(block, ("tm", "space"), route)


def next_slice(block):
    n = lax.axis_size("tm")
    return lax.ppermute(block, "tm", [(i, (i + 1) % n) for i in range(n)])


PAIRS = ((2, True), (2, False), (1, True), (1, False))


def exchange(packs):
    return tuple(swap(x, d, late) for x, (d, late) in zip(packs, PAIRS))


def plan():
    p = lax.axis_index("space")
    n = lax.axis_size("space")
    sends, fills, valid = [], [], []
    for distance, late in PAIRS:
        base = 0 if distance == 1 else 2
        ahead = ((p // distance) % 2 == 0) != late
        q = jnp.where(ahead, p + distance, p - distance)
        sends.append(jnp.where(ahead, base, base + 1))
        fills.append(jnp.where(ahead, base + 1, base))
        valid.append((q >= 0) & (q < n))
    leading = lax.axis_index("tm") == 0
    return jnp.stack([x.astype(jnp.int32) for x in sends + fills + valid + [leading]])


def pack(flags, lists, vb, packs):
    slots = packs[0].shape[0]
    for k, out in enumerate(packs):
        base = flags[k] * slots
        for j in range(slots):
            row = lists[base + j]
            block = vb[jnp.maximum(row, 0)]
            out[j] = jnp.where(row >= 0, block, jnp.zeros_like(block))


def first_kernel(flags, lists, u, vb, *packs):
    vb[...] = u[...].astype(bf16)
    pack(flags, lists, vb, packs)


def force_kernel(update, extras, keep, send, flags, lists, cols, cidx, u, vb, *refs):
    received, refs = refs[:4], refs[4:]
    coeffs, mix, refs = refs[0], refs[1], refs[2:]
    olds, refs = refs[:extras], refs[extras:]
    outs, ext = refs[:-1], refs[-1]
    nblocks = u.shape[0]
    slots = received[0].shape[0]
    terms = cols.shape[0] // nblocks
    ext[0:nblocks] = vb[...]
    for k, got in enumerate(received):
        live = flags[8 + k] > 0
        block = got[...]
        ext[pl.ds(nblocks + flags[4 + k] * slots, slots)] = jnp.where(live, block, jnp.zeros_like(block))
    mixv = mix[...]

    def body(i, carry):
        for j in range(UNROLL):
            b = i * UNROLL + j
            xs = [ext[cols[b * terms + t]] for t in range(terms)]
            ws = [coeffs[cidx[b * terms + t]] for t in range(terms)]
            field = u[b]
            th = jnp.tanh(field)
            hi = th.astype(bf16)
            lo = (th - hi.astype(f32)).astype(bf16)
            force = jnp.dot(
                jnp.concatenate(xs, axis=1), jnp.concatenate(ws, axis=0), preferred_element_type=f32
            )
            force += jnp.dot(mixv, jnp.concatenate([hi, hi, lo], axis=0), preferred_element_type=f32)
            at = 0
            if keep:
                outs[at][b] = force
                at += 1
            if update is None:
                outs[at][b] = force.astype(bf16)
                continue
            new = update(field, force, [old[b] for old in olds])
            outs[at][b] = new
            if send:
                outs[at + 1][b] = new.astype(bf16)
        return carry

    lax.fori_loop(0, nblocks // UNROLL, body, 0)
    if send:
        pack(flags, lists, outs[-5], outs[-4:])


def early_kernel(flags, lists, guess, incoming, force, moved, e0, u, vb, *packs):
    leading = flags[12] > 0
    g, q = node_gaps[0], sum(node_integrals[0])

    def body(b, carry):
        f = force[b]
        start = jnp.where(leading, guess[b], incoming[b])
        e = jnp.where(leading, f, moved[b].astype(f32))
        e0[b] = e
        new = start + step_size * (g * (e - f) + q * f)
        u[b] = new
        vb[b] = new.astype(bf16)
        return carry

    lax.fori_loop(0, u.shape[0], body, 0, unroll=8)
    pack(flags, lists, vb, packs)


def late_kernel(flags, lists, guess, incoming, moved, e0, e1, e2, e3, u, vb, *packs):
    leading = flags[12] > 0
    g, q = node_gaps[0], node_integrals[0]

    def body(b, carry):
        f = e0[b]
        start = jnp.where(leading, guess[b], incoming[b])
        e = jnp.where(leading, f, moved[b].astype(f32))
        quad = q[0] * e1[b] + q[1] * e2[b] + q[2] * e3[b]
        new = start + step_size * (g * (e - f) + quad)
        u[b] = new
        vb[b] = new.astype(bf16)
        return carry

    lax.fori_loop(0, u.shape[0], body, 0, unroll=8)
    pack(flags, lists, vb, packs)


def node_update_first(node):
    g, q = node_gaps[node], sum(node_integrals[node])

    def update(u, e, olds):
        (f,) = olds
        return u + step_size * (g * (e - f) + q * f)

    return update


def node_update_second(node):
    g, q = node_gaps[node], node_integrals[node]

    def update(u, e, olds):
        quad = q[0] * olds[0] + q[1] * olds[1] + q[2] * olds[2]
        return u + step_size * (g * (e - olds[node - 1]) + quad)

    return update


def per_device(guess, coeffs, coef_index, neighbours, send_lists, mixing):
    first = jnp.transpose(guess[0], (1, 0, 2))
    nblocks, species, cells = first.shape
    slots = send_lists.shape[1]
    own_rows = lax.broadcasted_iota(jnp.int32, (nblocks, 1), 0)
    cols = jnp.concatenate([own_rows, neighbours], axis=1).reshape(-1)
    cidx = coef_index.reshape(-1)
    lists = send_lists.reshape(-1)
    flags = plan()
    mix_hi = mixing.astype(bf16)
    mix_lo = (mixing - mix_hi.astype(f32)).astype(bf16)
    mix = jnp.concatenate([mix_hi, mix_lo, mix_hi], axis=1)

    state = jax.ShapeDtypeStruct((nblocks, species, cells), f32)
    rounded = jax.ShapeDtypeStruct((nblocks, species, cells), bf16)
    rim = jax.ShapeDtypeStruct((slots, species, cells), bf16)

    def call(kernel, outs, scalars, arrays, scratch=()):
        return pl.pallas_call(
            kernel,
            out_shape=outs,
            in_specs=[SMEM] * len(scalars) + [VMEM] * len(arrays),
            out_specs=[VMEM] * len(outs),
            scratch_shapes=scratch,
            compiler_params=PARAMS,
        )(*scalars, *arrays)

    ext = [pltpu.VMEM((nblocks + 4 * slots, species, cells), bf16)]

    def force(u, vb, received, update, olds, keep, send):
        outs = []
        if keep:
            outs.append(state)
        if update is None:
            outs.append(rounded)
        else:
            outs.append(state)
        if send:
            outs += [rounded] + [rim] * 4
        kernel = functools.partial(force_kernel, update, len(olds), keep, send)
        return call(
            kernel, outs, (flags, lists, cols, cidx), (u, vb, *received, coeffs, mix, *olds), ext
        )

    vb, *packs = call(first_kernel, [rounded] + [rim] * 4, (flags, lists), (first,))
    received = exchange(packs)
    came = next_slice(first)
    f, fb = force(first, vb, received, None, (), True, False)
    e0, u, vb, *packs = call(
        early_kernel,
        [state, state, rounded] + [rim] * 4,
        (flags, lists),
        (first, came, f, next_slice(fb)),
    )
    e1, u, vb, *packs = force(u, vb, exchange(packs), node_update_first(1), (f,), True, True)
    e2, u, vb, *packs = force(u, vb, exchange(packs), node_update_first(2), (f,), True, True)
    received = exchange(packs)
    came = next_slice(u)
    e3, e3b = force(u, vb, received, None, (), True, False)
    u, vb, *packs = call(
        late_kernel,
        [state, rounded] + [rim] * 4,
        (flags, lists),
        (first, came, next_slice(e3b), e0, e1, e2, e3),
    )
    olds = (e1, e2, e3)
    u, vb, *packs = force(u, vb, exchange(packs), node_update_second(1), olds, False, True)
    (end,) = force(u, vb, exchange(packs), node_update_second(2), olds, False, False)
    return jnp.transpose(end, (1, 0, 2))[None]


def solution(mesh):
    placed = (
        P("tm", None, "space", None),
        P(),
        P("space", None),
        P("space", None),
        P("space", None),
        P(),
    )
    return jax.shard_map(
        per_device,
        mesh=mesh,
        in_specs=placed,
        out_specs=P("tm", None, "space", None),
        check_vma=False,
    )
```

time: 299 us -> 110 us (0.37); the launches traced: 294 us -> 109 us
  starting transfers between devices: 126 us -> 37.9 us
  matrix products: 75.1 us -> 0 us
  local copies, waits for them, and re-layouts: 70.9 us -> 6.4 us
  waiting for transfers between devices: 11.3 us -> 38 us
  Pallas kernels: 0 us -> 25.4 us
  other arithmetic: 9.76 us -> 1.55 us
    ppermute x34 -> x28, starting transfers between devices: 126 us -> 37.9 us  [the longest x24 37.7 us: swap(): return lax.ppermute(block, ('tm', 'space'), route)]
    dot_general x16 -> x0, matrix products: 75.1 us -> none  [the longest x8 66.2 us: operate(): jnp.einsum('sbtc,btcd->sbd', picked, stack, preferred_element_type=jnp.fl...]
    gather x41 -> x0, local copies, waits for them, and re-layouts: 60.6 us -> none  [the longest x32 23.8 us: pack_rows(): taken = blocks[:, jnp.maximum(rows, 0), :]]
    ppermute x34 -> x28, waiting for transfers between devices: 11.3 us -> 38 us  [the longest x24 24 us: swap(): return lax.ppermute(block, ('tm', 'space'), route)]
    pallas_call x0 -> x9, Pallas kernels: none -> 25.4 us  [call(): pl.pallas_call(kernel, out_shape=outs, in_specs=[SMEM] * len(scalars) + [...]
    select_n x26 -> x0, other arithmetic: 5.5 us -> none  [the longest x24 5.49 us: pack_rows(): return jnp.where(live[None, :, None], taken, jnp.zeros((), blocks.dtype))]
    unnamed x10 -> x0, other arithmetic: 3.96 us -> none
    unnamed x84 -> x6, local copies, waits for them, and re-layouts: 8.09 us -> 4.31 us
  transfers between devices with their start and end apart: 34 -> 28, of which waited for: 12 -> 15; matrix products, arithmetic and copies ran while one was open for 15% -> 3% of each run, Pallas kernels for 0% -> 7%
where the time goes in v1:
time: 110 us; the launch traced here: 109 us
  waiting for transfers between devices  38 us (35%)
  starting transfers between devices  37.9 us (34%)
  Pallas kernels  25.4 us (23%)
  local copies, waits for them, and re-layouts  6.4 us (6%)
  other arithmetic  1.55 us (1%)
    ppermute x24, starting transfers between devices, swap(): return lax.ppermute(block, ('tm', 'space'), route)  37.7 us
    pallas_call x9, Pallas kernels, call(): pl.pallas_call(kernel, out_shape=outs, in_specs=[SMEM] * len(scalars) + [...  25.4 us
    ppermute x24, waiting for transfers between devices, swap(): return lax.ppermute(block, ('tm', 'space'), route)  24 us
    ppermute x4, waiting for transfers between devices, next_slice(): return lax.ppermute(block, 'tm', [(i, (i + 1) % n) for i in range(n)])  13.9 us
    unnamed x6, local copies, waits for them, and re-layouts  4.31 us
  transfers between devices with their start and end apart: 28, of which 15 were waited for; matrix products, arithmetic and copies ran while one was open for 3% of the time, Pallas kernels for 7%

profile of v1, /device:TPU:8, one launch (start us, length us, event | category | flops | bytes accessed | tf_op | source)
XLA Modules:
  0.0 109.4 jit_solution(5251445325159309610)
XLA Ops:
  0.0 1.3 %copy.14 = f32[1,16,64,128]{3,1,2,0:T(8,128)S(1)} copy(f32[1,16,64,128]{3,2,1,0:T(8,128)} %param.6) | data formatting | bytes 1048576 | tf_op args[0]
  1.4 0.0 collective-permute-start
  1.5 0.8 reshape.9.lists
  2.2 0.1 stack.75.flags
  2.3 0.7 shard_map.64
  3.1 6.3 %collective-permute-start.1 = (bf16[16,16,128]{2,1,0:T(8,128)(2,1)S(1)}, bf16[16,16,128]{2,1,0:T(8,128)(2,1)S(1)}, u32[]{:S(2)}, u32[]{:S(2)}) collective-permute-start(bf16[16,16,128]{2,1,0:T(8,128)(2,1)S(1)} %get-tuple-element.48), channel_id=1, source_target_pairs={{0,32},{1,33},{2,4},{3,5},{4,2},{5,3},{6,8},{7,9},{8,6},{9,7},{10,... | collective-permute-start | bytes 196616 | tf_op jit(solution)/shard_map/ppermute | solution.py:57
  9.3 1.6 %collective-permute-start.2 = (bf16[16,16,128]{2,1,0:T(8,128)(2,1)S(1)}, bf16[16,16,128]{2,1,0:T(8,128)(2,1)S(1)}, u32[]{:S(2)}, u32[]{:S(2)}) collective-permute-start(bf16[16,16,128]{2,1,0:T(8,128)(2,1)S(1)} %get-tuple-element.49), channel_id=1, source_target_pairs={{0,2},{1,3},{2,0},{3,1},{4,6},{5,7},{6,4},{7,5},{8,10},{9,11},{10,... | collective-permute-start | bytes 196616 | tf_op jit(solution)/shard_map/ppermute | solution.py:57
  10.9 1.9 %collective-permute-start.4 = (bf16[16,16,128]{2,1,0:T(8,128)(2,1)S(1)}, bf16[16,16,128]{2,1,0:T(8,128)(2,1)S(1)}, u32[]{:S(2)}, u32[]{:S(2)}) collective-permute-start(bf16[16,16,128]{2,1,0:T(8,128)(2,1)S(1)} %get-tuple-element.51), channel_id=1, source_target_pairs={{0,1},{1,0},{2,3},{3,2},{4,5},{5,4},{6,7},{7,6},{8,9},{9,8},{10,11... | collective-permute-start | bytes 196616 | tf_op jit(solution)/shard_map/ppermute | solution.py:57
  12.8 0.7 pad_add_fusion
  13.5 0.1 copy.9
  13.6 0.1 reshape.10.cols
  13.7 0.8 copy.10
  14.5 0.1 reshape.11.cidx
  14.6 0.8 subtract_convert_fusion
  15.4 0.1 pad_maximum_fusion.refs_5_
  15.4 1.0 collective-permute-done.2.refs_1_
  16.4 1.5 %collective-permute-done.3.refs_2_ = bf16[16,16,128]{2,1,0:T(8,128)(2,1)S(1)} collective-permute-done((bf16[16,16,128]{2,1,0:T(8,128)(2,1)S(1)}, bf16[16,16,128]{2,1,0:T(8,128)(2,1)S(1)}, u32[]{:S(2)}, u32[]{:S(2)}) %collective-permute-start.3) | collective-permute-done | bytes 65568 | tf_op jit(solution)/shard_map/ppermute | solution.py:57
  18.0 2.2 %copy-done = bf16[128,128,128]{2,1,0:T(8,128)(2,1)S(1)} copy-done((bf16[128,128,128]{2,1,0:T(8,128)(2,1)S(1)}, bf16[128,128,128]{2,1,0:T(8,128)(2,1)}, u32[]{:S(2)}) %copy-start) | copy-done | bytes 4194328
  20.1 3.6 %shard_map.65 = (f32[64,16,128]{2,1,0:T(8,128)S(1)}, bf16[64,16,128]{2,1,0:T(8,128)(2,1)S(1)}) custom-call(s32[13]{0:T(128)S(1)} %stack.75.flags, s32[64]{0:T(128)S(1)} %reshape.9.lists, s32[512]{0:T(512)S(1)} %reshape.10.cols, s32[512]{0:T(512)S(1)} %reshape.11.cidx, f32[64,16,128]{2,1,0:T(8,128)S(1)} %bitcast.23, ...), custom_call_target="tpu_custom_call" | custom-call | tf_op jit(solution)/shard_map/pallas_call | solution.py:222
  23.8 0.1 collective-permute-start.5
  23.9 6.9 %collective-permute-done.5.moved = bf16[64,16,128]{2,1,0:T(8,128)(2,1)S(1)} collective-permute-done((bf16[64,16,128]{2,1,0:T(8,128)(2,1)S(1)}, bf16[64,16,128]{2,1,0:T(8,128)(2,1)S(1)}, u32[]{:S(2)}, u32[]{:S(2)}) %collective-permute-start.5) | collective-permute-done | bytes 262176 | tf_op jit(solution)/shard_map/ppermute | solution.py:62
  30.8 0.9 shard_map.66
  31.7 1.6 %collective-permute-start.6 = (bf16[16,16,128]{2,1,0:T(8,128)(2,1)S(1)}, bf16[16,16,128]{2,1,0:T(8,128)(2,1)S(1)}, u32[]{:S(2)}, u32[]{:S(2)}) collective-permute-start(bf16[16,16,128]{2,1,0:T(8,128)(2,1)S(1)} %get-tuple-element.56), channel_id=1, source_target_pairs={{0,32},{1,33},{2,4},{3,5},{4,2},{5,3},{6,8},{7,9},{8,6},{9,7},{10,... | collective-permute-start | bytes 196616 | tf_op jit(solution)/shard_map/ppermute | solution.py:57
  33.3 1.2 %collective-permute-start.7 = (bf16[16,16,128]{2,1,0:T(8,128)(2,1)S(1)}, bf16[16,16,128]{2,1,0:T(8,128)(2,1)S(1)}, u32[]{:S(2)}, u32[]{:S(2)}) collective-permute-start(bf16[16,16,128]{2,1,0:T(8,128)(2,1)S(1)} %get-tuple-element.57), channel_id=1, source_target_pairs={{0,2},{1,3},{2,0},{3,1},{4,6},{5,7},{6,4},{7,5},{8,10},{9,11},{10,... | collective-permute-start | bytes 196616 | tf_op jit(solution)/shard_map/ppermute | solution.py:57
  34.5 1.3 %collective-permute-start.8 = (bf16[16,16,128]{2,1,0:T(8,128)(2,1)S(1)}, bf16[16,16,128]{2,1,0:T(8,128)(2,1)S(1)}, u32[]{:S(2)}, u32[]{:S(2)}) collective-permute-start(bf16[16,16,128]{2,1,0:T(8,128)(2,1)S(1)} %get-tuple-element.58), channel_id=1, source_target_pairs={{0,32},{1,2},{2,1},{3,4},{4,3},{5,6},{6,5},{7,8},{8,7},{9,10},{10,... | collective-permute-start | bytes 196616 | tf_op jit(solution)/shard_map/ppermute | solution.py:57
  35.8 1.0 collective-permute-start.9
  36.8 2.4 %collective-permute-done.6.refs_0_ = bf16[16,16,128]{2,1,0:T(8,128)(2,1)S(1)} collective-permute-done((bf16[16,16,128]{2,1,0:T(8,128)(2,1)S(1)}, bf16[16,16,128]{2,1,0:T(8,128)(2,1)S(1)}, u32[]{:S(2)}, u32[]{:S(2)}) %collective-permute-start.6) | collective-permute-done | bytes 65568 | tf_op jit(solution)/shard_map/ppermute | solution.py:57
  39.1 1.7 %collective-permute-done.8.refs_2_ = bf16[16,16,128]{2,1,0:T(8,128)(2,1)S(1)} collective-permute-done((bf16[16,16,128]{2,1,0:T(8,128)(2,1)S(1)}, bf16[16,16,128]{2,1,0:T(8,128)(2,1)S(1)}, u32[]{:S(2)}, u32[]{:S(2)}) %collective-permute-start.8) | collective-permute-done | bytes 65568 | tf_op jit(solution)/shard_map/ppermute | solution.py:57
  40.9 0.0 collective-permute-done.9.refs_3_
  40.9 3.9 %shard_map.67 = (f32[64,16,128]{2,1,0:T(8,128)S(1)}, f32[64,16,128]{2,1,0:T(8,128)S(1)}, bf16[64,16,128]{2,1,0:T(8,128)(2,1)S(1)}, bf16[16,16,128]{2,1,0:T(8,128...) custom-call(s32[13]{0:T(128)S(1)} %stack.75.flags, ...), custom_call_target="tpu_custom_call" | custom-call | tf_op jit(solution)/shard_map/pallas_call | solution.py:222
  44.7 2.2 %collective-permute-start.10 = (bf16[16,16,128]{2,1,0:T(8,128)(2,1)S(1)}, bf16[16,16,128]{2,1,0:T(8,128)(2,1)S(1)}, u32[]{:S(2)}, u32[]{:S(2)}) collective-permute-start(bf16[16,16,128]{2,1,0:T(8,128)(2,1)S(1)} %get-tuple-element.62), channel_id=1, source_target_pairs={{0,32},{1,33},{2,4},{3,5},{4,2},{5,3},{6,8},{7,9},{8,6},{9,7},{10,... | collective-permute-start | bytes 196616 | tf_op jit(solution)/shard_map/ppermute | solution.py:57
  46.9 2.4 %collective-permute-start.11 = (bf16[16,16,128]{2,1,0:T(8,128)(2,1)S(1)}, bf16[16,16,128]{2,1,0:T(8,128)(2,1)S(1)}, u32[]{:S(2)}, u32[]{:S(2)}) collective-permute-start(bf16[16,16,128]{2,1,0:T(8,128)(2,1)S(1)} %get-tuple-element.63), channel_id=1, source_target_pairs={{0,2},{1,3},{2,0},{3,1},{4,6},{5,7},{6,4},{7,5},{8,10},{9,11},{10,... | collective-permute-start | bytes 196616 | tf_op jit(solution)/shard_map/ppermute | solution.py:57
  49.3 1.9 %collective-permute-start.12 = (bf16[16,16,128]{2,1,0:T(8,128)(2,1)S(1)}, bf16[16,16,128]{2,1,0:T(8,128)(2,1)S(1)}, u32[]{:S(2)}, u32[]{:S(2)}) collective-permute-start(bf16[16,16,128]{2,1,0:T(8,128)(2,1)S(1)} %get-tuple-element.64), channel_id=1, source_target_pairs={{0,32},{1,2},{2,1},{3,4},{4,3},{5,6},{6,5},{7,8},{8,7},{9,10},{10,... | collective-permute-start | bytes 196616 | tf_op jit(solution)/shard_map/ppermute | solution.py:57
  51.2 2.0 %collective-permute-done.10.refs_0_ = bf16[16,16,128]{2,1,0:T(8,128)(2,1)S(1)} collective-permute-done((bf16[16,16,128]{2,1,0:T(8,128)(2,1)S(1)}, bf16[16,16,128]{2,1,0:T(8,128)(2,1)S(1)}, u32[]{:S(2)}, u32[]{:S(2)}) %collective-permute-start.10) | collective-permute-done | bytes 65568 | tf_op jit(solution)/shard_map/ppermute | solution.py:57
  53.3 2.4 %collective-permute-done.12.refs_2_ = bf16[16,16,128]{2,1,0:T(8,128)(2,1)S(1)} collective-permute-done((bf16[16,16,128]{2,1,0:T(8,128)(2,1)S(1)}, bf16[16,16,128]{2,1,0:T(8,128)(2,1)S(1)}, u32[]{:S(2)}, u32[]{:S(2)}) %collective-permute-start.12) | collective-permute-done | bytes 65568 | tf_op jit(solution)/shard_map/ppermute | solution.py:57
  55.7 3.9 %shard_map.68 = (f32[64,16,128]{2,1,0:T(8,128)S(1)}, f32[64,16,128]{2,1,0:T(8,128)S(1)}, bf16[64,16,128]{2,1,0:T(8,128)(2,1)S(1)}, bf16[16,16,128]{2,1,0:T(8,128...) custom-call(s32[13]{0:T(128)S(1)} %stack.75.flags, ...), custom_call_target="tpu_custom_call" | custom-call | tf_op jit(solution)/shard_map/pallas_call | solution.py:222
  59.6 0.0 collective-permute-start.14
  59.6 1.6 %collective-permute-start.15 = (bf16[16,16,128]{2,1,0:T(8,128)(2,1)S(1)}, bf16[16,16,128]{2,1,0:T(8,128)(2,1)S(1)}, u32[]{:S(2)}, u32[]{:S(2)}) collective-permute-start(bf16[16,16,128]{2,1,0:T(8,128)(2,1)S(1)} %get-tuple-element.68), channel_id=1, source_target_pairs={{0,32},{1,33},{2,4},{3,5},{4,2},{5,3},{6,8},{7,9},{8,6},{9,7},{10,... | collective-permute-start | bytes 196616 | tf_op jit(solution)/shard_map/ppermute | solution.py:57
  61.2 1.2 %collective-permute-start.16 = (bf16[16,16,128]{2,1,0:T(8,128)(2,1)S(1)}, bf16[16,16,128]{2,1,0:T(8,128)(2,1)S(1)}, u32[]{:S(2)}, u32[]{:S(2)}) collective-permute-start(bf16[16,16,128]{2,1,0:T(8,128)(2,1)S(1)} %get-tuple-element.69), channel_id=1, source_target_pairs={{0,2},{1,3},{2,0},{3,1},{4,6},{5,7},{6,4},{7,5},{8,10},{9,11},{10,... | collective-permute-start | bytes 196616 | tf_op jit(solution)/shard_map/ppermute | solution.py:57
  62.4 1.9 %collective-permute-start.17 = (bf16[16,16,128]{2,1,0:T(8,128)(2,1)S(1)}, bf16[16,16,128]{2,1,0:T(8,128)(2,1)S(1)}, u32[]{:S(2)}, u32[]{:S(2)}) collective-permute-start(bf16[16,16,128]{2,1,0:T(8,128)(2,1)S(1)} %get-tuple-element.70), channel_id=1, source_target_pairs={{0,32},{1,2},{2,1},{3,4},{4,3},{5,6},{6,5},{7,8},{8,7},{9,10},{10,... | collective-permute-start | bytes 196616 | tf_op jit(solution)/shard_map/ppermute | solution.py:57
  64.3 0.4 collective-permute-start.18
  64.6 3.5 %collective-permute-done.15.refs_0_ = bf16[16,16,128]{2,1,0:T(8,128)(2,1)S(1)} collective-permute-done((bf16[16,16,128]{2,1,0:T(8,128)(2,1)S(1)}, bf16[16,16,128]{2,1,0:T(8,128)(2,1)S(1)}, u32[]{:S(2)}, u32[]{:S(2)}) %collective-permute-start.15) | collective-permute-done | bytes 65568 | tf_op jit(solution)/shard_map/ppermute | solution.py:57
  68.2 0.1 collective-permute-done.16.refs_1_
  68.3 0.8 collective-permute-done.17.refs_2_
  69.1 0.0 collective-permute-done.18.refs_3_
  69.1 3.6 %shard_map.69 = (f32[64,16,128]{2,1,0:T(8,128)S(1)}, bf16[64,16,128]{2,1,0:T(8,128)(2,1)S(1)}) custom-call(s32[13]{0:T(128)S(1)} %stack.75.flags, s32[64]{0:T(128)S(1)} %reshape.9.lists, s32[512]{0:T(512)S(1)} %reshape.10.cols, s32[512]{0:T(512)S(1)} %reshape.11.cidx, f32[64,16,128]{2,1,0:T(8,128)S(1)} %get-tuple-element.66.u, ...), custom_call_target="tpu_custom_call" | custom-call | tf_op jit(solution)/shard_map/pallas_call | solution.py:222
  72.7 0.0 collective-permute-start.19
  72.8 7.0 %collective-permute-done.19.moved = bf16[64,16,128]{2,1,0:T(8,128)(2,1)S(1)} collective-permute-done((bf16[64,16,128]{2,1,0:T(8,128)(2,1)S(1)}, bf16[64,16,128]{2,1,0:T(8,128)(2,1)S(1)}, u32[]{:S(2)}, u32[]{:S(2)}) %collective-permute-start.19) | collective-permute-done | bytes 262176 | tf_op jit(solution)/shard_map/ppermute | solution.py:62
  79.8 0.0 collective-permute-done.14.incoming
  79.8 1.0 shard_map.70
  80.8 1.8 %collective-permute-start.20 = (bf16[16,16,128]{2,1,0:T(8,128)(2,1)S(1)}, bf16[16,16,128]{2,1,0:T(8,128)(2,1)S(1)}, u32[]{:S(2)}, u32[]{:S(2)}) collective-permute-start(bf16[16,16,128]{2,1,0:T(8,128)(2,1)S(1)} %get-tuple-element.79), channel_id=1, source_target_pairs={{0,32},{1,33},{2,4},{3,5},{4,2},{5,3},{6,8},{7,9},{8,6},{9,7},{10,... | collective-permute-start | bytes 196616 | tf_op jit(solution)/shard_map/ppermute | solution.py:57
  82.6 2.2 %collective-permute-start.21 = (bf16[16,16,128]{2,1,0:T(8,128)(2,1)S(1)}, bf16[16,16,128]{2,1,0:T(8,128)(2,1)S(1)}, u32[]{:S(2)}, u32[]{:S(2)}) collective-permute-start(bf16[16,16,128]{2,1,0:T(8,128)(2,1)S(1)} %get-tuple-element.80), channel_id=1, source_target_pairs={{0,2},{1,3},{2,0},{3,1},{4,6},{5,7},{6,4},{7,5},{8,10},{9,11},{10,... | collective-permute-start | bytes 196616 | tf_op jit(solution)/shard_map/ppermute | solution.py:57
  84.9 2.1 %collective-permute-start.22 = (bf16[16,16,128]{2,1,0:T(8,128)(2,1)S(1)}, bf16[16,16,128]{2,1,0:T(8,128)(2,1)S(1)}, u32[]{:S(2)}, u32[]{:S(2)}) collective-permute-start(bf16[16,16,128]{2,1,0:T(8,128)(2,1)S(1)} %get-tuple-element.81), channel_id=1, source_target_pairs={{0,32},{1,2},{2,1},{3,4},{4,3},{5,6},{6,5},{7,8},{8,7},{9,10},{10,... | collective-permute-start | bytes 196616 | tf_op jit(solution)/shard_map/ppermute | solution.py:57
  87.0 0.0 collective-permute-start.23
  87.0 1.7 %collective-permute-done.20.refs_0_ = bf16[16,16,128]{2,1,0:T(8,128)(2,1)S(1)} collective-permute-done((bf16[16,16,128]{2,1,0:T(8,128)(2,1)S(1)}, bf16[16,16,128]{2,1,0:T(8,128)(2,1)S(1)}, u32[]{:S(2)}, u32[]{:S(2)}) %collective-permute-start.20) | collective-permute-done | bytes 65568 | tf_op jit(solution)/shard_map/ppermute | solution.py:57
  88.7 2.6 %collective-permute-done.22.refs_2_ = bf16[16,16,128]{2,1,0:T(8,128)(2,1)S(1)} collective-permute-done((bf16[16,16,128]{2,1,0:T(8,128)(2,1)S(1)}, bf16[16,16,128]{2,1,0:T(8,128)(2,1)S(1)}, u32[]{:S(2)}, u32[]{:S(2)}) %collective-permute-start.22) | collective-permute-done | bytes 65568 | tf_op jit(solution)/shard_map/ppermute | solution.py:57
  91.2 4.0 %shard_map.71 = (f32[64,16,128]{2,1,0:T(8,128)S(1)}, bf16[64,16,128]{2,1,0:T(8,128)(2,1)S(1)}, bf16[16,16,128]{2,1,0:T(8,128)(2,1)S(1)}, bf16[16,16,128]{2,1,0:T...) custom-call(s32[13]{0:T(128)S(1)} %stack.75.flags, s32[64]{0:T(128)S(1)} %reshape.9.lists, ...), custom_call_target="tpu_custom_call" | custom-call | tf_op jit(solution)/shard_map/pallas_call | solution.py:222
  95.2 1.6 %collective-permute-start.24 = (bf16[16,16,128]{2,1,0:T(8,128)(2,1)S(1)}, bf16[16,16,128]{2,1,0:T(8,128)(2,1)S(1)}, u32[]{:S(2)}, u32[]{:S(2)}) collective-permute-start(bf16[16,16,128]{2,1,0:T(8,128)(2,1)S(1)} %get-tuple-element.85), channel_id=1, source_target_pairs={{0,32},{1,33},{2,4},{3,5},{4,2},{5,3},{6,8},{7,9},{8,6},{9,7},{10,... | collective-permute-start | bytes 196616 | tf_op jit(solution)/shard_map/ppermute | solution.py:57
  96.7 1.5 %collective-permute-start.25 = (bf16[16,16,128]{2,1,0:T(8,128)(2,1)S(1)}, bf16[16,16,128]{2,1,0:T(8,128)(2,1)S(1)}, u32[]{:S(2)}, u32[]{:S(2)}) collective-permute-start(bf16[16,16,128]{2,1,0:T(8,128)(2,1)S(1)} %get-tuple-element.86), channel_id=1, source_target_pairs={{0,2},{1,3},{2,0},{3,1},{4,6},{5,7},{6,4},{7,5},{8,10},{9,11},{10,... | collective-permute-start | bytes 196616 | tf_op jit(solution)/shard_map/ppermute | solution.py:57
  98.3 2.1 %collective-permute-start.26 = (bf16[16,16,128]{2,1,0:T(8,128)(2,1)S(1)}, bf16[16,16,128]{2,1,0:T(8,128)(2,1)S(1)}, u32[]{:S(2)}, u32[]{:S(2)}) collective-permute-start(bf16[16,16,128]{2,1,0:T(8,128)(2,1)S(1)} %get-tuple-element.87), channel_id=1, source_target_pairs={{0,32},{1,2},{2,1},{3,4},{4,3},{5,6},{6,5},{7,8},{8,7},{9,10},{10,... | collective-permute-start | bytes 196616 | tf_op jit(solution)/shard_map/ppermute | solution.py:57
  100.4 2.2 %collective-permute-done.24.refs_0_ = bf16[16,16,128]{2,1,0:T(8,128)(2,1)S(1)} collective-permute-done((bf16[16,16,128]{2,1,0:T(8,128)(2,1)S(1)}, bf16[16,16,128]{2,1,0:T(8,128)(2,1)S(1)}, u32[]{:S(2)}, u32[]{:S(2)}) %collective-permute-start.24) | collective-permute-done | bytes 65568 | tf_op jit(solution)/shard_map/ppermute | solution.py:57
  102.6 2.1 %collective-permute-done.26.refs_2_ = bf16[16,16,128]{2,1,0:T(8,128)(2,1)S(1)} collective-permute-done((bf16[16,16,128]{2,1,0:T(8,128)(2,1)S(1)}, bf16[16,16,128]{2,1,0:T(8,128)(2,1)S(1)}, u32[]{:S(2)}, u32[]{:S(2)}) %collective-permute-start.26) | collective-permute-done | bytes 65568 | tf_op jit(solution)/shard_map/ppermute | solution.py:57
  104.7 3.8 %shard_map.72 = f32[64,16,128]{2,1,0:T(8,128)S(1)} custom-call(s32[13]{0:T(128)S(1)} %stack.75.flags, s32[64]{0:T(128)S(1)} %reshape.9.lists, s32[512]{0:T(512)S(1)} %reshape.10.cols, s32[512]{0:T(512)S(1)} %reshape.11.cidx, f32[64,16,128]{2,1,0:T(8,128)S(1)} %get-tuple-element.83.u, bf16[64,16,128]{2,1,0:T(8,128)(2,1)S(1)} %get-tuple-element.84.vb, ...), custom_call_target="tpu_custom_call" | custom-call | tf_op jit(solution)/shard_map/pallas_call | solution.py:222
  108.4 1.0 copy.12
  (17 shorter events, 0.0 us)
Async XLA Ops:
  1.4 29.4 %collective-permute-start = (f32[64,16,128]{2,1,0:T(8,128)S(1)}, f32[64,16,128]{2,1,0:T(8,128)S(1)}, u32[]{:S(2)}, u32[]{:S(2)}) collective-permute-start(f32[64,16,128]{2,1,0:T(8,128)S(1)} %bitcast.21), channel_id=1, source_target_pairs={{0,32},{32,64},{64,96},{96,128},{128,160},{160,192},{192,224},{224... | collective-permute-start | bytes 1572872 | tf_op jit(solution)/shard_map/ppermute | solution.py:62
  3.1 12.4 %collective-permute-start.1 = (bf16[16,16,128]{2,1,0:T(8,128)(2,1)S(1)}, bf16[16,16,128]{2,1,0:T(8,128)(2,1)S(1)}, u32[]{:S(2)}, u32[]{:S(2)}) collective-permute-start(bf16[16,16,128]{2,1,0:T(8,128)(2,1)S(1)} %get-tuple-element.48), channel_id=1, source_target_pairs={{0,32},{1,33},{2,4},{3,5},{4,2},{5,3},{6,8},{7,9},{8,6},{9,7},{10,... | collective-permute-start | bytes 196616 | tf_op jit(solution)/shard_map/ppermute | solution.py:57
  9.3 7.1 %collective-permute-start.2 = (bf16[16,16,128]{2,1,0:T(8,128)(2,1)S(1)}, bf16[16,16,128]{2,1,0:T(8,128)(2,1)S(1)}, u32[]{:S(2)}, u32[]{:S(2)}) collective-permute-start(bf16[16,16,128]{2,1,0:T(8,128)(2,1)S(1)} %get-tuple-element.49), channel_id=1, source_target_pairs={{0,2},{1,3},{2,0},{3,1},{4,6},{5,7},{6,4},{7,5},{8,10},{9,11},{10,... | collective-permute-start | bytes 196616 | tf_op jit(solution)/shard_map/ppermute | solution.py:57
  10.9 7.0 %collective-permute-start.3 = (bf16[16,16,128]{2,1,0:T(8,128)(2,1)S(1)}, bf16[16,16,128]{2,1,0:T(8,128)(2,1)S(1)}, u32[]{:S(2)}, u32[]{:S(2)}) collective-permute-start(bf16[16,16,128]{2,1,0:T(8,128)(2,1)S(1)} %get-tuple-element.50), channel_id=1, source_target_pairs={{0,32},{1,2},{2,1},{3,4},{4,3},{5,6},{6,5},{7,8},{8,7},{9,10},{10,... | collective-permute-start | bytes 196616 | tf_op jit(solution)/shard_map/ppermute | solution.py:57
  10.9 7.0 %collective-permute-start.4 = (bf16[16,16,128]{2,1,0:T(8,128)(2,1)S(1)}, bf16[16,16,128]{2,1,0:T(8,128)(2,1)S(1)}, u32[]{:S(2)}, u32[]{:S(2)}) collective-permute-start(bf16[16,16,128]{2,1,0:T(8,128)(2,1)S(1)} %get-tuple-element.51), channel_id=1, source_target_pairs={{0,1},{1,0},{2,3},{3,2},{4,5},{5,4},{6,7},{7,6},{8,9},{9,8},{10,11... | collective-permute-start | bytes 196616 | tf_op jit(solution)/shard_map/ppermute | solution.py:57
  17.9 2.2 %copy-start = (bf16[128,128,128]{2,1,0:T(8,128)(2,1)S(1)}, bf16[128,128,128]{2,1,0:T(8,128)(2,1)}, u32[]{:S(2)}) copy-start(bf16[128,128,128]{2,1,0:T(8,128)(2,1)} %refs_4_.11) | copy-start | bytes 12582916
  20.1 20.7 %copy-start.1 = (bf16[128,128,128]{2,1,0:T(8,128)(2,1)S(1)}, bf16[128,128,128]{2,1,0:T(8,128)(2,1)}, u32[]{:S(2)}) copy-start(bf16[128,128,128]{2,1,0:T(8,128)(2,1)} %refs_4_.11) | copy-start | bytes 12582916
  23.8 7.0 %collective-permute-start.5 = (bf16[64,16,128]{2,1,0:T(8,128)(2,1)S(1)}, bf16[64,16,128]{2,1,0:T(8,128)(2,1)S(1)}, u32[]{:S(2)}, u32[]{:S(2)}) collective-permute-start(bf16[64,16,128]{2,1,0:T(8,128)(2,1)S(1)} %get-tuple-element.53), channel_id=1, source_target_pairs={{0,32},{32,64},{64,96},{96,128},{128,160},{160,192},{192,224},{224... | collective-permute-start | bytes 786440 | tf_op jit(solution)/shard_map/ppermute | solution.py:62
  31.7 7.4 %collective-permute-start.6 = (bf16[16,16,128]{2,1,0:T(8,128)(2,1)S(1)}, bf16[16,16,128]{2,1,0:T(8,128)(2,1)S(1)}, u32[]{:S(2)}, u32[]{:S(2)}) collective-permute-start(bf16[16,16,128]{2,1,0:T(8,128)(2,1)S(1)} %get-tuple-element.56), channel_id=1, source_target_pairs={{0,32},{1,33},{2,4},{3,5},{4,2},{5,3},{6,8},{7,9},{8,6},{9,7},{10,... | collective-permute-start | bytes 196616 | tf_op jit(solution)/shard_map/ppermute | solution.py:57
  33.3 5.8 %collective-permute-start.7 = (bf16[16,16,128]{2,1,0:T(8,128)(2,1)S(1)}, bf16[16,16,128]{2,1,0:T(8,128)(2,1)S(1)}, u32[]{:S(2)}, u32[]{:S(2)}) collective-permute-start(bf16[16,16,128]{2,1,0:T(8,128)(2,1)S(1)} %get-tuple-element.57), channel_id=1, source_target_pairs={{0,2},{1,3},{2,0},{3,1},{4,6},{5,7},{6,4},{7,5},{8,10},{9,11},{10,... | collective-permute-start | bytes 196616 | tf_op jit(solution)/shard_map/ppermute | solution.py:57
  34.5 6.4 %collective-permute-start.8 = (bf16[16,16,128]{2,1,0:T(8,128)(2,1)S(1)}, bf16[16,16,128]{2,1,0:T(8,128)(2,1)S(1)}, u32[]{:S(2)}, u32[]{:S(2)}) collective-permute-start(bf16[16,16,128]{2,1,0:T(8,128)(2,1)S(1)} %get-tuple-element.58), channel_id=1, source_target_pairs={{0,32},{1,2},{2,1},{3,4},{4,3},{5,6},{6,5},{7,8},{8,7},{9,10},{10,... | collective-permute-start | bytes 196616 | tf_op jit(solution)/shard_map/ppermute | solution.py:57
  35.8 5.1 %collective-permute-start.9 = (bf16[16,16,128]{2,1,0:T(8,128)(2,1)S(1)}, bf16[16,16,128]{2,1,0:T(8,128)(2,1)S(1)}, u32[]{:S(2)}, u32[]{:S(2)}) collective-permute-start(bf16[16,16,128]{2,1,0:T(8,128)(2,1)S(1)} %get-tuple-element.59), channel_id=1, source_target_pairs={{0,1},{1,0},{2,3},{3,2},{4,5},{5,4},{6,7},{7,6},{8,9},{9,8},{10,11... | collective-permute-start | bytes 196616 | tf_op jit(solution)/shard_map/ppermute | solution.py:57
  44.7 8.6 %collective-permute-start.10 = (bf16[16,16,128]{2,1,0:T(8,128)(2,1)S(1)}, bf16[16,16,128]{2,1,0:T(8,128)(2,1)S(1)}, u32[]{:S(2)}, u32[]{:S(2)}) collective-permute-start(bf16[16,16,128]{2,1,0:T(8,128)(2,1)S(1)} %get-tuple-element.62), channel_id=1, source_target_pairs={{0,32},{1,33},{2,4},{3,5},{4,2},{5,3},{6,8},{7,9},{8,6},{9,7},{10,... | collective-permute-start | bytes 196616 | tf_op jit(solution)/shard_map/ppermute | solution.py:57
  46.9 6.4 %collective-permute-start.11 = (bf16[16,16,128]{2,1,0:T(8,128)(2,1)S(1)}, bf16[16,16,128]{2,1,0:T(8,128)(2,1)S(1)}, u32[]{:S(2)}, u32[]{:S(2)}) collective-permute-start(bf16[16,16,128]{2,1,0:T(8,128)(2,1)S(1)} %get-tuple-element.63), channel_id=1, source_target_pairs={{0,2},{1,3},{2,0},{3,1},{4,6},{5,7},{6,4},{7,5},{8,10},{9,11},{10,... | collective-permute-start | bytes 196616 | tf_op jit(solution)/shard_map/ppermute | solution.py:57
  49.3 6.4 %collective-permute-start.12 = (bf16[16,16,128]{2,1,0:T(8,128)(2,1)S(1)}, bf16[16,16,128]{2,1,0:T(8,128)(2,1)S(1)}, u32[]{:S(2)}, u32[]{:S(2)}) collective-permute-start(bf16[16,16,128]{2,1,0:T(8,128)(2,1)S(1)} %get-tuple-element.64), channel_id=1, source_target_pairs={{0,32},{1,2},{2,1},{3,4},{4,3},{5,6},{6,5},{7,8},{8,7},{9,10},{10,... | collective-permute-start | bytes 196616 | tf_op jit(solution)/shard_map/ppermute | solution.py:57
  51.2 4.5 %collective-permute-start.13 = (bf16[16,16,128]{2,1,0:T(8,128)(2,1)S(1)}, bf16[16,16,128]{2,1,0:T(8,128)(2,1)S(1)}, u32[]{:S(2)}, u32[]{:S(2)}) collective-permute-start(bf16[16,16,128]{2,1,0:T(8,128)(2,1)S(1)} %get-tuple-element.65), channel_id=1, source_target_pairs={{0,1},{1,0},{2,3},{3,2},{4,5},{5,4},{6,7},{7,6},{8,9},{9,8},{10,11... | collective-permute-start | bytes 196616 | tf_op jit(solution)/shard_map/ppermute | solution.py:57
  59.6 20.2 %collective-permute-start.14 = (f32[64,16,128]{2,1,0:T(8,128)S(1)}, f32[64,16,128]{2,1,0:T(8,128)S(1)}, u32[]{:S(2)}, u32[]{:S(2)}) collective-permute-start(f32[64,16,128]{2,1,0:T(8,128)S(1)} %get-tuple-element.66.u), channel_id=1, source_target_pairs={{0,32},{32,64},{64,96},{96,128},{128,160},{160,192},{192,224},{224... | collective-permute-start | bytes 1572872 | tf_op jit(solution)/shard_map/ppermute | solution.py:62
  59.6 8.6 %collective-permute-start.15 = (bf16[16,16,128]{2,1,0:T(8,128)(2,1)S(1)}, bf16[16,16,128]{2,1,0:T(8,128)(2,1)S(1)}, u32[]{:S(2)}, u32[]{:S(2)}) collective-permute-start(bf16[16,16,128]{2,1,0:T(8,128)(2,1)S(1)} %get-tuple-element.68), channel_id=1, source_target_pairs={{0,32},{1,33},{2,4},{3,5},{4,2},{5,3},{6,8},{7,9},{8,6},{9,7},{10,... | collective-permute-start | bytes 196616 | tf_op jit(solution)/shard_map/ppermute | solution.py:57
  61.2 7.1 %collective-permute-start.16 = (bf16[16,16,128]{2,1,0:T(8,128)(2,1)S(1)}, bf16[16,16,128]{2,1,0:T(8,128)(2,1)S(1)}, u32[]{:S(2)}, u32[]{:S(2)}) collective-permute-start(bf16[16,16,128]{2,1,0:T(8,128)(2,1)S(1)} %get-tuple-element.69), channel_id=1, source_target_pairs={{0,2},{1,3},{2,0},{3,1},{4,6},{5,7},{6,4},{7,5},{8,10},{9,11},{10,... | collective-permute-start | bytes 196616 | tf_op jit(solution)/shard_map/ppermute | solution.py:57
  62.4 6.7 %collective-permute-start.17 = (bf16[16,16,128]{2,1,0:T(8,128)(2,1)S(1)}, bf16[16,16,128]{2,1,0:T(8,128)(2,1)S(1)}, u32[]{:S(2)}, u32[]{:S(2)}) collective-permute-start(bf16[16,16,128]{2,1,0:T(8,128)(2,1)S(1)} %get-tuple-element.70), channel_id=1, source_target_pairs={{0,32},{1,2},{2,1},{3,4},{4,3},{5,6},{6,5},{7,8},{8,7},{9,10},{10,... | collective-permute-start | bytes 196616 | tf_op jit(solution)/shard_map/ppermute | solution.py:57
  64.3 4.8 %collective-permute-start.18 = (bf16[16,16,128]{2,1,0:T(8,128)(2,1)S(1)}, bf16[16,16,128]{2,1,0:T(8,128)(2,1)S(1)}, u32[]{:S(2)}, u32[]{:S(2)}) collective-permute-start(bf16[16,16,128]{2,1,0:T(8,128)(2,1)S(1)} %get-tuple-element.71), channel_id=1, source_target_pairs={{0,1},{1,0},{2,3},{3,2},{4,5},{5,4},{6,7},{7,6},{8,9},{9,8},{10,11... | collective-permute-start | bytes 196616 | tf_op jit(solution)/shard_map/ppermute | solution.py:57
  72.7 7.0 %collective-permute-start.19 = (bf16[64,16,128]{2,1,0:T(8,128)(2,1)S(1)}, bf16[64,16,128]{2,1,0:T(8,128)(2,1)S(1)}, u32[]{:S(2)}, u32[]{:S(2)}) collective-permute-start(bf16[64,16,128]{2,1,0:T(8,128)(2,1)S(1)} %get-tuple-element.72), channel_id=1, source_target_pairs={{0,32},{32,64},{64,96},{96,128},{128,160},{160,192},{192,224},{224... | collective-permute-start | bytes 786440 | tf_op jit(solution)/shard_map/ppermute | solution.py:62
  80.8 7.9 %collective-permute-start.20 = (bf16[16,16,128]{2,1,0:T(8,128)(2,1)S(1)}, bf16[16,16,128]{2,1,0:T(8,128)(2,1)S(1)}, u32[]{:S(2)}, u32[]{:S(2)}) collective-permute-start(bf16[16,16,128]{2,1,0:T(8,128)(2,1)S(1)} %get-tuple-element.79), channel_id=1, source_target_pairs={{0,32},{1,33},{2,4},{3,5},{4,2},{5,3},{6,8},{7,9},{8,6},{9,7},{10,... | collective-permute-start | bytes 196616 | tf_op jit(solution)/shard_map/ppermute | solution.py:57
  82.6 6.0 %collective-permute-start.21 = (bf16[16,16,128]{2,1,0:T(8,128)(2,1)S(1)}, bf16[16,16,128]{2,1,0:T(8,128)(2,1)S(1)}, u32[]{:S(2)}, u32[]{:S(2)}) collective-permute-start(bf16[16,16,128]{2,1,0:T(8,128)(2,1)S(1)} %get-tuple-element.80), channel_id=1, source_target_pairs={{0,2},{1,3},{2,0},{3,1},{4,6},{5,7},{6,4},{7,5},{8,10},{9,11},{10,... | collective-permute-start | bytes 196616 | tf_op jit(solution)/shard_map/ppermute | solution.py:57
  84.9 6.4 %collective-permute-start.22 = (bf16[16,16,128]{2,1,0:T(8,128)(2,1)S(1)}, bf16[16,16,128]{2,1,0:T(8,128)(2,1)S(1)}, u32[]{:S(2)}, u32[]{:S(2)}) collective-permute-start(bf16[16,16,128]{2,1,0:T(8,128)(2,1)S(1)} %get-tuple-element.81), channel_id=1, source_target_pairs={{0,32},{1,2},{2,1},{3,4},{4,3},{5,6},{6,5},{7,8},{8,7},{9,10},{10,... | collective-permute-start | bytes 196616 | tf_op jit(solution)/shard_map/ppermute | solution.py:57
  87.0 4.3 %collective-permute-start.23 = (bf16[16,16,128]{2,1,0:T(8,128)(2,1)S(1)}, bf16[16,16,128]{2,1,0:T(8,128)(2,1)S(1)}, u32[]{:S(2)}, u32[]{:S(2)}) collective-permute-start(bf16[16,16,128]{2,1,0:T(8,128)(2,1)S(1)} %get-tuple-element.82), channel_id=1, source_target_pairs={{0,1},{1,0},{2,3},{3,2},{4,5},{5,4},{6,7},{7,6},{8,9},{9,8},{10,11... | collective-permute-start | bytes 196616 | tf_op jit(solution)/shard_map/ppermute | solution.py:57
  95.2 7.4 %collective-permute-start.24 = (bf16[16,16,128]{2,1,0:T(8,128)(2,1)S(1)}, bf16[16,16,128]{2,1,0:T(8,128)(2,1)S(1)}, u32[]{:S(2)}, u32[]{:S(2)}) collective-permute-start(bf16[16,16,128]{2,1,0:T(8,128)(2,1)S(1)} %get-tuple-element.85), channel_id=1, source_target_pairs={{0,32},{1,33},{2,4},{3,5},{4,2},{5,3},{6,8},{7,9},{8,6},{9,7},{10,... | collective-permute-start | bytes 196616 | tf_op jit(solution)/shard_map/ppermute | solution.py:57
  96.7 5.8 %collective-permute-start.25 = (bf16[16,16,128]{2,1,0:T(8,128)(2,1)S(1)}, bf16[16,16,128]{2,1,0:T(8,128)(2,1)S(1)}, u32[]{:S(2)}, u32[]{:S(2)}) collective-permute-start(bf16[16,16,128]{2,1,0:T(8,128)(2,1)S(1)} %get-tuple-element.86), channel_id=1, source_target_pairs={{0,2},{1,3},{2,0},{3,1},{4,6},{5,7},{6,4},{7,5},{8,10},{9,11},{10,... | collective-permute-start | bytes 196616 | tf_op jit(solution)/shard_map/ppermute | solution.py:57
  98.3 6.4 %collective-permute-start.26 = (bf16[16,16,128]{2,1,0:T(8,128)(2,1)S(1)}, bf16[16,16,128]{2,1,0:T(8,128)(2,1)S(1)}, u32[]{:S(2)}, u32[]{:S(2)}) collective-permute-start(bf16[16,16,128]{2,1,0:T(8,128)(2,1)S(1)} %get-tuple-element.87), channel_id=1, source_target_pairs={{0,32},{1,2},{2,1},{3,4},{4,3},{5,6},{6,5},{7,8},{8,7},{9,10},{10,... | collective-permute-start | bytes 196616 | tf_op jit(solution)/shard_map/ppermute | solution.py:57
  100.4 4.3 %collective-permute-start.27 = (bf16[16,16,128]{2,1,0:T(8,128)(2,1)S(1)}, bf16[16,16,128]{2,1,0:T(8,128)(2,1)S(1)}, u32[]{:S(2)}, u32[]{:S(2)}) collective-permute-start(bf16[16,16,128]{2,1,0:T(8,128)(2,1)S(1)} %get-tuple-element.88), channel_id=1, source_target_pairs={{0,1},{1,0},{2,3},{3,2},{4,5},{5,4},{6,7},{7,6},{8,9},{9,8},{10,11... | collective-permute-start | bytes 196616 | tf_op jit(solution)/shard_map/ppermute | solution.py:57

commit v2 on v1

--- a/solution.py
+++ b/solution.py
@@ -87,9 +87,8 @@
 def pack(flags, lists, vb, packs):
     slots = packs[0].shape[0]
     for k, out in enumerate(packs):
-        base = flags[k] * slots
         for j in range(slots):
-            row = lists[base + j]
+            row = lists[flags[k], j]
             block = vb[jnp.maximum(row, 0)]
             out[j] = jnp.where(row >= 0, block, jnp.zeros_like(block))
 
@@ -99,34 +98,47 @@
     pack(flags, lists, vb, packs)
 
 
-def force_kernel(update, extras, keep, send, flags, lists, cols, cidx, u, vb, *refs):
+def own_kernel(cidx, u, vb, coeffs, mixing, part):
+    m = mixing[...]
+    m_hi = m.astype(bf16)
+    m_lo = (m - m_hi.astype(f32)).astype(bf16)
+    mix = jnp.concatenate([m_hi, m_lo, m_hi], axis=1)
+
+    def body(i, carry):
+        for j in range(UNROLL):
+            b = i * UNROLL + j
+            th = jnp.tanh(u[b])
+            hi = th.astype(bf16)
+            lo = (th - hi.astype(f32)).astype(bf16)
+            own = jnp.dot(vb[b], coeffs[cidx[b, 0]], preferred_element_type=f32)
+            part[b] = own + jnp.dot(mix, jnp.concatenate([hi, hi, lo], axis=0), preferred_element_type=f32)
+        return carry
+
+    lax.fori_loop(0, u.shape[0] // UNROLL, body, 0)
+
+
+def force_kernel(update, extras, keep, send, flags, lists, cols, cidx, u, vb, part, *refs):
     received, refs = refs[:4], refs[4:]
-    coeffs, mix, refs = refs[0], refs[1], refs[2:]
+    coeffs, refs = refs[0], refs[1:]
     olds, refs = refs[:extras], refs[extras:]
     outs, ext = refs[:-1], refs[-1]
-    nblocks = u.shape[0]
+    nblocks = vb.shape[0]
     slots = received[0].shape[0]
-    terms = cols.shape[0] // nblocks
+    terms = cols.shape[1]
     ext[0:nblocks] = vb[...]
     for k, got in enumerate(received):
         live = flags[8 + k] > 0
         block = got[...]
         ext[pl.ds(nblocks + flags[4 + k] * slots, slots)] = jnp.where(live, block, jnp.zeros_like(block))
-    mixv = mix[...]
 
     def body(i, carry):
         for j in range(UNROLL):
             b = i * UNROLL + j
-            xs = [ext[cols[b * terms + t]] for t in range(terms)]
-            ws = [coeffs[cidx[b * terms + t]] for t in range(terms)]
-            field = u[b]
-            th = jnp.tanh(field)
-            hi = th.astype(bf16)
-            lo = (th - hi.astype(f32)).astype(bf16)
-            force = jnp.dot(
+            xs = [ext[cols[b, t]] for t in range(terms)]
+            ws = [coeffs[cidx[b, t + 1]] for t in range(terms)]
+            force = part[b] + jnp.dot(
                 jnp.concatenate(xs, axis=1), jnp.concatenate(ws, axis=0), preferred_element_type=f32
             )
-            force += jnp.dot(mixv, jnp.concatenate([hi, hi, lo], axis=0), preferred_element_type=f32)
             at = 0
             if keep:
                 outs[at][b] = force
@@ -134,7 +146,7 @@
             if update is None:
                 outs[at][b] = force.astype(bf16)
                 continue
-            new = update(field, force, [old[b] for old in olds])
+            new = update(u[b], force, [old[b] for old in olds])
             outs[at][b] = new
             if send:
                 outs[at + 1][b] = new.astype(bf16)
@@ -205,20 +217,14 @@
     first = jnp.transpose(guess[0], (1, 0, 2))
     nblocks, species, cells = first.shape
     slots = send_lists.shape[1]
-    own_rows = lax.broadcasted_iota(jnp.int32, (nblocks, 1), 0)
-    cols = jnp.concatenate([own_rows, neighbours], axis=1).reshape(-1)
-    cidx = coef_index.reshape(-1)
-    lists = send_lists.reshape(-1)
+    lists = send_lists
     flags = plan()
-    mix_hi = mixing.astype(bf16)
-    mix_lo = (mixing - mix_hi.astype(f32)).astype(bf16)
-    mix = jnp.concatenate([mix_hi, mix_lo, mix_hi], axis=1)
 
     state = jax.ShapeDtypeStruct((nblocks, species, cells), f32)
     rounded = jax.ShapeDtypeStruct((nblocks, species, cells), bf16)
     rim = jax.ShapeDtypeStruct((slots, species, cells), bf16)
 
-    def call(kernel, outs, scalars, arrays, scratch=()):
+    def call(kernel, outs, scalars, arrays, scratch=(), cost=4_000_000):
         return pl.pallas_call(
             kernel,
             out_shape=outs,
@@ -226,11 +232,13 @@
             out_specs=[VMEM] * len(outs),
             scratch_shapes=scratch,
             compiler_params=PARAMS,
+            cost_estimate=pl.CostEstimate(flops=cost, bytes_accessed=cost, transcendentals=0),
         )(*scalars, *arrays)
 
     ext = [pltpu.VMEM((nblocks + 4 * slots, species, cells), bf16)]
 
     def force(u, vb, received, update, olds, keep, send):
+        (part,) = call(own_kernel, [state], (coef_index,), (u, vb, coeffs, mixing))
         outs = []
         if keep:
             outs.append(state)
@@ -242,7 +250,11 @@
             outs += [rounded] + [rim] * 4
         kernel = functools.partial(force_kernel, update, len(olds), keep, send)
         return call(
-            kernel, outs, (flags, lists, cols, cidx), (u, vb, *received, coeffs, mix, *olds), ext
+            kernel,
+            outs,
+            (flags, lists, neighbours, coef_index),
+            (u, vb, part, *received, coeffs, *olds),
+            ext,
         )
 
     vb, *packs = call(first_kernel, [rounded] + [rim] * 4, (flags, lists), (first,))

time: 110 us -> 114 us (1.036)
  Pallas kernels: 25.4 us -> 44.1 us
  waiting for transfers between devices: 38 us -> 22.3 us
  starting transfers between devices: 37.9 us -> 39.9 us
  other arithmetic: 1.55 us -> 0 us
    pallas_call x9 -> x15, Pallas kernels: 25.4 us -> 44.1 us  [call(): pl.pallas_call(kernel, out_shape=outs, in_specs=[SMEM] * len(scalars) + [...]
    ppermute x24, waiting for transfers between devices: 24 us -> 8.63 us  [swap(): return lax.ppermute(block, ('tm', 'space'), route)]
    unnamed x6 -> x13, local copies, waits for them, and re-layouts: 4.31 us -> 6.48 us
    ppermute x24, starting transfers between devices: 37.7 us -> 39.5 us  [swap(): return lax.ppermute(block, ('tm', 'space'), route)]
  transfers between devices with their start and end apart: 28 -> 28, of which waited for: 15 -> 10; matrix products, arithmetic and copies ran while one was open for 3% -> 1% of each run, Pallas kernels for 7% -> 21%
where the time goes in v2:
time: 114 us
  Pallas kernels  44.1 us (39%)
  starting transfers between devices  39.9 us (35%)
  waiting for transfers between devices  22.3 us (20%)
  local copies, waits for them, and re-layouts  7.54 us (7%)
    pallas_call x15, Pallas kernels, call(): pl.pallas_call(kernel, out_shape=outs, in_specs=[SMEM] * len(scalars) + [...  44.1 us
    ppermute x24, starting transfers between devices, swap(): return lax.ppermute(block, ('tm', 'space'), route)  39.5 us
    ppermute x4, waiting for transfers between devices, next_slice(): return lax.ppermute(block, 'tm', [(i, (i + 1) % n) for i in range(n)])  13.6 us
    ppermute x24, waiting for transfers between devices, swap(): return lax.ppermute(block, ('tm', 'space'), route)  8.63 us
    unnamed x13, local copies, waits for them, and re-layouts  6.48 us
  transfers between devices with their start and end apart: 28, of which 10 were waited for; matrix products, arithmetic and copies ran while one was open for 1% of the time, Pallas kernels for 21%

profile of v2, /device:TPU:8, one launch (start us, length us, event | category | flops | bytes accessed | tf_op | source)
XLA Modules:
  0.0 114.1 jit_solution(6380087936907401257)
XLA Ops:
  0.0 1.4 %copy.28 = f32[1,16,64,128]{3,1,2,0:T(8,128)S(1)} copy(f32[1,16,64,128]{3,2,1,0:T(8,128)} %param.6) | data formatting | bytes 1048576 | tf_op args[0]
  1.4 0.0 collective-permute-start
  1.5 0.1 stack.75.flags
  1.6 0.0 copy-start.3
  1.6 0.7 copy-done.3
  2.3 0.7 shard_map.64
  3.0 6.3 %collective-permute-start.1 = (bf16[16,16,128]{2,1,0:T(8,128)(2,1)S(1)}, bf16[16,16,128]{2,1,0:T(8,128)(2,1)S(1)}, u32[]{:S(2)}, u32[]{:S(2)}) collective-permute-start(bf16[16,16,128]{2,1,0:T(8,128)(2,1)S(1)} %get-tuple-element.48), channel_id=1, source_target_pairs={{0,32},{1,33},{2,4},{3,5},{4,2},{5,3},{6,8},{7,9},{8,6},{9,7},{10,... | collective-permute-start | bytes 196616 | tf_op jit(solution)/shard_map/ppermute | solution.py:57
  9.3 1.6 %collective-permute-start.2 = (bf16[16,16,128]{2,1,0:T(8,128)(2,1)S(1)}, bf16[16,16,128]{2,1,0:T(8,128)(2,1)S(1)}, u32[]{:S(2)}, u32[]{:S(2)}) collective-permute-start(bf16[16,16,128]{2,1,0:T(8,128)(2,1)S(1)} %get-tuple-element.49), channel_id=1, source_target_pairs={{0,2},{1,3},{2,0},{3,1},{4,6},{5,7},{6,4},{7,5},{8,10},{9,11},{10,... | collective-permute-start | bytes 196616 | tf_op jit(solution)/shard_map/ppermute | solution.py:57
  10.9 0.0 collective-permute-start.3
  10.9 1.9 %collective-permute-start.4 = (bf16[16,16,128]{2,1,0:T(8,128)(2,1)S(1)}, bf16[16,16,128]{2,1,0:T(8,128)(2,1)S(1)}, u32[]{:S(2)}, u32[]{:S(2)}) collective-permute-start(bf16[16,16,128]{2,1,0:T(8,128)(2,1)S(1)} %get-tuple-element.51), channel_id=1, source_target_pairs={{0,1},{1,0},{2,3},{3,2},{4,5},{5,4},{6,7},{7,6},{8,9},{9,8},{10,11... | collective-permute-start | bytes 196616 | tf_op jit(solution)/shard_map/ppermute | solution.py:57
  12.8 0.8 copy.25.cidx
  13.5 0.8 copy.24.cols
  14.3 2.2 %copy-done = bf16[128,128,128]{2,1,0:T(8,128)(2,1)S(1)} copy-done((bf16[128,128,128]{2,1,0:T(8,128)(2,1)S(1)}, bf16[128,128,128]{2,1,0:T(8,128)(2,1)}, u32[]{:S(2)}) %copy-start) | copy-done | bytes 4194328
  16.5 0.7 copy-done.2
  17.2 2.4 %shard_map.65.part = f32[64,16,128]{2,1,0:T(8,128)S(1)} custom-call(s32[64,8]{1,0:T(8,128)S(1)} %copy.25.cidx, f32[64,16,128]{2,1,0:T(8,128)S(1)} %bitcast.23, bf16[64,16,128]{2,1,0:T(8,128)(2,1)S(1)} %get-tuple-element.47.vb, bf16[128,128,128]{2,1,0:T(8,128)(2,1)S(1)} %copy-done, f32[16,16]{1,0:T(8,128)S(1)} %copy-done.2), custom_call_target="tpu_custom_call" | custom-call | flops 4000000 | bytes 4000000 | tf_op jit(solution)/shard_map/pallas_call | solution.py:228
  19.6 0.0 collective-permute-done.2.refs_1_
  19.6 0.0 collective-permute-done.4.refs_3_
  19.7 4.4 %shard_map.66 = (f32[64,16,128]{2,1,0:T(8,128)S(1)}, bf16[64,16,128]{2,1,0:T(8,128)(2,1)S(1)}) custom-call(s32[13]{0:T(128)S(1)} %stack.75.flags, s32[4,16]{1,0:T(4,128)S(1)} %copy-done.4, s32[64,7]{1,0:T(8,128)S(1)} %copy.24.cols, s32[64,8]{1,0:T(8,128)S(1)} %copy.25.cidx, f32[64,16,128]{2,1,0:T(8,128)S(1)} %bitcast.24, ...), custom_call_target="tpu_custom_call" | custom-call | flops 4000000 | bytes 4000000 | tf_op jit(solution)/shard_map/pallas_call | solution.py:228
  24.1 0.4 collective-permute-start.5
  24.5 6.6 %collective-permute-done.5.moved = bf16[64,16,128]{2,1,0:T(8,128)(2,1)S(1)} collective-permute-done((bf16[64,16,128]{2,1,0:T(8,128)(2,1)S(1)}, bf16[64,16,128]{2,1,0:T(8,128)(2,1)S(1)}, u32[]{:S(2)}, u32[]{:S(2)}) %collective-permute-start.5) | collective-permute-done | bytes 262176 | tf_op jit(solution)/shard_map/ppermute | solution.py:62
  31.1 0.0 collective-permute-done.incoming
  31.1 1.0 shard_map.67
  32.1 3.8 %collective-permute-start.6 = (bf16[16,16,128]{2,1,0:T(8,128)(2,1)S(1)}, bf16[16,16,128]{2,1,0:T(8,128)(2,1)S(1)}, u32[]{:S(2)}, u32[]{:S(2)}) collective-permute-start(bf16[16,16,128]{2,1,0:T(8,128)(2,1)S(1)} %get-tuple-element.56), channel_id=1, source_target_pairs={{0,32},{1,33},{2,4},{3,5},{4,2},{5,3},{6,8},{7,9},{8,6},{9,7},{10,... | collective-permute-start | bytes 196616 | tf_op jit(solution)/shard_map/ppermute | solution.py:57
  35.8 1.5 %collective-permute-start.8 = (bf16[16,16,128]{2,1,0:T(8,128)(2,1)S(1)}, bf16[16,16,128]{2,1,0:T(8,128)(2,1)S(1)}, u32[]{:S(2)}, u32[]{:S(2)}) collective-permute-start(bf16[16,16,128]{2,1,0:T(8,128)(2,1)S(1)} %get-tuple-element.58), channel_id=1, source_target_pairs={{0,32},{1,2},{2,1},{3,4},{4,3},{5,6},{6,5},{7,8},{8,7},{9,10},{10,... | collective-permute-start | bytes 196616 | tf_op jit(solution)/shard_map/ppermute | solution.py:57
  37.3 2.0 %collective-permute-start.9 = (bf16[16,16,128]{2,1,0:T(8,128)(2,1)S(1)}, bf16[16,16,128]{2,1,0:T(8,128)(2,1)S(1)}, u32[]{:S(2)}, u32[]{:S(2)}) collective-permute-start(bf16[16,16,128]{2,1,0:T(8,128)(2,1)S(1)} %get-tuple-element.59), channel_id=1, source_target_pairs={{0,1},{1,0},{2,3},{3,2},{4,5},{5,4},{6,7},{7,6},{8,9},{9,8},{10,11... | collective-permute-start | bytes 196616 | tf_op jit(solution)/shard_map/ppermute | solution.py:57
  39.3 2.4 %shard_map.68.part = f32[64,16,128]{2,1,0:T(8,128)S(1)} custom-call(s32[64,8]{1,0:T(8,128)S(1)} %copy.25.cidx, f32[64,16,128]{2,1,0:T(8,128)S(1)} %get-tuple-element.54.u, bf16[64,16,128]{2,1,0:T(8,128)(2,1)S(1)} %get-tuple-element.55.vb, bf16[128,128,128]{2,1,0:T(8,128)(2,1)S(1)} %copy-done.1, f32[16,16]{1,0:T(8,128)S(1)} %copy-done.2), custom_call_target="tpu_custom_call" | custom-call | flops 4000000 | bytes 4000000 | tf_op jit(solution)/shard_map/pallas_call | solution.py:228
  41.7 0.0 collective-permute-done.7.refs_1_
  41.7 0.5 collective-permute-done.8.refs_2_
  42.2 4.6 %shard_map.69 = (f32[64,16,128]{2,1,0:T(8,128)S(1)}, f32[64,16,128]{2,1,0:T(8,128)S(1)}, bf16[64,16,128]{2,1,0:T(8,128)(2,1)S(1)}, bf16[16,16,128]{2,1,0:T(8,128...) custom-call(s32[13]{0:T(128)S(1)} %stack.75.flags, ...), custom_call_target="tpu_custom_call" | custom-call | flops 4000000 | bytes 4000000 | tf_op jit(solution)/shard_map/pallas_call | solution.py:228
  46.8 1.7 %collective-permute-start.10 = (bf16[16,16,128]{2,1,0:T(8,128)(2,1)S(1)}, bf16[16,16,128]{2,1,0:T(8,128)(2,1)S(1)}, u32[]{:S(2)}, u32[]{:S(2)}) collective-permute-start(bf16[16,16,128]{2,1,0:T(8,128)(2,1)S(1)} %get-tuple-element.62), channel_id=1, source_target_pairs={{0,32},{1,33},{2,4},{3,5},{4,2},{5,3},{6,8},{7,9},{8,6},{9,7},{10,... | collective-permute-start | bytes 196616 | tf_op jit(solution)/shard_map/ppermute | solution.py:57
  48.6 1.8 %collective-permute-start.11 = (bf16[16,16,128]{2,1,0:T(8,128)(2,1)S(1)}, bf16[16,16,128]{2,1,0:T(8,128)(2,1)S(1)}, u32[]{:S(2)}, u32[]{:S(2)}) collective-permute-start(bf16[16,16,128]{2,1,0:T(8,128)(2,1)S(1)} %get-tuple-element.63), channel_id=1, source_target_pairs={{0,2},{1,3},{2,0},{3,1},{4,6},{5,7},{6,4},{7,5},{8,10},{9,11},{10,... | collective-permute-start | bytes 196616 | tf_op jit(solution)/shard_map/ppermute | solution.py:57
  50.4 1.9 %collective-permute-start.12 = (bf16[16,16,128]{2,1,0:T(8,128)(2,1)S(1)}, bf16[16,16,128]{2,1,0:T(8,128)(2,1)S(1)}, u32[]{:S(2)}, u32[]{:S(2)}) collective-permute-start(bf16[16,16,128]{2,1,0:T(8,128)(2,1)S(1)} %get-tuple-element.64), channel_id=1, source_target_pairs={{0,32},{1,2},{2,1},{3,4},{4,3},{5,6},{6,5},{7,8},{8,7},{9,10},{10,... | collective-permute-start | bytes 196616 | tf_op jit(solution)/shard_map/ppermute | solution.py:57
  52.3 2.4 %shard_map.70.part = f32[64,16,128]{2,1,0:T(8,128)S(1)} custom-call(s32[64,8]{1,0:T(8,128)S(1)} %copy.25.cidx, f32[64,16,128]{2,1,0:T(8,128)S(1)} %get-tuple-element.60.u, bf16[64,16,128]{2,1,0:T(8,128)(2,1)S(1)} %get-tuple-element.61.vb, bf16[128,128,128]{2,1,0:T(8,128)(2,1)S(1)} %copy-done.1, f32[16,16]{1,0:T(8,128)S(1)} %copy-done.2), custom_call_target="tpu_custom_call" | custom-call | flops 4000000 | bytes 4000000 | tf_op jit(solution)/shard_map/pallas_call | solution.py:228
  54.7 0.1 collective-permute-done.10.refs_0_
  54.8 1.9 %collective-permute-done.12.refs_2_ = bf16[16,16,128]{2,1,0:T(8,128)(2,1)S(1)} collective-permute-done((bf16[16,16,128]{2,1,0:T(8,128)(2,1)S(1)}, bf16[16,16,128]{2,1,0:T(8,128)(2,1)S(1)}, u32[]{:S(2)}, u32[]{:S(2)}) %collective-permute-start.12) | collective-permute-done | bytes 65568 | tf_op jit(solution)/shard_map/ppermute | solution.py:57
  56.8 4.6 %shard_map.71 = (f32[64,16,128]{2,1,0:T(8,128)S(1)}, f32[64,16,128]{2,1,0:T(8,128)S(1)}, bf16[64,16,128]{2,1,0:T(8,128)(2,1)S(1)}, bf16[16,16,128]{2,1,0:T(8,128...) custom-call(s32[13]{0:T(128)S(1)} %stack.75.flags, ...), custom_call_target="tpu_custom_call" | custom-call | flops 4000000 | bytes 4000000 | tf_op jit(solution)/shard_map/pallas_call | solution.py:228
  61.4 0.0 collective-permute-start.14
  61.4 2.3 %collective-permute-start.15 = (bf16[16,16,128]{2,1,0:T(8,128)(2,1)S(1)}, bf16[16,16,128]{2,1,0:T(8,128)(2,1)S(1)}, u32[]{:S(2)}, u32[]{:S(2)}) collective-permute-start(bf16[16,16,128]{2,1,0:T(8,128)(2,1)S(1)} %get-tuple-element.68), channel_id=1, source_target_pairs={{0,32},{1,33},{2,4},{3,5},{4,2},{5,3},{6,8},{7,9},{8,6},{9,7},{10,... | collective-permute-start | bytes 196616 | tf_op jit(solution)/shard_map/ppermute | solution.py:57
  63.7 1.4 %collective-permute-start.16 = (bf16[16,16,128]{2,1,0:T(8,128)(2,1)S(1)}, bf16[16,16,128]{2,1,0:T(8,128)(2,1)S(1)}, u32[]{:S(2)}, u32[]{:S(2)}) collective-permute-start(bf16[16,16,128]{2,1,0:T(8,128)(2,1)S(1)} %get-tuple-element.69), channel_id=1, source_target_pairs={{0,2},{1,3},{2,0},{3,1},{4,6},{5,7},{6,4},{7,5},{8,10},{9,11},{10,... | collective-permute-start | bytes 196616 | tf_op jit(solution)/shard_map/ppermute | solution.py:57
  65.2 1.9 %collective-permute-start.17 = (bf16[16,16,128]{2,1,0:T(8,128)(2,1)S(1)}, bf16[16,16,128]{2,1,0:T(8,128)(2,1)S(1)}, u32[]{:S(2)}, u32[]{:S(2)}) collective-permute-start(bf16[16,16,128]{2,1,0:T(8,128)(2,1)S(1)} %get-tuple-element.70), channel_id=1, source_target_pairs={{0,32},{1,2},{2,1},{3,4},{4,3},{5,6},{6,5},{7,8},{8,7},{9,10},{10,... | collective-permute-start | bytes 196616 | tf_op jit(solution)/shard_map/ppermute | solution.py:57
  67.1 0.2 collective-permute-start.18
  67.2 2.4 %shard_map.72.part = f32[64,16,128]{2,1,0:T(8,128)S(1)} custom-call(s32[64,8]{1,0:T(8,128)S(1)} %copy.25.cidx, f32[64,16,128]{2,1,0:T(8,128)S(1)} %get-tuple-element.66.u, bf16[64,16,128]{2,1,0:T(8,128)(2,1)S(1)} %get-tuple-element.67.vb, bf16[128,128,128]{2,1,0:T(8,128)(2,1)S(1)} %copy-done.1, f32[16,16]{1,0:T(8,128)S(1)} %copy-done.2), custom_call_target="tpu_custom_call" | custom-call | flops 4000000 | bytes 4000000 | tf_op jit(solution)/shard_map/pallas_call | solution.py:228
  69.6 0.2 collective-permute-done.15.refs_0_
  69.8 0.9 collective-permute-done.16.refs_1_
  70.8 0.8 collective-permute-done.17.refs_2_
  71.6 4.4 %shard_map.73 = (f32[64,16,128]{2,1,0:T(8,128)S(1)}, bf16[64,16,128]{2,1,0:T(8,128)(2,1)S(1)}) custom-call(s32[13]{0:T(128)S(1)} %stack.75.flags, s32[4,16]{1,0:T(4,128)S(1)} %copy-done.4, s32[64,7]{1,0:T(8,128)S(1)} %copy.24.cols, s32[64,8]{1,0:T(8,128)S(1)} %copy.25.cidx, f32[64,16,128]{2,1,0:T(8,128)S(1)} %get-tuple-element.66.u, ...), custom_call_target="tpu_custom_call" | custom-call | flops 4000000 | bytes 4000000 | tf_op jit(solution)/shard_map/pallas_call | solution.py:228
  76.0 0.0 collective-permute-start.19
  76.0 7.0 %collective-permute-done.19.moved = bf16[64,16,128]{2,1,0:T(8,128)(2,1)S(1)} collective-permute-done((bf16[64,16,128]{2,1,0:T(8,128)(2,1)S(1)}, bf16[64,16,128]{2,1,0:T(8,128)(2,1)S(1)}, u32[]{:S(2)}, u32[]{:S(2)}) %collective-permute-start.19) | collective-permute-done | bytes 262176 | tf_op jit(solution)/shard_map/ppermute | solution.py:62
  83.0 1.0 shard_map.74
  84.0 1.7 %collective-permute-start.20 = (bf16[16,16,128]{2,1,0:T(8,128)(2,1)S(1)}, bf16[16,16,128]{2,1,0:T(8,128)(2,1)S(1)}, u32[]{:S(2)}, u32[]{:S(2)}) collective-permute-start(bf16[16,16,128]{2,1,0:T(8,128)(2,1)S(1)} %get-tuple-element.79), channel_id=1, source_target_pairs={{0,32},{1,33},{2,4},{3,5},{4,2},{5,3},{6,8},{7,9},{8,6},{9,7},{10,... | collective-permute-start | bytes 196616 | tf_op jit(solution)/shard_map/ppermute | solution.py:57
  85.8 1.9 %collective-permute-start.21 = (bf16[16,16,128]{2,1,0:T(8,128)(2,1)S(1)}, bf16[16,16,128]{2,1,0:T(8,128)(2,1)S(1)}, u32[]{:S(2)}, u32[]{:S(2)}) collective-permute-start(bf16[16,16,128]{2,1,0:T(8,128)(2,1)S(1)} %get-tuple-element.80), channel_id=1, source_target_pairs={{0,2},{1,3},{2,0},{3,1},{4,6},{5,7},{6,4},{7,5},{8,10},{9,11},{10,... | collective-permute-start | bytes 196616 | tf_op jit(solution)/shard_map/ppermute | solution.py:57
  87.6 1.9 %collective-permute-start.22 = (bf16[16,16,128]{2,1,0:T(8,128)(2,1)S(1)}, bf16[16,16,128]{2,1,0:T(8,128)(2,1)S(1)}, u32[]{:S(2)}, u32[]{:S(2)}) collective-permute-start(bf16[16,16,128]{2,1,0:T(8,128)(2,1)S(1)} %get-tuple-element.81), channel_id=1, source_target_pairs={{0,32},{1,2},{2,1},{3,4},{4,3},{5,6},{6,5},{7,8},{8,7},{9,10},{10,... | collective-permute-start | bytes 196616 | tf_op jit(solution)/shard_map/ppermute | solution.py:57
  89.5 2.4 %shard_map.75.part = f32[64,16,128]{2,1,0:T(8,128)S(1)} custom-call(s32[64,8]{1,0:T(8,128)S(1)} %copy.25.cidx, f32[64,16,128]{2,1,0:T(8,128)S(1)} %get-tuple-element.77.u, bf16[64,16,128]{2,1,0:T(8,128)(2,1)S(1)} %get-tuple-element.78.vb, bf16[128,128,128]{2,1,0:T(8,128)(2,1)S(1)} %copy-done.1, f32[16,16]{1,0:T(8,128)S(1)} %copy-done.2), custom_call_target="tpu_custom_call" | custom-call | flops 4000000 | bytes 4000000 | tf_op jit(solution)/shard_map/pallas_call | solution.py:228
  91.9 0.0 collective-permute-done.21.refs_1_
  91.9 2.1 %collective-permute-done.22.refs_2_ = bf16[16,16,128]{2,1,0:T(8,128)(2,1)S(1)} collective-permute-done((bf16[16,16,128]{2,1,0:T(8,128)(2,1)S(1)}, bf16[16,16,128]{2,1,0:T(8,128)(2,1)S(1)}, u32[]{:S(2)}, u32[]{:S(2)}) %collective-permute-start.22) | collective-permute-done | bytes 65568 | tf_op jit(solution)/shard_map/ppermute | solution.py:57
  94.0 4.6 %shard_map.76 = (f32[64,16,128]{2,1,0:T(8,128)S(1)}, bf16[64,16,128]{2,1,0:T(8,128)(2,1)S(1)}, bf16[16,16,128]{2,1,0:T(8,128)(2,1)S(1)}, bf16[16,16,128]{2,1,0:T...) custom-call(s32[13]{0:T(128)S(1)} %stack.75.flags, s32[4,16]{1,0:T(4,128)S(1)} %copy-done.4, ...), custom_call_target="tpu_custom_call" | custom-call | flops 4000000 | bytes 4000000 | tf_op jit(solution)/shard_map/pallas_call | solution.py:228
  98.6 1.7 %collective-permute-start.24 = (bf16[16,16,128]{2,1,0:T(8,128)(2,1)S(1)}, bf16[16,16,128]{2,1,0:T(8,128)(2,1)S(1)}, u32[]{:S(2)}, u32[]{:S(2)}) collective-permute-start(bf16[16,16,128]{2,1,0:T(8,128)(2,1)S(1)} %get-tuple-element.85), channel_id=1, source_target_pairs={{0,32},{1,33},{2,4},{3,5},{4,2},{5,3},{6,8},{7,9},{8,6},{9,7},{10,... | collective-permute-start | bytes 196616 | tf_op jit(solution)/shard_map/ppermute | solution.py:57
  100.3 2.0 %collective-permute-start.25 = (bf16[16,16,128]{2,1,0:T(8,128)(2,1)S(1)}, bf16[16,16,128]{2,1,0:T(8,128)(2,1)S(1)}, u32[]{:S(2)}, u32[]{:S(2)}) collective-permute-start(bf16[16,16,128]{2,1,0:T(8,128)(2,1)S(1)} %get-tuple-element.86), channel_id=1, source_target_pairs={{0,2},{1,3},{2,0},{3,1},{4,6},{5,7},{6,4},{7,5},{8,10},{9,11},{10,... | collective-permute-start | bytes 196616 | tf_op jit(solution)/shard_map/ppermute | solution.py:57
  102.3 2.0 %collective-permute-start.26 = (bf16[16,16,128]{2,1,0:T(8,128)(2,1)S(1)}, bf16[16,16,128]{2,1,0:T(8,128)(2,1)S(1)}, u32[]{:S(2)}, u32[]{:S(2)}) collective-permute-start(bf16[16,16,128]{2,1,0:T(8,128)(2,1)S(1)} %get-tuple-element.87), channel_id=1, source_target_pairs={{0,32},{1,2},{2,1},{3,4},{4,3},{5,6},{6,5},{7,8},{8,7},{9,10},{10,... | collective-permute-start | bytes 196616 | tf_op jit(solution)/shard_map/ppermute | solution.py:57
  104.3 2.4 %shard_map.77.part = f32[64,16,128]{2,1,0:T(8,128)S(1)} custom-call(s32[64,8]{1,0:T(8,128)S(1)} %copy.25.cidx, f32[64,16,128]{2,1,0:T(8,128)S(1)} %get-tuple-element.83.u, bf16[64,16,128]{2,1,0:T(8,128)(2,1)S(1)} %get-tuple-element.84.vb, bf16[128,128,128]{2,1,0:T(8,128)(2,1)S(1)} %copy-done.1, f32[16,16]{1,0:T(8,128)S(1)} %copy-done.2), custom_call_target="tpu_custom_call" | custom-call | flops 4000000 | bytes 4000000 | tf_op jit(solution)/shard_map/pallas_call | solution.py:228
  106.7 0.0 collective-permute-done.25.refs_1_
  106.7 2.0 %collective-permute-done.26.refs_2_ = bf16[16,16,128]{2,1,0:T(8,128)(2,1)S(1)} collective-permute-done((bf16[16,16,128]{2,1,0:T(8,128)(2,1)S(1)}, bf16[16,16,128]{2,1,0:T(8,128)(2,1)S(1)}, u32[]{:S(2)}, u32[]{:S(2)}) %collective-permute-start.26) | collective-permute-done | bytes 65568 | tf_op jit(solution)/shard_map/ppermute | solution.py:57
  108.7 4.4 %shard_map.78 = f32[64,16,128]{2,1,0:T(8,128)S(1)} custom-call(s32[13]{0:T(128)S(1)} %stack.75.flags, s32[4,16]{1,0:T(4,128)S(1)} %copy-done.4, s32[64,7]{1,0:T(8,128)S(1)} %copy.24.cols, s32[64,8]{1,0:T(8,128)S(1)} %copy.25.cidx, f32[64,16,128]{2,1,0:T(8,128)S(1)} %get-tuple-element.83.u, bf16[64,16,128]{2,1,0:T(8,128)(2,1)S(1)} %get-tuple-element.84.vb, ...), custom_call_target="tpu_custom_call" | custom-call | flops 4000000 | bytes 4000000 | tf_op jit(solution)/shard_map/pallas_call | solution.py:228
  113.1 1.0 copy.26
  (22 shorter events, 0.1 us)
Async XLA Ops:
  0.0 19.6 %copy-start.4 = (s32[4,16]{1,0:T(4,128)S(1)}, s32[4,16]{1,0:T(4,128)}, u32[]{:S(2)}) copy-start(s32[4,16]{1,0:T(4,128)} %lists.17) | copy-start | bytes 772
  1.4 29.7 %collective-permute-start = (f32[64,16,128]{2,1,0:T(8,128)S(1)}, f32[64,16,128]{2,1,0:T(8,128)S(1)}, u32[]{:S(2)}, u32[]{:S(2)}) collective-permute-start(f32[64,16,128]{2,1,0:T(8,128)S(1)} %bitcast.21), channel_id=1, source_target_pairs={{0,32},{32,64},{64,96},{96,128},{128,160},{160,192},{192,224},{224... | collective-permute-start | bytes 1572872 | tf_op jit(solution)/shard_map/ppermute | solution.py:62
  1.6 0.7 copy-start.3
  3.0 16.6 %collective-permute-start.1 = (bf16[16,16,128]{2,1,0:T(8,128)(2,1)S(1)}, bf16[16,16,128]{2,1,0:T(8,128)(2,1)S(1)}, u32[]{:S(2)}, u32[]{:S(2)}) collective-permute-start(bf16[16,16,128]{2,1,0:T(8,128)(2,1)S(1)} %get-tuple-element.48), channel_id=1, source_target_pairs={{0,32},{1,33},{2,4},{3,5},{4,2},{5,3},{6,8},{7,9},{8,6},{9,7},{10,... | collective-permute-start | bytes 196616 | tf_op jit(solution)/shard_map/ppermute | solution.py:57
  9.3 10.3 %collective-permute-start.2 = (bf16[16,16,128]{2,1,0:T(8,128)(2,1)S(1)}, bf16[16,16,128]{2,1,0:T(8,128)(2,1)S(1)}, u32[]{:S(2)}, u32[]{:S(2)}) collective-permute-start(bf16[16,16,128]{2,1,0:T(8,128)(2,1)S(1)} %get-tuple-element.49), channel_id=1, source_target_pairs={{0,2},{1,3},{2,0},{3,1},{4,6},{5,7},{6,4},{7,5},{8,10},{9,11},{10,... | collective-permute-start | bytes 196616 | tf_op jit(solution)/shard_map/ppermute | solution.py:57
  10.9 8.8 %collective-permute-start.3 = (bf16[16,16,128]{2,1,0:T(8,128)(2,1)S(1)}, bf16[16,16,128]{2,1,0:T(8,128)(2,1)S(1)}, u32[]{:S(2)}, u32[]{:S(2)}) collective-permute-start(bf16[16,16,128]{2,1,0:T(8,128)(2,1)S(1)} %get-tuple-element.50), channel_id=1, source_target_pairs={{0,32},{1,2},{2,1},{3,4},{4,3},{5,6},{6,5},{7,8},{8,7},{9,10},{10,... | collective-permute-start | bytes 196616 | tf_op jit(solution)/shard_map/ppermute | solution.py:57
  10.9 8.8 %collective-permute-start.4 = (bf16[16,16,128]{2,1,0:T(8,128)(2,1)S(1)}, bf16[16,16,128]{2,1,0:T(8,128)(2,1)S(1)}, u32[]{:S(2)}, u32[]{:S(2)}) collective-permute-start(bf16[16,16,128]{2,1,0:T(8,128)(2,1)S(1)} %get-tuple-element.51), channel_id=1, source_target_pairs={{0,1},{1,0},{2,3},{3,2},{4,5},{5,4},{6,7},{7,6},{8,9},{9,8},{10,11... | collective-permute-start | bytes 196616 | tf_op jit(solution)/shard_map/ppermute | solution.py:57
  14.3 2.2 %copy-start = (bf16[128,128,128]{2,1,0:T(8,128)(2,1)S(1)}, bf16[128,128,128]{2,1,0:T(8,128)(2,1)}, u32[]{:S(2)}) copy-start(bf16[128,128,128]{2,1,0:T(8,128)(2,1)} %refs_4_.11) | copy-start | bytes 12582916
  16.5 0.7 copy-start.2
  17.2 2.4 %copy-start.1 = (bf16[128,128,128]{2,1,0:T(8,128)(2,1)S(1)}, bf16[128,128,128]{2,1,0:T(8,128)(2,1)}, u32[]{:S(2)}) copy-start(bf16[128,128,128]{2,1,0:T(8,128)(2,1)} %refs_4_.11) | copy-start | bytes 12582916
  24.1 7.0 %collective-permute-start.5 = (bf16[64,16,128]{2,1,0:T(8,128)(2,1)S(1)}, bf16[64,16,128]{2,1,0:T(8,128)(2,1)S(1)}, u32[]{:S(2)}, u32[]{:S(2)}) collective-permute-start(bf16[64,16,128]{2,1,0:T(8,128)(2,1)S(1)} %get-tuple-element.53), channel_id=1, source_target_pairs={{0,32},{32,64},{64,96},{96,128},{128,160},{160,192},{192,224},{224... | collective-permute-start | bytes 786440 | tf_op jit(solution)/shard_map/ppermute | solution.py:62
  32.1 9.6 %collective-permute-start.6 = (bf16[16,16,128]{2,1,0:T(8,128)(2,1)S(1)}, bf16[16,16,128]{2,1,0:T(8,128)(2,1)S(1)}, u32[]{:S(2)}, u32[]{:S(2)}) collective-permute-start(bf16[16,16,128]{2,1,0:T(8,128)(2,1)S(1)} %get-tuple-element.56), channel_id=1, source_target_pairs={{0,32},{1,33},{2,4},{3,5},{4,2},{5,3},{6,8},{7,9},{8,6},{9,7},{10,... | collective-permute-start | bytes 196616 | tf_op jit(solution)/shard_map/ppermute | solution.py:57
  35.8 5.9 %collective-permute-start.7 = (bf16[16,16,128]{2,1,0:T(8,128)(2,1)S(1)}, bf16[16,16,128]{2,1,0:T(8,128)(2,1)S(1)}, u32[]{:S(2)}, u32[]{:S(2)}) collective-permute-start(bf16[16,16,128]{2,1,0:T(8,128)(2,1)S(1)} %get-tuple-element.57), channel_id=1, source_target_pairs={{0,2},{1,3},{2,0},{3,1},{4,6},{5,7},{6,4},{7,5},{8,10},{9,11},{10,... | collective-permute-start | bytes 196616 | tf_op jit(solution)/shard_map/ppermute | solution.py:57
  35.8 6.4 %collective-permute-start.8 = (bf16[16,16,128]{2,1,0:T(8,128)(2,1)S(1)}, bf16[16,16,128]{2,1,0:T(8,128)(2,1)S(1)}, u32[]{:S(2)}, u32[]{:S(2)}) collective-permute-start(bf16[16,16,128]{2,1,0:T(8,128)(2,1)S(1)} %get-tuple-element.58), channel_id=1, source_target_pairs={{0,32},{1,2},{2,1},{3,4},{4,3},{5,6},{6,5},{7,8},{8,7},{9,10},{10,... | collective-permute-start | bytes 196616 | tf_op jit(solution)/shard_map/ppermute | solution.py:57
  37.3 4.9 %collective-permute-start.9 = (bf16[16,16,128]{2,1,0:T(8,128)(2,1)S(1)}, bf16[16,16,128]{2,1,0:T(8,128)(2,1)S(1)}, u32[]{:S(2)}, u32[]{:S(2)}) collective-permute-start(bf16[16,16,128]{2,1,0:T(8,128)(2,1)S(1)} %get-tuple-element.59), channel_id=1, source_target_pairs={{0,1},{1,0},{2,3},{3,2},{4,5},{5,4},{6,7},{7,6},{8,9},{9,8},{10,11... | collective-permute-start | bytes 196616 | tf_op jit(solution)/shard_map/ppermute | solution.py:57
  46.8 8.0 %collective-permute-start.10 = (bf16[16,16,128]{2,1,0:T(8,128)(2,1)S(1)}, bf16[16,16,128]{2,1,0:T(8,128)(2,1)S(1)}, u32[]{:S(2)}, u32[]{:S(2)}) collective-permute-start(bf16[16,16,128]{2,1,0:T(8,128)(2,1)S(1)} %get-tuple-element.62), channel_id=1, source_target_pairs={{0,32},{1,33},{2,4},{3,5},{4,2},{5,3},{6,8},{7,9},{8,6},{9,7},{10,... | collective-permute-start | bytes 196616 | tf_op jit(solution)/shard_map/ppermute | solution.py:57
  48.6 6.3 %collective-permute-start.11 = (bf16[16,16,128]{2,1,0:T(8,128)(2,1)S(1)}, bf16[16,16,128]{2,1,0:T(8,128)(2,1)S(1)}, u32[]{:S(2)}, u32[]{:S(2)}) collective-permute-start(bf16[16,16,128]{2,1,0:T(8,128)(2,1)S(1)} %get-tuple-element.63), channel_id=1, source_target_pairs={{0,2},{1,3},{2,0},{3,1},{4,6},{5,7},{6,4},{7,5},{8,10},{9,11},{10,... | collective-permute-start | bytes 196616 | tf_op jit(solution)/shard_map/ppermute | solution.py:57
  50.4 6.4 %collective-permute-start.12 = (bf16[16,16,128]{2,1,0:T(8,128)(2,1)S(1)}, bf16[16,16,128]{2,1,0:T(8,128)(2,1)S(1)}, u32[]{:S(2)}, u32[]{:S(2)}) collective-permute-start(bf16[16,16,128]{2,1,0:T(8,128)(2,1)S(1)} %get-tuple-element.64), channel_id=1, source_target_pairs={{0,32},{1,2},{2,1},{3,4},{4,3},{5,6},{6,5},{7,8},{8,7},{9,10},{10,... | collective-permute-start | bytes 196616 | tf_op jit(solution)/shard_map/ppermute | solution.py:57
  52.3 4.5 %collective-permute-start.13 = (bf16[16,16,128]{2,1,0:T(8,128)(2,1)S(1)}, bf16[16,16,128]{2,1,0:T(8,128)(2,1)S(1)}, u32[]{:S(2)}, u32[]{:S(2)}) collective-permute-start(bf16[16,16,128]{2,1,0:T(8,128)(2,1)S(1)} %get-tuple-element.65), channel_id=1, source_target_pairs={{0,1},{1,0},{2,3},{3,2},{4,5},{5,4},{6,7},{7,6},{8,9},{9,8},{10,11... | collective-permute-start | bytes 196616 | tf_op jit(solution)/shard_map/ppermute | solution.py:57
  61.4 21.6 %collective-permute-start.14 = (f32[64,16,128]{2,1,0:T(8,128)S(1)}, f32[64,16,128]{2,1,0:T(8,128)S(1)}, u32[]{:S(2)}, u32[]{:S(2)}) collective-permute-start(f32[64,16,128]{2,1,0:T(8,128)S(1)} %get-tuple-element.66.u), channel_id=1, source_target_pairs={{0,32},{32,64},{64,96},{96,128},{128,160},{160,192},{192,224},{224... | collective-permute-start | bytes 1572872 | tf_op jit(solution)/shard_map/ppermute | solution.py:62
  61.4 8.4 %collective-permute-start.15 = (bf16[16,16,128]{2,1,0:T(8,128)(2,1)S(1)}, bf16[16,16,128]{2,1,0:T(8,128)(2,1)S(1)}, u32[]{:S(2)}, u32[]{:S(2)}) collective-permute-start(bf16[16,16,128]{2,1,0:T(8,128)(2,1)S(1)} %get-tuple-element.68), channel_id=1, source_target_pairs={{0,32},{1,33},{2,4},{3,5},{4,2},{5,3},{6,8},{7,9},{8,6},{9,7},{10,... | collective-permute-start | bytes 196616 | tf_op jit(solution)/shard_map/ppermute | solution.py:57
  63.7 7.0 %collective-permute-start.16 = (bf16[16,16,128]{2,1,0:T(8,128)(2,1)S(1)}, bf16[16,16,128]{2,1,0:T(8,128)(2,1)S(1)}, u32[]{:S(2)}, u32[]{:S(2)}) collective-permute-start(bf16[16,16,128]{2,1,0:T(8,128)(2,1)S(1)} %get-tuple-element.69), channel_id=1, source_target_pairs={{0,2},{1,3},{2,0},{3,1},{4,6},{5,7},{6,4},{7,5},{8,10},{9,11},{10,... | collective-permute-start | bytes 196616 | tf_op jit(solution)/shard_map/ppermute | solution.py:57
  65.2 6.4 %collective-permute-start.17 = (bf16[16,16,128]{2,1,0:T(8,128)(2,1)S(1)}, bf16[16,16,128]{2,1,0:T(8,128)(2,1)S(1)}, u32[]{:S(2)}, u32[]{:S(2)}) collective-permute-start(bf16[16,16,128]{2,1,0:T(8,128)(2,1)S(1)} %get-tuple-element.70), channel_id=1, source_target_pairs={{0,32},{1,2},{2,1},{3,4},{4,3},{5,6},{6,5},{7,8},{8,7},{9,10},{10,... | collective-permute-start | bytes 196616 | tf_op jit(solution)/shard_map/ppermute | solution.py:57
  67.1 4.5 %collective-permute-start.18 = (bf16[16,16,128]{2,1,0:T(8,128)(2,1)S(1)}, bf16[16,16,128]{2,1,0:T(8,128)(2,1)S(1)}, u32[]{:S(2)}, u32[]{:S(2)}) collective-permute-start(bf16[16,16,128]{2,1,0:T(8,128)(2,1)S(1)} %get-tuple-element.71), channel_id=1, source_target_pairs={{0,1},{1,0},{2,3},{3,2},{4,5},{5,4},{6,7},{7,6},{8,9},{9,8},{10,11... | collective-permute-start | bytes 196616 | tf_op jit(solution)/shard_map/ppermute | solution.py:57
  76.0 7.0 %collective-permute-start.19 = (bf16[64,16,128]{2,1,0:T(8,128)(2,1)S(1)}, bf16[64,16,128]{2,1,0:T(8,128)(2,1)S(1)}, u32[]{:S(2)}, u32[]{:S(2)}) collective-permute-start(bf16[64,16,128]{2,1,0:T(8,128)(2,1)S(1)} %get-tuple-element.72), channel_id=1, source_target_pairs={{0,32},{32,64},{64,96},{96,128},{128,160},{160,192},{192,224},{224... | collective-permute-start | bytes 786440 | tf_op jit(solution)/shard_map/ppermute | solution.py:62
  84.0 7.9 %collective-permute-start.20 = (bf16[16,16,128]{2,1,0:T(8,128)(2,1)S(1)}, bf16[16,16,128]{2,1,0:T(8,128)(2,1)S(1)}, u32[]{:S(2)}, u32[]{:S(2)}) collective-permute-start(bf16[16,16,128]{2,1,0:T(8,128)(2,1)S(1)} %get-tuple-element.79), channel_id=1, source_target_pairs={{0,32},{1,33},{2,4},{3,5},{4,2},{5,3},{6,8},{7,9},{8,6},{9,7},{10,... | collective-permute-start | bytes 196616 | tf_op jit(solution)/shard_map/ppermute | solution.py:57
  85.8 6.2 %collective-permute-start.21 = (bf16[16,16,128]{2,1,0:T(8,128)(2,1)S(1)}, bf16[16,16,128]{2,1,0:T(8,128)(2,1)S(1)}, u32[]{:S(2)}, u32[]{:S(2)}) collective-permute-start(bf16[16,16,128]{2,1,0:T(8,128)(2,1)S(1)} %get-tuple-element.80), channel_id=1, source_target_pairs={{0,2},{1,3},{2,0},{3,1},{4,6},{5,7},{6,4},{7,5},{8,10},{9,11},{10,... | collective-permute-start | bytes 196616 | tf_op jit(solution)/shard_map/ppermute | solution.py:57
  87.6 6.4 %collective-permute-start.22 = (bf16[16,16,128]{2,1,0:T(8,128)(2,1)S(1)}, bf16[16,16,128]{2,1,0:T(8,128)(2,1)S(1)}, u32[]{:S(2)}, u32[]{:S(2)}) collective-permute-start(bf16[16,16,128]{2,1,0:T(8,128)(2,1)S(1)} %get-tuple-element.81), channel_id=1, source_target_pairs={{0,32},{1,2},{2,1},{3,4},{4,3},{5,6},{6,5},{7,8},{8,7},{9,10},{10,... | collective-permute-start | bytes 196616 | tf_op jit(solution)/shard_map/ppermute | solution.py:57
  89.5 4.5 %collective-permute-start.23 = (bf16[16,16,128]{2,1,0:T(8,128)(2,1)S(1)}, bf16[16,16,128]{2,1,0:T(8,128)(2,1)S(1)}, u32[]{:S(2)}, u32[]{:S(2)}) collective-permute-start(bf16[16,16,128]{2,1,0:T(8,128)(2,1)S(1)} %get-tuple-element.82), channel_id=1, source_target_pairs={{0,1},{1,0},{2,3},{3,2},{4,5},{5,4},{6,7},{7,6},{8,9},{9,8},{10,11... | collective-permute-start | bytes 196616 | tf_op jit(solution)/shard_map/ppermute | solution.py:57
  98.6 8.1 %collective-permute-start.24 = (bf16[16,16,128]{2,1,0:T(8,128)(2,1)S(1)}, bf16[16,16,128]{2,1,0:T(8,128)(2,1)S(1)}, u32[]{:S(2)}, u32[]{:S(2)}) collective-permute-start(bf16[16,16,128]{2,1,0:T(8,128)(2,1)S(1)} %get-tuple-element.85), channel_id=1, source_target_pairs={{0,32},{1,33},{2,4},{3,5},{4,2},{5,3},{6,8},{7,9},{8,6},{9,7},{10,... | collective-permute-start | bytes 196616 | tf_op jit(solution)/shard_map/ppermute | solution.py:57
  100.3 6.3 %collective-permute-start.25 = (bf16[16,16,128]{2,1,0:T(8,128)(2,1)S(1)}, bf16[16,16,128]{2,1,0:T(8,128)(2,1)S(1)}, u32[]{:S(2)}, u32[]{:S(2)}) collective-permute-start(bf16[16,16,128]{2,1,0:T(8,128)(2,1)S(1)} %get-tuple-element.86), channel_id=1, source_target_pairs={{0,2},{1,3},{2,0},{3,1},{4,6},{5,7},{6,4},{7,5},{8,10},{9,11},{10,... | collective-permute-start | bytes 196616 | tf_op jit(solution)/shard_map/ppermute | solution.py:57
  102.3 6.4 %collective-permute-start.26 = (bf16[16,16,128]{2,1,0:T(8,128)(2,1)S(1)}, bf16[16,16,128]{2,1,0:T(8,128)(2,1)S(1)}, u32[]{:S(2)}, u32[]{:S(2)}) collective-permute-start(bf16[16,16,128]{2,1,0:T(8,128)(2,1)S(1)} %get-tuple-element.87), channel_id=1, source_target_pairs={{0,32},{1,2},{2,1},{3,4},{4,3},{5,6},{6,5},{7,8},{8,7},{9,10},{10,... | collective-permute-start | bytes 196616 | tf_op jit(solution)/shard_map/ppermute | solution.py:57
  104.3 4.4 %collective-permute-start.27 = (bf16[16,16,128]{2,1,0:T(8,128)(2,1)S(1)}, bf16[16,16,128]{2,1,0:T(8,128)(2,1)S(1)}, u32[]{:S(2)}, u32[]{:S(2)}) collective-permute-start(bf16[16,16,128]{2,1,0:T(8,128)(2,1)S(1)} %get-tuple-element.88), channel_id=1, source_target_pairs={{0,1},{1,0},{2,3},{3,2},{4,5},{5,4},{6,7},{7,6},{8,9},{9,8},{10,11... | collective-permute-start | bytes 196616 | tf_op jit(solution)/shard_map/ppermute | solution.py:57

commit v3 on v2

--- a/solution.py
+++ b/solution.py
@@ -37,7 +37,7 @@
 bf16 = jnp.bfloat16
 VMEM = pl.BlockSpec(memory_space=pltpu.VMEM)
 SMEM = pl.BlockSpec(memory_space=pltpu.SMEM)
-PARAMS = pltpu.CompilerParams(vmem_limit_bytes=32 * 1024 * 1024)
+PARAMS = pltpu.CompilerParams(vmem_limit_bytes=8 * 1024 * 1024)
 UNROLL = 16
 
 
@@ -62,6 +62,7 @@
     return lax.ppermute(block, "tm", [(i, (i + 1) % n) for i in range(n)])
 
 
+PLAN = 13
 PAIRS = ((2, True), (2, False), (1, True), (1, False))
 
 
@@ -84,47 +85,59 @@
     return jnp.stack([x.astype(jnp.int32) for x in sends + fills + valid + [leading]])
 
 
-def pack(flags, lists, vb, packs):
+def pack(flags, vb, packs):
     slots = packs[0].shape[0]
     for k, out in enumerate(packs):
+        first = PLAN + flags[k] * slots
         for j in range(slots):
-            row = lists[flags[k], j]
+            row = flags[first + j]
             block = vb[jnp.maximum(row, 0)]
             out[j] = jnp.where(row >= 0, block, jnp.zeros_like(block))
 
 
-def first_kernel(flags, lists, u, vb, *packs):
+def first_kernel(flags, u, vb, *packs):
     vb[...] = u[...].astype(bf16)
-    pack(flags, lists, vb, packs)
-
-
-def own_kernel(cidx, u, vb, coeffs, mixing, part):
+    pack(flags, vb, packs)
+
+
+def first_reaction_kernel(u, mixing, coeffs, part, mix):
+    del coeffs
     m = mixing[...]
     m_hi = m.astype(bf16)
     m_lo = (m - m_hi.astype(f32)).astype(bf16)
-    mix = jnp.concatenate([m_hi, m_lo, m_hi], axis=1)
+    mix[...] = jnp.concatenate([m_hi, m_lo, m_hi], axis=1)
+    reaction_kernel(None, 0, u, mix, part)
+
+
+def reaction_kernel(prepare, extras, u, mix, *refs):
+    olds, outs = refs[:extras], refs[extras:]
+    mixv = mix[...]
 
     def body(i, carry):
         for j in range(UNROLL):
             b = i * UNROLL + j
-            th = jnp.tanh(u[b])
+            field = u[b]
+            th = jnp.tanh(field)
             hi = th.astype(bf16)
             lo = (th - hi.astype(f32)).astype(bf16)
-            own = jnp.dot(vb[b], coeffs[cidx[b, 0]], preferred_element_type=f32)
-            part[b] = own + jnp.dot(mix, jnp.concatenate([hi, hi, lo], axis=0), preferred_element_type=f32)
+            outs[0][b] = jnp.dot(mixv, jnp.concatenate([hi, hi, lo], axis=0), preferred_element_type=f32)
+            if prepare is not None:
+                outs[1][b] = prepare(field, [old[b] for old in olds])
         return carry
 
     lax.fori_loop(0, u.shape[0] // UNROLL, body, 0)
 
 
-def force_kernel(update, extras, keep, send, flags, lists, cols, cidx, u, vb, part, *refs):
+def force_kernel(gap, keep, send, flags, table, vb, part, *refs):
     received, refs = refs[:4], refs[4:]
     coeffs, refs = refs[0], refs[1:]
-    olds, refs = refs[:extras], refs[extras:]
+    if gap is not None:
+        base, refs = refs[0], refs[1:]
     outs, ext = refs[:-1], refs[-1]
     nblocks = vb.shape[0]
     slots = received[0].shape[0]
-    terms = cols.shape[1]
+    width = table.shape[0] // nblocks
+    terms = (width + 1) // 2
     ext[0:nblocks] = vb[...]
     for k, got in enumerate(received):
         live = flags[8 + k] > 0
@@ -134,8 +147,8 @@
     def body(i, carry):
         for j in range(UNROLL):
             b = i * UNROLL + j
-            xs = [ext[cols[b, t]] for t in range(terms)]
-            ws = [coeffs[cidx[b, t + 1]] for t in range(terms)]
+            xs = [vb[b]] + [ext[table[b * width + terms + t]] for t in range(terms - 1)]
+            ws = [coeffs[table[b * width + t]] for t in range(terms)]
             force = part[b] + jnp.dot(
                 jnp.concatenate(xs, axis=1), jnp.concatenate(ws, axis=0), preferred_element_type=f32
             )
@@ -143,10 +156,10 @@
             if keep:
                 outs[at][b] = force
                 at += 1
-            if update is None:
+            if gap is None:
                 outs[at][b] = force.astype(bf16)
                 continue
-            new = update(u[b], force, [old[b] for old in olds])
+            new = base[b] + (step_size * gap) * force
             outs[at][b] = new
             if send:
                 outs[at + 1][b] = new.astype(bf16)
@@ -154,10 +167,10 @@
 
     lax.fori_loop(0, nblocks // UNROLL, body, 0)
     if send:
-        pack(flags, lists, outs[-5], outs[-4:])
-
-
-def early_kernel(flags, lists, guess, incoming, force, moved, e0, u, vb, *packs):
+        pack(flags, outs[-5], outs[-4:])
+
+
+def early_kernel(flags, guess, incoming, force, moved, e0, u, vb, *packs):
     leading = flags[12] > 0
     g, q = node_gaps[0], sum(node_integrals[0])
 
@@ -172,10 +185,10 @@
         return carry
 
     lax.fori_loop(0, u.shape[0], body, 0, unroll=8)
-    pack(flags, lists, vb, packs)
-
-
-def late_kernel(flags, lists, guess, incoming, moved, e0, e1, e2, e3, u, vb, *packs):
+    pack(flags, vb, packs)
+
+
+def late_kernel(flags, guess, incoming, moved, e0, e1, e2, e3, u, vb, *packs):
     leading = flags[12] > 0
     g, q = node_gaps[0], node_integrals[0]
 
@@ -190,35 +203,35 @@
         return carry
 
     lax.fori_loop(0, u.shape[0], body, 0, unroll=8)
-    pack(flags, lists, vb, packs)
-
-
-def node_update_first(node):
+    pack(flags, vb, packs)
+
+
+def prepare_first(node):
     g, q = node_gaps[node], sum(node_integrals[node])
 
-    def update(u, e, olds):
+    def prepare(u, olds):
         (f,) = olds
-        return u + step_size * (g * (e - f) + q * f)
-
-    return update
-
-
-def node_update_second(node):
+        return u + step_size * (q * f - g * f)
+
+    return prepare
+
+
+def prepare_second(node):
     g, q = node_gaps[node], node_integrals[node]
 
-    def update(u, e, olds):
+    def prepare(u, olds):
         quad = q[0] * olds[0] + q[1] * olds[1] + q[2] * olds[2]
-        return u + step_size * (g * (e - olds[node - 1]) + quad)
-
-    return update
+        return u + step_size * (quad - g * olds[node - 1])
+
+    return prepare
 
 
 def per_device(guess, coeffs, coef_index, neighbours, send_lists, mixing):
     first = jnp.transpose(guess[0], (1, 0, 2))
     nblocks, species, cells = first.shape
     slots = send_lists.shape[1]
-    lists = send_lists
-    flags = plan()
+    flags = jnp.concatenate([plan(), send_lists.reshape(-1)])
+    table = jnp.concatenate([coef_index, neighbours], axis=1).reshape(-1)
 
     state = jax.ShapeDtypeStruct((nblocks, species, cells), f32)
     rounded = jax.ShapeDtypeStruct((nblocks, species, cells), bf16)
@@ -236,51 +249,49 @@
         )(*scalars, *arrays)
 
     ext = [pltpu.VMEM((nblocks + 4 * slots, species, cells), bf16)]
-
-    def force(u, vb, received, update, olds, keep, send):
-        (part,) = call(own_kernel, [state], (coef_index,), (u, vb, coeffs, mixing))
-        outs = []
-        if keep:
-            outs.append(state)
-        if update is None:
-            outs.append(rounded)
-        else:
-            outs.append(state)
+    vb, *packs = call(first_kernel, [rounded] + [rim] * 4, (flags,), (first,))
+
+    part, mix = call(
+        first_reaction_kernel,
+        [state, jax.ShapeDtypeStruct((species, 3 * species), bf16)],
+        (),
+        (first, mixing, coeffs),
+    )
+
+    def force(u, vb, packs, node, prepare, olds, keep, send, part=None):
+        received = exchange(packs)
+        rest = ()
+        if part is None:
+            kernel = functools.partial(reaction_kernel, prepare, len(olds))
+            outs = [state] * (1 + (prepare is not None))
+            part, *rest = call(kernel, outs, (), (u, mix, *olds))
+        outs = [state] * keep + [rounded if node is None else state]
         if send:
             outs += [rounded] + [rim] * 4
-        kernel = functools.partial(force_kernel, update, len(olds), keep, send)
-        return call(
-            kernel,
-            outs,
-            (flags, lists, neighbours, coef_index),
-            (u, vb, part, *received, coeffs, *olds),
-            ext,
-        )
-
-    vb, *packs = call(first_kernel, [rounded] + [rim] * 4, (flags, lists), (first,))
-    received = exchange(packs)
-    came = next_slice(first)
-    f, fb = force(first, vb, received, None, (), True, False)
+        gap = None if node is None else node_gaps[node]
+        kernel = functools.partial(force_kernel, gap, keep, send)
+        return call(kernel, outs, (flags, table), (vb, part, *received, coeffs, *rest), ext)
+
+    f, fb = force(first, vb, packs, None, None, (), True, False, part)
     e0, u, vb, *packs = call(
         early_kernel,
         [state, state, rounded] + [rim] * 4,
-        (flags, lists),
-        (first, came, f, next_slice(fb)),
-    )
-    e1, u, vb, *packs = force(u, vb, exchange(packs), node_update_first(1), (f,), True, True)
-    e2, u, vb, *packs = force(u, vb, exchange(packs), node_update_first(2), (f,), True, True)
-    received = exchange(packs)
+        (flags,),
+        (first, next_slice(first), f, next_slice(fb)),
+    )
+    e1, u, vb, *packs = force(u, vb, packs, 1, prepare_first(1), (f,), True, True)
+    e2, u, vb, *packs = force(u, vb, packs, 2, prepare_first(2), (f,), True, True)
     came = next_slice(u)
-    e3, e3b = force(u, vb, received, None, (), True, False)
+    e3, e3b = force(u, vb, packs, None, None, (), True, False)
     u, vb, *packs = call(
         late_kernel,
         [state, rounded] + [rim] * 4,
-        (flags, lists),
+        (flags,),
         (first, came, next_slice(e3b), e0, e1, e2, e3),
     )
     olds = (e1, e2, e3)
-    u, vb, *packs = force(u, vb, exchange(packs), node_update_second(1), olds, False, True)
-    (end,) = force(u, vb, exchange(packs), node_update_second(2), olds, False, False)
+    u, vb, *packs = force(u, vb, packs, 1, prepare_second(1), olds, False, True)
+    (end,) = force(u, vb, packs, 2, prepare_second(2), olds, False, False)
     return jnp.transpose(end, (1, 0, 2))[None]
 
 

time: 114 us -> 108 us (0.947)
  Pallas kernels: 44.1 us -> 28.7 us
  waiting for transfers between devices: 22.3 us -> 30.8 us
    pallas_call x15, Pallas kernels: 44.1 us -> 28.7 us  [call(): pl.pallas_call(kernel, out_shape=outs, in_specs=[SMEM] * len(scalars) + [...]
    ppermute x24, waiting for transfers between devices: 8.63 us -> 17.2 us  [swap(): return lax.ppermute(block, ('tm', 'space'), route)]
    unnamed x13 -> x7, local copies, waits for them, and re-layouts: 6.48 us -> 5.13 us
  transfers between devices with their start and end apart: 28 -> 28, of which waited for: 10 -> 14; matrix products, arithmetic and copies ran while one was open for 1% -> 2% of each run, Pallas kernels for 21% -> 11%
where the time goes in v3:
time: 108 us
  starting transfers between devices  39.9 us (37%)
  waiting for transfers between devices  30.8 us (29%)
  Pallas kernels  28.7 us (27%)
  local copies, waits for them, and re-layouts  7.18 us (7%)
    ppermute x24, starting transfers between devices, swap(): return lax.ppermute(block, ('tm', 'space'), route)  39.5 us
    pallas_call x15, Pallas kernels, call(): pl.pallas_call(kernel, out_shape=outs, in_specs=[SMEM] * len(scalars) + [...  28.7 us
    ppermute x24, waiting for transfers between devices, swap(): return lax.ppermute(block, ('tm', 'space'), route)  17.2 us
    ppermute x4, waiting for transfers between devices, next_slice(): return lax.ppermute(block, 'tm', [(i, (i + 1) % n) for i in range(n)])  13.6 us
    unnamed x7, local copies, waits for them, and re-layouts  5.13 us
  transfers between devices with their start and end apart: 28, of which 14 were waited for; matrix products, arithmetic and copies ran while one was open for 2% of the time, Pallas kernels for 11%

profile of v3, /device:TPU:8, one launch (start us, length us, event | category | flops | bytes accessed | tf_op | source)
XLA Modules:
  0.0 107.6 jit_solution(7821688157815906043)
XLA Ops:
  0.0 1.3 %copy.13 = f32[1,16,64,128]{3,1,2,0:T(8,128)S(1)} copy(f32[1,16,64,128]{3,2,1,0:T(8,128)} %param.6) | data formatting | bytes 1048576 | tf_op args[0]
  1.4 0.0 collective-permute-start
  1.5 0.8 reshape.6
  2.2 0.1 concatenate.6.flags
  2.3 0.7 shard_map.64
  3.1 6.3 %collective-permute-start.1 = (bf16[16,16,128]{2,1,0:T(8,128)(2,1)S(1)}, bf16[16,16,128]{2,1,0:T(8,128)(2,1)S(1)}, u32[]{:S(2)}, u32[]{:S(2)}) collective-permute-start(bf16[16,16,128]{2,1,0:T(8,128)(2,1)S(1)} %get-tuple-element.59), channel_id=1, source_target_pairs={{0,32},{1,33},{2,4},{3,5},{4,2},{5,3},{6,8},{7,9},{8,6},{9,7},{10,... | collective-permute-start | bytes 196616 | tf_op jit(solution)/shard_map/ppermute | solution.py:57
  9.3 1.6 %collective-permute-start.2 = (bf16[16,16,128]{2,1,0:T(8,128)(2,1)S(1)}, bf16[16,16,128]{2,1,0:T(8,128)(2,1)S(1)}, u32[]{:S(2)}, u32[]{:S(2)}) collective-permute-start(bf16[16,16,128]{2,1,0:T(8,128)(2,1)S(1)} %get-tuple-element.60), channel_id=1, source_target_pairs={{0,2},{1,3},{2,0},{3,1},{4,6},{5,7},{6,4},{7,5},{8,10},{9,11},{10,... | collective-permute-start | bytes 196616 | tf_op jit(solution)/shard_map/ppermute | solution.py:57
  10.9 1.9 %collective-permute-start.4 = (bf16[16,16,128]{2,1,0:T(8,128)(2,1)S(1)}, bf16[16,16,128]{2,1,0:T(8,128)(2,1)S(1)}, u32[]{:S(2)}, u32[]{:S(2)}) collective-permute-start(bf16[16,16,128]{2,1,0:T(8,128)(2,1)S(1)} %get-tuple-element.62), channel_id=1, source_target_pairs={{0,1},{1,0},{2,3},{3,2},{4,5},{5,4},{6,7},{7,6},{8,9},{9,8},{10,11... | collective-permute-start | bytes 196616 | tf_op jit(solution)/shard_map/ppermute | solution.py:57
  12.8 0.7 pad_add_fusion
  13.5 0.1 copy.9
  13.6 0.1 reshape.7.table
  13.8 0.0 copy-start
  13.8 2.2 %copy-done = bf16[128,128,128]{2,1,0:T(8,128)(2,1)S(1)} copy-done((bf16[128,128,128]{2,1,0:T(8,128)(2,1)S(1)}, bf16[128,128,128]{2,1,0:T(8,128)(2,1)}, u32[]{:S(2)}) %copy-start) | copy-done | bytes 4194328
  16.0 0.7 copy-done.2
  16.7 0.8 shard_map.65
  17.5 0.0 collective-permute-done.1.refs_0_
  17.5 0.4 collective-permute-done.3.refs_2_
  18.0 0.9 copy-done.1
  18.9 3.5 %shard_map.66 = (f32[64,16,128]{2,1,0:T(8,128)S(1)}, bf16[64,16,128]{2,1,0:T(8,128)(2,1)S(1)}) custom-call(s32[77]{0:T(128)S(1)} %concatenate.6.flags, s32[960]{0:T(1024)S(1)} %reshape.7.table, bf16[64,16,128]{2,1,0:T(8,128)(2,1)S(1)} %get-tuple-element.57.vb, f32[64,16,128]{2,1,0:T(8,128)S(1)} %get-tuple-element.58.part, ...), custom_call_target="tpu_custom_call" | custom-call | flops 4000000 | bytes 4000000 | tf_op jit(solution)/shard_map/pallas_call | solution.py:241
  22.3 0.4 collective-permute-start.5
  22.7 6.6 %collective-permute-done.5.moved = bf16[64,16,128]{2,1,0:T(8,128)(2,1)S(1)} collective-permute-done((bf16[64,16,128]{2,1,0:T(8,128)(2,1)S(1)}, bf16[64,16,128]{2,1,0:T(8,128)(2,1)S(1)}, u32[]{:S(2)}, u32[]{:S(2)}) %collective-permute-start.5) | collective-permute-done | bytes 262176 | tf_op jit(solution)/shard_map/ppermute | solution.py:62
  29.3 0.9 shard_map.67
  30.3 3.8 %collective-permute-start.6 = (bf16[16,16,128]{2,1,0:T(8,128)(2,1)S(1)}, bf16[16,16,128]{2,1,0:T(8,128)(2,1)S(1)}, u32[]{:S(2)}, u32[]{:S(2)}) collective-permute-start(bf16[16,16,128]{2,1,0:T(8,128)(2,1)S(1)} %get-tuple-element.69), channel_id=1, source_target_pairs={{0,32},{1,33},{2,4},{3,5},{4,2},{5,3},{6,8},{7,9},{8,6},{9,7},{10,... | collective-permute-start | bytes 196616 | tf_op jit(solution)/shard_map/ppermute | solution.py:57
  34.1 1.5 %collective-permute-start.8 = (bf16[16,16,128]{2,1,0:T(8,128)(2,1)S(1)}, bf16[16,16,128]{2,1,0:T(8,128)(2,1)S(1)}, u32[]{:S(2)}, u32[]{:S(2)}) collective-permute-start(bf16[16,16,128]{2,1,0:T(8,128)(2,1)S(1)} %get-tuple-element.71), channel_id=1, source_target_pairs={{0,32},{1,2},{2,1},{3,4},{4,3},{5,6},{6,5},{7,8},{8,7},{9,10},{10,... | collective-permute-start | bytes 196616 | tf_op jit(solution)/shard_map/ppermute | solution.py:57
  35.5 2.0 %collective-permute-start.9 = (bf16[16,16,128]{2,1,0:T(8,128)(2,1)S(1)}, bf16[16,16,128]{2,1,0:T(8,128)(2,1)S(1)}, u32[]{:S(2)}, u32[]{:S(2)}) collective-permute-start(bf16[16,16,128]{2,1,0:T(8,128)(2,1)S(1)} %get-tuple-element.72), channel_id=1, source_target_pairs={{0,1},{1,0},{2,3},{3,2},{4,5},{5,4},{6,7},{7,6},{8,9},{9,8},{10,11... | collective-permute-start | bytes 196616 | tf_op jit(solution)/shard_map/ppermute | solution.py:57
  37.5 0.7 shard_map.68
  38.3 1.1 %collective-permute-done.7.refs_1_ = bf16[16,16,128]{2,1,0:T(8,128)(2,1)S(1)} collective-permute-done((bf16[16,16,128]{2,1,0:T(8,128)(2,1)S(1)}, bf16[16,16,128]{2,1,0:T(8,128)(2,1)S(1)}, u32[]{:S(2)}, u32[]{:S(2)}) %collective-permute-start.7) | collective-permute-done | bytes 65568 | tf_op jit(solution)/shard_map/ppermute | solution.py:57
  39.4 1.0 collective-permute-done.8.refs_2_
  40.4 3.7 %shard_map.69 = (f32[64,16,128]{2,1,0:T(8,128)S(1)}, f32[64,16,128]{2,1,0:T(8,128)S(1)}, bf16[64,16,128]{2,1,0:T(8,128)(2,1)S(1)}, bf16[16,16,128]{2,1,0:T(8,128...) custom-call(s32[77]{0:T(128)S(1)} %concatenate.6.flags, ...), custom_call_target="tpu_custom_call" | custom-call | flops 4000000 | bytes 4000000 | tf_op jit(solution)/shard_map/pallas_call | solution.py:241
  44.1 1.6 %collective-permute-start.10 = (bf16[16,16,128]{2,1,0:T(8,128)(2,1)S(1)}, bf16[16,16,128]{2,1,0:T(8,128)(2,1)S(1)}, u32[]{:S(2)}, u32[]{:S(2)}) collective-permute-start(bf16[16,16,128]{2,1,0:T(8,128)(2,1)S(1)} %get-tuple-element.77), channel_id=1, source_target_pairs={{0,32},{1,33},{2,4},{3,5},{4,2},{5,3},{6,8},{7,9},{8,6},{9,7},{10,... | collective-permute-start | bytes 196616 | tf_op jit(solution)/shard_map/ppermute | solution.py:57
  45.8 1.9 %collective-permute-start.11 = (bf16[16,16,128]{2,1,0:T(8,128)(2,1)S(1)}, bf16[16,16,128]{2,1,0:T(8,128)(2,1)S(1)}, u32[]{:S(2)}, u32[]{:S(2)}) collective-permute-start(bf16[16,16,128]{2,1,0:T(8,128)(2,1)S(1)} %get-tuple-element.78), channel_id=1, source_target_pairs={{0,2},{1,3},{2,0},{3,1},{4,6},{5,7},{6,4},{7,5},{8,10},{9,11},{10,... | collective-permute-start | bytes 196616 | tf_op jit(solution)/shard_map/ppermute | solution.py:57
  47.7 1.9 %collective-permute-start.12 = (bf16[16,16,128]{2,1,0:T(8,128)(2,1)S(1)}, bf16[16,16,128]{2,1,0:T(8,128)(2,1)S(1)}, u32[]{:S(2)}, u32[]{:S(2)}) collective-permute-start(bf16[16,16,128]{2,1,0:T(8,128)(2,1)S(1)} %get-tuple-element.79), channel_id=1, source_target_pairs={{0,32},{1,2},{2,1},{3,4},{4,3},{5,6},{6,5},{7,8},{8,7},{9,10},{10,... | collective-permute-start | bytes 196616 | tf_op jit(solution)/shard_map/ppermute | solution.py:57
  49.6 0.7 shard_map.70
  50.4 1.8 %collective-permute-done.10.refs_0_ = bf16[16,16,128]{2,1,0:T(8,128)(2,1)S(1)} collective-permute-done((bf16[16,16,128]{2,1,0:T(8,128)(2,1)S(1)}, bf16[16,16,128]{2,1,0:T(8,128)(2,1)S(1)}, u32[]{:S(2)}, u32[]{:S(2)}) %collective-permute-start.10) | collective-permute-done | bytes 65568 | tf_op jit(solution)/shard_map/ppermute | solution.py:57
  52.1 1.9 %collective-permute-done.12.refs_2_ = bf16[16,16,128]{2,1,0:T(8,128)(2,1)S(1)} collective-permute-done((bf16[16,16,128]{2,1,0:T(8,128)(2,1)S(1)}, bf16[16,16,128]{2,1,0:T(8,128)(2,1)S(1)}, u32[]{:S(2)}, u32[]{:S(2)}) %collective-permute-start.12) | collective-permute-done | bytes 65568 | tf_op jit(solution)/shard_map/ppermute | solution.py:57
  54.1 3.7 %shard_map.71 = (f32[64,16,128]{2,1,0:T(8,128)S(1)}, f32[64,16,128]{2,1,0:T(8,128)S(1)}, bf16[64,16,128]{2,1,0:T(8,128)(2,1)S(1)}, bf16[16,16,128]{2,1,0:T(8,128...) custom-call(s32[77]{0:T(128)S(1)} %concatenate.6.flags, ...), custom_call_target="tpu_custom_call" | custom-call | flops 4000000 | bytes 4000000 | tf_op jit(solution)/shard_map/pallas_call | solution.py:241
  57.8 0.0 collective-permute-start.14
  57.8 2.3 %collective-permute-start.15 = (bf16[16,16,128]{2,1,0:T(8,128)(2,1)S(1)}, bf16[16,16,128]{2,1,0:T(8,128)(2,1)S(1)}, u32[]{:S(2)}, u32[]{:S(2)}) collective-permute-start(bf16[16,16,128]{2,1,0:T(8,128)(2,1)S(1)} %get-tuple-element.84), channel_id=1, source_target_pairs={{0,32},{1,33},{2,4},{3,5},{4,2},{5,3},{6,8},{7,9},{8,6},{9,7},{10,... | collective-permute-start | bytes 196616 | tf_op jit(solution)/shard_map/ppermute | solution.py:57
  60.1 1.4 %collective-permute-start.16 = (bf16[16,16,128]{2,1,0:T(8,128)(2,1)S(1)}, bf16[16,16,128]{2,1,0:T(8,128)(2,1)S(1)}, u32[]{:S(2)}, u32[]{:S(2)}) collective-permute-start(bf16[16,16,128]{2,1,0:T(8,128)(2,1)S(1)} %get-tuple-element.85), channel_id=1, source_target_pairs={{0,2},{1,3},{2,0},{3,1},{4,6},{5,7},{6,4},{7,5},{8,10},{9,11},{10,... | collective-permute-start | bytes 196616 | tf_op jit(solution)/shard_map/ppermute | solution.py:57
  61.5 1.9 %collective-permute-start.17 = (bf16[16,16,128]{2,1,0:T(8,128)(2,1)S(1)}, bf16[16,16,128]{2,1,0:T(8,128)(2,1)S(1)}, u32[]{:S(2)}, u32[]{:S(2)}) collective-permute-start(bf16[16,16,128]{2,1,0:T(8,128)(2,1)S(1)} %get-tuple-element.86), channel_id=1, source_target_pairs={{0,32},{1,2},{2,1},{3,4},{4,3},{5,6},{6,5},{7,8},{8,7},{9,10},{10,... | collective-permute-start | bytes 196616 | tf_op jit(solution)/shard_map/ppermute | solution.py:57
  63.5 0.2 collective-permute-start.18
  63.6 0.7 shard_map.72.part
  64.4 1.8 %collective-permute-done.15.refs_0_ = bf16[16,16,128]{2,1,0:T(8,128)(2,1)S(1)} collective-permute-done((bf16[16,16,128]{2,1,0:T(8,128)(2,1)S(1)}, bf16[16,16,128]{2,1,0:T(8,128)(2,1)S(1)}, u32[]{:S(2)}, u32[]{:S(2)}) %collective-permute-start.15) | collective-permute-done | bytes 65568 | tf_op jit(solution)/shard_map/ppermute | solution.py:57
  66.2 1.0 collective-permute-done.16.refs_1_
  67.2 0.8 collective-permute-done.17.refs_2_
  67.9 3.5 %shard_map.73 = (f32[64,16,128]{2,1,0:T(8,128)S(1)}, bf16[64,16,128]{2,1,0:T(8,128)(2,1)S(1)}) custom-call(s32[77]{0:T(128)S(1)} %concatenate.6.flags, s32[960]{0:T(1024)S(1)} %reshape.7.table, bf16[64,16,128]{2,1,0:T(8,128)(2,1)S(1)} %get-tuple-element.83.vb, f32[64,16,128]{2,1,0:T(8,128)S(1)} %shard_map.72.part, ...), custom_call_target="tpu_custom_call" | custom-call | flops 4000000 | bytes 4000000 | tf_op jit(solution)/shard_map/pallas_call | solution.py:241
  71.4 0.0 collective-permute-start.19
  71.4 7.0 %collective-permute-done.19.moved = bf16[64,16,128]{2,1,0:T(8,128)(2,1)S(1)} collective-permute-done((bf16[64,16,128]{2,1,0:T(8,128)(2,1)S(1)}, bf16[64,16,128]{2,1,0:T(8,128)(2,1)S(1)}, u32[]{:S(2)}, u32[]{:S(2)}) %collective-permute-start.19) | collective-permute-done | bytes 262176 | tf_op jit(solution)/shard_map/ppermute | solution.py:62
  78.4 1.1 shard_map.74
  79.5 1.5 %collective-permute-start.20 = (bf16[16,16,128]{2,1,0:T(8,128)(2,1)S(1)}, bf16[16,16,128]{2,1,0:T(8,128)(2,1)S(1)}, u32[]{:S(2)}, u32[]{:S(2)}) collective-permute-start(bf16[16,16,128]{2,1,0:T(8,128)(2,1)S(1)} %get-tuple-element.96), channel_id=1, source_target_pairs={{0,32},{1,33},{2,4},{3,5},{4,2},{5,3},{6,8},{7,9},{8,6},{9,7},{10,... | collective-permute-start | bytes 196616 | tf_op jit(solution)/shard_map/ppermute | solution.py:57
  81.0 2.0 %collective-permute-start.21 = (bf16[16,16,128]{2,1,0:T(8,128)(2,1)S(1)}, bf16[16,16,128]{2,1,0:T(8,128)(2,1)S(1)}, u32[]{:S(2)}, u32[]{:S(2)}) collective-permute-start(bf16[16,16,128]{2,1,0:T(8,128)(2,1)S(1)} %get-tuple-element.97), channel_id=1, source_target_pairs={{0,2},{1,3},{2,0},{3,1},{4,6},{5,7},{6,4},{7,5},{8,10},{9,11},{10,... | collective-permute-start | bytes 196616 | tf_op jit(solution)/shard_map/ppermute | solution.py:57
  83.1 1.9 %collective-permute-start.22 = (bf16[16,16,128]{2,1,0:T(8,128)(2,1)S(1)}, bf16[16,16,128]{2,1,0:T(8,128)(2,1)S(1)}, u32[]{:S(2)}, u32[]{:S(2)}) collective-permute-start(bf16[16,16,128]{2,1,0:T(8,128)(2,1)S(1)} %get-tuple-element.98), channel_id=1, source_target_pairs={{0,32},{1,2},{2,1},{3,4},{4,3},{5,6},{6,5},{7,8},{8,7},{9,10},{10,... | collective-permute-start | bytes 196616 | tf_op jit(solution)/shard_map/ppermute | solution.py:57
  85.0 0.8 shard_map.75
  85.7 1.5 %collective-permute-done.20.refs_0_ = bf16[16,16,128]{2,1,0:T(8,128)(2,1)S(1)} collective-permute-done((bf16[16,16,128]{2,1,0:T(8,128)(2,1)S(1)}, bf16[16,16,128]{2,1,0:T(8,128)(2,1)S(1)}, u32[]{:S(2)}, u32[]{:S(2)}) %collective-permute-start.20) | collective-permute-done | bytes 65568 | tf_op jit(solution)/shard_map/ppermute | solution.py:57
  87.2 2.2 %collective-permute-done.22.refs_2_ = bf16[16,16,128]{2,1,0:T(8,128)(2,1)S(1)} collective-permute-done((bf16[16,16,128]{2,1,0:T(8,128)(2,1)S(1)}, bf16[16,16,128]{2,1,0:T(8,128)(2,1)S(1)}, u32[]{:S(2)}, u32[]{:S(2)}) %collective-permute-start.22) | collective-permute-done | bytes 65568 | tf_op jit(solution)/shard_map/ppermute | solution.py:57
  89.4 3.7 %shard_map.76 = (f32[64,16,128]{2,1,0:T(8,128)S(1)}, bf16[64,16,128]{2,1,0:T(8,128)(2,1)S(1)}, bf16[16,16,128]{2,1,0:T(8,128)(2,1)S(1)}, bf16[16,16,128]{2,1,0:T...) custom-call(s32[77]{0:T(128)S(1)} %concatenate.6.flags, s32[960]{0:T(1024)S(1)} %reshape.7.table, ...), custom_call_target="tpu_custom_call" | custom-call | flops 4000000 | bytes 4000000 | tf_op jit(solution)/shard_map/pallas_call | solution.py:241
  93.1 1.5 %collective-permute-start.24 = (bf16[16,16,128]{2,1,0:T(8,128)(2,1)S(1)}, bf16[16,16,128]{2,1,0:T(8,128)(2,1)S(1)}, u32[]{:S(2)}, u32[]{:S(2)}) collective-permute-start(bf16[16,16,128]{2,1,0:T(8,128)(2,1)S(1)} %get-tuple-element.104), channel_id=1, source_target_pairs={{0,32},{1,33},{2,4},{3,5},{4,2},{5,3},{6,8},{7,9},{8,6},{9,7},{10,... | collective-permute-start | bytes 196616 | tf_op jit(solution)/shard_map/ppermute | solution.py:57
  94.7 2.1 %collective-permute-start.25 = (bf16[16,16,128]{2,1,0:T(8,128)(2,1)S(1)}, bf16[16,16,128]{2,1,0:T(8,128)(2,1)S(1)}, u32[]{:S(2)}, u32[]{:S(2)}) collective-permute-start(bf16[16,16,128]{2,1,0:T(8,128)(2,1)S(1)} %get-tuple-element.105), channel_id=1, source_target_pairs={{0,2},{1,3},{2,0},{3,1},{4,6},{5,7},{6,4},{7,5},{8,10},{9,11},{10,... | collective-permute-start | bytes 196616 | tf_op jit(solution)/shard_map/ppermute | solution.py:57
  96.8 2.0 %collective-permute-start.26 = (bf16[16,16,128]{2,1,0:T(8,128)(2,1)S(1)}, bf16[16,16,128]{2,1,0:T(8,128)(2,1)S(1)}, u32[]{:S(2)}, u32[]{:S(2)}) collective-permute-start(bf16[16,16,128]{2,1,0:T(8,128)(2,1)S(1)} %get-tuple-element.106), channel_id=1, source_target_pairs={{0,32},{1,2},{2,1},{3,4},{4,3},{5,6},{6,5},{7,8},{8,7},{9,10},{10,... | collective-permute-start | bytes 196616 | tf_op jit(solution)/shard_map/ppermute | solution.py:57
  98.8 0.8 shard_map.77
  99.6 0.9 collective-permute-done.24.refs_0_
  100.5 2.7 %collective-permute-done.26.refs_2_ = bf16[16,16,128]{2,1,0:T(8,128)(2,1)S(1)} collective-permute-done((bf16[16,16,128]{2,1,0:T(8,128)(2,1)S(1)}, bf16[16,16,128]{2,1,0:T(8,128)(2,1)S(1)}, u32[]{:S(2)}, u32[]{:S(2)}) %collective-permute-start.26) | collective-permute-done | bytes 65568 | tf_op jit(solution)/shard_map/ppermute | solution.py:57
  103.2 3.5 %shard_map.78 = f32[64,16,128]{2,1,0:T(8,128)S(1)} custom-call(s32[77]{0:T(128)S(1)} %concatenate.6.flags, s32[960]{0:T(1024)S(1)} %reshape.7.table, bf16[64,16,128]{2,1,0:T(8,128)(2,1)S(1)} %get-tuple-element.101.vb, f32[64,16,128]{2,1,0:T(8,128)S(1)} %get-tuple-element.103.part, bf16[16,16,128]{2,1,0:T(8,128)(2,1)S(1)} %collective-permute-done.24.refs_0_, ...), custom_call_target="tpu_custom_call" | custom-call | flops 4000000 | bytes 4000000 | tf_op jit(solution)/shard_map/pallas_call | solution.py:241
  106.7 1.0 copy.11
  (20 shorter events, 0.1 us)
Async XLA Ops:
  1.4 28.0 %collective-permute-start = (f32[64,16,128]{2,1,0:T(8,128)S(1)}, f32[64,16,128]{2,1,0:T(8,128)S(1)}, u32[]{:S(2)}, u32[]{:S(2)}) collective-permute-start(f32[64,16,128]{2,1,0:T(8,128)S(1)} %bitcast.21), channel_id=1, source_target_pairs={{0,32},{32,64},{64,96},{96,128},{128,160},{160,192},{192,224},{224... | collective-permute-start | bytes 1572872 | tf_op jit(solution)/shard_map/ppermute | solution.py:62
  3.1 14.4 %collective-permute-start.1 = (bf16[16,16,128]{2,1,0:T(8,128)(2,1)S(1)}, bf16[16,16,128]{2,1,0:T(8,128)(2,1)S(1)}, u32[]{:S(2)}, u32[]{:S(2)}) collective-permute-start(bf16[16,16,128]{2,1,0:T(8,128)(2,1)S(1)} %get-tuple-element.59), channel_id=1, source_target_pairs={{0,32},{1,33},{2,4},{3,5},{4,2},{5,3},{6,8},{7,9},{8,6},{9,7},{10,... | collective-permute-start | bytes 196616 | tf_op jit(solution)/shard_map/ppermute | solution.py:57
  9.3 8.2 %collective-permute-start.2 = (bf16[16,16,128]{2,1,0:T(8,128)(2,1)S(1)}, bf16[16,16,128]{2,1,0:T(8,128)(2,1)S(1)}, u32[]{:S(2)}, u32[]{:S(2)}) collective-permute-start(bf16[16,16,128]{2,1,0:T(8,128)(2,1)S(1)} %get-tuple-element.60), channel_id=1, source_target_pairs={{0,2},{1,3},{2,0},{3,1},{4,6},{5,7},{6,4},{7,5},{8,10},{9,11},{10,... | collective-permute-start | bytes 196616 | tf_op jit(solution)/shard_map/ppermute | solution.py:57
  10.9 7.0 %collective-permute-start.3 = (bf16[16,16,128]{2,1,0:T(8,128)(2,1)S(1)}, bf16[16,16,128]{2,1,0:T(8,128)(2,1)S(1)}, u32[]{:S(2)}, u32[]{:S(2)}) collective-permute-start(bf16[16,16,128]{2,1,0:T(8,128)(2,1)S(1)} %get-tuple-element.61), channel_id=1, source_target_pairs={{0,32},{1,2},{2,1},{3,4},{4,3},{5,6},{6,5},{7,8},{8,7},{9,10},{10,... | collective-permute-start | bytes 196616 | tf_op jit(solution)/shard_map/ppermute | solution.py:57
  10.9 7.0 %collective-permute-start.4 = (bf16[16,16,128]{2,1,0:T(8,128)(2,1)S(1)}, bf16[16,16,128]{2,1,0:T(8,128)(2,1)S(1)}, u32[]{:S(2)}, u32[]{:S(2)}) collective-permute-start(bf16[16,16,128]{2,1,0:T(8,128)(2,1)S(1)} %get-tuple-element.62), channel_id=1, source_target_pairs={{0,1},{1,0},{2,3},{3,2},{4,5},{5,4},{6,7},{7,6},{8,9},{9,8},{10,11... | collective-permute-start | bytes 196616 | tf_op jit(solution)/shard_map/ppermute | solution.py:57
  13.8 2.2 %copy-start = (bf16[128,128,128]{2,1,0:T(8,128)(2,1)S(1)}, bf16[128,128,128]{2,1,0:T(8,128)(2,1)}, u32[]{:S(2)}) copy-start(bf16[128,128,128]{2,1,0:T(8,128)(2,1)} %refs_4_.11) | copy-start | bytes 12582916
  16.0 0.7 copy-start.2
  16.7 2.2 %copy-start.1 = (bf16[128,128,128]{2,1,0:T(8,128)(2,1)S(1)}, bf16[128,128,128]{2,1,0:T(8,128)(2,1)}, u32[]{:S(2)}) copy-start(bf16[128,128,128]{2,1,0:T(8,128)(2,1)} %refs_4_.11) | copy-start | bytes 12582916
  22.3 7.0 %collective-permute-start.5 = (bf16[64,16,128]{2,1,0:T(8,128)(2,1)S(1)}, bf16[64,16,128]{2,1,0:T(8,128)(2,1)S(1)}, u32[]{:S(2)}, u32[]{:S(2)}) collective-permute-start(bf16[64,16,128]{2,1,0:T(8,128)(2,1)S(1)} %get-tuple-element.64), channel_id=1, source_target_pairs={{0,32},{32,64},{64,96},{96,128},{128,160},{160,192},{192,224},{224... | collective-permute-start | bytes 786440 | tf_op jit(solution)/shard_map/ppermute | solution.py:62
  30.3 8.0 %collective-permute-start.6 = (bf16[16,16,128]{2,1,0:T(8,128)(2,1)S(1)}, bf16[16,16,128]{2,1,0:T(8,128)(2,1)S(1)}, u32[]{:S(2)}, u32[]{:S(2)}) collective-permute-start(bf16[16,16,128]{2,1,0:T(8,128)(2,1)S(1)} %get-tuple-element.69), channel_id=1, source_target_pairs={{0,32},{1,33},{2,4},{3,5},{4,2},{5,3},{6,8},{7,9},{8,6},{9,7},{10,... | collective-permute-start | bytes 196616 | tf_op jit(solution)/shard_map/ppermute | solution.py:57
  34.1 5.3 %collective-permute-start.7 = (bf16[16,16,128]{2,1,0:T(8,128)(2,1)S(1)}, bf16[16,16,128]{2,1,0:T(8,128)(2,1)S(1)}, u32[]{:S(2)}, u32[]{:S(2)}) collective-permute-start(bf16[16,16,128]{2,1,0:T(8,128)(2,1)S(1)} %get-tuple-element.70), channel_id=1, source_target_pairs={{0,2},{1,3},{2,0},{3,1},{4,6},{5,7},{6,4},{7,5},{8,10},{9,11},{10,... | collective-permute-start | bytes 196616 | tf_op jit(solution)/shard_map/ppermute | solution.py:57
  34.1 6.4 %collective-permute-start.8 = (bf16[16,16,128]{2,1,0:T(8,128)(2,1)S(1)}, bf16[16,16,128]{2,1,0:T(8,128)(2,1)S(1)}, u32[]{:S(2)}, u32[]{:S(2)}) collective-permute-start(bf16[16,16,128]{2,1,0:T(8,128)(2,1)S(1)} %get-tuple-element.71), channel_id=1, source_target_pairs={{0,32},{1,2},{2,1},{3,4},{4,3},{5,6},{6,5},{7,8},{8,7},{9,10},{10,... | collective-permute-start | bytes 196616 | tf_op jit(solution)/shard_map/ppermute | solution.py:57
  35.5 4.9 %collective-permute-start.9 = (bf16[16,16,128]{2,1,0:T(8,128)(2,1)S(1)}, bf16[16,16,128]{2,1,0:T(8,128)(2,1)S(1)}, u32[]{:S(2)}, u32[]{:S(2)}) collective-permute-start(bf16[16,16,128]{2,1,0:T(8,128)(2,1)S(1)} %get-tuple-element.72), channel_id=1, source_target_pairs={{0,1},{1,0},{2,3},{3,2},{4,5},{5,4},{6,7},{7,6},{8,9},{9,8},{10,11... | collective-permute-start | bytes 196616 | tf_op jit(solution)/shard_map/ppermute | solution.py:57
  44.1 8.0 %collective-permute-start.10 = (bf16[16,16,128]{2,1,0:T(8,128)(2,1)S(1)}, bf16[16,16,128]{2,1,0:T(8,128)(2,1)S(1)}, u32[]{:S(2)}, u32[]{:S(2)}) collective-permute-start(bf16[16,16,128]{2,1,0:T(8,128)(2,1)S(1)} %get-tuple-element.77), channel_id=1, source_target_pairs={{0,32},{1,33},{2,4},{3,5},{4,2},{5,3},{6,8},{7,9},{8,6},{9,7},{10,... | collective-permute-start | bytes 196616 | tf_op jit(solution)/shard_map/ppermute | solution.py:57
  45.8 6.4 %collective-permute-start.11 = (bf16[16,16,128]{2,1,0:T(8,128)(2,1)S(1)}, bf16[16,16,128]{2,1,0:T(8,128)(2,1)S(1)}, u32[]{:S(2)}, u32[]{:S(2)}) collective-permute-start(bf16[16,16,128]{2,1,0:T(8,128)(2,1)S(1)} %get-tuple-element.78), channel_id=1, source_target_pairs={{0,2},{1,3},{2,0},{3,1},{4,6},{5,7},{6,4},{7,5},{8,10},{9,11},{10,... | collective-permute-start | bytes 196616 | tf_op jit(solution)/shard_map/ppermute | solution.py:57
  47.7 6.4 %collective-permute-start.12 = (bf16[16,16,128]{2,1,0:T(8,128)(2,1)S(1)}, bf16[16,16,128]{2,1,0:T(8,128)(2,1)S(1)}, u32[]{:S(2)}, u32[]{:S(2)}) collective-permute-start(bf16[16,16,128]{2,1,0:T(8,128)(2,1)S(1)} %get-tuple-element.79), channel_id=1, source_target_pairs={{0,32},{1,2},{2,1},{3,4},{4,3},{5,6},{6,5},{7,8},{8,7},{9,10},{10,... | collective-permute-start | bytes 196616 | tf_op jit(solution)/shard_map/ppermute | solution.py:57
  49.6 4.5 %collective-permute-start.13 = (bf16[16,16,128]{2,1,0:T(8,128)(2,1)S(1)}, bf16[16,16,128]{2,1,0:T(8,128)(2,1)S(1)}, u32[]{:S(2)}, u32[]{:S(2)}) collective-permute-start(bf16[16,16,128]{2,1,0:T(8,128)(2,1)S(1)} %get-tuple-element.80), channel_id=1, source_target_pairs={{0,1},{1,0},{2,3},{3,2},{4,5},{5,4},{6,7},{7,6},{8,9},{9,8},{10,11... | collective-permute-start | bytes 196616 | tf_op jit(solution)/shard_map/ppermute | solution.py:57
  57.8 20.7 %collective-permute-start.14 = (f32[64,16,128]{2,1,0:T(8,128)S(1)}, f32[64,16,128]{2,1,0:T(8,128)S(1)}, u32[]{:S(2)}, u32[]{:S(2)}) collective-permute-start(f32[64,16,128]{2,1,0:T(8,128)S(1)} %get-tuple-element.82.u), channel_id=1, source_target_pairs={{0,32},{32,64},{64,96},{96,128},{128,160},{160,192},{192,224},{224... | collective-permute-start | bytes 1572872 | tf_op jit(solution)/shard_map/ppermute | solution.py:62
  57.8 8.4 %collective-permute-start.15 = (bf16[16,16,128]{2,1,0:T(8,128)(2,1)S(1)}, bf16[16,16,128]{2,1,0:T(8,128)(2,1)S(1)}, u32[]{:S(2)}, u32[]{:S(2)}) collective-permute-start(bf16[16,16,128]{2,1,0:T(8,128)(2,1)S(1)} %get-tuple-element.84), channel_id=1, source_target_pairs={{0,32},{1,33},{2,4},{3,5},{4,2},{5,3},{6,8},{7,9},{8,6},{9,7},{10,... | collective-permute-start | bytes 196616 | tf_op jit(solution)/shard_map/ppermute | solution.py:57
  60.1 7.0 %collective-permute-start.16 = (bf16[16,16,128]{2,1,0:T(8,128)(2,1)S(1)}, bf16[16,16,128]{2,1,0:T(8,128)(2,1)S(1)}, u32[]{:S(2)}, u32[]{:S(2)}) collective-permute-start(bf16[16,16,128]{2,1,0:T(8,128)(2,1)S(1)} %get-tuple-element.85), channel_id=1, source_target_pairs={{0,2},{1,3},{2,0},{3,1},{4,6},{5,7},{6,4},{7,5},{8,10},{9,11},{10,... | collective-permute-start | bytes 196616 | tf_op jit(solution)/shard_map/ppermute | solution.py:57
  61.5 6.4 %collective-permute-start.17 = (bf16[16,16,128]{2,1,0:T(8,128)(2,1)S(1)}, bf16[16,16,128]{2,1,0:T(8,128)(2,1)S(1)}, u32[]{:S(2)}, u32[]{:S(2)}) collective-permute-start(bf16[16,16,128]{2,1,0:T(8,128)(2,1)S(1)} %get-tuple-element.86), channel_id=1, source_target_pairs={{0,32},{1,2},{2,1},{3,4},{4,3},{5,6},{6,5},{7,8},{8,7},{9,10},{10,... | collective-permute-start | bytes 196616 | tf_op jit(solution)/shard_map/ppermute | solution.py:57
  63.5 4.5 %collective-permute-start.18 = (bf16[16,16,128]{2,1,0:T(8,128)(2,1)S(1)}, bf16[16,16,128]{2,1,0:T(8,128)(2,1)S(1)}, u32[]{:S(2)}, u32[]{:S(2)}) collective-permute-start(bf16[16,16,128]{2,1,0:T(8,128)(2,1)S(1)} %get-tuple-element.87), channel_id=1, source_target_pairs={{0,1},{1,0},{2,3},{3,2},{4,5},{5,4},{6,7},{7,6},{8,9},{9,8},{10,11... | collective-permute-start | bytes 196616 | tf_op jit(solution)/shard_map/ppermute | solution.py:57
  71.4 7.0 %collective-permute-start.19 = (bf16[64,16,128]{2,1,0:T(8,128)(2,1)S(1)}, bf16[64,16,128]{2,1,0:T(8,128)(2,1)S(1)}, u32[]{:S(2)}, u32[]{:S(2)}) collective-permute-start(bf16[64,16,128]{2,1,0:T(8,128)(2,1)S(1)} %get-tuple-element.88), channel_id=1, source_target_pairs={{0,32},{32,64},{64,96},{96,128},{128,160},{160,192},{192,224},{224... | collective-permute-start | bytes 786440 | tf_op jit(solution)/shard_map/ppermute | solution.py:62
  79.5 7.7 %collective-permute-start.20 = (bf16[16,16,128]{2,1,0:T(8,128)(2,1)S(1)}, bf16[16,16,128]{2,1,0:T(8,128)(2,1)S(1)}, u32[]{:S(2)}, u32[]{:S(2)}) collective-permute-start(bf16[16,16,128]{2,1,0:T(8,128)(2,1)S(1)} %get-tuple-element.96), channel_id=1, source_target_pairs={{0,32},{1,33},{2,4},{3,5},{4,2},{5,3},{6,8},{7,9},{8,6},{9,7},{10,... | collective-permute-start | bytes 196616 | tf_op jit(solution)/shard_map/ppermute | solution.py:57
  81.0 6.2 %collective-permute-start.21 = (bf16[16,16,128]{2,1,0:T(8,128)(2,1)S(1)}, bf16[16,16,128]{2,1,0:T(8,128)(2,1)S(1)}, u32[]{:S(2)}, u32[]{:S(2)}) collective-permute-start(bf16[16,16,128]{2,1,0:T(8,128)(2,1)S(1)} %get-tuple-element.97), channel_id=1, source_target_pairs={{0,2},{1,3},{2,0},{3,1},{4,6},{5,7},{6,4},{7,5},{8,10},{9,11},{10,... | collective-permute-start | bytes 196616 | tf_op jit(solution)/shard_map/ppermute | solution.py:57
  83.1 6.4 %collective-permute-start.22 = (bf16[16,16,128]{2,1,0:T(8,128)(2,1)S(1)}, bf16[16,16,128]{2,1,0:T(8,128)(2,1)S(1)}, u32[]{:S(2)}, u32[]{:S(2)}) collective-permute-start(bf16[16,16,128]{2,1,0:T(8,128)(2,1)S(1)} %get-tuple-element.98), channel_id=1, source_target_pairs={{0,32},{1,2},{2,1},{3,4},{4,3},{5,6},{6,5},{7,8},{8,7},{9,10},{10,... | collective-permute-start | bytes 196616 | tf_op jit(solution)/shard_map/ppermute | solution.py:57
  85.0 4.5 %collective-permute-start.23 = (bf16[16,16,128]{2,1,0:T(8,128)(2,1)S(1)}, bf16[16,16,128]{2,1,0:T(8,128)(2,1)S(1)}, u32[]{:S(2)}, u32[]{:S(2)}) collective-permute-start(bf16[16,16,128]{2,1,0:T(8,128)(2,1)S(1)} %get-tuple-element.99), channel_id=1, source_target_pairs={{0,1},{1,0},{2,3},{3,2},{4,5},{5,4},{6,7},{7,6},{8,9},{9,8},{10,11... | collective-permute-start | bytes 196616 | tf_op jit(solution)/shard_map/ppermute | solution.py:57
  93.1 7.4 %collective-permute-start.24 = (bf16[16,16,128]{2,1,0:T(8,128)(2,1)S(1)}, bf16[16,16,128]{2,1,0:T(8,128)(2,1)S(1)}, u32[]{:S(2)}, u32[]{:S(2)}) collective-permute-start(bf16[16,16,128]{2,1,0:T(8,128)(2,1)S(1)} %get-tuple-element.104), channel_id=1, source_target_pairs={{0,32},{1,33},{2,4},{3,5},{4,2},{5,3},{6,8},{7,9},{8,6},{9,7},{10,... | collective-permute-start | bytes 196616 | tf_op jit(solution)/shard_map/ppermute | solution.py:57
  94.7 5.8 %collective-permute-start.25 = (bf16[16,16,128]{2,1,0:T(8,128)(2,1)S(1)}, bf16[16,16,128]{2,1,0:T(8,128)(2,1)S(1)}, u32[]{:S(2)}, u32[]{:S(2)}) collective-permute-start(bf16[16,16,128]{2,1,0:T(8,128)(2,1)S(1)} %get-tuple-element.105), channel_id=1, source_target_pairs={{0,2},{1,3},{2,0},{3,1},{4,6},{5,7},{6,4},{7,5},{8,10},{9,11},{10,... | collective-permute-start | bytes 196616 | tf_op jit(solution)/shard_map/ppermute | solution.py:57
  96.8 6.4 %collective-permute-start.26 = (bf16[16,16,128]{2,1,0:T(8,128)(2,1)S(1)}, bf16[16,16,128]{2,1,0:T(8,128)(2,1)S(1)}, u32[]{:S(2)}, u32[]{:S(2)}) collective-permute-start(bf16[16,16,128]{2,1,0:T(8,128)(2,1)S(1)} %get-tuple-element.106), channel_id=1, source_target_pairs={{0,32},{1,2},{2,1},{3,4},{4,3},{5,6},{6,5},{7,8},{8,7},{9,10},{10,... | collective-permute-start | bytes 196616 | tf_op jit(solution)/shard_map/ppermute | solution.py:57
  98.8 4.4 %collective-permute-start.27 = (bf16[16,16,128]{2,1,0:T(8,128)(2,1)S(1)}, bf16[16,16,128]{2,1,0:T(8,128)(2,1)S(1)}, u32[]{:S(2)}, u32[]{:S(2)}) collective-permute-start(bf16[16,16,128]{2,1,0:T(8,128)(2,1)S(1)} %get-tuple-element.107), channel_id=1, source_target_pairs={{0,1},{1,0},{2,3},{3,2},{4,5},{5,4},{6,7},{7,6},{8,9},{9,8},{10,11... | collective-permute-start | bytes 196616 | tf_op jit(solution)/shard_map/ppermute | solution.py:57

commit v4 on v3

v4 whole, which is shorter than its diff:
```python
import functools
import math

import jax
import jax.numpy as jnp
from jax import lax
from jax.experimental import pallas as pl
from jax.experimental.pallas import tpu as pltpu
from jax.sharding import PartitionSpec as P

SWEEPS = 2

step_size = 0.3
root_six = math.sqrt(6.0)
node_times = ((4.0 - root_six) / 10.0, (4.0 + root_six) / 10.0, 1.0)
radau_rows = (
    (
        (88.0 - 7.0 * root_six) / 360.0,
        (296.0 - 169.0 * root_six) / 1800.0,
        (-2.0 + 3.0 * root_six) / 225.0,
    ),
    (
        (296.0 + 169.0 * root_six) / 1800.0,
        (88.0 + 7.0 * root_six) / 360.0,
        (-2.0 - 3.0 * root_six) / 225.0,
    ),
    ((16.0 - root_six) / 36.0, (16.0 + root_six) / 36.0, 1.0 / 9.0),
)
node_gaps = (node_times[0], node_times[1] - node_times[0], node_times[2] - node_times[1])
node_integrals = (
    radau_rows[0],
    tuple((radau_rows[1][j] - radau_rows[0][j] for j in range(3))),
    tuple((radau_rows[2][j] - radau_rows[1][j] for j in range(3))),
)

f32 = jnp.float32
bf16 = jnp.bfloat16
VMEM = pl.BlockSpec(memory_space=pltpu.VMEM)
SMEM = pl.BlockSpec(memory_space=pltpu.SMEM)
PARAMS = pltpu.CompilerParams(vmem_limit_bytes=8 * 1024 * 1024)
UNROLL = 32


def pairing(slices, parts, distance, late):
    route = []
    for a in range(slices):
        for p in range(parts):
            ahead = ((p // distance) % 2 == 0) != late
            q = p + distance if ahead else p - distance
            b, q = (a, q) if 0 <= q < parts else (a ^ 1, p)
            route.append((a * parts + p, b * parts + q))
    return route


def swap(block, distance, late):
    route = pairing(lax.axis_size("tm"), lax.axis_size("space"), distance, late)
    return lax.ppermute(block, ("tm", "space"), route)


def next_slice(block):
    n = lax.axis_size("tm")
    return lax.ppermute(block, "tm", [(i, (i + 1) % n) for i in range(n)])


PLAN = 13
PAIRS = ((2, True), (2, False), (1, True), (1, False))


def exchange(packs):
    return tuple(swap(x, d, late) for x, (d, late) in zip(packs, PAIRS))


def plan():
    p = lax.axis_index("space")
    n = lax.axis_size("space")
    sends, fills, valid = [], [], []
    for distance, late in PAIRS:
        base = 0 if distance == 1 else 2
        ahead = ((p // distance) % 2 == 0) != late
        q = jnp.where(ahead, p + distance, p - distance)
        sends.append(jnp.where(ahead, base, base + 1))
        fills.append(jnp.where(ahead, base + 1, base))
        valid.append((q >= 0) & (q < n))
    leading = lax.axis_index("tm") == 0
    return jnp.stack([x.astype(jnp.int32) for x in sends + fills + valid + [leading]])


def pack(flags, vb, packs):
    slots = packs[0].shape[0]
    for k, out in enumerate(packs):
        first = PLAN + flags[k] * slots
        for j in range(slots):
            out[j] = vb[flags[first + j]]


def first_kernel(flags, u, vb, *packs):
    nblocks = u.shape[0]
    vb[0:nblocks] = u[...].astype(bf16)
    vb[nblocks] = jnp.zeros(vb.shape[1:], bf16)
    pack(flags, vb, packs)


def react(mix, field):
    th = jnp.tanh(field)
    hi = th.astype(bf16)
    lo = (th - hi.astype(f32)).astype(bf16)
    return jnp.dot(mix, jnp.concatenate([hi, hi, lo], axis=0), preferred_element_type=f32)


def per_block(count, body):
    def several(i, carry):
        for j in range(UNROLL):
            body(i * UNROLL + j)
        return carry

    lax.fori_loop(0, count // UNROLL, several, 0)


def first_reaction_kernel(u, mixing, coeffs, part, mix):
    del coeffs
    m = mixing[...]
    m_hi = m.astype(bf16)
    m_lo = (m - m_hi.astype(f32)).astype(bf16)
    mix[...] = jnp.concatenate([m_hi, m_lo, m_hi], axis=1)
    mixv = mix[...]

    def body(b):
        part[b] = react(mixv, u[b])

    per_block(u.shape[0], body)


def reaction_kernel(prepare, extras, u, mix, *refs):
    olds, (part, base) = refs[:extras], refs[extras:]
    mixv = mix[...]

    def body(b):
        field = u[b]
        part[b] = react(mixv, field)
        base[b] = prepare(field, [old[b] for old in olds])

    per_block(u.shape[0], body)


def moved_pack_kernel(step, extras, flags, *refs):
    arrays, packs = refs[:extras], refs[extras:]
    nblocks = arrays[0].shape[0]
    slots = packs[0].shape[0]
    leading = flags[PLAN - 1] > 0
    for k, out in enumerate(packs):
        first = PLAN + flags[k] * slots
        for j in range(slots):
            row = flags[first + j]
            block = step(leading, arrays, jnp.minimum(row, nblocks - 1))[0].astype(bf16)
            out[j] = jnp.where(row < nblocks, block, jnp.zeros_like(block))


def moved_reaction_kernel(step, prepare, extras, inputs, keep, flags, mix, *refs):
    arrays, olds, outs = refs[:extras], refs[extras:inputs], refs[inputs:]
    part, base, vb = outs[:3]
    nblocks = part.shape[0]
    leading = flags[PLAN - 1] > 0
    mixv = mix[...]
    vb[nblocks] = jnp.zeros(vb.shape[1:], bf16)

    def body(b):
        field, force = step(leading, arrays, b)
        if keep:
            outs[3][b] = force
        vb[b] = field.astype(bf16)
        part[b] = react(mixv, field)
        base[b] = prepare(field, [old[b] for old in olds])

    per_block(nblocks, body)


def force_kernel(weight, keep, shift, send, flags, table, vb, part, *refs):
    received, refs = refs[:4], refs[4:]
    coeffs, refs = refs[0], refs[1:]
    if weight is not None:
        base, refs = refs[0], refs[1:]
    outs, ext = list(refs[:-1]), refs[-1]
    forces = outs.pop(0) if keep else None
    shifted = outs.pop(0) if shift else None
    states = outs.pop(0) if weight is not None else None
    rounded = outs.pop(0) if send else None
    nblocks = part.shape[0]
    slots = received[0].shape[0]
    width = table.shape[0] // nblocks
    terms = (width + 1) // 2
    ext[0:nblocks] = vb[0:nblocks]
    for k, got in enumerate(received):
        live = flags[8 + k] > 0
        block = got[...]
        ext[pl.ds(nblocks + flags[4 + k] * slots, slots)] = jnp.where(live, block, jnp.zeros_like(block))

    def body(b):
        xs = [vb[b]] + [ext[table[b * width + terms + t]] for t in range(terms - 1)]
        ws = [coeffs[table[b * width + t]] for t in range(terms)]
        force = part[b] + jnp.dot(
            jnp.concatenate(xs, axis=1), jnp.concatenate(ws, axis=0), preferred_element_type=f32
        )
        if keep:
            forces[b] = force
        if shift:
            shifted[b] = force.astype(bf16)
        if weight is not None:
            new = base[b] + weight * force
            states[b] = new
            if send:
                rounded[b] = new.astype(bf16)

    per_block(nblocks, body)
    if send:
        rounded[nblocks] = jnp.zeros(rounded.shape[1:], bf16)
        pack(flags, rounded, outs)


def early_step(leading, arrays, b):
    guess, incoming, force, moved = arrays
    g, q = node_gaps[0], sum(node_integrals[0])
    f = force[b]
    start = jnp.where(leading, guess[b], incoming[b])
    e = jnp.where(leading, f, moved[b].astype(f32))
    return start + step_size * (g * (e - f) + q * f), e


def late_step(leading, arrays, b):
    guess, incoming, force, moved, olds = arrays
    start = jnp.where(leading, guess[b], incoming[b])
    e = jnp.where(leading, force[b], moved[b].astype(f32))
    return start + olds[b] + (step_size * node_gaps[0]) * e, e


def prepare_first(node):
    g, q = node_gaps[node], sum(node_integrals[node])

    def prepare(u, olds):
        (f,) = olds
        return u + step_size * (q * f - g * f)

    return prepare


def prepare_second(node):
    g, q = node_gaps[node], node_integrals[node]

    def prepare(u, olds):
        quad = q[0] * olds[0] + q[1] * olds[1] + q[2] * olds[2]
        return u + step_size * (quad - g * olds[node - 1])

    return prepare


def prepare_late(u, olds):
    e0, e1, e2 = olds
    q = node_integrals[0]
    return step_size * (q[0] * e1 + q[1] * e2 - node_gaps[0] * e0)


def per_device(guess, coeffs, coef_index, neighbours, send_lists, mixing):
    first = jnp.transpose(guess[0], (1, 0, 2))
    nblocks, species, cells = first.shape
    slots = send_lists.shape[1]
    rows = jnp.where(send_lists < 0, nblocks, send_lists)
    flags = jnp.concatenate([plan(), rows.reshape(-1)])
    table = jnp.concatenate([coef_index, neighbours], axis=1).reshape(-1)

    state = jax.ShapeDtypeStruct((nblocks, species, cells), f32)
    shifted = jax.ShapeDtypeStruct((nblocks, species, cells), bf16)
    rounded = jax.ShapeDtypeStruct((nblocks + 1, species, cells), bf16)
    rims = [jax.ShapeDtypeStruct((slots, species, cells), bf16)] * 4
    ext = [pltpu.VMEM((nblocks + 4 * slots, species, cells), bf16)]

    def call(kernel, outs, scalars, arrays, scratch=(), cost=4_000_000):
        return pl.pallas_call(
            kernel,
            out_shape=outs,
            in_specs=[SMEM] * len(scalars) + [VMEM] * len(arrays),
            out_specs=[VMEM] * len(outs),
            scratch_shapes=scratch,
            compiler_params=PARAMS,
            cost_estimate=pl.CostEstimate(flops=cost, bytes_accessed=cost, transcendentals=0),
        )(*scalars, *arrays)

    def react_and_prepare(u, prepare, olds):
        kernel = functools.partial(reaction_kernel, prepare, len(olds))
        return call(kernel, [state, state], (), (u, mix, *olds))

    def move_and_prepare(step, arrays, prepare, olds, keep):
        inputs = len(arrays) + len(olds)
        kernel = functools.partial(moved_reaction_kernel, step, prepare, len(arrays), inputs, keep)
        outs = [state, state, rounded] + [state] * keep
        return call(kernel, outs, (flags,), (mix, *arrays, *olds))

    def moved_packs(step, arrays):
        kernel = functools.partial(moved_pack_kernel, step, len(arrays))
        return call(kernel, rims, (flags,), arrays)

    def force(received, vb, part, weight=None, base=None, keep=True, shift=False, send=False):
        outs = [state] * keep + [shifted] * shift + [state] * (weight is not None)
        if send:
            outs += [rounded] + rims
        kernel = functools.partial(force_kernel, weight, keep, shift, send)
        base = () if weight is None else (base,)
        return call(kernel, outs, (flags, table), (vb, part, *received, coeffs, *base), ext)

    h, gaps = step_size, node_gaps
    vb, *packs = call(first_kernel, [rounded] + rims, (flags,), (first,))
    received = exchange(packs)
    split = jax.ShapeDtypeStruct((species, 3 * species), bf16)
    part, mix = call(first_reaction_kernel, [state, split], (), (first, mixing, coeffs))
    f, fb = force(received, vb, part, shift=True)

    arrays = (first, next_slice(first), f, next_slice(fb))
    received = exchange(moved_packs(early_step, arrays))
    part, base, vb, e0 = move_and_prepare(early_step, arrays, prepare_first(1), (f,), True)
    e1, u, vb, *packs = force(received, vb, part, h * gaps[1], base, send=True)

    received = exchange(packs)
    part, base = react_and_prepare(u, prepare_first(2), (f,))
    e2, u, vb, *packs = force(received, vb, part, h * gaps[2], base, send=True)

    came = next_slice(u)
    received = exchange(packs)
    part, base = react_and_prepare(u, prepare_late, (e0, e1, e2))
    e3, e3b, olds = force(received, vb, part, h * node_integrals[0][2], base, shift=True)

    arrays = (first, came, e0, next_slice(e3b), olds)
    received = exchange(moved_packs(late_step, arrays))
    olds = (e1, e2, e3)
    part, base, vb = move_and_prepare(late_step, arrays, prepare_second(1), olds, False)
    u, vb, *packs = force(received, vb, part, h * gaps[1], base, keep=False, send=True)

    received = exchange(packs)
    part, base = react_and_prepare(u, prepare_second(2), olds)
    (end,) = force(received, vb, part, h * gaps[2], base, keep=False)
    return jnp.transpose(end, (1, 0, 2))[None]


def solution(mesh):
    placed = (
        P("tm", None, "space", None),
        P(),
        P("space", None),
        P("space", None),
        P("space", None),
        P(),
    )
    return jax.shard_map(
        per_device,
        mesh=mesh,
        in_specs=placed,
        out_specs=P("tm", None, "space", None),
        check_vma=False,
    )
```

time: 108 us -> 106 us (0.981)
  Pallas kernels: 28.7 us -> 26.5 us
    pallas_call x15, Pallas kernels: 28.7 us -> 26.5 us  [call(): pl.pallas_call(kernel, out_shape=outs, in_specs=[SMEM] * len(scalars) + [...]
where the time goes in v4:
time: 106 us
  starting transfers between devices  40 us (38%)
  waiting for transfers between devices  31 us (29%)
  Pallas kernels  26.5 us (25%)
  local copies, waits for them, and re-layouts  6.5 us (6%)
  other arithmetic  1.39 us (1%)
    ppermute x24, starting transfers between devices, swap(): return lax.ppermute(block, ('tm', 'space'), route)  39.5 us
    pallas_call x15, Pallas kernels, call(): pl.pallas_call(kernel, out_shape=outs, in_specs=[SMEM] * len(scalars) + [...  26.5 us
    ppermute x24, waiting for transfers between devices, swap(): return lax.ppermute(block, ('tm', 'space'), route)  17.4 us
    ppermute x4, waiting for transfers between devices, next_slice(): return lax.ppermute(block, 'tm', [(i, (i + 1) % n) for i in range(n)])  13.6 us
    unnamed x7, local copies, waits for them, and re-layouts  5.13 us
  transfers between devices with their start and end apart: 28, of which 14 were waited for; matrix products, arithmetic and copies ran while one was open for 2% of the time, Pallas kernels for 11%

profile of v4, /device:TPU:8, one launch (start us, length us, event | category | flops | bytes accessed | tf_op | source)
XLA Modules:
  0.0 105.6 jit_solution(6143293403478507510)
XLA Ops:
  0.0 1.3 %copy.13 = f32[1,16,64,128]{3,1,2,0:T(8,128)S(1)} copy(f32[1,16,64,128]{3,2,1,0:T(8,128)} %param.6) | data formatting | bytes 1048576 | tf_op args[0]
  1.4 0.0 collective-permute-start
  1.5 0.7 compare_select_fusion
  2.2 0.1 reshape.6
  2.2 0.1 concatenate.6.flags
  2.3 0.6 shard_map.65
  3.0 6.3 %collective-permute-start.1 = (bf16[16,16,128]{2,1,0:T(8,128)(2,1)S(1)}, bf16[16,16,128]{2,1,0:T(8,128)(2,1)S(1)}, u32[]{:S(2)}, u32[]{:S(2)}) collective-permute-start(bf16[16,16,128]{2,1,0:T(8,128)(2,1)S(1)} %get-tuple-element.61), channel_id=1, source_target_pairs={{0,32},{1,33},{2,4},{3,5},{4,2},{5,3},{6,8},{7,9},{8,6},{9,7},{10,... | collective-permute-start | bytes 196616 | tf_op jit(solution)/shard_map/ppermute | solution.py:57
  9.2 1.6 %collective-permute-start.2 = (bf16[16,16,128]{2,1,0:T(8,128)(2,1)S(1)}, bf16[16,16,128]{2,1,0:T(8,128)(2,1)S(1)}, u32[]{:S(2)}, u32[]{:S(2)}) collective-permute-start(bf16[16,16,128]{2,1,0:T(8,128)(2,1)S(1)} %get-tuple-element.62), channel_id=1, source_target_pairs={{0,2},{1,3},{2,0},{3,1},{4,6},{5,7},{6,4},{7,5},{8,10},{9,11},{10,... | collective-permute-start | bytes 196616 | tf_op jit(solution)/shard_map/ppermute | solution.py:57
  10.8 1.9 %collective-permute-start.4 = (bf16[16,16,128]{2,1,0:T(8,128)(2,1)S(1)}, bf16[16,16,128]{2,1,0:T(8,128)(2,1)S(1)}, u32[]{:S(2)}, u32[]{:S(2)}) collective-permute-start(bf16[16,16,128]{2,1,0:T(8,128)(2,1)S(1)} %get-tuple-element.64), channel_id=1, source_target_pairs={{0,1},{1,0},{2,3},{3,2},{4,5},{5,4},{6,7},{7,6},{8,9},{9,8},{10,11... | collective-permute-start | bytes 196616 | tf_op jit(solution)/shard_map/ppermute | solution.py:57
  12.7 0.7 pad_add_fusion
  13.4 0.1 copy.9
  13.5 0.1 reshape.7.table
  13.7 0.0 copy-start
  13.7 2.2 %copy-done = bf16[128,128,128]{2,1,0:T(8,128)(2,1)S(1)} copy-done((bf16[128,128,128]{2,1,0:T(8,128)(2,1)S(1)}, bf16[128,128,128]{2,1,0:T(8,128)(2,1)}, u32[]{:S(2)}) %copy-start) | copy-done | bytes 4194328
  15.9 0.7 copy-done.2
  16.6 0.6 shard_map.64
  17.2 0.7 collective-permute-done.3.refs_2_
  17.9 0.9 copy-done.1
  18.8 3.2 %shard_map.66 = (f32[64,16,128]{2,1,0:T(8,128)S(1)}, bf16[64,16,128]{2,1,0:T(8,128)(2,1)S(1)}) custom-call(s32[77]{0:T(128)S(1)} %concatenate.6.flags, s32[960]{0:T(1024)S(1)} %reshape.7.table, bf16[65,16,128]{2,1,0:T(8,128)(2,1)S(1)} %get-tuple-element.59.vb, f32[64,16,128]{2,1,0:T(8,128)S(1)} %get-tuple-element.60.part, ...), custom_call_target="tpu_custom_call" | custom-call | flops 4000000 | bytes 4000000 | tf_op jit(solution)/shard_map/pallas_call | solution.py:276
  21.9 0.4 collective-permute-start.5
  22.3 6.6 %collective-permute-done.5.refs_3_ = bf16[64,16,128]{2,1,0:T(8,128)(2,1)S(1)} collective-permute-done((bf16[64,16,128]{2,1,0:T(8,128)(2,1)S(1)}, bf16[64,16,128]{2,1,0:T(8,128)(2,1)S(1)}, u32[]{:S(2)}, u32[]{:S(2)}) %collective-permute-start.5) | collective-permute-done | bytes 262176 | tf_op jit(solution)/shard_map/ppermute | solution.py:62
  29.0 0.8 shard_map.68
  29.8 3.8 %collective-permute-start.6 = (bf16[16,16,128]{2,1,0:T(8,128)(2,1)S(1)}, bf16[16,16,128]{2,1,0:T(8,128)(2,1)S(1)}, u32[]{:S(2)}, u32[]{:S(2)}) collective-permute-start(bf16[16,16,128]{2,1,0:T(8,128)(2,1)S(1)} %get-tuple-element.69), channel_id=1, source_target_pairs={{0,32},{1,33},{2,4},{3,5},{4,2},{5,3},{6,8},{7,9},{8,6},{9,7},{10,... | collective-permute-start | bytes 196616 | tf_op jit(solution)/shard_map/ppermute | solution.py:57
  33.6 1.5 %collective-permute-start.8 = (bf16[16,16,128]{2,1,0:T(8,128)(2,1)S(1)}, bf16[16,16,128]{2,1,0:T(8,128)(2,1)S(1)}, u32[]{:S(2)}, u32[]{:S(2)}) collective-permute-start(bf16[16,16,128]{2,1,0:T(8,128)(2,1)S(1)} %get-tuple-element.71), channel_id=1, source_target_pairs={{0,32},{1,2},{2,1},{3,4},{4,3},{5,6},{6,5},{7,8},{8,7},{9,10},{10,... | collective-permute-start | bytes 196616 | tf_op jit(solution)/shard_map/ppermute | solution.py:57
  35.0 2.0 %collective-permute-start.9 = (bf16[16,16,128]{2,1,0:T(8,128)(2,1)S(1)}, bf16[16,16,128]{2,1,0:T(8,128)(2,1)S(1)}, u32[]{:S(2)}, u32[]{:S(2)}) collective-permute-start(bf16[16,16,128]{2,1,0:T(8,128)(2,1)S(1)} %get-tuple-element.72), channel_id=1, source_target_pairs={{0,1},{1,0},{2,3},{3,2},{4,5},{5,4},{6,7},{7,6},{8,9},{9,8},{10,11... | collective-permute-start | bytes 196616 | tf_op jit(solution)/shard_map/ppermute | solution.py:57
  37.0 1.1 %shard_map.67 = (f32[64,16,128]{2,1,0:T(8,128)S(1)}, f32[64,16,128]{2,1,0:T(8,128)S(1)}, bf16[65,16,128]{2,1,0:T(8,128)(2,1)S(1)}, f32[64,16,128]{2,1,0:T(8,128)S(1)}) custom-call(s32[77]{0:T(128)S(1)} %concatenate.6.flags, bf16[16,48]{1,0:T(8,128)(2,1)S(1)} %get-tuple-element.58.mix, f32[64,16,128]{2,1,0:T(8,128)S(1)} %bitcast.25, ...), custom_call_target="tpu_custom_call" | custom-call | flops 4000000 | bytes 4000000 | tf_op jit(solution)/shard_map/pallas_call | solution.py:276
  38.2 0.7 collective-permute-done.7.refs_1_
  38.9 1.0 collective-permute-done.8.refs_2_
  39.9 3.4 %shard_map.69 = (f32[64,16,128]{2,1,0:T(8,128)S(1)}, f32[64,16,128]{2,1,0:T(8,128)S(1)}, bf16[65,16,128]{2,1,0:T(8,128)(2,1)S(1)}, bf16[16,16,128]{2,1,0:T(8,128...) custom-call(s32[77]{0:T(128)S(1)} %concatenate.6.flags, ...), custom_call_target="tpu_custom_call" | custom-call | flops 4000000 | bytes 4000000 | tf_op jit(solution)/shard_map/pallas_call | solution.py:276
  43.3 1.6 %collective-permute-start.10 = (bf16[16,16,128]{2,1,0:T(8,128)(2,1)S(1)}, bf16[16,16,128]{2,1,0:T(8,128)(2,1)S(1)}, u32[]{:S(2)}, u32[]{:S(2)}) collective-permute-start(bf16[16,16,128]{2,1,0:T(8,128)(2,1)S(1)} %get-tuple-element.77), channel_id=1, source_target_pairs={{0,32},{1,33},{2,4},{3,5},{4,2},{5,3},{6,8},{7,9},{8,6},{9,7},{10,... | collective-permute-start | bytes 196616 | tf_op jit(solution)/shard_map/ppermute | solution.py:57
  45.0 1.9 %collective-permute-start.11 = (bf16[16,16,128]{2,1,0:T(8,128)(2,1)S(1)}, bf16[16,16,128]{2,1,0:T(8,128)(2,1)S(1)}, u32[]{:S(2)}, u32[]{:S(2)}) collective-permute-start(bf16[16,16,128]{2,1,0:T(8,128)(2,1)S(1)} %get-tuple-element.78), channel_id=1, source_target_pairs={{0,2},{1,3},{2,0},{3,1},{4,6},{5,7},{6,4},{7,5},{8,10},{9,11},{10,... | collective-permute-start | bytes 196616 | tf_op jit(solution)/shard_map/ppermute | solution.py:57
  46.9 1.9 %collective-permute-start.12 = (bf16[16,16,128]{2,1,0:T(8,128)(2,1)S(1)}, bf16[16,16,128]{2,1,0:T(8,128)(2,1)S(1)}, u32[]{:S(2)}, u32[]{:S(2)}) collective-permute-start(bf16[16,16,128]{2,1,0:T(8,128)(2,1)S(1)} %get-tuple-element.79), channel_id=1, source_target_pairs={{0,32},{1,2},{2,1},{3,4},{4,3},{5,6},{6,5},{7,8},{8,7},{9,10},{10,... | collective-permute-start | bytes 196616 | tf_op jit(solution)/shard_map/ppermute | solution.py:57
  48.8 0.5 shard_map.70
  49.3 2.0 %collective-permute-done.10.refs_0_ = bf16[16,16,128]{2,1,0:T(8,128)(2,1)S(1)} collective-permute-done((bf16[16,16,128]{2,1,0:T(8,128)(2,1)S(1)}, bf16[16,16,128]{2,1,0:T(8,128)(2,1)S(1)}, u32[]{:S(2)}, u32[]{:S(2)}) %collective-permute-start.10) | collective-permute-done | bytes 65568 | tf_op jit(solution)/shard_map/ppermute | solution.py:57
  51.3 1.9 %collective-permute-done.12.refs_2_ = bf16[16,16,128]{2,1,0:T(8,128)(2,1)S(1)} collective-permute-done((bf16[16,16,128]{2,1,0:T(8,128)(2,1)S(1)}, bf16[16,16,128]{2,1,0:T(8,128)(2,1)S(1)}, u32[]{:S(2)}, u32[]{:S(2)}) %collective-permute-start.12) | collective-permute-done | bytes 65568 | tf_op jit(solution)/shard_map/ppermute | solution.py:57
  53.3 3.4 %shard_map.71 = (f32[64,16,128]{2,1,0:T(8,128)S(1)}, f32[64,16,128]{2,1,0:T(8,128)S(1)}, bf16[65,16,128]{2,1,0:T(8,128)(2,1)S(1)}, bf16[16,16,128]{2,1,0:T(8,128...) custom-call(s32[77]{0:T(128)S(1)} %concatenate.6.flags, ...), custom_call_target="tpu_custom_call" | custom-call | flops 4000000 | bytes 4000000 | tf_op jit(solution)/shard_map/pallas_call | solution.py:276
  56.7 0.0 collective-permute-start.14
  56.7 2.4 %collective-permute-start.15 = (bf16[16,16,128]{2,1,0:T(8,128)(2,1)S(1)}, bf16[16,16,128]{2,1,0:T(8,128)(2,1)S(1)}, u32[]{:S(2)}, u32[]{:S(2)}) collective-permute-start(bf16[16,16,128]{2,1,0:T(8,128)(2,1)S(1)} %get-tuple-element.88), channel_id=1, source_target_pairs={{0,32},{1,33},{2,4},{3,5},{4,2},{5,3},{6,8},{7,9},{8,6},{9,7},{10,... | collective-permute-start | bytes 196616 | tf_op jit(solution)/shard_map/ppermute | solution.py:57
  59.0 1.4 %collective-permute-start.16 = (bf16[16,16,128]{2,1,0:T(8,128)(2,1)S(1)}, bf16[16,16,128]{2,1,0:T(8,128)(2,1)S(1)}, u32[]{:S(2)}, u32[]{:S(2)}) collective-permute-start(bf16[16,16,128]{2,1,0:T(8,128)(2,1)S(1)} %get-tuple-element.89), channel_id=1, source_target_pairs={{0,2},{1,3},{2,0},{3,1},{4,6},{5,7},{6,4},{7,5},{8,10},{9,11},{10,... | collective-permute-start | bytes 196616 | tf_op jit(solution)/shard_map/ppermute | solution.py:57
  60.5 1.9 %collective-permute-start.17 = (bf16[16,16,128]{2,1,0:T(8,128)(2,1)S(1)}, bf16[16,16,128]{2,1,0:T(8,128)(2,1)S(1)}, u32[]{:S(2)}, u32[]{:S(2)}) collective-permute-start(bf16[16,16,128]{2,1,0:T(8,128)(2,1)S(1)} %get-tuple-element.90), channel_id=1, source_target_pairs={{0,32},{1,2},{2,1},{3,4},{4,3},{5,6},{6,5},{7,8},{8,7},{9,10},{10,... | collective-permute-start | bytes 196616 | tf_op jit(solution)/shard_map/ppermute | solution.py:57
  62.4 0.2 collective-permute-start.18
  62.5 0.6 shard_map.72
  63.1 2.0 %collective-permute-done.15.refs_0_ = bf16[16,16,128]{2,1,0:T(8,128)(2,1)S(1)} collective-permute-done((bf16[16,16,128]{2,1,0:T(8,128)(2,1)S(1)}, bf16[16,16,128]{2,1,0:T(8,128)(2,1)S(1)}, u32[]{:S(2)}, u32[]{:S(2)}) %collective-permute-start.15) | collective-permute-done | bytes 65568 | tf_op jit(solution)/shard_map/ppermute | solution.py:57
  65.1 1.0 collective-permute-done.16.refs_1_
  66.1 0.8 collective-permute-done.17.refs_2_
  66.8 3.3 %shard_map.73 = (f32[64,16,128]{2,1,0:T(8,128)S(1)}, bf16[64,16,128]{2,1,0:T(8,128)(2,1)S(1)}, f32[64,16,128]{2,1,0:T(8,128)S(1)}) custom-call(s32[77]{0:T(128)S(1)} %concatenate.6.flags, s32[960]{0:T(1024)S(1)} %reshape.7.table, bf16[65,16,128]{2,1,0:T(8,128)(2,1)S(1)} %get-tuple-element.84.vb, f32[64,16,128]{2,1,0:T(8,128)S(1)} %get-tuple-element.87.part, ...), custom_call_target="tpu_custom_call" | custom-call | flops 4000000 | bytes 4000000 | tf_op jit(solution)/shard_map/pallas_call | solution.py:276
  70.1 0.0 collective-permute-start.19
  70.1 7.0 %collective-permute-done.19.refs_3_ = bf16[64,16,128]{2,1,0:T(8,128)(2,1)S(1)} collective-permute-done((bf16[64,16,128]{2,1,0:T(8,128)(2,1)S(1)}, bf16[64,16,128]{2,1,0:T(8,128)(2,1)S(1)}, u32[]{:S(2)}, u32[]{:S(2)}) %collective-permute-start.19) | collective-permute-done | bytes 262176 | tf_op jit(solution)/shard_map/ppermute | solution.py:62
  77.1 0.8 shard_map.75
  78.0 1.6 %collective-permute-start.20 = (bf16[16,16,128]{2,1,0:T(8,128)(2,1)S(1)}, bf16[16,16,128]{2,1,0:T(8,128)(2,1)S(1)}, u32[]{:S(2)}, u32[]{:S(2)}) collective-permute-start(bf16[16,16,128]{2,1,0:T(8,128)(2,1)S(1)} %get-tuple-element.98), channel_id=1, source_target_pairs={{0,32},{1,33},{2,4},{3,5},{4,2},{5,3},{6,8},{7,9},{8,6},{9,7},{10,... | collective-permute-start | bytes 196616 | tf_op jit(solution)/shard_map/ppermute | solution.py:57
  79.5 2.0 %collective-permute-start.21 = (bf16[16,16,128]{2,1,0:T(8,128)(2,1)S(1)}, bf16[16,16,128]{2,1,0:T(8,128)(2,1)S(1)}, u32[]{:S(2)}, u32[]{:S(2)}) collective-permute-start(bf16[16,16,128]{2,1,0:T(8,128)(2,1)S(1)} %get-tuple-element.99), channel_id=1, source_target_pairs={{0,2},{1,3},{2,0},{3,1},{4,6},{5,7},{6,4},{7,5},{8,10},{9,11},{10,... | collective-permute-start | bytes 196616 | tf_op jit(solution)/shard_map/ppermute | solution.py:57
  81.5 1.9 %collective-permute-start.22 = (bf16[16,16,128]{2,1,0:T(8,128)(2,1)S(1)}, bf16[16,16,128]{2,1,0:T(8,128)(2,1)S(1)}, u32[]{:S(2)}, u32[]{:S(2)}) collective-permute-start(bf16[16,16,128]{2,1,0:T(8,128)(2,1)S(1)} %get-tuple-element.100), channel_id=1, source_target_pairs={{0,32},{1,2},{2,1},{3,4},{4,3},{5,6},{6,5},{7,8},{8,7},{9,10},{10,... | collective-permute-start | bytes 196616 | tf_op jit(solution)/shard_map/ppermute | solution.py:57
  83.5 1.1 %shard_map.74 = (f32[64,16,128]{2,1,0:T(8,128)S(1)}, f32[64,16,128]{2,1,0:T(8,128)S(1)}, bf16[65,16,128]{2,1,0:T(8,128)(2,1)S(1)}) custom-call(s32[77]{0:T(128)S(1)} %concatenate.6.flags, bf16[16,48]{1,0:T(8,128)(2,1)S(1)} %get-tuple-element.58.mix, f32[64,16,128]{2,1,0:T(8,128)S(1)} %bitcast.27, f32[64,16,128]{2,1,0:T(8,128)S(1)} %collective-permute-done.14.refs_1_, ...), custom_call_target="tpu_custom_call" | custom-call | flops 4000000 | bytes 4000000 | tf_op jit(solution)/shard_map/pallas_call | solution.py:276
  84.6 1.1 %collective-permute-done.20.refs_0_ = bf16[16,16,128]{2,1,0:T(8,128)(2,1)S(1)} collective-permute-done((bf16[16,16,128]{2,1,0:T(8,128)(2,1)S(1)}, bf16[16,16,128]{2,1,0:T(8,128)(2,1)S(1)}, u32[]{:S(2)}, u32[]{:S(2)}) %collective-permute-start.20) | collective-permute-done | bytes 65568 | tf_op jit(solution)/shard_map/ppermute | solution.py:57
  85.7 2.2 %collective-permute-done.22.refs_2_ = bf16[16,16,128]{2,1,0:T(8,128)(2,1)S(1)} collective-permute-done((bf16[16,16,128]{2,1,0:T(8,128)(2,1)S(1)}, bf16[16,16,128]{2,1,0:T(8,128)(2,1)S(1)}, u32[]{:S(2)}, u32[]{:S(2)}) %collective-permute-start.22) | collective-permute-done | bytes 65568 | tf_op jit(solution)/shard_map/ppermute | solution.py:57
  87.9 3.4 %shard_map.76 = (f32[64,16,128]{2,1,0:T(8,128)S(1)}, bf16[65,16,128]{2,1,0:T(8,128)(2,1)S(1)}, bf16[16,16,128]{2,1,0:T(8,128)(2,1)S(1)}, bf16[16,16,128]{2,1,0:T...) custom-call(s32[77]{0:T(128)S(1)} %concatenate.6.flags, s32[960]{0:T(1024)S(1)} %reshape.7.table, ...), custom_call_target="tpu_custom_call" | custom-call | flops 4000000 | bytes 4000000 | tf_op jit(solution)/shard_map/pallas_call | solution.py:276
  91.3 1.5 %collective-permute-start.24 = (bf16[16,16,128]{2,1,0:T(8,128)(2,1)S(1)}, bf16[16,16,128]{2,1,0:T(8,128)(2,1)S(1)}, u32[]{:S(2)}, u32[]{:S(2)}) collective-permute-start(bf16[16,16,128]{2,1,0:T(8,128)(2,1)S(1)} %get-tuple-element.106), channel_id=1, source_target_pairs={{0,32},{1,33},{2,4},{3,5},{4,2},{5,3},{6,8},{7,9},{8,6},{9,7},{10,... | collective-permute-start | bytes 196616 | tf_op jit(solution)/shard_map/ppermute | solution.py:57
  92.9 2.1 %collective-permute-start.25 = (bf16[16,16,128]{2,1,0:T(8,128)(2,1)S(1)}, bf16[16,16,128]{2,1,0:T(8,128)(2,1)S(1)}, u32[]{:S(2)}, u32[]{:S(2)}) collective-permute-start(bf16[16,16,128]{2,1,0:T(8,128)(2,1)S(1)} %get-tuple-element.107), channel_id=1, source_target_pairs={{0,2},{1,3},{2,0},{3,1},{4,6},{5,7},{6,4},{7,5},{8,10},{9,11},{10,... | collective-permute-start | bytes 196616 | tf_op jit(solution)/shard_map/ppermute | solution.py:57
  95.0 2.0 %collective-permute-start.26 = (bf16[16,16,128]{2,1,0:T(8,128)(2,1)S(1)}, bf16[16,16,128]{2,1,0:T(8,128)(2,1)S(1)}, u32[]{:S(2)}, u32[]{:S(2)}) collective-permute-start(bf16[16,16,128]{2,1,0:T(8,128)(2,1)S(1)} %get-tuple-element.108), channel_id=1, source_target_pairs={{0,32},{1,2},{2,1},{3,4},{4,3},{5,6},{6,5},{7,8},{8,7},{9,10},{10,... | collective-permute-start | bytes 196616 | tf_op jit(solution)/shard_map/ppermute | solution.py:57
  97.0 0.5 shard_map.77
  97.5 1.2 %collective-permute-done.24.refs_0_ = bf16[16,16,128]{2,1,0:T(8,128)(2,1)S(1)} collective-permute-done((bf16[16,16,128]{2,1,0:T(8,128)(2,1)S(1)}, bf16[16,16,128]{2,1,0:T(8,128)(2,1)S(1)}, u32[]{:S(2)}, u32[]{:S(2)}) %collective-permute-start.24) | collective-permute-done | bytes 65568 | tf_op jit(solution)/shard_map/ppermute | solution.py:57
  98.7 2.7 %collective-permute-done.26.refs_2_ = bf16[16,16,128]{2,1,0:T(8,128)(2,1)S(1)} collective-permute-done((bf16[16,16,128]{2,1,0:T(8,128)(2,1)S(1)}, bf16[16,16,128]{2,1,0:T(8,128)(2,1)S(1)}, u32[]{:S(2)}, u32[]{:S(2)}) %collective-permute-start.26) | collective-permute-done | bytes 65568 | tf_op jit(solution)/shard_map/ppermute | solution.py:57
  101.4 3.3 %shard_map.78 = f32[64,16,128]{2,1,0:T(8,128)S(1)} custom-call(s32[77]{0:T(128)S(1)} %concatenate.6.flags, s32[960]{0:T(1024)S(1)} %reshape.7.table, bf16[65,16,128]{2,1,0:T(8,128)(2,1)S(1)} %get-tuple-element.103.vb, f32[64,16,128]{2,1,0:T(8,128)S(1)} %get-tuple-element.105.part, bf16[16,16,128]{2,1,0:T(8,128)(2,1)S(1)} %collective-permute-done.24.refs_0_, ...), custom_call_target="tpu_custom_call" | custom-call | flops 4000000 | bytes 4000000 | tf_op jit(solution)/shard_map/pallas_call | solution.py:276
  104.7 1.0 copy.11
  (21 shorter events, 0.1 us)
Async XLA Ops:
  1.4 27.6 %collective-permute-start = (f32[64,16,128]{2,1,0:T(8,128)S(1)}, f32[64,16,128]{2,1,0:T(8,128)S(1)}, u32[]{:S(2)}, u32[]{:S(2)}) collective-permute-start(f32[64,16,128]{2,1,0:T(8,128)S(1)} %bitcast.21), channel_id=1, source_target_pairs={{0,32},{32,64},{64,96},{96,128},{128,160},{160,192},{192,224},{224... | collective-permute-start | bytes 1572872 | tf_op jit(solution)/shard_map/ppermute | solution.py:62
  3.0 14.2 %collective-permute-start.1 = (bf16[16,16,128]{2,1,0:T(8,128)(2,1)S(1)}, bf16[16,16,128]{2,1,0:T(8,128)(2,1)S(1)}, u32[]{:S(2)}, u32[]{:S(2)}) collective-permute-start(bf16[16,16,128]{2,1,0:T(8,128)(2,1)S(1)} %get-tuple-element.61), channel_id=1, source_target_pairs={{0,32},{1,33},{2,4},{3,5},{4,2},{5,3},{6,8},{7,9},{8,6},{9,7},{10,... | collective-permute-start | bytes 196616 | tf_op jit(solution)/shard_map/ppermute | solution.py:57
  9.2 7.9 %collective-permute-start.2 = (bf16[16,16,128]{2,1,0:T(8,128)(2,1)S(1)}, bf16[16,16,128]{2,1,0:T(8,128)(2,1)S(1)}, u32[]{:S(2)}, u32[]{:S(2)}) collective-permute-start(bf16[16,16,128]{2,1,0:T(8,128)(2,1)S(1)} %get-tuple-element.62), channel_id=1, source_target_pairs={{0,2},{1,3},{2,0},{3,1},{4,6},{5,7},{6,4},{7,5},{8,10},{9,11},{10,... | collective-permute-start | bytes 196616 | tf_op jit(solution)/shard_map/ppermute | solution.py:57
  10.8 7.0 %collective-permute-start.3 = (bf16[16,16,128]{2,1,0:T(8,128)(2,1)S(1)}, bf16[16,16,128]{2,1,0:T(8,128)(2,1)S(1)}, u32[]{:S(2)}, u32[]{:S(2)}) collective-permute-start(bf16[16,16,128]{2,1,0:T(8,128)(2,1)S(1)} %get-tuple-element.63), channel_id=1, source_target_pairs={{0,32},{1,2},{2,1},{3,4},{4,3},{5,6},{6,5},{7,8},{8,7},{9,10},{10,... | collective-permute-start | bytes 196616 | tf_op jit(solution)/shard_map/ppermute | solution.py:57
  10.8 7.0 %collective-permute-start.4 = (bf16[16,16,128]{2,1,0:T(8,128)(2,1)S(1)}, bf16[16,16,128]{2,1,0:T(8,128)(2,1)S(1)}, u32[]{:S(2)}, u32[]{:S(2)}) collective-permute-start(bf16[16,16,128]{2,1,0:T(8,128)(2,1)S(1)} %get-tuple-element.64), channel_id=1, source_target_pairs={{0,1},{1,0},{2,3},{3,2},{4,5},{5,4},{6,7},{7,6},{8,9},{9,8},{10,11... | collective-permute-start | bytes 196616 | tf_op jit(solution)/shard_map/ppermute | solution.py:57
  13.7 2.2 %copy-start = (bf16[128,128,128]{2,1,0:T(8,128)(2,1)S(1)}, bf16[128,128,128]{2,1,0:T(8,128)(2,1)}, u32[]{:S(2)}) copy-start(bf16[128,128,128]{2,1,0:T(8,128)(2,1)} %refs_4_.11) | copy-start | bytes 12582916
  15.9 0.7 copy-start.2
  16.6 2.2 %copy-start.1 = (bf16[128,128,128]{2,1,0:T(8,128)(2,1)S(1)}, bf16[128,128,128]{2,1,0:T(8,128)(2,1)}, u32[]{:S(2)}) copy-start(bf16[128,128,128]{2,1,0:T(8,128)(2,1)} %refs_4_.11) | copy-start | bytes 12582916
  21.9 7.0 %collective-permute-start.5 = (bf16[64,16,128]{2,1,0:T(8,128)(2,1)S(1)}, bf16[64,16,128]{2,1,0:T(8,128)(2,1)S(1)}, u32[]{:S(2)}, u32[]{:S(2)}) collective-permute-start(bf16[64,16,128]{2,1,0:T(8,128)(2,1)S(1)} %get-tuple-element.66), channel_id=1, source_target_pairs={{0,32},{32,64},{64,96},{96,128},{128,160},{160,192},{192,224},{224... | collective-permute-start | bytes 786440 | tf_op jit(solution)/shard_map/ppermute | solution.py:62
  29.8 8.4 %collective-permute-start.6 = (bf16[16,16,128]{2,1,0:T(8,128)(2,1)S(1)}, bf16[16,16,128]{2,1,0:T(8,128)(2,1)S(1)}, u32[]{:S(2)}, u32[]{:S(2)}) collective-permute-start(bf16[16,16,128]{2,1,0:T(8,128)(2,1)S(1)} %get-tuple-element.69), channel_id=1, source_target_pairs={{0,32},{1,33},{2,4},{3,5},{4,2},{5,3},{6,8},{7,9},{8,6},{9,7},{10,... | collective-permute-start | bytes 196616 | tf_op jit(solution)/shard_map/ppermute | solution.py:57
  33.6 5.3 %collective-permute-start.7 = (bf16[16,16,128]{2,1,0:T(8,128)(2,1)S(1)}, bf16[16,16,128]{2,1,0:T(8,128)(2,1)S(1)}, u32[]{:S(2)}, u32[]{:S(2)}) collective-permute-start(bf16[16,16,128]{2,1,0:T(8,128)(2,1)S(1)} %get-tuple-element.70), channel_id=1, source_target_pairs={{0,2},{1,3},{2,0},{3,1},{4,6},{5,7},{6,4},{7,5},{8,10},{9,11},{10,... | collective-permute-start | bytes 196616 | tf_op jit(solution)/shard_map/ppermute | solution.py:57
  33.6 6.4 %collective-permute-start.8 = (bf16[16,16,128]{2,1,0:T(8,128)(2,1)S(1)}, bf16[16,16,128]{2,1,0:T(8,128)(2,1)S(1)}, u32[]{:S(2)}, u32[]{:S(2)}) collective-permute-start(bf16[16,16,128]{2,1,0:T(8,128)(2,1)S(1)} %get-tuple-element.71), channel_id=1, source_target_pairs={{0,32},{1,2},{2,1},{3,4},{4,3},{5,6},{6,5},{7,8},{8,7},{9,10},{10,... | collective-permute-start | bytes 196616 | tf_op jit(solution)/shard_map/ppermute | solution.py:57
  35.0 4.9 %collective-permute-start.9 = (bf16[16,16,128]{2,1,0:T(8,128)(2,1)S(1)}, bf16[16,16,128]{2,1,0:T(8,128)(2,1)S(1)}, u32[]{:S(2)}, u32[]{:S(2)}) collective-permute-start(bf16[16,16,128]{2,1,0:T(8,128)(2,1)S(1)} %get-tuple-element.72), channel_id=1, source_target_pairs={{0,1},{1,0},{2,3},{3,2},{4,5},{5,4},{6,7},{7,6},{8,9},{9,8},{10,11... | collective-permute-start | bytes 196616 | tf_op jit(solution)/shard_map/ppermute | solution.py:57
  43.3 8.0 %collective-permute-start.10 = (bf16[16,16,128]{2,1,0:T(8,128)(2,1)S(1)}, bf16[16,16,128]{2,1,0:T(8,128)(2,1)S(1)}, u32[]{:S(2)}, u32[]{:S(2)}) collective-permute-start(bf16[16,16,128]{2,1,0:T(8,128)(2,1)S(1)} %get-tuple-element.77), channel_id=1, source_target_pairs={{0,32},{1,33},{2,4},{3,5},{4,2},{5,3},{6,8},{7,9},{8,6},{9,7},{10,... | collective-permute-start | bytes 196616 | tf_op jit(solution)/shard_map/ppermute | solution.py:57
  45.0 6.4 %collective-permute-start.11 = (bf16[16,16,128]{2,1,0:T(8,128)(2,1)S(1)}, bf16[16,16,128]{2,1,0:T(8,128)(2,1)S(1)}, u32[]{:S(2)}, u32[]{:S(2)}) collective-permute-start(bf16[16,16,128]{2,1,0:T(8,128)(2,1)S(1)} %get-tuple-element.78), channel_id=1, source_target_pairs={{0,2},{1,3},{2,0},{3,1},{4,6},{5,7},{6,4},{7,5},{8,10},{9,11},{10,... | collective-permute-start | bytes 196616 | tf_op jit(solution)/shard_map/ppermute | solution.py:57
  46.9 6.4 %collective-permute-start.12 = (bf16[16,16,128]{2,1,0:T(8,128)(2,1)S(1)}, bf16[16,16,128]{2,1,0:T(8,128)(2,1)S(1)}, u32[]{:S(2)}, u32[]{:S(2)}) collective-permute-start(bf16[16,16,128]{2,1,0:T(8,128)(2,1)S(1)} %get-tuple-element.79), channel_id=1, source_target_pairs={{0,32},{1,2},{2,1},{3,4},{4,3},{5,6},{6,5},{7,8},{8,7},{9,10},{10,... | collective-permute-start | bytes 196616 | tf_op jit(solution)/shard_map/ppermute | solution.py:57
  48.8 4.5 %collective-permute-start.13 = (bf16[16,16,128]{2,1,0:T(8,128)(2,1)S(1)}, bf16[16,16,128]{2,1,0:T(8,128)(2,1)S(1)}, u32[]{:S(2)}, u32[]{:S(2)}) collective-permute-start(bf16[16,16,128]{2,1,0:T(8,128)(2,1)S(1)} %get-tuple-element.80), channel_id=1, source_target_pairs={{0,1},{1,0},{2,3},{3,2},{4,5},{5,4},{6,7},{7,6},{8,9},{9,8},{10,11... | collective-permute-start | bytes 196616 | tf_op jit(solution)/shard_map/ppermute | solution.py:57
  56.7 20.5 %collective-permute-start.14 = (f32[64,16,128]{2,1,0:T(8,128)S(1)}, f32[64,16,128]{2,1,0:T(8,128)S(1)}, u32[]{:S(2)}, u32[]{:S(2)}) collective-permute-start(f32[64,16,128]{2,1,0:T(8,128)S(1)} %get-tuple-element.82.u), channel_id=1, source_target_pairs={{0,32},{32,64},{64,96},{96,128},{128,160},{160,192},{192,224},{224... | collective-permute-start | bytes 1572872 | tf_op jit(solution)/shard_map/ppermute | solution.py:62
  56.7 8.4 %collective-permute-start.15 = (bf16[16,16,128]{2,1,0:T(8,128)(2,1)S(1)}, bf16[16,16,128]{2,1,0:T(8,128)(2,1)S(1)}, u32[]{:S(2)}, u32[]{:S(2)}) collective-permute-start(bf16[16,16,128]{2,1,0:T(8,128)(2,1)S(1)} %get-tuple-element.88), channel_id=1, source_target_pairs={{0,32},{1,33},{2,4},{3,5},{4,2},{5,3},{6,8},{7,9},{8,6},{9,7},{10,... | collective-permute-start | bytes 196616 | tf_op jit(solution)/shard_map/ppermute | solution.py:57
  59.0 7.0 %collective-permute-start.16 = (bf16[16,16,128]{2,1,0:T(8,128)(2,1)S(1)}, bf16[16,16,128]{2,1,0:T(8,128)(2,1)S(1)}, u32[]{:S(2)}, u32[]{:S(2)}) collective-permute-start(bf16[16,16,128]{2,1,0:T(8,128)(2,1)S(1)} %get-tuple-element.89), channel_id=1, source_target_pairs={{0,2},{1,3},{2,0},{3,1},{4,6},{5,7},{6,4},{7,5},{8,10},{9,11},{10,... | collective-permute-start | bytes 196616 | tf_op jit(solution)/shard_map/ppermute | solution.py:57
  60.5 6.4 %collective-permute-start.17 = (bf16[16,16,128]{2,1,0:T(8,128)(2,1)S(1)}, bf16[16,16,128]{2,1,0:T(8,128)(2,1)S(1)}, u32[]{:S(2)}, u32[]{:S(2)}) collective-permute-start(bf16[16,16,128]{2,1,0:T(8,128)(2,1)S(1)} %get-tuple-element.90), channel_id=1, source_target_pairs={{0,32},{1,2},{2,1},{3,4},{4,3},{5,6},{6,5},{7,8},{8,7},{9,10},{10,... | collective-permute-start | bytes 196616 | tf_op jit(solution)/shard_map/ppermute | solution.py:57
  62.4 4.5 %collective-permute-start.18 = (bf16[16,16,128]{2,1,0:T(8,128)(2,1)S(1)}, bf16[16,16,128]{2,1,0:T(8,128)(2,1)S(1)}, u32[]{:S(2)}, u32[]{:S(2)}) collective-permute-start(bf16[16,16,128]{2,1,0:T(8,128)(2,1)S(1)} %get-tuple-element.91), channel_id=1, source_target_pairs={{0,1},{1,0},{2,3},{3,2},{4,5},{5,4},{6,7},{7,6},{8,9},{9,8},{10,11... | collective-permute-start | bytes 196616 | tf_op jit(solution)/shard_map/ppermute | solution.py:57
  70.1 7.0 %collective-permute-start.19 = (bf16[64,16,128]{2,1,0:T(8,128)(2,1)S(1)}, bf16[64,16,128]{2,1,0:T(8,128)(2,1)S(1)}, u32[]{:S(2)}, u32[]{:S(2)}) collective-permute-start(bf16[64,16,128]{2,1,0:T(8,128)(2,1)S(1)} %get-tuple-element.93), channel_id=1, source_target_pairs={{0,32},{32,64},{64,96},{96,128},{128,160},{160,192},{192,224},{224... | collective-permute-start | bytes 786440 | tf_op jit(solution)/shard_map/ppermute | solution.py:62
  78.0 7.7 %collective-permute-start.20 = (bf16[16,16,128]{2,1,0:T(8,128)(2,1)S(1)}, bf16[16,16,128]{2,1,0:T(8,128)(2,1)S(1)}, u32[]{:S(2)}, u32[]{:S(2)}) collective-permute-start(bf16[16,16,128]{2,1,0:T(8,128)(2,1)S(1)} %get-tuple-element.98), channel_id=1, source_target_pairs={{0,32},{1,33},{2,4},{3,5},{4,2},{5,3},{6,8},{7,9},{8,6},{9,7},{10,... | collective-permute-start | bytes 196616 | tf_op jit(solution)/shard_map/ppermute | solution.py:57
  79.5 6.2 %collective-permute-start.21 = (bf16[16,16,128]{2,1,0:T(8,128)(2,1)S(1)}, bf16[16,16,128]{2,1,0:T(8,128)(2,1)S(1)}, u32[]{:S(2)}, u32[]{:S(2)}) collective-permute-start(bf16[16,16,128]{2,1,0:T(8,128)(2,1)S(1)} %get-tuple-element.99), channel_id=1, source_target_pairs={{0,2},{1,3},{2,0},{3,1},{4,6},{5,7},{6,4},{7,5},{8,10},{9,11},{10,... | collective-permute-start | bytes 196616 | tf_op jit(solution)/shard_map/ppermute | solution.py:57
  81.5 6.4 %collective-permute-start.22 = (bf16[16,16,128]{2,1,0:T(8,128)(2,1)S(1)}, bf16[16,16,128]{2,1,0:T(8,128)(2,1)S(1)}, u32[]{:S(2)}, u32[]{:S(2)}) collective-permute-start(bf16[16,16,128]{2,1,0:T(8,128)(2,1)S(1)} %get-tuple-element.100), channel_id=1, source_target_pairs={{0,32},{1,2},{2,1},{3,4},{4,3},{5,6},{6,5},{7,8},{8,7},{9,10},{10,... | collective-permute-start | bytes 196616 | tf_op jit(solution)/shard_map/ppermute | solution.py:57
  83.5 4.5 %collective-permute-start.23 = (bf16[16,16,128]{2,1,0:T(8,128)(2,1)S(1)}, bf16[16,16,128]{2,1,0:T(8,128)(2,1)S(1)}, u32[]{:S(2)}, u32[]{:S(2)}) collective-permute-start(bf16[16,16,128]{2,1,0:T(8,128)(2,1)S(1)} %get-tuple-element.101), channel_id=1, source_target_pairs={{0,1},{1,0},{2,3},{3,2},{4,5},{5,4},{6,7},{7,6},{8,9},{9,8},{10,11... | collective-permute-start | bytes 196616 | tf_op jit(solution)/shard_map/ppermute | solution.py:57
  91.3 7.4 %collective-permute-start.24 = (bf16[16,16,128]{2,1,0:T(8,128)(2,1)S(1)}, bf16[16,16,128]{2,1,0:T(8,128)(2,1)S(1)}, u32[]{:S(2)}, u32[]{:S(2)}) collective-permute-start(bf16[16,16,128]{2,1,0:T(8,128)(2,1)S(1)} %get-tuple-element.106), channel_id=1, source_target_pairs={{0,32},{1,33},{2,4},{3,5},{4,2},{5,3},{6,8},{7,9},{8,6},{9,7},{10,... | collective-permute-start | bytes 196616 | tf_op jit(solution)/shard_map/ppermute | solution.py:57
  92.9 5.8 %collective-permute-start.25 = (bf16[16,16,128]{2,1,0:T(8,128)(2,1)S(1)}, bf16[16,16,128]{2,1,0:T(8,128)(2,1)S(1)}, u32[]{:S(2)}, u32[]{:S(2)}) collective-permute-start(bf16[16,16,128]{2,1,0:T(8,128)(2,1)S(1)} %get-tuple-element.107), channel_id=1, source_target_pairs={{0,2},{1,3},{2,0},{3,1},{4,6},{5,7},{6,4},{7,5},{8,10},{9,11},{10,... | collective-permute-start | bytes 196616 | tf_op jit(solution)/shard_map/ppermute | solution.py:57
  95.0 6.4 %collective-permute-start.26 = (bf16[16,16,128]{2,1,0:T(8,128)(2,1)S(1)}, bf16[16,16,128]{2,1,0:T(8,128)(2,1)S(1)}, u32[]{:S(2)}, u32[]{:S(2)}) collective-permute-start(bf16[16,16,128]{2,1,0:T(8,128)(2,1)S(1)} %get-tuple-element.108), channel_id=1, source_target_pairs={{0,32},{1,2},{2,1},{3,4},{4,3},{5,6},{6,5},{7,8},{8,7},{9,10},{10,... | collective-permute-start | bytes 196616 | tf_op jit(solution)/shard_map/ppermute | solution.py:57
  97.0 4.4 %collective-permute-start.27 = (bf16[16,16,128]{2,1,0:T(8,128)(2,1)S(1)}, bf16[16,16,128]{2,1,0:T(8,128)(2,1)S(1)}, u32[]{:S(2)}, u32[]{:S(2)}) collective-permute-start(bf16[16,16,128]{2,1,0:T(8,128)(2,1)S(1)} %get-tuple-element.109), channel_id=1, source_target_pairs={{0,1},{1,0},{2,3},{3,2},{4,5},{5,4},{6,7},{7,6},{8,9},{9,8},{10,11... | collective-permute-start | bytes 196616 | tf_op jit(solution)/shard_map/ppermute | solution.py:57

commit v5 on v4

--- a/solution.py
+++ b/solution.py
@@ -39,6 +39,8 @@
 SMEM = pl.BlockSpec(memory_space=pltpu.SMEM)
 PARAMS = pltpu.CompilerParams(vmem_limit_bytes=8 * 1024 * 1024)
 UNROLL = 32
+TERMS = 8
+WIDTH = 2 * TERMS
 
 
 def pairing(slices, parts, distance, late):
@@ -116,6 +118,17 @@
     lax.fori_loop(0, count // UNROLL, several, 0)
 
 
+def local_terms(table, coeffs, vb, b):
+    nblocks = vb.shape[0] - 1
+    at = b * WIDTH
+    other = jnp.minimum(table[at + TERMS], nblocks)
+    return jnp.dot(
+        jnp.concatenate([vb[b], vb[other]], axis=1),
+        jnp.concatenate([coeffs[table[at]], coeffs[table[at + 1]]], axis=0),
+        preferred_element_type=f32,
+    )
+
+
 def first_reaction_kernel(u, mixing, coeffs, part, mix):
     del coeffs
     m = mixing[...]
@@ -130,32 +143,67 @@
     per_block(u.shape[0], body)
 
 
-def reaction_kernel(prepare, extras, u, mix, *refs):
+def table_kernel(given, after, table, mark):
+    nblocks = after.shape[0]
+    mark[...] = jnp.zeros_like(mark)
+
+    def body(b, count):
+        source, at = b * (WIDTH - 1), b * WIDTH
+        values = [given[source + t] for t in range(WIDTH - 1)]
+        mats, cols = values[1:TERMS], values[TERMS:]
+        chosen, mat, col = jnp.int32(0), mats[0], cols[0]
+        lonely = jnp.int32(1)
+        for t in reversed(range(TERMS - 1)):
+            local = cols[t] < nblocks
+            chosen = jnp.where(local, t, chosen)
+            mat = jnp.where(local, mats[t], mat)
+            col = jnp.where(local, cols[t], col)
+            lonely = jnp.where(local, 0, lonely)
+        table[at] = values[0]
+        table[at + 1] = mat
+        table[at + TERMS] = col
+        for t in range(1, TERMS - 1):
+            here = chosen == t
+            table[at + 1 + t] = jnp.where(here, mats[0], mats[t])
+            table[at + TERMS + t] = jnp.where(here, cols[0], cols[t])
+        table[count * WIDTH + WIDTH - 1] = b
+        return count + lonely
+
+    table[nblocks * WIDTH] = lax.fori_loop(0, nblocks, body, jnp.int32(0), unroll=4)
+
+
+def reaction_kernel(prepare, extras, table, u, vb, mix, coeffs, *refs):
     olds, (part, base) = refs[:extras], refs[extras:]
     mixv = mix[...]
 
     def body(b):
         field = u[b]
-        part[b] = react(mixv, field)
+        part[b] = react(mixv, field) + local_terms(table, coeffs, vb, b)
         base[b] = prepare(field, [old[b] for old in olds])
 
     per_block(u.shape[0], body)
 
 
-def moved_pack_kernel(step, extras, flags, *refs):
+def moved_pack_kernel(step, extras, flags, mark, *refs):
+    del mark
     arrays, packs = refs[:extras], refs[extras:]
     nblocks = arrays[0].shape[0]
     slots = packs[0].shape[0]
     leading = flags[PLAN - 1] > 0
-    for k, out in enumerate(packs):
-        first = PLAN + flags[k] * slots
-        for j in range(slots):
-            row = flags[first + j]
-            block = step(leading, arrays, jnp.minimum(row, nblocks - 1))[0].astype(bf16)
-            out[j] = jnp.where(row < nblocks, block, jnp.zeros_like(block))
-
-
-def moved_reaction_kernel(step, prepare, extras, inputs, keep, flags, mix, *refs):
+
+    def fill(lead):
+        for k, out in enumerate(packs):
+            first = PLAN + flags[k] * slots
+            for j in range(slots):
+                row = flags[first + j]
+                block = step(lead, arrays, jnp.minimum(row, nblocks - 1))[0].astype(bf16)
+                out[j] = jnp.where(row < nblocks, block, jnp.zeros_like(block))
+
+    pl.when(leading)(lambda: fill(True))
+    pl.when(jnp.logical_not(leading))(lambda: fill(False))
+
+
+def moved_reaction_kernel(step, prepare, extras, inputs, keep, flags, table, mix, coeffs, *refs):
     arrays, olds, outs = refs[:extras], refs[extras:inputs], refs[inputs:]
     part, base, vb = outs[:3]
     nblocks = part.shape[0]
@@ -171,10 +219,14 @@
         part[b] = react(mixv, field)
         base[b] = prepare(field, [old[b] for old in olds])
 
+    def add(b):
+        part[b] += local_terms(table, coeffs, vb, b)
+
     per_block(nblocks, body)
-
-
-def force_kernel(weight, keep, shift, send, flags, table, vb, part, *refs):
+    per_block(nblocks, add)
+
+
+def force_kernel(weight, keep, shift, send, whole, flags, table, vb, part, *refs):
     received, refs = refs[:4], refs[4:]
     coeffs, refs = refs[0], refs[1:]
     if weight is not None:
@@ -186,8 +238,6 @@
     rounded = outs.pop(0) if send else None
     nblocks = part.shape[0]
     slots = received[0].shape[0]
-    width = table.shape[0] // nblocks
-    terms = (width + 1) // 2
     ext[0:nblocks] = vb[0:nblocks]
     for k, got in enumerate(received):
         live = flags[8 + k] > 0
@@ -195,8 +245,14 @@
         ext[pl.ds(nblocks + flags[4 + k] * slots, slots)] = jnp.where(live, block, jnp.zeros_like(block))
 
     def body(b):
-        xs = [vb[b]] + [ext[table[b * width + terms + t]] for t in range(terms - 1)]
-        ws = [coeffs[table[b * width + t]] for t in range(terms)]
+        if whole:
+            at = b * (WIDTH - 1)
+            xs = [vb[b]] + [ext[table[at + TERMS + t]] for t in range(TERMS - 1)]
+            ws = [coeffs[table[at + t]] for t in range(TERMS)]
+        else:
+            at = b * WIDTH
+            xs = [ext[table[at + TERMS + t]] for t in range(1, TERMS - 1)]
+            ws = [coeffs[table[at + 1 + t]] for t in range(1, TERMS - 1)]
         force = part[b] + jnp.dot(
             jnp.concatenate(xs, axis=1), jnp.concatenate(ws, axis=0), preferred_element_type=f32
         )
@@ -210,25 +266,49 @@
             if send:
                 rounded[b] = new.astype(bf16)
 
+    def late(i, carry):
+        b = table[i * WIDTH + WIDTH - 1]
+        at = b * WIDTH
+        more = jnp.dot(ext[table[at + TERMS]], coeffs[table[at + 1]], preferred_element_type=f32)
+        if keep:
+            force = forces[b] + more
+            forces[b] = force
+            if shift:
+                shifted[b] = force.astype(bf16)
+        if weight is not None:
+            new = states[b] + weight * more
+            states[b] = new
+            if send:
+                rounded[b] = new.astype(bf16)
+        return carry
+
     per_block(nblocks, body)
+    if not whole:
+        lax.fori_loop(0, table[nblocks * WIDTH], late, 0)
     if send:
         rounded[nblocks] = jnp.zeros(rounded.shape[1:], bf16)
         pack(flags, rounded, outs)
+
+
+def pick(which, one, other):
+    if isinstance(which, bool):
+        return one() if which else other()
+    return jnp.where(which, one(), other())
 
 
 def early_step(leading, arrays, b):
     guess, incoming, force, moved = arrays
     g, q = node_gaps[0], sum(node_integrals[0])
     f = force[b]
-    start = jnp.where(leading, guess[b], incoming[b])
-    e = jnp.where(leading, f, moved[b].astype(f32))
+    start = pick(leading, lambda: guess[b], lambda: incoming[b])
+    e = pick(leading, lambda: f, lambda: moved[b].astype(f32))
     return start + step_size * (g * (e - f) + q * f), e
 
 
 def late_step(leading, arrays, b):
     guess, incoming, force, moved, olds = arrays
-    start = jnp.where(leading, guess[b], incoming[b])
-    e = jnp.where(leading, force[b], moved[b].astype(f32))
+    start = pick(leading, lambda: guess[b], lambda: incoming[b])
+    e = pick(leading, lambda: force[b], lambda: moved[b].astype(f32))
     return start + olds[b] + (step_size * node_gaps[0]) * e, e
 
 
@@ -264,7 +344,7 @@
     slots = send_lists.shape[1]
     rows = jnp.where(send_lists < 0, nblocks, send_lists)
     flags = jnp.concatenate([plan(), rows.reshape(-1)])
-    table = jnp.concatenate([coef_index, neighbours], axis=1).reshape(-1)
+    given = jnp.concatenate([coef_index, neighbours], axis=1).reshape(-1)
 
     state = jax.ShapeDtypeStruct((nblocks, species, cells), f32)
     shifted = jax.ShapeDtypeStruct((nblocks, species, cells), bf16)
@@ -283,34 +363,43 @@
             cost_estimate=pl.CostEstimate(flops=cost, bytes_accessed=cost, transcendentals=0),
         )(*scalars, *arrays)
 
-    def react_and_prepare(u, prepare, olds):
+    def react_and_prepare(u, vb, prepare, olds):
         kernel = functools.partial(reaction_kernel, prepare, len(olds))
-        return call(kernel, [state, state], (), (u, mix, *olds))
+        return call(kernel, [state, state], (table,), (u, vb, mix, coeffs, *olds))
 
     def move_and_prepare(step, arrays, prepare, olds, keep):
         inputs = len(arrays) + len(olds)
         kernel = functools.partial(moved_reaction_kernel, step, prepare, len(arrays), inputs, keep)
         outs = [state, state, rounded] + [state] * keep
-        return call(kernel, outs, (flags,), (mix, *arrays, *olds))
+        return call(kernel, outs, (flags, table), (mix, coeffs, *arrays, *olds))
 
     def moved_packs(step, arrays):
         kernel = functools.partial(moved_pack_kernel, step, len(arrays))
-        return call(kernel, rims, (flags,), arrays)
-
-    def force(received, vb, part, weight=None, base=None, keep=True, shift=False, send=False):
+        return call(kernel, rims, (flags,), (mark, *arrays))
+
+    def force(received, vb, part, weight=None, base=None, keep=True, shift=False, send=False, whole=False):
         outs = [state] * keep + [shifted] * shift + [state] * (weight is not None)
         if send:
             outs += [rounded] + rims
-        kernel = functools.partial(force_kernel, weight, keep, shift, send)
+        kernel = functools.partial(force_kernel, weight, keep, shift, send, whole)
         base = () if weight is None else (base,)
-        return call(kernel, outs, (flags, table), (vb, part, *received, coeffs, *base), ext)
+        terms = given if whole else table
+        return call(kernel, outs, (flags, terms), (vb, part, *received, coeffs, *base), ext)
 
     h, gaps = step_size, node_gaps
     vb, *packs = call(first_kernel, [rounded] + rims, (flags,), (first,))
     received = exchange(packs)
     split = jax.ShapeDtypeStruct((species, 3 * species), bf16)
     part, mix = call(first_reaction_kernel, [state, split], (), (first, mixing, coeffs))
-    f, fb = force(received, vb, part, shift=True)
+    f, fb = force(received, vb, part, shift=True, whole=True)
+    table, mark = pl.pallas_call(
+        table_kernel,
+        out_shape=[jax.ShapeDtypeStruct((nblocks * WIDTH + 1,), jnp.int32), jax.ShapeDtypeStruct((8, 128), f32)],
+        in_specs=[SMEM, VMEM],
+        out_specs=[SMEM, VMEM],
+        compiler_params=PARAMS,
+        cost_estimate=pl.CostEstimate(flops=1_000_000, bytes_accessed=1_000_000, transcendentals=0),
+    )(given, f)
 
     arrays = (first, next_slice(first), f, next_slice(fb))
     received = exchange(moved_packs(early_step, arrays))
@@ -318,12 +407,12 @@
     e1, u, vb, *packs = force(received, vb, part, h * gaps[1], base, send=True)
 
     received = exchange(packs)
-    part, base = react_and_prepare(u, prepare_first(2), (f,))
+    part, base = react_and_prepare(u, vb, prepare_first(2), (f,))
     e2, u, vb, *packs = force(received, vb, part, h * gaps[2], base, send=True)
 
     came = next_slice(u)
     received = exchange(packs)
-    part, base = react_and_prepare(u, prepare_late, (e0, e1, e2))
+    part, base = react_and_prepare(u, vb, prepare_late, (e0, e1, e2))
     e3, e3b, olds = force(received, vb, part, h * node_integrals[0][2], base, shift=True)
 
     arrays = (first, came, e0, next_slice(e3b), olds)
@@ -333,7 +422,7 @@
     u, vb, *packs = force(received, vb, part, h * gaps[1], base, keep=False, send=True)
 
     received = exchange(packs)
-    part, base = react_and_prepare(u, prepare_second(2), olds)
+    part, base = react_and_prepare(u, vb, prepare_second(2), olds)
     (end,) = force(received, vb, part, h * gaps[2], base, keep=False)
     return jnp.transpose(end, (1, 0, 2))[None]
 

time: 106 us -> 104 us (0.981)
  waiting for transfers between devices: 31 us -> 21.5 us
  Pallas kernels: 26.5 us -> 32.6 us
    ppermute x24, waiting for transfers between devices: 17.4 us -> 11.7 us  [swap(): return lax.ppermute(block, ('tm', 'space'), route)]
    ppermute x4, waiting for transfers between devices: 13.6 us -> 9.73 us  [next_slice(): return lax.ppermute(block, 'tm', [(i, (i + 1) % n) for i in range(n)])]
    pallas_call x0 -> x1, Pallas kernels: none -> 3.9 us  [per_device(): pl.pallas_call(table_kernel, out_shape=[jax.ShapeDtypeStruct((nblocks * W...]
    pallas_call x15, Pallas kernels: 26.5 us -> 28.7 us  [call(): pl.pallas_call(kernel, out_shape=outs, in_specs=[SMEM] * len(scalars) + [...]
  transfers between devices with their start and end apart: 28 -> 28, of which waited for: 14 -> 12; matrix products, arithmetic and copies ran while one was open for 2% -> 2% of each run, Pallas kernels for 11% -> 19%
where the time goes in v5:
time: 104 us; the launch traced here: 103 us
  starting transfers between devices  40.7 us (39%)
  Pallas kernels  32.6 us (31%)
  waiting for transfers between devices  21.5 us (21%)
  local copies, waits for them, and re-layouts  6.5 us (6%)
  other arithmetic  1.39 us (1%)
    ppermute x24, starting transfers between devices, swap(): return lax.ppermute(block, ('tm', 'space'), route)  40.3 us
    pallas_call x15, Pallas kernels, call(): pl.pallas_call(kernel, out_shape=outs, in_specs=[SMEM] * len(scalars) + [...  28.7 us
    ppermute x24, waiting for transfers between devices, swap(): return lax.ppermute(block, ('tm', 'space'), route)  11.7 us
    ppermute x4, waiting for transfers between devices, next_slice(): return lax.ppermute(block, 'tm', [(i, (i + 1) % n) for i in range(n)])  9.73 us
    unnamed x7, local copies, waits for them, and re-layouts  5.13 us
    pallas_call x1, Pallas kernels, per_device(): pl.pallas_call(table_kernel, out_shape=[jax.ShapeDtypeStruct((nblocks * W...  3.9 us
  transfers between devices with their start and end apart: 28, of which 12 were waited for; matrix products, arithmetic and copies ran while one was open for 2% of the time, Pallas kernels for 19%

profile of v5, /device:TPU:8, one launch (start us, length us, event | category | flops | bytes accessed | tf_op | source)
XLA Modules:
  0.0 103.0 jit_solution(14134131093835191121)
XLA Ops:
  0.0 1.3 %copy.13 = f32[1,16,64,128]{3,1,2,0:T(8,128)S(1)} copy(f32[1,16,64,128]{3,2,1,0:T(8,128)} %param.6) | data formatting | bytes 1048576 | tf_op args[0]
  1.4 0.0 collective-permute-start.4
  1.5 0.7 compare_select_fusion
  2.2 0.1 reshape.6
  2.2 0.1 concatenate.6.flags
  2.3 0.6 shard_map.64
  3.0 6.3 %collective-permute-start = (bf16[16,16,128]{2,1,0:T(8,128)(2,1)S(1)}, bf16[16,16,128]{2,1,0:T(8,128)(2,1)S(1)}, u32[]{:S(2)}, u32[]{:S(2)}) collective-permute-start(bf16[16,16,128]{2,1,0:T(8,128)(2,1)S(1)} %get-tuple-element.62), channel_id=1, source_target_pairs={{0,32},{1,33},{2,4},{3,5},{4,2},{5,3},{6,8},{7,9},{8,6},{9,7},{10,... | collective-permute-start | bytes 196616 | tf_op jit(solution)/shard_map/ppermute | solution.py:59
  9.3 1.6 %collective-permute-start.1 = (bf16[16,16,128]{2,1,0:T(8,128)(2,1)S(1)}, bf16[16,16,128]{2,1,0:T(8,128)(2,1)S(1)}, u32[]{:S(2)}, u32[]{:S(2)}) collective-permute-start(bf16[16,16,128]{2,1,0:T(8,128)(2,1)S(1)} %get-tuple-element.63), channel_id=1, source_target_pairs={{0,2},{1,3},{2,0},{3,1},{4,6},{5,7},{6,4},{7,5},{8,10},{9,11},{10,... | collective-permute-start | bytes 196616 | tf_op jit(solution)/shard_map/ppermute | solution.py:59
  10.8 1.9 %collective-permute-start.3 = (bf16[16,16,128]{2,1,0:T(8,128)(2,1)S(1)}, bf16[16,16,128]{2,1,0:T(8,128)(2,1)S(1)}, u32[]{:S(2)}, u32[]{:S(2)}) collective-permute-start(bf16[16,16,128]{2,1,0:T(8,128)(2,1)S(1)} %get-tuple-element.65), channel_id=1, source_target_pairs={{0,1},{1,0},{2,3},{3,2},{4,5},{5,4},{6,7},{7,6},{8,9},{9,8},{10,11... | collective-permute-start | bytes 196616 | tf_op jit(solution)/shard_map/ppermute | solution.py:59
  12.7 0.7 pad_add_fusion
  13.4 0.1 copy.9
  13.5 0.1 reshape.7.table.given
  13.7 2.2 %copy-done = bf16[128,128,128]{2,1,0:T(8,128)(2,1)S(1)} copy-done((bf16[128,128,128]{2,1,0:T(8,128)(2,1)S(1)}, bf16[128,128,128]{2,1,0:T(8,128)(2,1)}, u32[]{:S(2)}) %copy-start) | copy-done | bytes 4194328
  15.9 0.7 copy-done.2
  16.6 0.6 shard_map.65
  17.2 0.7 collective-permute-done.2.refs_2_
  17.9 0.9 copy-done.1
  18.8 3.2 %shard_map.66 = (f32[64,16,128]{2,1,0:T(8,128)S(1)}, bf16[64,16,128]{2,1,0:T(8,128)(2,1)S(1)}) custom-call(s32[77]{0:T(128)S(1)} %concatenate.6.flags, s32[960]{0:T(1024)S(1)} %reshape.7.table.given, bf16[65,16,128]{2,1,0:T(8,128)(2,1)S(1)} %get-tuple-element.60.vb, f32[64,16,128]{2,1,0:T(8,128)S(1)} %get-tuple-element.61.part, ...), custom_call_target="tpu_custom_call" | custom-call | flops 4000000 | bytes 4000000 | tf_op jit(solution)/shard_map/pallas_call | solution.py:356
  22.0 0.4 collective-permute-start.5
  22.3 3.9 %shard_map.67 = (s32[1025]{0:T(1024)S(1)}, f32[8,128]{1,0:T(8,128)S(1)}) custom-call(s32[960]{0:T(1024)S(1)} %reshape.7.table.given, f32[64,16,128]{2,1,0:T(8,128)S(1)} %get-tuple-element.66.after.refs_2_.refs_4_.refs_0_), custom_call_target="tpu_custom_call" | custom-call | flops 1000000 | bytes 1000000 | tf_op jit(solution)/shard_map/pallas_call | solution.py:395
  26.2 2.7 %collective-permute-done.5.refs_3_ = bf16[64,16,128]{2,1,0:T(8,128)(2,1)S(1)} collective-permute-done((bf16[64,16,128]{2,1,0:T(8,128)(2,1)S(1)}, bf16[64,16,128]{2,1,0:T(8,128)(2,1)S(1)}, u32[]{:S(2)}, u32[]{:S(2)}) %collective-permute-start.5) | collective-permute-done | bytes 262176 | tf_op jit(solution)/shard_map/ppermute | solution.py:64
  29.0 0.8 shard_map.69
  29.8 3.8 %collective-permute-start.6 = (bf16[16,16,128]{2,1,0:T(8,128)(2,1)S(1)}, bf16[16,16,128]{2,1,0:T(8,128)(2,1)S(1)}, u32[]{:S(2)}, u32[]{:S(2)}) collective-permute-start(bf16[16,16,128]{2,1,0:T(8,128)(2,1)S(1)} %get-tuple-element.73), channel_id=1, source_target_pairs={{0,32},{1,33},{2,4},{3,5},{4,2},{5,3},{6,8},{7,9},{8,6},{9,7},{10,... | collective-permute-start | bytes 196616 | tf_op jit(solution)/shard_map/ppermute | solution.py:59
  33.5 1.5 %collective-permute-start.8 = (bf16[16,16,128]{2,1,0:T(8,128)(2,1)S(1)}, bf16[16,16,128]{2,1,0:T(8,128)(2,1)S(1)}, u32[]{:S(2)}, u32[]{:S(2)}) collective-permute-start(bf16[16,16,128]{2,1,0:T(8,128)(2,1)S(1)} %get-tuple-element.75), channel_id=1, source_target_pairs={{0,32},{1,2},{2,1},{3,4},{4,3},{5,6},{6,5},{7,8},{8,7},{9,10},{10,... | collective-permute-start | bytes 196616 | tf_op jit(solution)/shard_map/ppermute | solution.py:59
  35.0 2.0 %collective-permute-start.9 = (bf16[16,16,128]{2,1,0:T(8,128)(2,1)S(1)}, bf16[16,16,128]{2,1,0:T(8,128)(2,1)S(1)}, u32[]{:S(2)}, u32[]{:S(2)}) collective-permute-start(bf16[16,16,128]{2,1,0:T(8,128)(2,1)S(1)} %get-tuple-element.76), channel_id=1, source_target_pairs={{0,1},{1,0},{2,3},{3,2},{4,5},{5,4},{6,7},{7,6},{8,9},{9,8},{10,11... | collective-permute-start | bytes 196616 | tf_op jit(solution)/shard_map/ppermute | solution.py:59
  37.0 2.0 %shard_map.68 = (f32[64,16,128]{2,1,0:T(8,128)S(1)}, f32[64,16,128]{2,1,0:T(8,128)S(1)}, bf16[65,16,128]{2,1,0:T(8,128)(2,1)S(1)}, f32[64,16,128]{2,1,0:T(8,128)S(1)}) custom-call(s32[77]{0:T(128)S(1)} %concatenate.6.flags, s32[1025]{0:T(1024)S(1)} %get-tuple-element.67.table, bf16[16,48]{1,0:T(8,128)(2,1)S(1)} %get-tuple-element.68.mix, ...), custom_call_target="tpu_custom_call" | custom-call | flops 4000000 | bytes 4000000 | tf_op jit(solution)/shard_map/pallas_call | solution.py:356
  39.1 0.9 collective-permute-done.8.refs_2_
  39.9 2.8 %shard_map.70 = (f32[64,16,128]{2,1,0:T(8,128)S(1)}, f32[64,16,128]{2,1,0:T(8,128)S(1)}, bf16[65,16,128]{2,1,0:T(8,128)(2,1)S(1)}, bf16[16,16,128]{2,1,0:T(8,128...) custom-call(s32[77]{0:T(128)S(1)} %concatenate.6.flags, ...), custom_call_target="tpu_custom_call" | custom-call | flops 4000000 | bytes 4000000 | tf_op jit(solution)/shard_map/pallas_call | solution.py:356
  42.7 1.8 %collective-permute-start.10 = (bf16[16,16,128]{2,1,0:T(8,128)(2,1)S(1)}, bf16[16,16,128]{2,1,0:T(8,128)(2,1)S(1)}, u32[]{:S(2)}, u32[]{:S(2)}) collective-permute-start(bf16[16,16,128]{2,1,0:T(8,128)(2,1)S(1)} %get-tuple-element.81), channel_id=1, source_target_pairs={{0,32},{1,33},{2,4},{3,5},{4,2},{5,3},{6,8},{7,9},{8,6},{9,7},{10,... | collective-permute-start | bytes 196616 | tf_op jit(solution)/shard_map/ppermute | solution.py:59
  44.5 1.9 %collective-permute-start.11 = (bf16[16,16,128]{2,1,0:T(8,128)(2,1)S(1)}, bf16[16,16,128]{2,1,0:T(8,128)(2,1)S(1)}, u32[]{:S(2)}, u32[]{:S(2)}) collective-permute-start(bf16[16,16,128]{2,1,0:T(8,128)(2,1)S(1)} %get-tuple-element.82), channel_id=1, source_target_pairs={{0,2},{1,3},{2,0},{3,1},{4,6},{5,7},{6,4},{7,5},{8,10},{9,11},{10,... | collective-permute-start | bytes 196616 | tf_op jit(solution)/shard_map/ppermute | solution.py:59
  46.4 1.9 %collective-permute-start.12 = (bf16[16,16,128]{2,1,0:T(8,128)(2,1)S(1)}, bf16[16,16,128]{2,1,0:T(8,128)(2,1)S(1)}, u32[]{:S(2)}, u32[]{:S(2)}) collective-permute-start(bf16[16,16,128]{2,1,0:T(8,128)(2,1)S(1)} %get-tuple-element.83), channel_id=1, source_target_pairs={{0,32},{1,2},{2,1},{3,4},{4,3},{5,6},{6,5},{7,8},{8,7},{9,10},{10,... | collective-permute-start | bytes 196616 | tf_op jit(solution)/shard_map/ppermute | solution.py:59
  48.4 1.6 %shard_map.71 = (f32[64,16,128]{2,1,0:T(8,128)S(1)}, f32[64,16,128]{2,1,0:T(8,128)S(1)}) custom-call(s32[1025]{0:T(1024)S(1)} %get-tuple-element.67.table, f32[64,16,128]{2,1,0:T(8,128)S(1)} %get-tuple-element.79.u, bf16[65,16,128]{2,1,0:T(8,128)(2,1)S(1)} %get-tuple-element.78.vb, bf16[16,48]{1,0:T(8,128)(2,1)S(1)} %get-tuple-element.68.mix, ...), custom_call_target="tpu_custom_call" | custom-call | flops 4000000 | bytes 4000000 | tf_op jit(solution)/shard_map/pallas_call | solution.py:356
  50.0 1.0 collective-permute-done.10.refs_0_
  51.0 1.9 %collective-permute-done.12.refs_2_ = bf16[16,16,128]{2,1,0:T(8,128)(2,1)S(1)} collective-permute-done((bf16[16,16,128]{2,1,0:T(8,128)(2,1)S(1)}, bf16[16,16,128]{2,1,0:T(8,128)(2,1)S(1)}, u32[]{:S(2)}, u32[]{:S(2)}) %collective-permute-start.12) | collective-permute-done | bytes 65568 | tf_op jit(solution)/shard_map/ppermute | solution.py:59
  52.8 2.8 %shard_map.72 = (f32[64,16,128]{2,1,0:T(8,128)S(1)}, f32[64,16,128]{2,1,0:T(8,128)S(1)}, bf16[65,16,128]{2,1,0:T(8,128)(2,1)S(1)}, bf16[16,16,128]{2,1,0:T(8,128...) custom-call(s32[77]{0:T(128)S(1)} %concatenate.6.flags, ...), custom_call_target="tpu_custom_call" | custom-call | flops 4000000 | bytes 4000000 | tf_op jit(solution)/shard_map/pallas_call | solution.py:356
  55.6 0.0 collective-permute-start.14
  55.6 2.8 %collective-permute-start.15 = (bf16[16,16,128]{2,1,0:T(8,128)(2,1)S(1)}, bf16[16,16,128]{2,1,0:T(8,128)(2,1)S(1)}, u32[]{:S(2)}, u32[]{:S(2)}) collective-permute-start(bf16[16,16,128]{2,1,0:T(8,128)(2,1)S(1)} %get-tuple-element.92), channel_id=1, source_target_pairs={{0,32},{1,33},{2,4},{3,5},{4,2},{5,3},{6,8},{7,9},{8,6},{9,7},{10,... | collective-permute-start | bytes 196616 | tf_op jit(solution)/shard_map/ppermute | solution.py:59
  58.4 1.0 collective-permute-start.16
  59.4 1.9 %collective-permute-start.17 = (bf16[16,16,128]{2,1,0:T(8,128)(2,1)S(1)}, bf16[16,16,128]{2,1,0:T(8,128)(2,1)S(1)}, u32[]{:S(2)}, u32[]{:S(2)}) collective-permute-start(bf16[16,16,128]{2,1,0:T(8,128)(2,1)S(1)} %get-tuple-element.94), channel_id=1, source_target_pairs={{0,32},{1,2},{2,1},{3,4},{4,3},{5,6},{6,5},{7,8},{8,7},{9,10},{10,... | collective-permute-start | bytes 196616 | tf_op jit(solution)/shard_map/ppermute | solution.py:59
  61.3 0.6 collective-permute-start.18
  61.9 1.7 %shard_map.73 = (f32[64,16,128]{2,1,0:T(8,128)S(1)}, f32[64,16,128]{2,1,0:T(8,128)S(1)}) custom-call(s32[1025]{0:T(1024)S(1)} %get-tuple-element.67.table, f32[64,16,128]{2,1,0:T(8,128)S(1)} %get-tuple-element.86.u, bf16[65,16,128]{2,1,0:T(8,128)(2,1)S(1)} %get-tuple-element.88.vb, bf16[16,48]{1,0:T(8,128)(2,1)S(1)} %get-tuple-element.68.mix, ...), custom_call_target="tpu_custom_call" | custom-call | flops 4000000 | bytes 4000000 | tf_op jit(solution)/shard_map/pallas_call | solution.py:356
  63.6 0.5 collective-permute-done.15.refs_0_
  64.1 1.3 %collective-permute-done.16.refs_1_ = bf16[16,16,128]{2,1,0:T(8,128)(2,1)S(1)} collective-permute-done((bf16[16,16,128]{2,1,0:T(8,128)(2,1)S(1)}, bf16[16,16,128]{2,1,0:T(8,128)(2,1)S(1)}, u32[]{:S(2)}, u32[]{:S(2)}) %collective-permute-start.16) | collective-permute-done | bytes 65568 | tf_op jit(solution)/shard_map/ppermute | solution.py:59
  65.4 0.4 collective-permute-done.17.refs_2_
  65.8 0.0 collective-permute-done.18.refs_3_
  65.8 2.7 %shard_map.74 = (f32[64,16,128]{2,1,0:T(8,128)S(1)}, bf16[64,16,128]{2,1,0:T(8,128)(2,1)S(1)}, f32[64,16,128]{2,1,0:T(8,128)S(1)}) custom-call(s32[77]{0:T(128)S(1)} %concatenate.6.flags, s32[1025]{0:T(1024)S(1)} %get-tuple-element.67.table, bf16[65,16,128]{2,1,0:T(8,128)(2,1)S(1)} %get-tuple-element.88.vb, f32[64,16,128]{2,1,0:T(8,128)S(1)} %get-tuple-element.91.part, ...), custom_call_target="tpu_custom_call" | custom-call | flops 4000000 | bytes 4000000 | tf_op jit(solution)/shard_map/pallas_call | solution.py:356
  68.6 7.0 %collective-permute-done.19.refs_3_ = bf16[64,16,128]{2,1,0:T(8,128)(2,1)S(1)} collective-permute-done((bf16[64,16,128]{2,1,0:T(8,128)(2,1)S(1)}, bf16[64,16,128]{2,1,0:T(8,128)(2,1)S(1)}, u32[]{:S(2)}, u32[]{:S(2)}) %collective-permute-start.19) | collective-permute-done | bytes 262176 | tf_op jit(solution)/shard_map/ppermute | solution.py:64
  75.6 0.8 shard_map.76
  76.4 2.1 %collective-permute-start.20 = (bf16[16,16,128]{2,1,0:T(8,128)(2,1)S(1)}, bf16[16,16,128]{2,1,0:T(8,128)(2,1)S(1)}, u32[]{:S(2)}, u32[]{:S(2)}) collective-permute-start(bf16[16,16,128]{2,1,0:T(8,128)(2,1)S(1)} %get-tuple-element.102), channel_id=1, source_target_pairs={{0,32},{1,33},{2,4},{3,5},{4,2},{5,3},{6,8},{7,9},{8,6},{9,7},{10,... | collective-permute-start | bytes 196616 | tf_op jit(solution)/shard_map/ppermute | solution.py:59
  78.5 1.6 %collective-permute-start.21 = (bf16[16,16,128]{2,1,0:T(8,128)(2,1)S(1)}, bf16[16,16,128]{2,1,0:T(8,128)(2,1)S(1)}, u32[]{:S(2)}, u32[]{:S(2)}) collective-permute-start(bf16[16,16,128]{2,1,0:T(8,128)(2,1)S(1)} %get-tuple-element.103), channel_id=1, source_target_pairs={{0,2},{1,3},{2,0},{3,1},{4,6},{5,7},{6,4},{7,5},{8,10},{9,11},{10,... | collective-permute-start | bytes 196616 | tf_op jit(solution)/shard_map/ppermute | solution.py:59
  80.0 1.9 %collective-permute-start.22 = (bf16[16,16,128]{2,1,0:T(8,128)(2,1)S(1)}, bf16[16,16,128]{2,1,0:T(8,128)(2,1)S(1)}, u32[]{:S(2)}, u32[]{:S(2)}) collective-permute-start(bf16[16,16,128]{2,1,0:T(8,128)(2,1)S(1)} %get-tuple-element.104), channel_id=1, source_target_pairs={{0,32},{1,2},{2,1},{3,4},{4,3},{5,6},{6,5},{7,8},{8,7},{9,10},{10,... | collective-permute-start | bytes 196616 | tf_op jit(solution)/shard_map/ppermute | solution.py:59
  82.0 2.0 %shard_map.75 = (f32[64,16,128]{2,1,0:T(8,128)S(1)}, f32[64,16,128]{2,1,0:T(8,128)S(1)}, bf16[65,16,128]{2,1,0:T(8,128)(2,1)S(1)}) custom-call(s32[77]{0:T(128)S(1)} %concatenate.6.flags, s32[1025]{0:T(1024)S(1)} %get-tuple-element.67.table, bf16[16,48]{1,0:T(8,128)(2,1)S(1)} %get-tuple-element.68.mix, bf16[128,128,128]{2,1,0:T(8,128)(2,1)S(1)} %copy-done.1, ...), custom_call_target="tpu_custom_call" | custom-call | flops 4000000 | bytes 4000000 | tf_op jit(solution)/shard_map/pallas_call | solution.py:356
  84.0 0.2 collective-permute-done.20.refs_0_
  84.2 2.2 %collective-permute-done.22.refs_2_ = bf16[16,16,128]{2,1,0:T(8,128)(2,1)S(1)} collective-permute-done((bf16[16,16,128]{2,1,0:T(8,128)(2,1)S(1)}, bf16[16,16,128]{2,1,0:T(8,128)(2,1)S(1)}, u32[]{:S(2)}, u32[]{:S(2)}) %collective-permute-start.22) | collective-permute-done | bytes 65568 | tf_op jit(solution)/shard_map/ppermute | solution.py:59
  86.4 2.8 %shard_map.77 = (f32[64,16,128]{2,1,0:T(8,128)S(1)}, bf16[65,16,128]{2,1,0:T(8,128)(2,1)S(1)}, bf16[16,16,128]{2,1,0:T(8,128)(2,1)S(1)}, bf16[16,16,128]{2,1,0:T...) custom-call(s32[77]{0:T(128)S(1)} %concatenate.6.flags, ...), custom_call_target="tpu_custom_call" | custom-call | flops 4000000 | bytes 4000000 | tf_op jit(solution)/shard_map/pallas_call | solution.py:356
  89.2 2.3 %collective-permute-start.24 = (bf16[16,16,128]{2,1,0:T(8,128)(2,1)S(1)}, bf16[16,16,128]{2,1,0:T(8,128)(2,1)S(1)}, u32[]{:S(2)}, u32[]{:S(2)}) collective-permute-start(bf16[16,16,128]{2,1,0:T(8,128)(2,1)S(1)} %get-tuple-element.110), channel_id=1, source_target_pairs={{0,32},{1,33},{2,4},{3,5},{4,2},{5,3},{6,8},{7,9},{8,6},{9,7},{10,... | collective-permute-start | bytes 196616 | tf_op jit(solution)/shard_map/ppermute | solution.py:59
  91.6 1.4 %collective-permute-start.25 = (bf16[16,16,128]{2,1,0:T(8,128)(2,1)S(1)}, bf16[16,16,128]{2,1,0:T(8,128)(2,1)S(1)}, u32[]{:S(2)}, u32[]{:S(2)}) collective-permute-start(bf16[16,16,128]{2,1,0:T(8,128)(2,1)S(1)} %get-tuple-element.111), channel_id=1, source_target_pairs={{0,2},{1,3},{2,0},{3,1},{4,6},{5,7},{6,4},{7,5},{8,10},{9,11},{10,... | collective-permute-start | bytes 196616 | tf_op jit(solution)/shard_map/ppermute | solution.py:59
  93.0 2.0 %collective-permute-start.26 = (bf16[16,16,128]{2,1,0:T(8,128)(2,1)S(1)}, bf16[16,16,128]{2,1,0:T(8,128)(2,1)S(1)}, u32[]{:S(2)}, u32[]{:S(2)}) collective-permute-start(bf16[16,16,128]{2,1,0:T(8,128)(2,1)S(1)} %get-tuple-element.112), channel_id=1, source_target_pairs={{0,32},{1,2},{2,1},{3,4},{4,3},{5,6},{6,5},{7,8},{8,7},{9,10},{10,... | collective-permute-start | bytes 196616 | tf_op jit(solution)/shard_map/ppermute | solution.py:59
  94.9 0.1 collective-permute-start.27
  95.0 1.6 %shard_map.78 = (f32[64,16,128]{2,1,0:T(8,128)S(1)}, f32[64,16,128]{2,1,0:T(8,128)S(1)}) custom-call(s32[1025]{0:T(1024)S(1)} %get-tuple-element.67.table, f32[64,16,128]{2,1,0:T(8,128)S(1)} %get-tuple-element.108.u, bf16[65,16,128]{2,1,0:T(8,128)(2,1)S(1)} %get-tuple-element.107.vb, bf16[16,48]{1,0:T(8,128)(2,1)S(1)} %get-tuple-element.68.mix, ...), custom_call_target="tpu_custom_call" | custom-call | flops 4000000 | bytes 4000000 | tf_op jit(solution)/shard_map/pallas_call | solution.py:356
  96.7 0.0 collective-permute-done.25.refs_1_
  96.7 2.6 %collective-permute-done.26.refs_2_ = bf16[16,16,128]{2,1,0:T(8,128)(2,1)S(1)} collective-permute-done((bf16[16,16,128]{2,1,0:T(8,128)(2,1)S(1)}, bf16[16,16,128]{2,1,0:T(8,128)(2,1)S(1)}, u32[]{:S(2)}, u32[]{:S(2)}) %collective-permute-start.26) | collective-permute-done | bytes 65568 | tf_op jit(solution)/shard_map/ppermute | solution.py:59
  99.3 2.7 %shard_map.79 = f32[64,16,128]{2,1,0:T(8,128)S(1)} custom-call(s32[77]{0:T(128)S(1)} %concatenate.6.flags, s32[1025]{0:T(1024)S(1)} %get-tuple-element.67.table, bf16[65,16,128]{2,1,0:T(8,128)(2,1)S(1)} %get-tuple-element.107.vb, f32[64,16,128]{2,1,0:T(8,128)S(1)} %get-tuple-element.109.part, bf16[16,16,128]{2,1,0:T(8,128)(2,1)S(1)} %collective-permute-done.24.refs_0_, ...), custom_call_target="tpu_custom_call" | custom-call | flops 4000000 | bytes 4000000 | tf_op jit(solution)/shard_map/pallas_call | solution.py:356
  102.0 1.0 copy.11
  (22 shorter events, 0.1 us)
Async XLA Ops:
  1.4 27.6 %collective-permute-start.4 = (f32[64,16,128]{2,1,0:T(8,128)S(1)}, f32[64,16,128]{2,1,0:T(8,128)S(1)}, u32[]{:S(2)}, u32[]{:S(2)}) collective-permute-start(f32[64,16,128]{2,1,0:T(8,128)S(1)} %bitcast.21), channel_id=1, source_target_pairs={{0,32},{32,64},{64,96},{96,128},{128,160},{160,192},{192,224},{224... | collective-permute-start | bytes 1572872 | tf_op jit(solution)/shard_map/ppermute | solution.py:64
  3.0 14.2 %collective-permute-start = (bf16[16,16,128]{2,1,0:T(8,128)(2,1)S(1)}, bf16[16,16,128]{2,1,0:T(8,128)(2,1)S(1)}, u32[]{:S(2)}, u32[]{:S(2)}) collective-permute-start(bf16[16,16,128]{2,1,0:T(8,128)(2,1)S(1)} %get-tuple-element.62), channel_id=1, source_target_pairs={{0,32},{1,33},{2,4},{3,5},{4,2},{5,3},{6,8},{7,9},{8,6},{9,7},{10,... | collective-permute-start | bytes 196616 | tf_op jit(solution)/shard_map/ppermute | solution.py:59
  9.3 7.9 %collective-permute-start.1 = (bf16[16,16,128]{2,1,0:T(8,128)(2,1)S(1)}, bf16[16,16,128]{2,1,0:T(8,128)(2,1)S(1)}, u32[]{:S(2)}, u32[]{:S(2)}) collective-permute-start(bf16[16,16,128]{2,1,0:T(8,128)(2,1)S(1)} %get-tuple-element.63), channel_id=1, source_target_pairs={{0,2},{1,3},{2,0},{3,1},{4,6},{5,7},{6,4},{7,5},{8,10},{9,11},{10,... | collective-permute-start | bytes 196616 | tf_op jit(solution)/shard_map/ppermute | solution.py:59
  10.8 7.0 %collective-permute-start.2 = (bf16[16,16,128]{2,1,0:T(8,128)(2,1)S(1)}, bf16[16,16,128]{2,1,0:T(8,128)(2,1)S(1)}, u32[]{:S(2)}, u32[]{:S(2)}) collective-permute-start(bf16[16,16,128]{2,1,0:T(8,128)(2,1)S(1)} %get-tuple-element.64), channel_id=1, source_target_pairs={{0,32},{1,2},{2,1},{3,4},{4,3},{5,6},{6,5},{7,8},{8,7},{9,10},{10,... | collective-permute-start | bytes 196616 | tf_op jit(solution)/shard_map/ppermute | solution.py:59
  10.8 7.0 %collective-permute-start.3 = (bf16[16,16,128]{2,1,0:T(8,128)(2,1)S(1)}, bf16[16,16,128]{2,1,0:T(8,128)(2,1)S(1)}, u32[]{:S(2)}, u32[]{:S(2)}) collective-permute-start(bf16[16,16,128]{2,1,0:T(8,128)(2,1)S(1)} %get-tuple-element.65), channel_id=1, source_target_pairs={{0,1},{1,0},{2,3},{3,2},{4,5},{5,4},{6,7},{7,6},{8,9},{9,8},{10,11... | collective-permute-start | bytes 196616 | tf_op jit(solution)/shard_map/ppermute | solution.py:59
  13.7 2.2 %copy-start = (bf16[128,128,128]{2,1,0:T(8,128)(2,1)S(1)}, bf16[128,128,128]{2,1,0:T(8,128)(2,1)}, u32[]{:S(2)}) copy-start(bf16[128,128,128]{2,1,0:T(8,128)(2,1)} %refs_4_.11) | copy-start | bytes 12582916
  15.9 0.7 copy-start.2
  16.6 2.2 %copy-start.1 = (bf16[128,128,128]{2,1,0:T(8,128)(2,1)S(1)}, bf16[128,128,128]{2,1,0:T(8,128)(2,1)}, u32[]{:S(2)}) copy-start(bf16[128,128,128]{2,1,0:T(8,128)(2,1)} %refs_4_.11) | copy-start | bytes 12582916
  22.0 7.0 %collective-permute-start.5 = (bf16[64,16,128]{2,1,0:T(8,128)(2,1)S(1)}, bf16[64,16,128]{2,1,0:T(8,128)(2,1)S(1)}, u32[]{:S(2)}, u32[]{:S(2)}) collective-permute-start(bf16[64,16,128]{2,1,0:T(8,128)(2,1)S(1)} %get-tuple-element.69), channel_id=1, source_target_pairs={{0,32},{32,64},{64,96},{96,128},{128,160},{160,192},{192,224},{224... | collective-permute-start | bytes 786440 | tf_op jit(solution)/shard_map/ppermute | solution.py:64
  29.8 9.3 %collective-permute-start.6 = (bf16[16,16,128]{2,1,0:T(8,128)(2,1)S(1)}, bf16[16,16,128]{2,1,0:T(8,128)(2,1)S(1)}, u32[]{:S(2)}, u32[]{:S(2)}) collective-permute-start(bf16[16,16,128]{2,1,0:T(8,128)(2,1)S(1)} %get-tuple-element.73), channel_id=1, source_target_pairs={{0,32},{1,33},{2,4},{3,5},{4,2},{5,3},{6,8},{7,9},{8,6},{9,7},{10,... | collective-permute-start | bytes 196616 | tf_op jit(solution)/shard_map/ppermute | solution.py:59
  33.5 5.5 %collective-permute-start.7 = (bf16[16,16,128]{2,1,0:T(8,128)(2,1)S(1)}, bf16[16,16,128]{2,1,0:T(8,128)(2,1)S(1)}, u32[]{:S(2)}, u32[]{:S(2)}) collective-permute-start(bf16[16,16,128]{2,1,0:T(8,128)(2,1)S(1)} %get-tuple-element.74), channel_id=1, source_target_pairs={{0,2},{1,3},{2,0},{3,1},{4,6},{5,7},{6,4},{7,5},{8,10},{9,11},{10,... | collective-permute-start | bytes 196616 | tf_op jit(solution)/shard_map/ppermute | solution.py:59
  33.5 6.4 %collective-permute-start.8 = (bf16[16,16,128]{2,1,0:T(8,128)(2,1)S(1)}, bf16[16,16,128]{2,1,0:T(8,128)(2,1)S(1)}, u32[]{:S(2)}, u32[]{:S(2)}) collective-permute-start(bf16[16,16,128]{2,1,0:T(8,128)(2,1)S(1)} %get-tuple-element.75), channel_id=1, source_target_pairs={{0,32},{1,2},{2,1},{3,4},{4,3},{5,6},{6,5},{7,8},{8,7},{9,10},{10,... | collective-permute-start | bytes 196616 | tf_op jit(solution)/shard_map/ppermute | solution.py:59
  35.0 4.9 %collective-permute-start.9 = (bf16[16,16,128]{2,1,0:T(8,128)(2,1)S(1)}, bf16[16,16,128]{2,1,0:T(8,128)(2,1)S(1)}, u32[]{:S(2)}, u32[]{:S(2)}) collective-permute-start(bf16[16,16,128]{2,1,0:T(8,128)(2,1)S(1)} %get-tuple-element.76), channel_id=1, source_target_pairs={{0,1},{1,0},{2,3},{3,2},{4,5},{5,4},{6,7},{7,6},{8,9},{9,8},{10,11... | collective-permute-start | bytes 196616 | tf_op jit(solution)/shard_map/ppermute | solution.py:59
  42.7 8.2 %collective-permute-start.10 = (bf16[16,16,128]{2,1,0:T(8,128)(2,1)S(1)}, bf16[16,16,128]{2,1,0:T(8,128)(2,1)S(1)}, u32[]{:S(2)}, u32[]{:S(2)}) collective-permute-start(bf16[16,16,128]{2,1,0:T(8,128)(2,1)S(1)} %get-tuple-element.81), channel_id=1, source_target_pairs={{0,32},{1,33},{2,4},{3,5},{4,2},{5,3},{6,8},{7,9},{8,6},{9,7},{10,... | collective-permute-start | bytes 196616 | tf_op jit(solution)/shard_map/ppermute | solution.py:59
  44.5 6.4 %collective-permute-start.11 = (bf16[16,16,128]{2,1,0:T(8,128)(2,1)S(1)}, bf16[16,16,128]{2,1,0:T(8,128)(2,1)S(1)}, u32[]{:S(2)}, u32[]{:S(2)}) collective-permute-start(bf16[16,16,128]{2,1,0:T(8,128)(2,1)S(1)} %get-tuple-element.82), channel_id=1, source_target_pairs={{0,2},{1,3},{2,0},{3,1},{4,6},{5,7},{6,4},{7,5},{8,10},{9,11},{10,... | collective-permute-start | bytes 196616 | tf_op jit(solution)/shard_map/ppermute | solution.py:59
  46.4 6.4 %collective-permute-start.12 = (bf16[16,16,128]{2,1,0:T(8,128)(2,1)S(1)}, bf16[16,16,128]{2,1,0:T(8,128)(2,1)S(1)}, u32[]{:S(2)}, u32[]{:S(2)}) collective-permute-start(bf16[16,16,128]{2,1,0:T(8,128)(2,1)S(1)} %get-tuple-element.83), channel_id=1, source_target_pairs={{0,32},{1,2},{2,1},{3,4},{4,3},{5,6},{6,5},{7,8},{8,7},{9,10},{10,... | collective-permute-start | bytes 196616 | tf_op jit(solution)/shard_map/ppermute | solution.py:59
  48.3 4.5 %collective-permute-start.13 = (bf16[16,16,128]{2,1,0:T(8,128)(2,1)S(1)}, bf16[16,16,128]{2,1,0:T(8,128)(2,1)S(1)}, u32[]{:S(2)}, u32[]{:S(2)}) collective-permute-start(bf16[16,16,128]{2,1,0:T(8,128)(2,1)S(1)} %get-tuple-element.84), channel_id=1, source_target_pairs={{0,1},{1,0},{2,3},{3,2},{4,5},{5,4},{6,7},{7,6},{8,9},{9,8},{10,11... | collective-permute-start | bytes 196616 | tf_op jit(solution)/shard_map/ppermute | solution.py:59
  55.6 19.9 %collective-permute-start.14 = (f32[64,16,128]{2,1,0:T(8,128)S(1)}, f32[64,16,128]{2,1,0:T(8,128)S(1)}, u32[]{:S(2)}, u32[]{:S(2)}) collective-permute-start(f32[64,16,128]{2,1,0:T(8,128)S(1)} %get-tuple-element.86.u), channel_id=1, source_target_pairs={{0,32},{32,64},{64,96},{96,128},{128,160},{160,192},{192,224},{224... | collective-permute-start | bytes 1572872 | tf_op jit(solution)/shard_map/ppermute | solution.py:64
  55.6 8.4 %collective-permute-start.15 = (bf16[16,16,128]{2,1,0:T(8,128)(2,1)S(1)}, bf16[16,16,128]{2,1,0:T(8,128)(2,1)S(1)}, u32[]{:S(2)}, u32[]{:S(2)}) collective-permute-start(bf16[16,16,128]{2,1,0:T(8,128)(2,1)S(1)} %get-tuple-element.92), channel_id=1, source_target_pairs={{0,32},{1,33},{2,4},{3,5},{4,2},{5,3},{6,8},{7,9},{8,6},{9,7},{10,... | collective-permute-start | bytes 196616 | tf_op jit(solution)/shard_map/ppermute | solution.py:59
  58.4 7.0 %collective-permute-start.16 = (bf16[16,16,128]{2,1,0:T(8,128)(2,1)S(1)}, bf16[16,16,128]{2,1,0:T(8,128)(2,1)S(1)}, u32[]{:S(2)}, u32[]{:S(2)}) collective-permute-start(bf16[16,16,128]{2,1,0:T(8,128)(2,1)S(1)} %get-tuple-element.93), channel_id=1, source_target_pairs={{0,2},{1,3},{2,0},{3,1},{4,6},{5,7},{6,4},{7,5},{8,10},{9,11},{10,... | collective-permute-start | bytes 196616 | tf_op jit(solution)/shard_map/ppermute | solution.py:59
  59.4 6.4 %collective-permute-start.17 = (bf16[16,16,128]{2,1,0:T(8,128)(2,1)S(1)}, bf16[16,16,128]{2,1,0:T(8,128)(2,1)S(1)}, u32[]{:S(2)}, u32[]{:S(2)}) collective-permute-start(bf16[16,16,128]{2,1,0:T(8,128)(2,1)S(1)} %get-tuple-element.94), channel_id=1, source_target_pairs={{0,32},{1,2},{2,1},{3,4},{4,3},{5,6},{6,5},{7,8},{8,7},{9,10},{10,... | collective-permute-start | bytes 196616 | tf_op jit(solution)/shard_map/ppermute | solution.py:59
  61.3 4.5 %collective-permute-start.18 = (bf16[16,16,128]{2,1,0:T(8,128)(2,1)S(1)}, bf16[16,16,128]{2,1,0:T(8,128)(2,1)S(1)}, u32[]{:S(2)}, u32[]{:S(2)}) collective-permute-start(bf16[16,16,128]{2,1,0:T(8,128)(2,1)S(1)} %get-tuple-element.95), channel_id=1, source_target_pairs={{0,1},{1,0},{2,3},{3,2},{4,5},{5,4},{6,7},{7,6},{8,9},{9,8},{10,11... | collective-permute-start | bytes 196616 | tf_op jit(solution)/shard_map/ppermute | solution.py:59
  68.5 7.0 %collective-permute-start.19 = (bf16[64,16,128]{2,1,0:T(8,128)(2,1)S(1)}, bf16[64,16,128]{2,1,0:T(8,128)(2,1)S(1)}, u32[]{:S(2)}, u32[]{:S(2)}) collective-permute-start(bf16[64,16,128]{2,1,0:T(8,128)(2,1)S(1)} %get-tuple-element.97), channel_id=1, source_target_pairs={{0,32},{32,64},{64,96},{96,128},{128,160},{160,192},{192,224},{224... | collective-permute-start | bytes 786440 | tf_op jit(solution)/shard_map/ppermute | solution.py:64
  76.4 7.8 %collective-permute-start.20 = (bf16[16,16,128]{2,1,0:T(8,128)(2,1)S(1)}, bf16[16,16,128]{2,1,0:T(8,128)(2,1)S(1)}, u32[]{:S(2)}, u32[]{:S(2)}) collective-permute-start(bf16[16,16,128]{2,1,0:T(8,128)(2,1)S(1)} %get-tuple-element.102), channel_id=1, source_target_pairs={{0,32},{1,33},{2,4},{3,5},{4,2},{5,3},{6,8},{7,9},{8,6},{9,7},{10,... | collective-permute-start | bytes 196616 | tf_op jit(solution)/shard_map/ppermute | solution.py:59
  78.5 5.7 %collective-permute-start.21 = (bf16[16,16,128]{2,1,0:T(8,128)(2,1)S(1)}, bf16[16,16,128]{2,1,0:T(8,128)(2,1)S(1)}, u32[]{:S(2)}, u32[]{:S(2)}) collective-permute-start(bf16[16,16,128]{2,1,0:T(8,128)(2,1)S(1)} %get-tuple-element.103), channel_id=1, source_target_pairs={{0,2},{1,3},{2,0},{3,1},{4,6},{5,7},{6,4},{7,5},{8,10},{9,11},{10,... | collective-permute-start | bytes 196616 | tf_op jit(solution)/shard_map/ppermute | solution.py:59
  80.0 6.4 %collective-permute-start.22 = (bf16[16,16,128]{2,1,0:T(8,128)(2,1)S(1)}, bf16[16,16,128]{2,1,0:T(8,128)(2,1)S(1)}, u32[]{:S(2)}, u32[]{:S(2)}) collective-permute-start(bf16[16,16,128]{2,1,0:T(8,128)(2,1)S(1)} %get-tuple-element.104), channel_id=1, source_target_pairs={{0,32},{1,2},{2,1},{3,4},{4,3},{5,6},{6,5},{7,8},{8,7},{9,10},{10,... | collective-permute-start | bytes 196616 | tf_op jit(solution)/shard_map/ppermute | solution.py:59
  82.0 4.5 %collective-permute-start.23 = (bf16[16,16,128]{2,1,0:T(8,128)(2,1)S(1)}, bf16[16,16,128]{2,1,0:T(8,128)(2,1)S(1)}, u32[]{:S(2)}, u32[]{:S(2)}) collective-permute-start(bf16[16,16,128]{2,1,0:T(8,128)(2,1)S(1)} %get-tuple-element.105), channel_id=1, source_target_pairs={{0,1},{1,0},{2,3},{3,2},{4,5},{5,4},{6,7},{7,6},{8,9},{9,8},{10,11... | collective-permute-start | bytes 196616 | tf_op jit(solution)/shard_map/ppermute | solution.py:59
  89.2 7.4 %collective-permute-start.24 = (bf16[16,16,128]{2,1,0:T(8,128)(2,1)S(1)}, bf16[16,16,128]{2,1,0:T(8,128)(2,1)S(1)}, u32[]{:S(2)}, u32[]{:S(2)}) collective-permute-start(bf16[16,16,128]{2,1,0:T(8,128)(2,1)S(1)} %get-tuple-element.110), channel_id=1, source_target_pairs={{0,32},{1,33},{2,4},{3,5},{4,2},{5,3},{6,8},{7,9},{8,6},{9,7},{10,... | collective-permute-start | bytes 196616 | tf_op jit(solution)/shard_map/ppermute | solution.py:59
  91.6 5.2 %collective-permute-start.25 = (bf16[16,16,128]{2,1,0:T(8,128)(2,1)S(1)}, bf16[16,16,128]{2,1,0:T(8,128)(2,1)S(1)}, u32[]{:S(2)}, u32[]{:S(2)}) collective-permute-start(bf16[16,16,128]{2,1,0:T(8,128)(2,1)S(1)} %get-tuple-element.111), channel_id=1, source_target_pairs={{0,2},{1,3},{2,0},{3,1},{4,6},{5,7},{6,4},{7,5},{8,10},{9,11},{10,... | collective-permute-start | bytes 196616 | tf_op jit(solution)/shard_map/ppermute | solution.py:59
  93.0 6.4 %collective-permute-start.26 = (bf16[16,16,128]{2,1,0:T(8,128)(2,1)S(1)}, bf16[16,16,128]{2,1,0:T(8,128)(2,1)S(1)}, u32[]{:S(2)}, u32[]{:S(2)}) collective-permute-start(bf16[16,16,128]{2,1,0:T(8,128)(2,1)S(1)} %get-tuple-element.112), channel_id=1, source_target_pairs={{0,32},{1,2},{2,1},{3,4},{4,3},{5,6},{6,5},{7,8},{8,7},{9,10},{10,... | collective-permute-start | bytes 196616 | tf_op jit(solution)/shard_map/ppermute | solution.py:59
  94.9 4.4 %collective-permute-start.27 = (bf16[16,16,128]{2,1,0:T(8,128)(2,1)S(1)}, bf16[16,16,128]{2,1,0:T(8,128)(2,1)S(1)}, u32[]{:S(2)}, u32[]{:S(2)}) collective-permute-start(bf16[16,16,128]{2,1,0:T(8,128)(2,1)S(1)} %get-tuple-element.113), channel_id=1, source_target_pairs={{0,1},{1,0},{2,3},{3,2},{4,5},{5,4},{6,7},{7,6},{8,9},{9,8},{10,11... | collective-permute-start | bytes 196616 | tf_op jit(solution)/shard_map/ppermute | solution.py:59

commit v6 on v5

--- a/solution.py
+++ b/solution.py
@@ -129,8 +129,9 @@
     )
 
 
-def first_reaction_kernel(u, mixing, coeffs, part, mix):
-    del coeffs
+def first_reaction_kernel(u, mixing, coeffs, part, mix, matrices, arrival):
+    fetch = pltpu.make_async_copy(coeffs, matrices, arrival)
+    fetch.start()
     m = mixing[...]
     m_hi = m.astype(bf16)
     m_lo = (m - m_hi.astype(f32)).astype(bf16)
@@ -141,6 +142,7 @@
         part[b] = react(mixv, u[b])
 
     per_block(u.shape[0], body)
+    fetch.wait()
 
 
 def table_kernel(given, after, table, mark):
@@ -390,7 +392,15 @@
     vb, *packs = call(first_kernel, [rounded] + rims, (flags,), (first,))
     received = exchange(packs)
     split = jax.ShapeDtypeStruct((species, 3 * species), bf16)
-    part, mix = call(first_reaction_kernel, [state, split], (), (first, mixing, coeffs))
+    part, mix, coeffs = pl.pallas_call(
+        first_reaction_kernel,
+        out_shape=[state, split, jax.ShapeDtypeStruct(coeffs.shape, bf16)],
+        in_specs=[VMEM, VMEM, pl.BlockSpec(memory_space=pltpu.HBM)],
+        out_specs=[VMEM] * 3,
+        scratch_shapes=[pltpu.SemaphoreType.DMA],
+        compiler_params=pltpu.CompilerParams(vmem_limit_bytes=48 * 1024 * 1024),
+        cost_estimate=pl.CostEstimate(flops=4_000_000, bytes_accessed=4_000_000, transcendentals=0),
+    )(first, mixing, coeffs)
     f, fb = force(received, vb, part, shift=True, whole=True)
     table, mark = pl.pallas_call(
         table_kernel,

time: 104 us -> 102 us (0.981)
  Pallas kernels: 32.6 us -> 35.7 us
  local copies, waits for them, and re-layouts: 6.5 us -> 3.41 us
  starting transfers between devices: 40.7 us -> 38.3 us
  waiting for transfers between devices: 21.5 us -> 22.9 us
    unnamed x7 -> x3, local copies, waits for them, and re-layouts: 5.13 us -> 2.04 us
    pallas_call x0 -> x1, Pallas kernels: none -> 2.2 us  [per_device(): pl.pallas_call(first_reaction_kernel, out_shape=[state, split, jax.ShapeD...]
    ppermute x24, starting transfers between devices: 40.3 us -> 38.2 us  [swap(): return lax.ppermute(block, ('tm', 'space'), route)]
    ppermute x24, waiting for transfers between devices: 11.7 us -> 12.8 us  [swap(): return lax.ppermute(block, ('tm', 'space'), route)]
    pallas_call x15 -> x14, Pallas kernels: 28.7 us -> 29.6 us  [call(): pl.pallas_call(kernel, out_shape=outs, in_specs=[SMEM] * len(scalars) + [...]
  transfers between devices with their start and end apart: 28 -> 28, of which waited for: 12 -> 13; matrix products, arithmetic and copies ran while one was open for 2% -> 2% of each run, Pallas kernels for 19% -> 21%
where the time goes in v6:
time: 102 us
  starting transfers between devices  38.3 us (38%)
  Pallas kernels  35.7 us (35%)
  waiting for transfers between devices  22.9 us (22%)
  local copies, waits for them, and re-layouts  3.41 us (3%)
  other arithmetic  1.39 us (1%)
    ppermute x24, starting transfers between devices, swap(): return lax.ppermute(block, ('tm', 'space'), route)  38.2 us
    pallas_call x14, Pallas kernels, call(): pl.pallas_call(kernel, out_shape=outs, in_specs=[SMEM] * len(scalars) + [...  29.6 us
    ppermute x24, waiting for transfers between devices, swap(): return lax.ppermute(block, ('tm', 'space'), route)  12.8 us
    ppermute x4, waiting for transfers between devices, next_slice(): return lax.ppermute(block, 'tm', [(i, (i + 1) % n) for i in range(n)])  10.1 us
    pallas_call x1, Pallas kernels, per_device(): pl.pallas_call(table_kernel, out_shape=[jax.ShapeDtypeStruct((nblocks * W...  3.9 us
    pallas_call x1, Pallas kernels, per_device(): pl.pallas_call(first_reaction_kernel, out_shape=[state, split, jax.ShapeD...  2.2 us
    unnamed x3, local copies, waits for them, and re-layouts  2.04 us
  transfers between devices with their start and end apart: 28, of which 13 were waited for; matrix products, arithmetic and copies ran while one was open for 2% of the time, Pallas kernels for 21%

profile of v6, /device:TPU:8, one launch (start us, length us, event | category | flops | bytes accessed | tf_op | source)
XLA Modules:
  0.0 102.0 jit_solution(15657248159373786013)
XLA Ops:
  0.0 1.3 %copy.13 = f32[1,16,64,128]{3,1,2,0:T(8,128)S(1)} copy(f32[1,16,64,128]{3,2,1,0:T(8,128)} %param.6) | data formatting | bytes 1048576 | tf_op args[0]
  1.4 0.0 collective-permute-start.4
  1.5 0.7 compare_select_fusion
  2.2 0.1 reshape.6
  2.2 0.1 concatenate.6.flags
  2.3 0.6 shard_map.64
  3.0 6.3 %collective-permute-start = (bf16[16,16,128]{2,1,0:T(8,128)(2,1)S(1)}, bf16[16,16,128]{2,1,0:T(8,128)(2,1)S(1)}, u32[]{:S(2)}, u32[]{:S(2)}) collective-permute-start(bf16[16,16,128]{2,1,0:T(8,128)(2,1)S(1)} %get-tuple-element.63), channel_id=1, source_target_pairs={{0,32},{1,33},{2,4},{3,5},{4,2},{5,3},{6,8},{7,9},{8,6},{9,7},{10,... | collective-permute-start | bytes 196616 | tf_op jit(solution)/shard_map/ppermute | solution.py:59
  9.3 1.6 %collective-permute-start.1 = (bf16[16,16,128]{2,1,0:T(8,128)(2,1)S(1)}, bf16[16,16,128]{2,1,0:T(8,128)(2,1)S(1)}, u32[]{:S(2)}, u32[]{:S(2)}) collective-permute-start(bf16[16,16,128]{2,1,0:T(8,128)(2,1)S(1)} %get-tuple-element.64), channel_id=1, source_target_pairs={{0,2},{1,3},{2,0},{3,1},{4,6},{5,7},{6,4},{7,5},{8,10},{9,11},{10,... | collective-permute-start | bytes 196616 | tf_op jit(solution)/shard_map/ppermute | solution.py:59
  10.8 1.9 %collective-permute-start.3 = (bf16[16,16,128]{2,1,0:T(8,128)(2,1)S(1)}, bf16[16,16,128]{2,1,0:T(8,128)(2,1)S(1)}, u32[]{:S(2)}, u32[]{:S(2)}) collective-permute-start(bf16[16,16,128]{2,1,0:T(8,128)(2,1)S(1)} %get-tuple-element.66), channel_id=1, source_target_pairs={{0,1},{1,0},{2,3},{3,2},{4,5},{5,4},{6,7},{7,6},{8,9},{9,8},{10,11... | collective-permute-start | bytes 196616 | tf_op jit(solution)/shard_map/ppermute | solution.py:59
  12.7 0.7 pad_add_fusion
  13.4 0.1 copy.9
  13.5 0.1 reshape.7.table.given
  13.7 0.0 copy-start
  13.7 0.7 copy-done
  14.4 2.2 %shard_map.65 = (f32[64,16,128]{2,1,0:T(8,128)S(1)}, bf16[16,48]{1,0:T(8,128)(2,1)S(1)}, bf16[128,128,128]{2,1,0:T(8,128)(2,1)S(1)}) custom-call(f32[64,16,128]{2,1,0:T(8,128)S(1)} %bitcast.23, f32[16,16]{1,0:T(8,128)S(1)} %copy-done, bf16[128,128,128]{2,1,0:T(8,128)(2,1)} %coeffs.1), custom_call_target="tpu_custom_call" | custom-call | flops 4000000 | bytes 4000000 | tf_op jit(solution)/shard_map/pallas_call | solution.py:395
  16.6 1.2 %collective-permute-done.2.refs_2_ = bf16[16,16,128]{2,1,0:T(8,128)(2,1)S(1)} collective-permute-done((bf16[16,16,128]{2,1,0:T(8,128)(2,1)S(1)}, bf16[16,16,128]{2,1,0:T(8,128)(2,1)S(1)}, u32[]{:S(2)}, u32[]{:S(2)}) %collective-permute-start.2) | collective-permute-done | bytes 65568 | tf_op jit(solution)/shard_map/ppermute | solution.py:59
  17.9 3.2 %shard_map.66 = (f32[64,16,128]{2,1,0:T(8,128)S(1)}, bf16[64,16,128]{2,1,0:T(8,128)(2,1)S(1)}) custom-call(s32[77]{0:T(128)S(1)} %concatenate.6.flags, s32[960]{0:T(1024)S(1)} %reshape.7.table.given, bf16[65,16,128]{2,1,0:T(8,128)(2,1)S(1)} %get-tuple-element.61.vb, f32[64,16,128]{2,1,0:T(8,128)S(1)} %get-tuple-element.62.part, ...), custom_call_target="tpu_custom_call" | custom-call | flops 4000000 | bytes 4000000 | tf_op jit(solution)/shard_map/pallas_call | solution.py:358
  21.1 0.1 collective-permute-start.5
  21.1 3.9 %shard_map.67 = (s32[1025]{0:T(1024)S(1)}, f32[8,128]{1,0:T(8,128)S(1)}) custom-call(s32[960]{0:T(1024)S(1)} %reshape.7.table.given, f32[64,16,128]{2,1,0:T(8,128)S(1)} %get-tuple-element.68.after.refs_2_.refs_4_.refs_0_), custom_call_target="tpu_custom_call" | custom-call | flops 1000000 | bytes 1000000 | tf_op jit(solution)/shard_map/pallas_call | solution.py:405
  25.1 3.0 %collective-permute-done.5.refs_3_ = bf16[64,16,128]{2,1,0:T(8,128)(2,1)S(1)} collective-permute-done((bf16[64,16,128]{2,1,0:T(8,128)(2,1)S(1)}, bf16[64,16,128]{2,1,0:T(8,128)(2,1)S(1)}, u32[]{:S(2)}, u32[]{:S(2)}) %collective-permute-start.5) | collective-permute-done | bytes 262176 | tf_op jit(solution)/shard_map/ppermute | solution.py:64
  28.1 0.8 shard_map.69
  28.9 2.5 %collective-permute-start.6 = (bf16[16,16,128]{2,1,0:T(8,128)(2,1)S(1)}, bf16[16,16,128]{2,1,0:T(8,128)(2,1)S(1)}, u32[]{:S(2)}, u32[]{:S(2)}) collective-permute-start(bf16[16,16,128]{2,1,0:T(8,128)(2,1)S(1)} %get-tuple-element.75), channel_id=1, source_target_pairs={{0,32},{1,33},{2,4},{3,5},{4,2},{5,3},{6,8},{7,9},{8,6},{9,7},{10,... | collective-permute-start | bytes 196616 | tf_op jit(solution)/shard_map/ppermute | solution.py:59
  31.4 0.2 collective-permute-start.7
  31.6 1.3 %collective-permute-start.8 = (bf16[16,16,128]{2,1,0:T(8,128)(2,1)S(1)}, bf16[16,16,128]{2,1,0:T(8,128)(2,1)S(1)}, u32[]{:S(2)}, u32[]{:S(2)}) collective-permute-start(bf16[16,16,128]{2,1,0:T(8,128)(2,1)S(1)} %get-tuple-element.77), channel_id=1, source_target_pairs={{0,32},{1,2},{2,1},{3,4},{4,3},{5,6},{6,5},{7,8},{8,7},{9,10},{10,... | collective-permute-start | bytes 196616 | tf_op jit(solution)/shard_map/ppermute | solution.py:59
  32.9 2.0 %collective-permute-start.9 = (bf16[16,16,128]{2,1,0:T(8,128)(2,1)S(1)}, bf16[16,16,128]{2,1,0:T(8,128)(2,1)S(1)}, u32[]{:S(2)}, u32[]{:S(2)}) collective-permute-start(bf16[16,16,128]{2,1,0:T(8,128)(2,1)S(1)} %get-tuple-element.78), channel_id=1, source_target_pairs={{0,1},{1,0},{2,3},{3,2},{4,5},{5,4},{6,7},{7,6},{8,9},{9,8},{10,11... | collective-permute-start | bytes 196616 | tf_op jit(solution)/shard_map/ppermute | solution.py:59
  34.9 2.0 %shard_map.68 = (f32[64,16,128]{2,1,0:T(8,128)S(1)}, f32[64,16,128]{2,1,0:T(8,128)S(1)}, bf16[65,16,128]{2,1,0:T(8,128)(2,1)S(1)}, f32[64,16,128]{2,1,0:T(8,128)S(1)}) custom-call(s32[77]{0:T(128)S(1)} %concatenate.6.flags, s32[1025]{0:T(1024)S(1)} %get-tuple-element.69.table, bf16[16,48]{1,0:T(8,128)(2,1)S(1)} %get-tuple-element.70.mix, ...), custom_call_target="tpu_custom_call" | custom-call | flops 4000000 | bytes 4000000 | tf_op jit(solution)/shard_map/pallas_call | solution.py:358
  36.9 0.0 collective-permute-done.6.refs_0_
  36.9 1.1 %collective-permute-done.8.refs_2_ = bf16[16,16,128]{2,1,0:T(8,128)(2,1)S(1)} collective-permute-done((bf16[16,16,128]{2,1,0:T(8,128)(2,1)S(1)}, bf16[16,16,128]{2,1,0:T(8,128)(2,1)S(1)}, u32[]{:S(2)}, u32[]{:S(2)}) %collective-permute-start.8) | collective-permute-done | bytes 65568 | tf_op jit(solution)/shard_map/ppermute | solution.py:59
  38.0 3.1 %shard_map.70 = (f32[64,16,128]{2,1,0:T(8,128)S(1)}, f32[64,16,128]{2,1,0:T(8,128)S(1)}, bf16[65,16,128]{2,1,0:T(8,128)(2,1)S(1)}, bf16[16,16,128]{2,1,0:T(8,128...) custom-call(s32[77]{0:T(128)S(1)} %concatenate.6.flags, ...), custom_call_target="tpu_custom_call" | custom-call | flops 4000000 | bytes 4000000 | tf_op jit(solution)/shard_map/pallas_call | solution.py:358
  41.1 1.9 %collective-permute-start.10 = (bf16[16,16,128]{2,1,0:T(8,128)(2,1)S(1)}, bf16[16,16,128]{2,1,0:T(8,128)(2,1)S(1)}, u32[]{:S(2)}, u32[]{:S(2)}) collective-permute-start(bf16[16,16,128]{2,1,0:T(8,128)(2,1)S(1)} %get-tuple-element.83), channel_id=1, source_target_pairs={{0,32},{1,33},{2,4},{3,5},{4,2},{5,3},{6,8},{7,9},{8,6},{9,7},{10,... | collective-permute-start | bytes 196616 | tf_op jit(solution)/shard_map/ppermute | solution.py:59
  43.0 2.4 %collective-permute-start.11 = (bf16[16,16,128]{2,1,0:T(8,128)(2,1)S(1)}, bf16[16,16,128]{2,1,0:T(8,128)(2,1)S(1)}, u32[]{:S(2)}, u32[]{:S(2)}) collective-permute-start(bf16[16,16,128]{2,1,0:T(8,128)(2,1)S(1)} %get-tuple-element.84), channel_id=1, source_target_pairs={{0,2},{1,3},{2,0},{3,1},{4,6},{5,7},{6,4},{7,5},{8,10},{9,11},{10,... | collective-permute-start | bytes 196616 | tf_op jit(solution)/shard_map/ppermute | solution.py:59
  45.4 2.1 %collective-permute-start.12 = (bf16[16,16,128]{2,1,0:T(8,128)(2,1)S(1)}, bf16[16,16,128]{2,1,0:T(8,128)(2,1)S(1)}, u32[]{:S(2)}, u32[]{:S(2)}) collective-permute-start(bf16[16,16,128]{2,1,0:T(8,128)(2,1)S(1)} %get-tuple-element.85), channel_id=1, source_target_pairs={{0,32},{1,2},{2,1},{3,4},{4,3},{5,6},{6,5},{7,8},{8,7},{9,10},{10,... | collective-permute-start | bytes 196616 | tf_op jit(solution)/shard_map/ppermute | solution.py:59
  47.5 0.0 collective-permute-start.13
  47.5 1.6 %shard_map.71 = (f32[64,16,128]{2,1,0:T(8,128)S(1)}, f32[64,16,128]{2,1,0:T(8,128)S(1)}) custom-call(s32[1025]{0:T(1024)S(1)} %get-tuple-element.69.table, f32[64,16,128]{2,1,0:T(8,128)S(1)} %get-tuple-element.81.u, bf16[65,16,128]{2,1,0:T(8,128)(2,1)S(1)} %get-tuple-element.80.vb, bf16[16,48]{1,0:T(8,128)(2,1)S(1)} %get-tuple-element.70.mix, ...), custom_call_target="tpu_custom_call" | custom-call | flops 4000000 | bytes 4000000 | tf_op jit(solution)/shard_map/pallas_call | solution.py:358
  49.1 0.1 collective-permute-done.10.refs_0_
  49.2 2.6 %collective-permute-done.12.refs_2_ = bf16[16,16,128]{2,1,0:T(8,128)(2,1)S(1)} collective-permute-done((bf16[16,16,128]{2,1,0:T(8,128)(2,1)S(1)}, bf16[16,16,128]{2,1,0:T(8,128)(2,1)S(1)}, u32[]{:S(2)}, u32[]{:S(2)}) %collective-permute-start.12) | collective-permute-done | bytes 65568 | tf_op jit(solution)/shard_map/ppermute | solution.py:59
  51.8 3.1 %shard_map.72 = (f32[64,16,128]{2,1,0:T(8,128)S(1)}, f32[64,16,128]{2,1,0:T(8,128)S(1)}, bf16[65,16,128]{2,1,0:T(8,128)(2,1)S(1)}, bf16[16,16,128]{2,1,0:T(8,128...) custom-call(s32[77]{0:T(128)S(1)} %concatenate.6.flags, ...), custom_call_target="tpu_custom_call" | custom-call | flops 4000000 | bytes 4000000 | tf_op jit(solution)/shard_map/pallas_call | solution.py:358
  54.9 0.0 collective-permute-start.14
  54.9 1.3 %collective-permute-start.15 = (bf16[16,16,128]{2,1,0:T(8,128)(2,1)S(1)}, bf16[16,16,128]{2,1,0:T(8,128)(2,1)S(1)}, u32[]{:S(2)}, u32[]{:S(2)}) collective-permute-start(bf16[16,16,128]{2,1,0:T(8,128)(2,1)S(1)} %get-tuple-element.94), channel_id=1, source_target_pairs={{0,32},{1,33},{2,4},{3,5},{4,2},{5,3},{6,8},{7,9},{8,6},{9,7},{10,... | collective-permute-start | bytes 196616 | tf_op jit(solution)/shard_map/ppermute | solution.py:59
  56.2 1.3 %collective-permute-start.16 = (bf16[16,16,128]{2,1,0:T(8,128)(2,1)S(1)}, bf16[16,16,128]{2,1,0:T(8,128)(2,1)S(1)}, u32[]{:S(2)}, u32[]{:S(2)}) collective-permute-start(bf16[16,16,128]{2,1,0:T(8,128)(2,1)S(1)} %get-tuple-element.95), channel_id=1, source_target_pairs={{0,2},{1,3},{2,0},{3,1},{4,6},{5,7},{6,4},{7,5},{8,10},{9,11},{10,... | collective-permute-start | bytes 196616 | tf_op jit(solution)/shard_map/ppermute | solution.py:59
  57.5 2.2 %collective-permute-start.17 = (bf16[16,16,128]{2,1,0:T(8,128)(2,1)S(1)}, bf16[16,16,128]{2,1,0:T(8,128)(2,1)S(1)}, u32[]{:S(2)}, u32[]{:S(2)}) collective-permute-start(bf16[16,16,128]{2,1,0:T(8,128)(2,1)S(1)} %get-tuple-element.96), channel_id=1, source_target_pairs={{0,32},{1,2},{2,1},{3,4},{4,3},{5,6},{6,5},{7,8},{8,7},{9,10},{10,... | collective-permute-start | bytes 196616 | tf_op jit(solution)/shard_map/ppermute | solution.py:59
  59.7 1.7 %shard_map.73 = (f32[64,16,128]{2,1,0:T(8,128)S(1)}, f32[64,16,128]{2,1,0:T(8,128)S(1)}) custom-call(s32[1025]{0:T(1024)S(1)} %get-tuple-element.69.table, f32[64,16,128]{2,1,0:T(8,128)S(1)} %get-tuple-element.88.u, bf16[65,16,128]{2,1,0:T(8,128)(2,1)S(1)} %get-tuple-element.90.vb, bf16[16,48]{1,0:T(8,128)(2,1)S(1)} %get-tuple-element.70.mix, ...), custom_call_target="tpu_custom_call" | custom-call | flops 4000000 | bytes 4000000 | tf_op jit(solution)/shard_map/pallas_call | solution.py:358
  61.4 2.5 %collective-permute-done.15.refs_0_ = bf16[16,16,128]{2,1,0:T(8,128)(2,1)S(1)} collective-permute-done((bf16[16,16,128]{2,1,0:T(8,128)(2,1)S(1)}, bf16[16,16,128]{2,1,0:T(8,128)(2,1)S(1)}, u32[]{:S(2)}, u32[]{:S(2)}) %collective-permute-start.15) | collective-permute-done | bytes 65568 | tf_op jit(solution)/shard_map/ppermute | solution.py:59
  63.9 0.5 collective-permute-done.17.refs_2_
  64.4 3.0 %shard_map.74 = (f32[64,16,128]{2,1,0:T(8,128)S(1)}, bf16[64,16,128]{2,1,0:T(8,128)(2,1)S(1)}, f32[64,16,128]{2,1,0:T(8,128)S(1)}) custom-call(s32[77]{0:T(128)S(1)} %concatenate.6.flags, s32[1025]{0:T(1024)S(1)} %get-tuple-element.69.table, bf16[65,16,128]{2,1,0:T(8,128)(2,1)S(1)} %get-tuple-element.90.vb, f32[64,16,128]{2,1,0:T(8,128)S(1)} %get-tuple-element.93.part, ...), custom_call_target="tpu_custom_call" | custom-call | flops 4000000 | bytes 4000000 | tf_op jit(solution)/shard_map/pallas_call | solution.py:358
  67.4 7.0 %collective-permute-done.19.refs_3_ = bf16[64,16,128]{2,1,0:T(8,128)(2,1)S(1)} collective-permute-done((bf16[64,16,128]{2,1,0:T(8,128)(2,1)S(1)}, bf16[64,16,128]{2,1,0:T(8,128)(2,1)S(1)}, u32[]{:S(2)}, u32[]{:S(2)}) %collective-permute-start.19) | collective-permute-done | bytes 262176 | tf_op jit(solution)/shard_map/ppermute | solution.py:64
  74.4 0.8 shard_map.76
  75.2 1.6 %collective-permute-start.20 = (bf16[16,16,128]{2,1,0:T(8,128)(2,1)S(1)}, bf16[16,16,128]{2,1,0:T(8,128)(2,1)S(1)}, u32[]{:S(2)}, u32[]{:S(2)}) collective-permute-start(bf16[16,16,128]{2,1,0:T(8,128)(2,1)S(1)} %get-tuple-element.104), channel_id=1, source_target_pairs={{0,32},{1,33},{2,4},{3,5},{4,2},{5,3},{6,8},{7,9},{8,6},{9,7},{10,... | collective-permute-start | bytes 196616 | tf_op jit(solution)/shard_map/ppermute | solution.py:59
  76.8 2.0 %collective-permute-start.21 = (bf16[16,16,128]{2,1,0:T(8,128)(2,1)S(1)}, bf16[16,16,128]{2,1,0:T(8,128)(2,1)S(1)}, u32[]{:S(2)}, u32[]{:S(2)}) collective-permute-start(bf16[16,16,128]{2,1,0:T(8,128)(2,1)S(1)} %get-tuple-element.105), channel_id=1, source_target_pairs={{0,2},{1,3},{2,0},{3,1},{4,6},{5,7},{6,4},{7,5},{8,10},{9,11},{10,... | collective-permute-start | bytes 196616 | tf_op jit(solution)/shard_map/ppermute | solution.py:59
  78.8 2.4 %collective-permute-start.22 = (bf16[16,16,128]{2,1,0:T(8,128)(2,1)S(1)}, bf16[16,16,128]{2,1,0:T(8,128)(2,1)S(1)}, u32[]{:S(2)}, u32[]{:S(2)}) collective-permute-start(bf16[16,16,128]{2,1,0:T(8,128)(2,1)S(1)} %get-tuple-element.106), channel_id=1, source_target_pairs={{0,32},{1,2},{2,1},{3,4},{4,3},{5,6},{6,5},{7,8},{8,7},{9,10},{10,... | collective-permute-start | bytes 196616 | tf_op jit(solution)/shard_map/ppermute | solution.py:59
  81.2 2.1 %shard_map.75 = (f32[64,16,128]{2,1,0:T(8,128)S(1)}, f32[64,16,128]{2,1,0:T(8,128)S(1)}, bf16[65,16,128]{2,1,0:T(8,128)(2,1)S(1)}) custom-call(s32[77]{0:T(128)S(1)} %concatenate.6.flags, s32[1025]{0:T(1024)S(1)} %get-tuple-element.69.table, bf16[16,48]{1,0:T(8,128)(2,1)S(1)} %get-tuple-element.70.mix, ...), custom_call_target="tpu_custom_call" | custom-call | flops 4000000 | bytes 4000000 | tf_op jit(solution)/shard_map/pallas_call | solution.py:358
  83.3 0.0 collective-permute-done.20.refs_0_
  83.3 1.9 %collective-permute-done.22.refs_2_ = bf16[16,16,128]{2,1,0:T(8,128)(2,1)S(1)} collective-permute-done((bf16[16,16,128]{2,1,0:T(8,128)(2,1)S(1)}, bf16[16,16,128]{2,1,0:T(8,128)(2,1)S(1)}, u32[]{:S(2)}, u32[]{:S(2)}) %collective-permute-start.22) | collective-permute-done | bytes 65568 | tf_op jit(solution)/shard_map/ppermute | solution.py:59
  85.2 0.3 collective-permute-done.23.refs_3_
  85.5 3.1 %shard_map.77 = (f32[64,16,128]{2,1,0:T(8,128)S(1)}, bf16[65,16,128]{2,1,0:T(8,128)(2,1)S(1)}, bf16[16,16,128]{2,1,0:T(8,128)(2,1)S(1)}, bf16[16,16,128]{2,1,0:T...) custom-call(s32[77]{0:T(128)S(1)} %concatenate.6.flags, ...), custom_call_target="tpu_custom_call" | custom-call | flops 4000000 | bytes 4000000 | tf_op jit(solution)/shard_map/pallas_call | solution.py:358
  88.6 1.0 collective-permute-start.24
  89.6 1.7 %collective-permute-start.25 = (bf16[16,16,128]{2,1,0:T(8,128)(2,1)S(1)}, bf16[16,16,128]{2,1,0:T(8,128)(2,1)S(1)}, u32[]{:S(2)}, u32[]{:S(2)}) collective-permute-start(bf16[16,16,128]{2,1,0:T(8,128)(2,1)S(1)} %get-tuple-element.113), channel_id=1, source_target_pairs={{0,2},{1,3},{2,0},{3,1},{4,6},{5,7},{6,4},{7,5},{8,10},{9,11},{10,... | collective-permute-start | bytes 196616 | tf_op jit(solution)/shard_map/ppermute | solution.py:59
  91.3 2.5 %collective-permute-start.26 = (bf16[16,16,128]{2,1,0:T(8,128)(2,1)S(1)}, bf16[16,16,128]{2,1,0:T(8,128)(2,1)S(1)}, u32[]{:S(2)}, u32[]{:S(2)}) collective-permute-start(bf16[16,16,128]{2,1,0:T(8,128)(2,1)S(1)} %get-tuple-element.114), channel_id=1, source_target_pairs={{0,32},{1,2},{2,1},{3,4},{4,3},{5,6},{6,5},{7,8},{8,7},{9,10},{10,... | collective-permute-start | bytes 196616 | tf_op jit(solution)/shard_map/ppermute | solution.py:59
  93.8 1.7 %shard_map.78 = (f32[64,16,128]{2,1,0:T(8,128)S(1)}, f32[64,16,128]{2,1,0:T(8,128)S(1)}) custom-call(s32[1025]{0:T(1024)S(1)} %get-tuple-element.69.table, f32[64,16,128]{2,1,0:T(8,128)S(1)} %get-tuple-element.110.u, bf16[65,16,128]{2,1,0:T(8,128)(2,1)S(1)} %get-tuple-element.109.vb, bf16[16,48]{1,0:T(8,128)(2,1)S(1)} %get-tuple-element.70.mix, ...), custom_call_target="tpu_custom_call" | custom-call | flops 4000000 | bytes 4000000 | tf_op jit(solution)/shard_map/pallas_call | solution.py:358
  95.5 0.5 collective-permute-done.24.refs_0_
  96.0 1.7 %collective-permute-done.26.refs_2_ = bf16[16,16,128]{2,1,0:T(8,128)(2,1)S(1)} collective-permute-done((bf16[16,16,128]{2,1,0:T(8,128)(2,1)S(1)}, bf16[16,16,128]{2,1,0:T(8,128)(2,1)S(1)}, u32[]{:S(2)}, u32[]{:S(2)}) %collective-permute-start.26) | collective-permute-done | bytes 65568 | tf_op jit(solution)/shard_map/ppermute | solution.py:59
  97.7 0.4 collective-permute-done.27.refs_3_
  98.1 3.0 %shard_map.79 = f32[64,16,128]{2,1,0:T(8,128)S(1)} custom-call(s32[77]{0:T(128)S(1)} %concatenate.6.flags, s32[1025]{0:T(1024)S(1)} %get-tuple-element.69.table, bf16[65,16,128]{2,1,0:T(8,128)(2,1)S(1)} %get-tuple-element.109.vb, f32[64,16,128]{2,1,0:T(8,128)S(1)} %get-tuple-element.111.part, bf16[16,16,128]{2,1,0:T(8,128)(2,1)S(1)} %collective-permute-done.24.refs_0_, ...), custom_call_target="tpu_custom_call" | custom-call | flops 4000000 | bytes 4000000 | tf_op jit(solution)/shard_map/pallas_call | solution.py:358
  101.1 1.0 copy.11
  (18 shorter events, 0.0 us)
Async XLA Ops:
  1.4 26.7 %collective-permute-start.4 = (f32[64,16,128]{2,1,0:T(8,128)S(1)}, f32[64,16,128]{2,1,0:T(8,128)S(1)}, u32[]{:S(2)}, u32[]{:S(2)}) collective-permute-start(f32[64,16,128]{2,1,0:T(8,128)S(1)} %bitcast.21), channel_id=1, source_target_pairs={{0,32},{32,64},{64,96},{96,128},{128,160},{160,192},{192,224},{224... | collective-permute-start | bytes 1572872 | tf_op jit(solution)/shard_map/ppermute | solution.py:64
  3.0 13.6 %collective-permute-start = (bf16[16,16,128]{2,1,0:T(8,128)(2,1)S(1)}, bf16[16,16,128]{2,1,0:T(8,128)(2,1)S(1)}, u32[]{:S(2)}, u32[]{:S(2)}) collective-permute-start(bf16[16,16,128]{2,1,0:T(8,128)(2,1)S(1)} %get-tuple-element.63), channel_id=1, source_target_pairs={{0,32},{1,33},{2,4},{3,5},{4,2},{5,3},{6,8},{7,9},{8,6},{9,7},{10,... | collective-permute-start | bytes 196616 | tf_op jit(solution)/shard_map/ppermute | solution.py:59
  9.3 7.3 %collective-permute-start.1 = (bf16[16,16,128]{2,1,0:T(8,128)(2,1)S(1)}, bf16[16,16,128]{2,1,0:T(8,128)(2,1)S(1)}, u32[]{:S(2)}, u32[]{:S(2)}) collective-permute-start(bf16[16,16,128]{2,1,0:T(8,128)(2,1)S(1)} %get-tuple-element.64), channel_id=1, source_target_pairs={{0,2},{1,3},{2,0},{3,1},{4,6},{5,7},{6,4},{7,5},{8,10},{9,11},{10,... | collective-permute-start | bytes 196616 | tf_op jit(solution)/shard_map/ppermute | solution.py:59
  10.8 7.0 %collective-permute-start.2 = (bf16[16,16,128]{2,1,0:T(8,128)(2,1)S(1)}, bf16[16,16,128]{2,1,0:T(8,128)(2,1)S(1)}, u32[]{:S(2)}, u32[]{:S(2)}) collective-permute-start(bf16[16,16,128]{2,1,0:T(8,128)(2,1)S(1)} %get-tuple-element.65), channel_id=1, source_target_pairs={{0,32},{1,2},{2,1},{3,4},{4,3},{5,6},{6,5},{7,8},{8,7},{9,10},{10,... | collective-permute-start | bytes 196616 | tf_op jit(solution)/shard_map/ppermute | solution.py:59
  10.8 7.0 %collective-permute-start.3 = (bf16[16,16,128]{2,1,0:T(8,128)(2,1)S(1)}, bf16[16,16,128]{2,1,0:T(8,128)(2,1)S(1)}, u32[]{:S(2)}, u32[]{:S(2)}) collective-permute-start(bf16[16,16,128]{2,1,0:T(8,128)(2,1)S(1)} %get-tuple-element.66), channel_id=1, source_target_pairs={{0,1},{1,0},{2,3},{3,2},{4,5},{5,4},{6,7},{7,6},{8,9},{9,8},{10,11... | collective-permute-start | bytes 196616 | tf_op jit(solution)/shard_map/ppermute | solution.py:59
  13.7 0.7 copy-start
  21.1 7.0 %collective-permute-start.5 = (bf16[64,16,128]{2,1,0:T(8,128)(2,1)S(1)}, bf16[64,16,128]{2,1,0:T(8,128)(2,1)S(1)}, u32[]{:S(2)}, u32[]{:S(2)}) collective-permute-start(bf16[64,16,128]{2,1,0:T(8,128)(2,1)S(1)} %get-tuple-element.71), channel_id=1, source_target_pairs={{0,32},{32,64},{64,96},{96,128},{128,160},{160,192},{192,224},{224... | collective-permute-start | bytes 786440 | tf_op jit(solution)/shard_map/ppermute | solution.py:64
  28.9 8.0 %collective-permute-start.6 = (bf16[16,16,128]{2,1,0:T(8,128)(2,1)S(1)}, bf16[16,16,128]{2,1,0:T(8,128)(2,1)S(1)}, u32[]{:S(2)}, u32[]{:S(2)}) collective-permute-start(bf16[16,16,128]{2,1,0:T(8,128)(2,1)S(1)} %get-tuple-element.75), channel_id=1, source_target_pairs={{0,32},{1,33},{2,4},{3,5},{4,2},{5,3},{6,8},{7,9},{8,6},{9,7},{10,... | collective-permute-start | bytes 196616 | tf_op jit(solution)/shard_map/ppermute | solution.py:59
  31.4 5.5 %collective-permute-start.7 = (bf16[16,16,128]{2,1,0:T(8,128)(2,1)S(1)}, bf16[16,16,128]{2,1,0:T(8,128)(2,1)S(1)}, u32[]{:S(2)}, u32[]{:S(2)}) collective-permute-start(bf16[16,16,128]{2,1,0:T(8,128)(2,1)S(1)} %get-tuple-element.76), channel_id=1, source_target_pairs={{0,2},{1,3},{2,0},{3,1},{4,6},{5,7},{6,4},{7,5},{8,10},{9,11},{10,... | collective-permute-start | bytes 196616 | tf_op jit(solution)/shard_map/ppermute | solution.py:59
  31.6 6.4 %collective-permute-start.8 = (bf16[16,16,128]{2,1,0:T(8,128)(2,1)S(1)}, bf16[16,16,128]{2,1,0:T(8,128)(2,1)S(1)}, u32[]{:S(2)}, u32[]{:S(2)}) collective-permute-start(bf16[16,16,128]{2,1,0:T(8,128)(2,1)S(1)} %get-tuple-element.77), channel_id=1, source_target_pairs={{0,32},{1,2},{2,1},{3,4},{4,3},{5,6},{6,5},{7,8},{8,7},{9,10},{10,... | collective-permute-start | bytes 196616 | tf_op jit(solution)/shard_map/ppermute | solution.py:59
  32.9 5.1 %collective-permute-start.9 = (bf16[16,16,128]{2,1,0:T(8,128)(2,1)S(1)}, bf16[16,16,128]{2,1,0:T(8,128)(2,1)S(1)}, u32[]{:S(2)}, u32[]{:S(2)}) collective-permute-start(bf16[16,16,128]{2,1,0:T(8,128)(2,1)S(1)} %get-tuple-element.78), channel_id=1, source_target_pairs={{0,1},{1,0},{2,3},{3,2},{4,5},{5,4},{6,7},{7,6},{8,9},{9,8},{10,11... | collective-permute-start | bytes 196616 | tf_op jit(solution)/shard_map/ppermute | solution.py:59
  41.1 8.1 %collective-permute-start.10 = (bf16[16,16,128]{2,1,0:T(8,128)(2,1)S(1)}, bf16[16,16,128]{2,1,0:T(8,128)(2,1)S(1)}, u32[]{:S(2)}, u32[]{:S(2)}) collective-permute-start(bf16[16,16,128]{2,1,0:T(8,128)(2,1)S(1)} %get-tuple-element.83), channel_id=1, source_target_pairs={{0,32},{1,33},{2,4},{3,5},{4,2},{5,3},{6,8},{7,9},{8,6},{9,7},{10,... | collective-permute-start | bytes 196616 | tf_op jit(solution)/shard_map/ppermute | solution.py:59
  43.0 6.2 %collective-permute-start.11 = (bf16[16,16,128]{2,1,0:T(8,128)(2,1)S(1)}, bf16[16,16,128]{2,1,0:T(8,128)(2,1)S(1)}, u32[]{:S(2)}, u32[]{:S(2)}) collective-permute-start(bf16[16,16,128]{2,1,0:T(8,128)(2,1)S(1)} %get-tuple-element.84), channel_id=1, source_target_pairs={{0,2},{1,3},{2,0},{3,1},{4,6},{5,7},{6,4},{7,5},{8,10},{9,11},{10,... | collective-permute-start | bytes 196616 | tf_op jit(solution)/shard_map/ppermute | solution.py:59
  45.4 6.4 %collective-permute-start.12 = (bf16[16,16,128]{2,1,0:T(8,128)(2,1)S(1)}, bf16[16,16,128]{2,1,0:T(8,128)(2,1)S(1)}, u32[]{:S(2)}, u32[]{:S(2)}) collective-permute-start(bf16[16,16,128]{2,1,0:T(8,128)(2,1)S(1)} %get-tuple-element.85), channel_id=1, source_target_pairs={{0,32},{1,2},{2,1},{3,4},{4,3},{5,6},{6,5},{7,8},{8,7},{9,10},{10,... | collective-permute-start | bytes 196616 | tf_op jit(solution)/shard_map/ppermute | solution.py:59
  47.5 4.3 %collective-permute-start.13 = (bf16[16,16,128]{2,1,0:T(8,128)(2,1)S(1)}, bf16[16,16,128]{2,1,0:T(8,128)(2,1)S(1)}, u32[]{:S(2)}, u32[]{:S(2)}) collective-permute-start(bf16[16,16,128]{2,1,0:T(8,128)(2,1)S(1)} %get-tuple-element.86), channel_id=1, source_target_pairs={{0,1},{1,0},{2,3},{3,2},{4,5},{5,4},{6,7},{7,6},{8,9},{9,8},{10,11... | collective-permute-start | bytes 196616 | tf_op jit(solution)/shard_map/ppermute | solution.py:59
  54.9 19.5 %collective-permute-start.14 = (f32[64,16,128]{2,1,0:T(8,128)S(1)}, f32[64,16,128]{2,1,0:T(8,128)S(1)}, u32[]{:S(2)}, u32[]{:S(2)}) collective-permute-start(f32[64,16,128]{2,1,0:T(8,128)S(1)} %get-tuple-element.88.u), channel_id=1, source_target_pairs={{0,32},{32,64},{64,96},{96,128},{128,160},{160,192},{192,224},{224... | collective-permute-start | bytes 1572872 | tf_op jit(solution)/shard_map/ppermute | solution.py:64
  54.9 9.0 %collective-permute-start.15 = (bf16[16,16,128]{2,1,0:T(8,128)(2,1)S(1)}, bf16[16,16,128]{2,1,0:T(8,128)(2,1)S(1)}, u32[]{:S(2)}, u32[]{:S(2)}) collective-permute-start(bf16[16,16,128]{2,1,0:T(8,128)(2,1)S(1)} %get-tuple-element.94), channel_id=1, source_target_pairs={{0,32},{1,33},{2,4},{3,5},{4,2},{5,3},{6,8},{7,9},{8,6},{9,7},{10,... | collective-permute-start | bytes 196616 | tf_op jit(solution)/shard_map/ppermute | solution.py:59
  56.2 7.7 %collective-permute-start.16 = (bf16[16,16,128]{2,1,0:T(8,128)(2,1)S(1)}, bf16[16,16,128]{2,1,0:T(8,128)(2,1)S(1)}, u32[]{:S(2)}, u32[]{:S(2)}) collective-permute-start(bf16[16,16,128]{2,1,0:T(8,128)(2,1)S(1)} %get-tuple-element.95), channel_id=1, source_target_pairs={{0,2},{1,3},{2,0},{3,1},{4,6},{5,7},{6,4},{7,5},{8,10},{9,11},{10,... | collective-permute-start | bytes 196616 | tf_op jit(solution)/shard_map/ppermute | solution.py:59
  57.5 6.9 %collective-permute-start.17 = (bf16[16,16,128]{2,1,0:T(8,128)(2,1)S(1)}, bf16[16,16,128]{2,1,0:T(8,128)(2,1)S(1)}, u32[]{:S(2)}, u32[]{:S(2)}) collective-permute-start(bf16[16,16,128]{2,1,0:T(8,128)(2,1)S(1)} %get-tuple-element.96), channel_id=1, source_target_pairs={{0,32},{1,2},{2,1},{3,4},{4,3},{5,6},{6,5},{7,8},{8,7},{9,10},{10,... | collective-permute-start | bytes 196616 | tf_op jit(solution)/shard_map/ppermute | solution.py:59
  59.7 4.7 %collective-permute-start.18 = (bf16[16,16,128]{2,1,0:T(8,128)(2,1)S(1)}, bf16[16,16,128]{2,1,0:T(8,128)(2,1)S(1)}, u32[]{:S(2)}, u32[]{:S(2)}) collective-permute-start(bf16[16,16,128]{2,1,0:T(8,128)(2,1)S(1)} %get-tuple-element.97), channel_id=1, source_target_pairs={{0,1},{1,0},{2,3},{3,2},{4,5},{5,4},{6,7},{7,6},{8,9},{9,8},{10,11... | collective-permute-start | bytes 196616 | tf_op jit(solution)/shard_map/ppermute | solution.py:59
  67.4 7.0 %collective-permute-start.19 = (bf16[64,16,128]{2,1,0:T(8,128)(2,1)S(1)}, bf16[64,16,128]{2,1,0:T(8,128)(2,1)S(1)}, u32[]{:S(2)}, u32[]{:S(2)}) collective-permute-start(bf16[64,16,128]{2,1,0:T(8,128)(2,1)S(1)} %get-tuple-element.99), channel_id=1, source_target_pairs={{0,32},{32,64},{64,96},{96,128},{128,160},{160,192},{192,224},{224... | collective-permute-start | bytes 786440 | tf_op jit(solution)/shard_map/ppermute | solution.py:64
  75.2 8.1 %collective-permute-start.20 = (bf16[16,16,128]{2,1,0:T(8,128)(2,1)S(1)}, bf16[16,16,128]{2,1,0:T(8,128)(2,1)S(1)}, u32[]{:S(2)}, u32[]{:S(2)}) collective-permute-start(bf16[16,16,128]{2,1,0:T(8,128)(2,1)S(1)} %get-tuple-element.104), channel_id=1, source_target_pairs={{0,32},{1,33},{2,4},{3,5},{4,2},{5,3},{6,8},{7,9},{8,6},{9,7},{10,... | collective-permute-start | bytes 196616 | tf_op jit(solution)/shard_map/ppermute | solution.py:59
  76.8 6.5 %collective-permute-start.21 = (bf16[16,16,128]{2,1,0:T(8,128)(2,1)S(1)}, bf16[16,16,128]{2,1,0:T(8,128)(2,1)S(1)}, u32[]{:S(2)}, u32[]{:S(2)}) collective-permute-start(bf16[16,16,128]{2,1,0:T(8,128)(2,1)S(1)} %get-tuple-element.105), channel_id=1, source_target_pairs={{0,2},{1,3},{2,0},{3,1},{4,6},{5,7},{6,4},{7,5},{8,10},{9,11},{10,... | collective-permute-start | bytes 196616 | tf_op jit(solution)/shard_map/ppermute | solution.py:59
  78.8 6.4 %collective-permute-start.22 = (bf16[16,16,128]{2,1,0:T(8,128)(2,1)S(1)}, bf16[16,16,128]{2,1,0:T(8,128)(2,1)S(1)}, u32[]{:S(2)}, u32[]{:S(2)}) collective-permute-start(bf16[16,16,128]{2,1,0:T(8,128)(2,1)S(1)} %get-tuple-element.106), channel_id=1, source_target_pairs={{0,32},{1,2},{2,1},{3,4},{4,3},{5,6},{6,5},{7,8},{8,7},{9,10},{10,... | collective-permute-start | bytes 196616 | tf_op jit(solution)/shard_map/ppermute | solution.py:59
  81.2 4.3 %collective-permute-start.23 = (bf16[16,16,128]{2,1,0:T(8,128)(2,1)S(1)}, bf16[16,16,128]{2,1,0:T(8,128)(2,1)S(1)}, u32[]{:S(2)}, u32[]{:S(2)}) collective-permute-start(bf16[16,16,128]{2,1,0:T(8,128)(2,1)S(1)} %get-tuple-element.107), channel_id=1, source_target_pairs={{0,1},{1,0},{2,3},{3,2},{4,5},{5,4},{6,7},{7,6},{8,9},{9,8},{10,11... | collective-permute-start | bytes 196616 | tf_op jit(solution)/shard_map/ppermute | solution.py:59
  88.6 7.4 %collective-permute-start.24 = (bf16[16,16,128]{2,1,0:T(8,128)(2,1)S(1)}, bf16[16,16,128]{2,1,0:T(8,128)(2,1)S(1)}, u32[]{:S(2)}, u32[]{:S(2)}) collective-permute-start(bf16[16,16,128]{2,1,0:T(8,128)(2,1)S(1)} %get-tuple-element.112), channel_id=1, source_target_pairs={{0,32},{1,33},{2,4},{3,5},{4,2},{5,3},{6,8},{7,9},{8,6},{9,7},{10,... | collective-permute-start | bytes 196616 | tf_op jit(solution)/shard_map/ppermute | solution.py:59
  89.6 6.4 %collective-permute-start.25 = (bf16[16,16,128]{2,1,0:T(8,128)(2,1)S(1)}, bf16[16,16,128]{2,1,0:T(8,128)(2,1)S(1)}, u32[]{:S(2)}, u32[]{:S(2)}) collective-permute-start(bf16[16,16,128]{2,1,0:T(8,128)(2,1)S(1)} %get-tuple-element.113), channel_id=1, source_target_pairs={{0,2},{1,3},{2,0},{3,1},{4,6},{5,7},{6,4},{7,5},{8,10},{9,11},{10,... | collective-permute-start | bytes 196616 | tf_op jit(solution)/shard_map/ppermute | solution.py:59
  91.3 6.4 %collective-permute-start.26 = (bf16[16,16,128]{2,1,0:T(8,128)(2,1)S(1)}, bf16[16,16,128]{2,1,0:T(8,128)(2,1)S(1)}, u32[]{:S(2)}, u32[]{:S(2)}) collective-permute-start(bf16[16,16,128]{2,1,0:T(8,128)(2,1)S(1)} %get-tuple-element.114), channel_id=1, source_target_pairs={{0,32},{1,2},{2,1},{3,4},{4,3},{5,6},{6,5},{7,8},{8,7},{9,10},{10,... | collective-permute-start | bytes 196616 | tf_op jit(solution)/shard_map/ppermute | solution.py:59
  93.8 4.3 %collective-permute-start.27 = (bf16[16,16,128]{2,1,0:T(8,128)(2,1)S(1)}, bf16[16,16,128]{2,1,0:T(8,128)(2,1)S(1)}, u32[]{:S(2)}, u32[]{:S(2)}) collective-permute-start(bf16[16,16,128]{2,1,0:T(8,128)(2,1)S(1)} %get-tuple-element.115), channel_id=1, source_target_pairs={{0,1},{1,0},{2,3},{3,2},{4,5},{5,4},{6,7},{7,6},{8,9},{9,8},{10,11... | collective-permute-start | bytes 196616 | tf_op jit(solution)/shard_map/ppermute | solution.py:59

commit v7 on v6

--- a/solution.py
+++ b/solution.py
@@ -153,23 +153,24 @@
         source, at = b * (WIDTH - 1), b * WIDTH
         values = [given[source + t] for t in range(WIDTH - 1)]
         mats, cols = values[1:TERMS], values[TERMS:]
-        chosen, mat, col = jnp.int32(0), mats[0], cols[0]
-        lonely = jnp.int32(1)
+        chosen, mat, col = jnp.int32(TERMS), mats[0], cols[0]
         for t in reversed(range(TERMS - 1)):
             local = cols[t] < nblocks
             chosen = jnp.where(local, t, chosen)
             mat = jnp.where(local, mats[t], mat)
             col = jnp.where(local, cols[t], col)
-            lonely = jnp.where(local, 0, lonely)
+        lonely = chosen == TERMS
+        chosen = jnp.where(lonely, 0, chosen)
         table[at] = values[0]
+        for t in range(1, TERMS - 1):
+            table[at + 1 + t] = mats[t]
+            table[at + TERMS + t] = cols[t]
+        table[at + 1 + chosen] = mats[0]
+        table[at + TERMS + chosen] = cols[0]
         table[at + 1] = mat
         table[at + TERMS] = col
-        for t in range(1, TERMS - 1):
-            here = chosen == t
-            table[at + 1 + t] = jnp.where(here, mats[0], mats[t])
-            table[at + TERMS + t] = jnp.where(here, cols[0], cols[t])
         table[count * WIDTH + WIDTH - 1] = b
-        return count + lonely
+        return count + lonely.astype(jnp.int32)
 
     table[nblocks * WIDTH] = lax.fori_loop(0, nblocks, body, jnp.int32(0), unroll=4)
 

time: 102 us -> 102 us (level)
  Pallas kernels: 35.7 us -> 33.8 us
  starting transfers between devices: 38.3 us -> 39.4 us
    pallas_call x14, Pallas kernels: 29.6 us -> 28.2 us  [call(): pl.pallas_call(kernel, out_shape=outs, in_specs=[SMEM] * len(scalars) + [...]
    ppermute x24, starting transfers between devices: 38.2 us -> 39.2 us  [swap(): return lax.ppermute(block, ('tm', 'space'), route)]
  transfers between devices with their start and end apart: 28 -> 28, of which waited for: 13 -> 12; matrix products, arithmetic and copies ran while one was open for 2% -> 2% of each run, Pallas kernels for 21% -> 21%
where the time goes in v7:
time: 102 us
  starting transfers between devices  39.4 us (39%)
  Pallas kernels  33.8 us (33%)
  waiting for transfers between devices  23.2 us (23%)
  local copies, waits for them, and re-layouts  3.41 us (3%)
  other arithmetic  1.39 us (1%)
    ppermute x24, starting transfers between devices, swap(): return lax.ppermute(block, ('tm', 'space'), route)  39.2 us
    pallas_call x14, Pallas kernels, call(): pl.pallas_call(kernel, out_shape=outs, in_specs=[SMEM] * len(scalars) + [...  28.2 us
    ppermute x24, waiting for transfers between devices, swap(): return lax.ppermute(block, ('tm', 'space'), route)  12.6 us
    ppermute x4, waiting for transfers between devices, next_slice(): return lax.ppermute(block, 'tm', [(i, (i + 1) % n) for i in range(n)])  10.6 us
    pallas_call x1, Pallas kernels, per_device(): pl.pallas_call(table_kernel, out_shape=[jax.ShapeDtypeStruct((nblocks * W...  3.32 us
    pallas_call x1, Pallas kernels, per_device(): pl.pallas_call(first_reaction_kernel, out_shape=[state, split, jax.ShapeD...  2.2 us
    unnamed x3, local copies, waits for them, and re-layouts  2.04 us
  transfers between devices with their start and end apart: 28, of which 12 were waited for; matrix products, arithmetic and copies ran while one was open for 2% of the time, Pallas kernels for 21%

profile of v7, /device:TPU:8, one launch (start us, length us, event | category | flops | bytes accessed | tf_op | source)
XLA Modules:
  0.0 101.5 jit_solution(633754957979478637)
XLA Ops:
  0.0 1.3 %copy.13 = f32[1,16,64,128]{3,1,2,0:T(8,128)S(1)} copy(f32[1,16,64,128]{3,2,1,0:T(8,128)} %param.6) | data formatting | bytes 1048576 | tf_op args[0]
  1.4 0.0 collective-permute-start.4
  1.5 0.7 compare_select_fusion
  2.2 0.1 reshape.6
  2.2 0.1 concatenate.6.flags
  2.3 0.6 shard_map.64
  3.0 6.3 %collective-permute-start = (bf16[16,16,128]{2,1,0:T(8,128)(2,1)S(1)}, bf16[16,16,128]{2,1,0:T(8,128)(2,1)S(1)}, u32[]{:S(2)}, u32[]{:S(2)}) collective-permute-start(bf16[16,16,128]{2,1,0:T(8,128)(2,1)S(1)} %get-tuple-element.63), channel_id=1, source_target_pairs={{0,32},{1,33},{2,4},{3,5},{4,2},{5,3},{6,8},{7,9},{8,6},{9,7},{10,... | collective-permute-start | bytes 196616 | tf_op jit(solution)/shard_map/ppermute | solution.py:59
  9.3 1.6 %collective-permute-start.1 = (bf16[16,16,128]{2,1,0:T(8,128)(2,1)S(1)}, bf16[16,16,128]{2,1,0:T(8,128)(2,1)S(1)}, u32[]{:S(2)}, u32[]{:S(2)}) collective-permute-start(bf16[16,16,128]{2,1,0:T(8,128)(2,1)S(1)} %get-tuple-element.64), channel_id=1, source_target_pairs={{0,2},{1,3},{2,0},{3,1},{4,6},{5,7},{6,4},{7,5},{8,10},{9,11},{10,... | collective-permute-start | bytes 196616 | tf_op jit(solution)/shard_map/ppermute | solution.py:59
  10.8 1.9 %collective-permute-start.3 = (bf16[16,16,128]{2,1,0:T(8,128)(2,1)S(1)}, bf16[16,16,128]{2,1,0:T(8,128)(2,1)S(1)}, u32[]{:S(2)}, u32[]{:S(2)}) collective-permute-start(bf16[16,16,128]{2,1,0:T(8,128)(2,1)S(1)} %get-tuple-element.66), channel_id=1, source_target_pairs={{0,1},{1,0},{2,3},{3,2},{4,5},{5,4},{6,7},{7,6},{8,9},{9,8},{10,11... | collective-permute-start | bytes 196616 | tf_op jit(solution)/shard_map/ppermute | solution.py:59
  12.7 0.7 pad_add_fusion
  13.4 0.1 copy.9
  13.5 0.1 reshape.7.table.given
  13.7 0.7 copy-done
  14.4 2.2 %shard_map.65 = (f32[64,16,128]{2,1,0:T(8,128)S(1)}, bf16[16,48]{1,0:T(8,128)(2,1)S(1)}, bf16[128,128,128]{2,1,0:T(8,128)(2,1)S(1)}) custom-call(f32[64,16,128]{2,1,0:T(8,128)S(1)} %bitcast.23, f32[16,16]{1,0:T(8,128)S(1)} %copy-done, bf16[128,128,128]{2,1,0:T(8,128)(2,1)} %coeffs.1), custom_call_target="tpu_custom_call" | custom-call | flops 4000000 | bytes 4000000 | tf_op jit(solution)/shard_map/pallas_call | solution.py:396
  16.6 1.2 %collective-permute-done.2.refs_2_ = bf16[16,16,128]{2,1,0:T(8,128)(2,1)S(1)} collective-permute-done((bf16[16,16,128]{2,1,0:T(8,128)(2,1)S(1)}, bf16[16,16,128]{2,1,0:T(8,128)(2,1)S(1)}, u32[]{:S(2)}, u32[]{:S(2)}) %collective-permute-start.2) | collective-permute-done | bytes 65568 | tf_op jit(solution)/shard_map/ppermute | solution.py:59
  17.9 3.2 %shard_map.66 = (f32[64,16,128]{2,1,0:T(8,128)S(1)}, bf16[64,16,128]{2,1,0:T(8,128)(2,1)S(1)}) custom-call(s32[77]{0:T(128)S(1)} %concatenate.6.flags, s32[960]{0:T(1024)S(1)} %reshape.7.table.given, bf16[65,16,128]{2,1,0:T(8,128)(2,1)S(1)} %get-tuple-element.61.vb, f32[64,16,128]{2,1,0:T(8,128)S(1)} %get-tuple-element.62.part, ...), custom_call_target="tpu_custom_call" | custom-call | flops 4000000 | bytes 4000000 | tf_op jit(solution)/shard_map/pallas_call | solution.py:359
  21.1 0.1 collective-permute-start.5
  21.1 3.3 %shard_map.67 = (s32[1025]{0:T(1024)S(1)}, f32[8,128]{1,0:T(8,128)S(1)}) custom-call(s32[960]{0:T(1024)S(1)} %reshape.7.table.given, f32[64,16,128]{2,1,0:T(8,128)S(1)} %get-tuple-element.68.after.refs_2_.refs_4_.refs_0_), custom_call_target="tpu_custom_call" | custom-call | flops 1000000 | bytes 1000000 | tf_op jit(solution)/shard_map/pallas_call | solution.py:406
  24.5 3.6 %collective-permute-done.5.refs_3_ = bf16[64,16,128]{2,1,0:T(8,128)(2,1)S(1)} collective-permute-done((bf16[64,16,128]{2,1,0:T(8,128)(2,1)S(1)}, bf16[64,16,128]{2,1,0:T(8,128)(2,1)S(1)}, u32[]{:S(2)}, u32[]{:S(2)}) %collective-permute-start.5) | collective-permute-done | bytes 262176 | tf_op jit(solution)/shard_map/ppermute | solution.py:64
  28.1 0.8 shard_map.69
  28.9 2.5 %collective-permute-start.6 = (bf16[16,16,128]{2,1,0:T(8,128)(2,1)S(1)}, bf16[16,16,128]{2,1,0:T(8,128)(2,1)S(1)}, u32[]{:S(2)}, u32[]{:S(2)}) collective-permute-start(bf16[16,16,128]{2,1,0:T(8,128)(2,1)S(1)} %get-tuple-element.75), channel_id=1, source_target_pairs={{0,32},{1,33},{2,4},{3,5},{4,2},{5,3},{6,8},{7,9},{8,6},{9,7},{10,... | collective-permute-start | bytes 196616 | tf_op jit(solution)/shard_map/ppermute | solution.py:59
  31.4 0.2 collective-permute-start.7
  31.6 1.3 %collective-permute-start.8 = (bf16[16,16,128]{2,1,0:T(8,128)(2,1)S(1)}, bf16[16,16,128]{2,1,0:T(8,128)(2,1)S(1)}, u32[]{:S(2)}, u32[]{:S(2)}) collective-permute-start(bf16[16,16,128]{2,1,0:T(8,128)(2,1)S(1)} %get-tuple-element.77), channel_id=1, source_target_pairs={{0,32},{1,2},{2,1},{3,4},{4,3},{5,6},{6,5},{7,8},{8,7},{9,10},{10,... | collective-permute-start | bytes 196616 | tf_op jit(solution)/shard_map/ppermute | solution.py:59
  32.9 2.0 %collective-permute-start.9 = (bf16[16,16,128]{2,1,0:T(8,128)(2,1)S(1)}, bf16[16,16,128]{2,1,0:T(8,128)(2,1)S(1)}, u32[]{:S(2)}, u32[]{:S(2)}) collective-permute-start(bf16[16,16,128]{2,1,0:T(8,128)(2,1)S(1)} %get-tuple-element.78), channel_id=1, source_target_pairs={{0,1},{1,0},{2,3},{3,2},{4,5},{5,4},{6,7},{7,6},{8,9},{9,8},{10,11... | collective-permute-start | bytes 196616 | tf_op jit(solution)/shard_map/ppermute | solution.py:59
  34.9 2.0 %shard_map.68 = (f32[64,16,128]{2,1,0:T(8,128)S(1)}, f32[64,16,128]{2,1,0:T(8,128)S(1)}, bf16[65,16,128]{2,1,0:T(8,128)(2,1)S(1)}, f32[64,16,128]{2,1,0:T(8,128)S(1)}) custom-call(s32[77]{0:T(128)S(1)} %concatenate.6.flags, s32[1025]{0:T(1024)S(1)} %get-tuple-element.69.table, bf16[16,48]{1,0:T(8,128)(2,1)S(1)} %get-tuple-element.70.mix, ...), custom_call_target="tpu_custom_call" | custom-call | flops 4000000 | bytes 4000000 | tf_op jit(solution)/shard_map/pallas_call | solution.py:359
  36.9 0.5 collective-permute-done.7.refs_1_
  37.4 0.6 collective-permute-done.8.refs_2_
  38.0 2.8 %shard_map.70 = (f32[64,16,128]{2,1,0:T(8,128)S(1)}, f32[64,16,128]{2,1,0:T(8,128)S(1)}, bf16[65,16,128]{2,1,0:T(8,128)(2,1)S(1)}, bf16[16,16,128]{2,1,0:T(8,128...) custom-call(s32[77]{0:T(128)S(1)} %concatenate.6.flags, ...), custom_call_target="tpu_custom_call" | custom-call | flops 4000000 | bytes 4000000 | tf_op jit(solution)/shard_map/pallas_call | solution.py:359
  40.8 2.2 %collective-permute-start.10 = (bf16[16,16,128]{2,1,0:T(8,128)(2,1)S(1)}, bf16[16,16,128]{2,1,0:T(8,128)(2,1)S(1)}, u32[]{:S(2)}, u32[]{:S(2)}) collective-permute-start(bf16[16,16,128]{2,1,0:T(8,128)(2,1)S(1)} %get-tuple-element.83), channel_id=1, source_target_pairs={{0,32},{1,33},{2,4},{3,5},{4,2},{5,3},{6,8},{7,9},{8,6},{9,7},{10,... | collective-permute-start | bytes 196616 | tf_op jit(solution)/shard_map/ppermute | solution.py:59
  43.0 2.4 %collective-permute-start.11 = (bf16[16,16,128]{2,1,0:T(8,128)(2,1)S(1)}, bf16[16,16,128]{2,1,0:T(8,128)(2,1)S(1)}, u32[]{:S(2)}, u32[]{:S(2)}) collective-permute-start(bf16[16,16,128]{2,1,0:T(8,128)(2,1)S(1)} %get-tuple-element.84), channel_id=1, source_target_pairs={{0,2},{1,3},{2,0},{3,1},{4,6},{5,7},{6,4},{7,5},{8,10},{9,11},{10,... | collective-permute-start | bytes 196616 | tf_op jit(solution)/shard_map/ppermute | solution.py:59
  45.4 2.2 %collective-permute-start.12 = (bf16[16,16,128]{2,1,0:T(8,128)(2,1)S(1)}, bf16[16,16,128]{2,1,0:T(8,128)(2,1)S(1)}, u32[]{:S(2)}, u32[]{:S(2)}) collective-permute-start(bf16[16,16,128]{2,1,0:T(8,128)(2,1)S(1)} %get-tuple-element.85), channel_id=1, source_target_pairs={{0,32},{1,2},{2,1},{3,4},{4,3},{5,6},{6,5},{7,8},{8,7},{9,10},{10,... | collective-permute-start | bytes 196616 | tf_op jit(solution)/shard_map/ppermute | solution.py:59
  47.6 1.6 %shard_map.71 = (f32[64,16,128]{2,1,0:T(8,128)S(1)}, f32[64,16,128]{2,1,0:T(8,128)S(1)}) custom-call(s32[1025]{0:T(1024)S(1)} %get-tuple-element.69.table, f32[64,16,128]{2,1,0:T(8,128)S(1)} %get-tuple-element.81.u, bf16[65,16,128]{2,1,0:T(8,128)(2,1)S(1)} %get-tuple-element.80.vb, bf16[16,48]{1,0:T(8,128)(2,1)S(1)} %get-tuple-element.70.mix, ...), custom_call_target="tpu_custom_call" | custom-call | flops 4000000 | bytes 4000000 | tf_op jit(solution)/shard_map/pallas_call | solution.py:359
  49.3 2.5 %collective-permute-done.12.refs_2_ = bf16[16,16,128]{2,1,0:T(8,128)(2,1)S(1)} collective-permute-done((bf16[16,16,128]{2,1,0:T(8,128)(2,1)S(1)}, bf16[16,16,128]{2,1,0:T(8,128)(2,1)S(1)}, u32[]{:S(2)}, u32[]{:S(2)}) %collective-permute-start.12) | collective-permute-done | bytes 65568 | tf_op jit(solution)/shard_map/ppermute | solution.py:59
  51.8 0.1 collective-permute-done.13.refs_3_
  51.9 2.8 %shard_map.72 = (f32[64,16,128]{2,1,0:T(8,128)S(1)}, f32[64,16,128]{2,1,0:T(8,128)S(1)}, bf16[65,16,128]{2,1,0:T(8,128)(2,1)S(1)}, bf16[16,16,128]{2,1,0:T(8,128...) custom-call(s32[77]{0:T(128)S(1)} %concatenate.6.flags, ...), custom_call_target="tpu_custom_call" | custom-call | flops 4000000 | bytes 4000000 | tf_op jit(solution)/shard_map/pallas_call | solution.py:359
  54.7 0.0 collective-permute-start.14
  54.7 1.5 %collective-permute-start.15 = (bf16[16,16,128]{2,1,0:T(8,128)(2,1)S(1)}, bf16[16,16,128]{2,1,0:T(8,128)(2,1)S(1)}, u32[]{:S(2)}, u32[]{:S(2)}) collective-permute-start(bf16[16,16,128]{2,1,0:T(8,128)(2,1)S(1)} %get-tuple-element.94), channel_id=1, source_target_pairs={{0,32},{1,33},{2,4},{3,5},{4,2},{5,3},{6,8},{7,9},{8,6},{9,7},{10,... | collective-permute-start | bytes 196616 | tf_op jit(solution)/shard_map/ppermute | solution.py:59
  56.2 1.2 %collective-permute-start.16 = (bf16[16,16,128]{2,1,0:T(8,128)(2,1)S(1)}, bf16[16,16,128]{2,1,0:T(8,128)(2,1)S(1)}, u32[]{:S(2)}, u32[]{:S(2)}) collective-permute-start(bf16[16,16,128]{2,1,0:T(8,128)(2,1)S(1)} %get-tuple-element.95), channel_id=1, source_target_pairs={{0,2},{1,3},{2,0},{3,1},{4,6},{5,7},{6,4},{7,5},{8,10},{9,11},{10,... | collective-permute-start | bytes 196616 | tf_op jit(solution)/shard_map/ppermute | solution.py:59
  57.4 2.2 %collective-permute-start.17 = (bf16[16,16,128]{2,1,0:T(8,128)(2,1)S(1)}, bf16[16,16,128]{2,1,0:T(8,128)(2,1)S(1)}, u32[]{:S(2)}, u32[]{:S(2)}) collective-permute-start(bf16[16,16,128]{2,1,0:T(8,128)(2,1)S(1)} %get-tuple-element.96), channel_id=1, source_target_pairs={{0,32},{1,2},{2,1},{3,4},{4,3},{5,6},{6,5},{7,8},{8,7},{9,10},{10,... | collective-permute-start | bytes 196616 | tf_op jit(solution)/shard_map/ppermute | solution.py:59
  59.6 0.1 collective-permute-start.18
  59.7 1.7 %shard_map.73 = (f32[64,16,128]{2,1,0:T(8,128)S(1)}, f32[64,16,128]{2,1,0:T(8,128)S(1)}) custom-call(s32[1025]{0:T(1024)S(1)} %get-tuple-element.69.table, f32[64,16,128]{2,1,0:T(8,128)S(1)} %get-tuple-element.88.u, bf16[65,16,128]{2,1,0:T(8,128)(2,1)S(1)} %get-tuple-element.90.vb, bf16[16,48]{1,0:T(8,128)(2,1)S(1)} %get-tuple-element.70.mix, ...), custom_call_target="tpu_custom_call" | custom-call | flops 4000000 | bytes 4000000 | tf_op jit(solution)/shard_map/pallas_call | solution.py:359
  61.3 2.0 %collective-permute-done.15.refs_0_ = bf16[16,16,128]{2,1,0:T(8,128)(2,1)S(1)} collective-permute-done((bf16[16,16,128]{2,1,0:T(8,128)(2,1)S(1)}, bf16[16,16,128]{2,1,0:T(8,128)(2,1)S(1)}, u32[]{:S(2)}, u32[]{:S(2)}) %collective-permute-start.15) | collective-permute-done | bytes 65568 | tf_op jit(solution)/shard_map/ppermute | solution.py:59
  63.3 0.6 collective-permute-done.17.refs_2_
  63.9 0.0 collective-permute-done.18.refs_3_
  64.0 2.7 %shard_map.74 = (f32[64,16,128]{2,1,0:T(8,128)S(1)}, bf16[64,16,128]{2,1,0:T(8,128)(2,1)S(1)}, f32[64,16,128]{2,1,0:T(8,128)S(1)}) custom-call(s32[77]{0:T(128)S(1)} %concatenate.6.flags, s32[1025]{0:T(1024)S(1)} %get-tuple-element.69.table, bf16[65,16,128]{2,1,0:T(8,128)(2,1)S(1)} %get-tuple-element.90.vb, f32[64,16,128]{2,1,0:T(8,128)S(1)} %get-tuple-element.93.part, ...), custom_call_target="tpu_custom_call" | custom-call | flops 4000000 | bytes 4000000 | tf_op jit(solution)/shard_map/pallas_call | solution.py:359
  66.7 0.0 collective-permute-start.19
  66.7 7.0 %collective-permute-done.19.refs_3_ = bf16[64,16,128]{2,1,0:T(8,128)(2,1)S(1)} collective-permute-done((bf16[64,16,128]{2,1,0:T(8,128)(2,1)S(1)}, bf16[64,16,128]{2,1,0:T(8,128)(2,1)S(1)}, u32[]{:S(2)}, u32[]{:S(2)}) %collective-permute-start.19) | collective-permute-done | bytes 262176 | tf_op jit(solution)/shard_map/ppermute | solution.py:64
  73.7 0.8 shard_map.76
  74.5 2.2 %collective-permute-start.20 = (bf16[16,16,128]{2,1,0:T(8,128)(2,1)S(1)}, bf16[16,16,128]{2,1,0:T(8,128)(2,1)S(1)}, u32[]{:S(2)}, u32[]{:S(2)}) collective-permute-start(bf16[16,16,128]{2,1,0:T(8,128)(2,1)S(1)} %get-tuple-element.104), channel_id=1, source_target_pairs={{0,32},{1,33},{2,4},{3,5},{4,2},{5,3},{6,8},{7,9},{8,6},{9,7},{10,... | collective-permute-start | bytes 196616 | tf_op jit(solution)/shard_map/ppermute | solution.py:59
  76.7 2.3 %collective-permute-start.21 = (bf16[16,16,128]{2,1,0:T(8,128)(2,1)S(1)}, bf16[16,16,128]{2,1,0:T(8,128)(2,1)S(1)}, u32[]{:S(2)}, u32[]{:S(2)}) collective-permute-start(bf16[16,16,128]{2,1,0:T(8,128)(2,1)S(1)} %get-tuple-element.105), channel_id=1, source_target_pairs={{0,2},{1,3},{2,0},{3,1},{4,6},{5,7},{6,4},{7,5},{8,10},{9,11},{10,... | collective-permute-start | bytes 196616 | tf_op jit(solution)/shard_map/ppermute | solution.py:59
  79.0 2.1 %collective-permute-start.22 = (bf16[16,16,128]{2,1,0:T(8,128)(2,1)S(1)}, bf16[16,16,128]{2,1,0:T(8,128)(2,1)S(1)}, u32[]{:S(2)}, u32[]{:S(2)}) collective-permute-start(bf16[16,16,128]{2,1,0:T(8,128)(2,1)S(1)} %get-tuple-element.106), channel_id=1, source_target_pairs={{0,32},{1,2},{2,1},{3,4},{4,3},{5,6},{6,5},{7,8},{8,7},{9,10},{10,... | collective-permute-start | bytes 196616 | tf_op jit(solution)/shard_map/ppermute | solution.py:59
  81.2 2.1 %shard_map.75 = (f32[64,16,128]{2,1,0:T(8,128)S(1)}, f32[64,16,128]{2,1,0:T(8,128)S(1)}, bf16[65,16,128]{2,1,0:T(8,128)(2,1)S(1)}) custom-call(s32[77]{0:T(128)S(1)} %concatenate.6.flags, s32[1025]{0:T(1024)S(1)} %get-tuple-element.69.table, bf16[16,48]{1,0:T(8,128)(2,1)S(1)} %get-tuple-element.70.mix, ...), custom_call_target="tpu_custom_call" | custom-call | flops 4000000 | bytes 4000000 | tf_op jit(solution)/shard_map/pallas_call | solution.py:359
  83.3 2.1 %collective-permute-done.22.refs_2_ = bf16[16,16,128]{2,1,0:T(8,128)(2,1)S(1)} collective-permute-done((bf16[16,16,128]{2,1,0:T(8,128)(2,1)S(1)}, bf16[16,16,128]{2,1,0:T(8,128)(2,1)S(1)}, u32[]{:S(2)}, u32[]{:S(2)}) %collective-permute-start.22) | collective-permute-done | bytes 65568 | tf_op jit(solution)/shard_map/ppermute | solution.py:59
  85.4 0.0 collective-permute-done.23.refs_3_
  85.4 2.8 %shard_map.77 = (f32[64,16,128]{2,1,0:T(8,128)S(1)}, bf16[65,16,128]{2,1,0:T(8,128)(2,1)S(1)}, bf16[16,16,128]{2,1,0:T(8,128)(2,1)S(1)}, bf16[16,16,128]{2,1,0:T...) custom-call(s32[77]{0:T(128)S(1)} %concatenate.6.flags, ...), custom_call_target="tpu_custom_call" | custom-call | flops 4000000 | bytes 4000000 | tf_op jit(solution)/shard_map/pallas_call | solution.py:359
  88.2 1.5 %collective-permute-start.24 = (bf16[16,16,128]{2,1,0:T(8,128)(2,1)S(1)}, bf16[16,16,128]{2,1,0:T(8,128)(2,1)S(1)}, u32[]{:S(2)}, u32[]{:S(2)}) collective-permute-start(bf16[16,16,128]{2,1,0:T(8,128)(2,1)S(1)} %get-tuple-element.112), channel_id=1, source_target_pairs={{0,32},{1,33},{2,4},{3,5},{4,2},{5,3},{6,8},{7,9},{8,6},{9,7},{10,... | collective-permute-start | bytes 196616 | tf_op jit(solution)/shard_map/ppermute | solution.py:59
  89.8 1.7 %collective-permute-start.25 = (bf16[16,16,128]{2,1,0:T(8,128)(2,1)S(1)}, bf16[16,16,128]{2,1,0:T(8,128)(2,1)S(1)}, u32[]{:S(2)}, u32[]{:S(2)}) collective-permute-start(bf16[16,16,128]{2,1,0:T(8,128)(2,1)S(1)} %get-tuple-element.113), channel_id=1, source_target_pairs={{0,2},{1,3},{2,0},{3,1},{4,6},{5,7},{6,4},{7,5},{8,10},{9,11},{10,... | collective-permute-start | bytes 196616 | tf_op jit(solution)/shard_map/ppermute | solution.py:59
  91.4 1.8 %collective-permute-start.26 = (bf16[16,16,128]{2,1,0:T(8,128)(2,1)S(1)}, bf16[16,16,128]{2,1,0:T(8,128)(2,1)S(1)}, u32[]{:S(2)}, u32[]{:S(2)}) collective-permute-start(bf16[16,16,128]{2,1,0:T(8,128)(2,1)S(1)} %get-tuple-element.114), channel_id=1, source_target_pairs={{0,32},{1,2},{2,1},{3,4},{4,3},{5,6},{6,5},{7,8},{8,7},{9,10},{10,... | collective-permute-start | bytes 196616 | tf_op jit(solution)/shard_map/ppermute | solution.py:59
  93.2 0.0 collective-permute-start.27
  93.3 1.7 %shard_map.78 = (f32[64,16,128]{2,1,0:T(8,128)S(1)}, f32[64,16,128]{2,1,0:T(8,128)S(1)}) custom-call(s32[1025]{0:T(1024)S(1)} %get-tuple-element.69.table, f32[64,16,128]{2,1,0:T(8,128)S(1)} %get-tuple-element.110.u, bf16[65,16,128]{2,1,0:T(8,128)(2,1)S(1)} %get-tuple-element.109.vb, bf16[16,48]{1,0:T(8,128)(2,1)S(1)} %get-tuple-element.70.mix, ...), custom_call_target="tpu_custom_call" | custom-call | flops 4000000 | bytes 4000000 | tf_op jit(solution)/shard_map/pallas_call | solution.py:359
  94.9 0.7 collective-permute-done.24.refs_0_
  95.6 2.2 %collective-permute-done.26.refs_2_ = bf16[16,16,128]{2,1,0:T(8,128)(2,1)S(1)} collective-permute-done((bf16[16,16,128]{2,1,0:T(8,128)(2,1)S(1)}, bf16[16,16,128]{2,1,0:T(8,128)(2,1)S(1)}, u32[]{:S(2)}, u32[]{:S(2)}) %collective-permute-start.26) | collective-permute-done | bytes 65568 | tf_op jit(solution)/shard_map/ppermute | solution.py:59
  97.8 2.7 %shard_map.79 = f32[64,16,128]{2,1,0:T(8,128)S(1)} custom-call(s32[77]{0:T(128)S(1)} %concatenate.6.flags, s32[1025]{0:T(1024)S(1)} %get-tuple-element.69.table, bf16[65,16,128]{2,1,0:T(8,128)(2,1)S(1)} %get-tuple-element.109.vb, f32[64,16,128]{2,1,0:T(8,128)S(1)} %get-tuple-element.111.part, bf16[16,16,128]{2,1,0:T(8,128)(2,1)S(1)} %collective-permute-done.24.refs_0_, ...), custom_call_target="tpu_custom_call" | custom-call | flops 4000000 | bytes 4000000 | tf_op jit(solution)/shard_map/pallas_call | solution.py:359
  100.5 1.0 copy.11
  (18 shorter events, 0.1 us)
Async XLA Ops:
  1.4 26.7 %collective-permute-start.4 = (f32[64,16,128]{2,1,0:T(8,128)S(1)}, f32[64,16,128]{2,1,0:T(8,128)S(1)}, u32[]{:S(2)}, u32[]{:S(2)}) collective-permute-start(f32[64,16,128]{2,1,0:T(8,128)S(1)} %bitcast.21), channel_id=1, source_target_pairs={{0,32},{32,64},{64,96},{96,128},{128,160},{160,192},{192,224},{224... | collective-permute-start | bytes 1572872 | tf_op jit(solution)/shard_map/ppermute | solution.py:64
  3.0 13.6 %collective-permute-start = (bf16[16,16,128]{2,1,0:T(8,128)(2,1)S(1)}, bf16[16,16,128]{2,1,0:T(8,128)(2,1)S(1)}, u32[]{:S(2)}, u32[]{:S(2)}) collective-permute-start(bf16[16,16,128]{2,1,0:T(8,128)(2,1)S(1)} %get-tuple-element.63), channel_id=1, source_target_pairs={{0,32},{1,33},{2,4},{3,5},{4,2},{5,3},{6,8},{7,9},{8,6},{9,7},{10,... | collective-permute-start | bytes 196616 | tf_op jit(solution)/shard_map/ppermute | solution.py:59
  9.3 7.3 %collective-permute-start.1 = (bf16[16,16,128]{2,1,0:T(8,128)(2,1)S(1)}, bf16[16,16,128]{2,1,0:T(8,128)(2,1)S(1)}, u32[]{:S(2)}, u32[]{:S(2)}) collective-permute-start(bf16[16,16,128]{2,1,0:T(8,128)(2,1)S(1)} %get-tuple-element.64), channel_id=1, source_target_pairs={{0,2},{1,3},{2,0},{3,1},{4,6},{5,7},{6,4},{7,5},{8,10},{9,11},{10,... | collective-permute-start | bytes 196616 | tf_op jit(solution)/shard_map/ppermute | solution.py:59
  10.8 7.0 %collective-permute-start.2 = (bf16[16,16,128]{2,1,0:T(8,128)(2,1)S(1)}, bf16[16,16,128]{2,1,0:T(8,128)(2,1)S(1)}, u32[]{:S(2)}, u32[]{:S(2)}) collective-permute-start(bf16[16,16,128]{2,1,0:T(8,128)(2,1)S(1)} %get-tuple-element.65), channel_id=1, source_target_pairs={{0,32},{1,2},{2,1},{3,4},{4,3},{5,6},{6,5},{7,8},{8,7},{9,10},{10,... | collective-permute-start | bytes 196616 | tf_op jit(solution)/shard_map/ppermute | solution.py:59
  10.8 7.0 %collective-permute-start.3 = (bf16[16,16,128]{2,1,0:T(8,128)(2,1)S(1)}, bf16[16,16,128]{2,1,0:T(8,128)(2,1)S(1)}, u32[]{:S(2)}, u32[]{:S(2)}) collective-permute-start(bf16[16,16,128]{2,1,0:T(8,128)(2,1)S(1)} %get-tuple-element.66), channel_id=1, source_target_pairs={{0,1},{1,0},{2,3},{3,2},{4,5},{5,4},{6,7},{7,6},{8,9},{9,8},{10,11... | collective-permute-start | bytes 196616 | tf_op jit(solution)/shard_map/ppermute | solution.py:59
  13.7 0.7 copy-start
  21.1 7.0 %collective-permute-start.5 = (bf16[64,16,128]{2,1,0:T(8,128)(2,1)S(1)}, bf16[64,16,128]{2,1,0:T(8,128)(2,1)S(1)}, u32[]{:S(2)}, u32[]{:S(2)}) collective-permute-start(bf16[64,16,128]{2,1,0:T(8,128)(2,1)S(1)} %get-tuple-element.71), channel_id=1, source_target_pairs={{0,32},{32,64},{64,96},{96,128},{128,160},{160,192},{192,224},{224... | collective-permute-start | bytes 786440 | tf_op jit(solution)/shard_map/ppermute | solution.py:64
  28.9 8.0 %collective-permute-start.6 = (bf16[16,16,128]{2,1,0:T(8,128)(2,1)S(1)}, bf16[16,16,128]{2,1,0:T(8,128)(2,1)S(1)}, u32[]{:S(2)}, u32[]{:S(2)}) collective-permute-start(bf16[16,16,128]{2,1,0:T(8,128)(2,1)S(1)} %get-tuple-element.75), channel_id=1, source_target_pairs={{0,32},{1,33},{2,4},{3,5},{4,2},{5,3},{6,8},{7,9},{8,6},{9,7},{10,... | collective-permute-start | bytes 196616 | tf_op jit(solution)/shard_map/ppermute | solution.py:59
  31.4 6.0 %collective-permute-start.7 = (bf16[16,16,128]{2,1,0:T(8,128)(2,1)S(1)}, bf16[16,16,128]{2,1,0:T(8,128)(2,1)S(1)}, u32[]{:S(2)}, u32[]{:S(2)}) collective-permute-start(bf16[16,16,128]{2,1,0:T(8,128)(2,1)S(1)} %get-tuple-element.76), channel_id=1, source_target_pairs={{0,2},{1,3},{2,0},{3,1},{4,6},{5,7},{6,4},{7,5},{8,10},{9,11},{10,... | collective-permute-start | bytes 196616 | tf_op jit(solution)/shard_map/ppermute | solution.py:59
  31.6 6.4 %collective-permute-start.8 = (bf16[16,16,128]{2,1,0:T(8,128)(2,1)S(1)}, bf16[16,16,128]{2,1,0:T(8,128)(2,1)S(1)}, u32[]{:S(2)}, u32[]{:S(2)}) collective-permute-start(bf16[16,16,128]{2,1,0:T(8,128)(2,1)S(1)} %get-tuple-element.77), channel_id=1, source_target_pairs={{0,32},{1,2},{2,1},{3,4},{4,3},{5,6},{6,5},{7,8},{8,7},{9,10},{10,... | collective-permute-start | bytes 196616 | tf_op jit(solution)/shard_map/ppermute | solution.py:59
  32.9 5.1 %collective-permute-start.9 = (bf16[16,16,128]{2,1,0:T(8,128)(2,1)S(1)}, bf16[16,16,128]{2,1,0:T(8,128)(2,1)S(1)}, u32[]{:S(2)}, u32[]{:S(2)}) collective-permute-start(bf16[16,16,128]{2,1,0:T(8,128)(2,1)S(1)} %get-tuple-element.78), channel_id=1, source_target_pairs={{0,1},{1,0},{2,3},{3,2},{4,5},{5,4},{6,7},{7,6},{8,9},{9,8},{10,11... | collective-permute-start | bytes 196616 | tf_op jit(solution)/shard_map/ppermute | solution.py:59
  40.8 8.4 %collective-permute-start.10 = (bf16[16,16,128]{2,1,0:T(8,128)(2,1)S(1)}, bf16[16,16,128]{2,1,0:T(8,128)(2,1)S(1)}, u32[]{:S(2)}, u32[]{:S(2)}) collective-permute-start(bf16[16,16,128]{2,1,0:T(8,128)(2,1)S(1)} %get-tuple-element.83), channel_id=1, source_target_pairs={{0,32},{1,33},{2,4},{3,5},{4,2},{5,3},{6,8},{7,9},{8,6},{9,7},{10,... | collective-permute-start | bytes 196616 | tf_op jit(solution)/shard_map/ppermute | solution.py:59
  43.0 6.2 %collective-permute-start.11 = (bf16[16,16,128]{2,1,0:T(8,128)(2,1)S(1)}, bf16[16,16,128]{2,1,0:T(8,128)(2,1)S(1)}, u32[]{:S(2)}, u32[]{:S(2)}) collective-permute-start(bf16[16,16,128]{2,1,0:T(8,128)(2,1)S(1)} %get-tuple-element.84), channel_id=1, source_target_pairs={{0,2},{1,3},{2,0},{3,1},{4,6},{5,7},{6,4},{7,5},{8,10},{9,11},{10,... | collective-permute-start | bytes 196616 | tf_op jit(solution)/shard_map/ppermute | solution.py:59
  45.4 6.4 %collective-permute-start.12 = (bf16[16,16,128]{2,1,0:T(8,128)(2,1)S(1)}, bf16[16,16,128]{2,1,0:T(8,128)(2,1)S(1)}, u32[]{:S(2)}, u32[]{:S(2)}) collective-permute-start(bf16[16,16,128]{2,1,0:T(8,128)(2,1)S(1)} %get-tuple-element.85), channel_id=1, source_target_pairs={{0,32},{1,2},{2,1},{3,4},{4,3},{5,6},{6,5},{7,8},{8,7},{9,10},{10,... | collective-permute-start | bytes 196616 | tf_op jit(solution)/shard_map/ppermute | solution.py:59
  47.6 4.3 %collective-permute-start.13 = (bf16[16,16,128]{2,1,0:T(8,128)(2,1)S(1)}, bf16[16,16,128]{2,1,0:T(8,128)(2,1)S(1)}, u32[]{:S(2)}, u32[]{:S(2)}) collective-permute-start(bf16[16,16,128]{2,1,0:T(8,128)(2,1)S(1)} %get-tuple-element.86), channel_id=1, source_target_pairs={{0,1},{1,0},{2,3},{3,2},{4,5},{5,4},{6,7},{7,6},{8,9},{9,8},{10,11... | collective-permute-start | bytes 196616 | tf_op jit(solution)/shard_map/ppermute | solution.py:59
  54.7 19.0 %collective-permute-start.14 = (f32[64,16,128]{2,1,0:T(8,128)S(1)}, f32[64,16,128]{2,1,0:T(8,128)S(1)}, u32[]{:S(2)}, u32[]{:S(2)}) collective-permute-start(f32[64,16,128]{2,1,0:T(8,128)S(1)} %get-tuple-element.88.u), channel_id=1, source_target_pairs={{0,32},{32,64},{64,96},{96,128},{128,160},{160,192},{192,224},{224... | collective-permute-start | bytes 1572872 | tf_op jit(solution)/shard_map/ppermute | solution.py:64
  54.7 8.6 %collective-permute-start.15 = (bf16[16,16,128]{2,1,0:T(8,128)(2,1)S(1)}, bf16[16,16,128]{2,1,0:T(8,128)(2,1)S(1)}, u32[]{:S(2)}, u32[]{:S(2)}) collective-permute-start(bf16[16,16,128]{2,1,0:T(8,128)(2,1)S(1)} %get-tuple-element.94), channel_id=1, source_target_pairs={{0,32},{1,33},{2,4},{3,5},{4,2},{5,3},{6,8},{7,9},{8,6},{9,7},{10,... | collective-permute-start | bytes 196616 | tf_op jit(solution)/shard_map/ppermute | solution.py:59
  56.2 7.1 %collective-permute-start.16 = (bf16[16,16,128]{2,1,0:T(8,128)(2,1)S(1)}, bf16[16,16,128]{2,1,0:T(8,128)(2,1)S(1)}, u32[]{:S(2)}, u32[]{:S(2)}) collective-permute-start(bf16[16,16,128]{2,1,0:T(8,128)(2,1)S(1)} %get-tuple-element.95), channel_id=1, source_target_pairs={{0,2},{1,3},{2,0},{3,1},{4,6},{5,7},{6,4},{7,5},{8,10},{9,11},{10,... | collective-permute-start | bytes 196616 | tf_op jit(solution)/shard_map/ppermute | solution.py:59
  57.4 6.5 %collective-permute-start.17 = (bf16[16,16,128]{2,1,0:T(8,128)(2,1)S(1)}, bf16[16,16,128]{2,1,0:T(8,128)(2,1)S(1)}, u32[]{:S(2)}, u32[]{:S(2)}) collective-permute-start(bf16[16,16,128]{2,1,0:T(8,128)(2,1)S(1)} %get-tuple-element.96), channel_id=1, source_target_pairs={{0,32},{1,2},{2,1},{3,4},{4,3},{5,6},{6,5},{7,8},{8,7},{9,10},{10,... | collective-permute-start | bytes 196616 | tf_op jit(solution)/shard_map/ppermute | solution.py:59
  59.6 4.4 %collective-permute-start.18 = (bf16[16,16,128]{2,1,0:T(8,128)(2,1)S(1)}, bf16[16,16,128]{2,1,0:T(8,128)(2,1)S(1)}, u32[]{:S(2)}, u32[]{:S(2)}) collective-permute-start(bf16[16,16,128]{2,1,0:T(8,128)(2,1)S(1)} %get-tuple-element.97), channel_id=1, source_target_pairs={{0,1},{1,0},{2,3},{3,2},{4,5},{5,4},{6,7},{7,6},{8,9},{9,8},{10,11... | collective-permute-start | bytes 196616 | tf_op jit(solution)/shard_map/ppermute | solution.py:59
  66.7 7.0 %collective-permute-start.19 = (bf16[64,16,128]{2,1,0:T(8,128)(2,1)S(1)}, bf16[64,16,128]{2,1,0:T(8,128)(2,1)S(1)}, u32[]{:S(2)}, u32[]{:S(2)}) collective-permute-start(bf16[64,16,128]{2,1,0:T(8,128)(2,1)S(1)} %get-tuple-element.99), channel_id=1, source_target_pairs={{0,32},{32,64},{64,96},{96,128},{128,160},{160,192},{192,224},{224... | collective-permute-start | bytes 786440 | tf_op jit(solution)/shard_map/ppermute | solution.py:64
  74.5 8.7 %collective-permute-start.20 = (bf16[16,16,128]{2,1,0:T(8,128)(2,1)S(1)}, bf16[16,16,128]{2,1,0:T(8,128)(2,1)S(1)}, u32[]{:S(2)}, u32[]{:S(2)}) collective-permute-start(bf16[16,16,128]{2,1,0:T(8,128)(2,1)S(1)} %get-tuple-element.104), channel_id=1, source_target_pairs={{0,32},{1,33},{2,4},{3,5},{4,2},{5,3},{6,8},{7,9},{8,6},{9,7},{10,... | collective-permute-start | bytes 196616 | tf_op jit(solution)/shard_map/ppermute | solution.py:59
  76.7 6.5 %collective-permute-start.21 = (bf16[16,16,128]{2,1,0:T(8,128)(2,1)S(1)}, bf16[16,16,128]{2,1,0:T(8,128)(2,1)S(1)}, u32[]{:S(2)}, u32[]{:S(2)}) collective-permute-start(bf16[16,16,128]{2,1,0:T(8,128)(2,1)S(1)} %get-tuple-element.105), channel_id=1, source_target_pairs={{0,2},{1,3},{2,0},{3,1},{4,6},{5,7},{6,4},{7,5},{8,10},{9,11},{10,... | collective-permute-start | bytes 196616 | tf_op jit(solution)/shard_map/ppermute | solution.py:59
  79.0 6.4 %collective-permute-start.22 = (bf16[16,16,128]{2,1,0:T(8,128)(2,1)S(1)}, bf16[16,16,128]{2,1,0:T(8,128)(2,1)S(1)}, u32[]{:S(2)}, u32[]{:S(2)}) collective-permute-start(bf16[16,16,128]{2,1,0:T(8,128)(2,1)S(1)} %get-tuple-element.106), channel_id=1, source_target_pairs={{0,32},{1,2},{2,1},{3,4},{4,3},{5,6},{6,5},{7,8},{8,7},{9,10},{10,... | collective-permute-start | bytes 196616 | tf_op jit(solution)/shard_map/ppermute | solution.py:59
  81.2 4.3 %collective-permute-start.23 = (bf16[16,16,128]{2,1,0:T(8,128)(2,1)S(1)}, bf16[16,16,128]{2,1,0:T(8,128)(2,1)S(1)}, u32[]{:S(2)}, u32[]{:S(2)}) collective-permute-start(bf16[16,16,128]{2,1,0:T(8,128)(2,1)S(1)} %get-tuple-element.107), channel_id=1, source_target_pairs={{0,1},{1,0},{2,3},{3,2},{4,5},{5,4},{6,7},{7,6},{8,9},{9,8},{10,11... | collective-permute-start | bytes 196616 | tf_op jit(solution)/shard_map/ppermute | solution.py:59
  88.2 7.4 %collective-permute-start.24 = (bf16[16,16,128]{2,1,0:T(8,128)(2,1)S(1)}, bf16[16,16,128]{2,1,0:T(8,128)(2,1)S(1)}, u32[]{:S(2)}, u32[]{:S(2)}) collective-permute-start(bf16[16,16,128]{2,1,0:T(8,128)(2,1)S(1)} %get-tuple-element.112), channel_id=1, source_target_pairs={{0,32},{1,33},{2,4},{3,5},{4,2},{5,3},{6,8},{7,9},{8,6},{9,7},{10,... | collective-permute-start | bytes 196616 | tf_op jit(solution)/shard_map/ppermute | solution.py:59
  89.8 5.8 %collective-permute-start.25 = (bf16[16,16,128]{2,1,0:T(8,128)(2,1)S(1)}, bf16[16,16,128]{2,1,0:T(8,128)(2,1)S(1)}, u32[]{:S(2)}, u32[]{:S(2)}) collective-permute-start(bf16[16,16,128]{2,1,0:T(8,128)(2,1)S(1)} %get-tuple-element.113), channel_id=1, source_target_pairs={{0,2},{1,3},{2,0},{3,1},{4,6},{5,7},{6,4},{7,5},{8,10},{9,11},{10,... | collective-permute-start | bytes 196616 | tf_op jit(solution)/shard_map/ppermute | solution.py:59
  91.4 6.4 %collective-permute-start.26 = (bf16[16,16,128]{2,1,0:T(8,128)(2,1)S(1)}, bf16[16,16,128]{2,1,0:T(8,128)(2,1)S(1)}, u32[]{:S(2)}, u32[]{:S(2)}) collective-permute-start(bf16[16,16,128]{2,1,0:T(8,128)(2,1)S(1)} %get-tuple-element.114), channel_id=1, source_target_pairs={{0,32},{1,2},{2,1},{3,4},{4,3},{5,6},{6,5},{7,8},{8,7},{9,10},{10,... | collective-permute-start | bytes 196616 | tf_op jit(solution)/shard_map/ppermute | solution.py:59
  93.2 4.6 %collective-permute-start.27 = (bf16[16,16,128]{2,1,0:T(8,128)(2,1)S(1)}, bf16[16,16,128]{2,1,0:T(8,128)(2,1)S(1)}, u32[]{:S(2)}, u32[]{:S(2)}) collective-permute-start(bf16[16,16,128]{2,1,0:T(8,128)(2,1)S(1)} %get-tuple-element.115), channel_id=1, source_target_pairs={{0,1},{1,0},{2,3},{3,2},{4,5},{5,4},{6,7},{7,6},{8,9},{9,8},{10,11... | collective-permute-start | bytes 196616 | tf_op jit(solution)/shard_map/ppermute | solution.py:59

commit v8 on v7

--- a/solution.py
+++ b/solution.py
@@ -95,9 +95,15 @@
             out[j] = vb[flags[first + j]]
 
 
-def first_kernel(flags, u, vb, *packs):
-    nblocks = u.shape[0]
-    vb[0:nblocks] = u[...].astype(bf16)
+def first_kernel(flags, guess, u, vb, *packs):
+    nblocks, species, _ = u.shape
+
+    def body(b):
+        field = guess[pl.ds(b, species, stride=nblocks), :]
+        u[b] = field
+        vb[b] = field.astype(bf16)
+
+    per_block(nblocks, body)
     vb[nblocks] = jnp.zeros(vb.shape[1:], bf16)
     pack(flags, vb, packs)
 
@@ -342,8 +348,7 @@
 
 
 def per_device(guess, coeffs, coef_index, neighbours, send_lists, mixing):
-    first = jnp.transpose(guess[0], (1, 0, 2))
-    nblocks, species, cells = first.shape
+    species, nblocks, cells = guess.shape[1:]
     slots = send_lists.shape[1]
     rows = jnp.where(send_lists < 0, nblocks, send_lists)
     flags = jnp.concatenate([plan(), rows.reshape(-1)])
@@ -390,7 +395,9 @@
         return call(kernel, outs, (flags, terms), (vb, part, *received, coeffs, *base), ext)
 
     h, gaps = step_size, node_gaps
-    vb, *packs = call(first_kernel, [rounded] + rims, (flags,), (first,))
+    first, vb, *packs = call(
+        first_kernel, [state, rounded] + rims, (flags,), (guess.reshape(species * nblocks, cells),)
+    )
     received = exchange(packs)
     split = jax.ShapeDtypeStruct((species, 3 * species), bf16)
     part, mix, coeffs = pl.pallas_call(

time: 102 us -> 102 us (level)
    unnamed x3 -> x4, local copies, waits for them, and re-layouts: 2.04 us -> 1.73 us
  transfers between devices with their start and end apart: 28 -> 28, of which waited for: 12 -> 12; matrix products, arithmetic and copies ran while one was open for 2% -> 1% of each run, Pallas kernels for 21% -> 20%
where the time goes in v8:
time: 102 us; the launch traced here: 101 us
  starting transfers between devices  39 us (38%)
  Pallas kernels  34.1 us (33%)
  waiting for transfers between devices  23.6 us (23%)
  local copies, waits for them, and re-layouts  3.1 us (3%)
  other arithmetic  1.39 us (1%)
    ppermute x24, starting transfers between devices, swap(): return lax.ppermute(block, ('tm', 'space'), route)  38.9 us
    pallas_call x14, Pallas kernels, call(): pl.pallas_call(kernel, out_shape=outs, in_specs=[SMEM] * len(scalars) + [...  28.5 us
    ppermute x24, waiting for transfers between devices, swap(): return lax.ppermute(block, ('tm', 'space'), route)  13 us
    ppermute x4, waiting for transfers between devices, next_slice(): return lax.ppermute(block, 'tm', [(i, (i + 1) % n) for i in range(n)])  10.6 us
    pallas_call x1, Pallas kernels, per_device(): pl.pallas_call(table_kernel, out_shape=[jax.ShapeDtypeStruct((nblocks * W...  3.32 us
    pallas_call x1, Pallas kernels, per_device(): pl.pallas_call(first_reaction_kernel, out_shape=[state, split, jax.ShapeD...  2.2 us
  transfers between devices with their start and end apart: 28, of which 12 were waited for; matrix products, arithmetic and copies ran while one was open for 1% of the time, Pallas kernels for 20%

profile of v8, /device:TPU:8, one launch (start us, length us, event | category | flops | bytes accessed | tf_op | source)
XLA Modules:
  0.0 101.5 jit_solution(4247322906454378389)
XLA Ops:
  0.0 0.7 compare_select_fusion
  0.7 0.1 reshape.9
  0.8 0.1 concatenate.6.flags
  0.9 0.0 copy-start
  0.9 1.0 %copy-done = f32[1,16,64,128]{3,2,1,0:T(8,128)S(1)} copy-done((f32[1,16,64,128]{3,2,1,0:T(8,128)S(1)}, f32[1,16,64,128]{3,2,1,0:T(8,128)}, u32[]{:S(2)}) %copy-start) | copy-done | bytes 524312
  1.9 0.9 shard_map.64
  2.8 0.0 collective-permute-start.4
  2.9 6.3 %collective-permute-start = (bf16[16,16,128]{2,1,0:T(8,128)(2,1)S(1)}, bf16[16,16,128]{2,1,0:T(8,128)(2,1)S(1)}, u32[]{:S(2)}, u32[]{:S(2)}) collective-permute-start(bf16[16,16,128]{2,1,0:T(8,128)(2,1)S(1)} %get-tuple-element.65), channel_id=1, source_target_pairs={{0,32},{1,33},{2,4},{3,5},{4,2},{5,3},{6,8},{7,9},{8,6},{9,7},{10,... | collective-permute-start | bytes 196616 | tf_op jit(solution)/shard_map/ppermute | solution.py:59
  9.1 1.6 %collective-permute-start.1 = (bf16[16,16,128]{2,1,0:T(8,128)(2,1)S(1)}, bf16[16,16,128]{2,1,0:T(8,128)(2,1)S(1)}, u32[]{:S(2)}, u32[]{:S(2)}) collective-permute-start(bf16[16,16,128]{2,1,0:T(8,128)(2,1)S(1)} %get-tuple-element.66), channel_id=1, source_target_pairs={{0,2},{1,3},{2,0},{3,1},{4,6},{5,7},{6,4},{7,5},{8,10},{9,11},{10,... | collective-permute-start | bytes 196616 | tf_op jit(solution)/shard_map/ppermute | solution.py:59
  10.7 1.9 %collective-permute-start.3 = (bf16[16,16,128]{2,1,0:T(8,128)(2,1)S(1)}, bf16[16,16,128]{2,1,0:T(8,128)(2,1)S(1)}, u32[]{:S(2)}, u32[]{:S(2)}) collective-permute-start(bf16[16,16,128]{2,1,0:T(8,128)(2,1)S(1)} %get-tuple-element.68), channel_id=1, source_target_pairs={{0,1},{1,0},{2,3},{3,2},{4,5},{5,4},{6,7},{7,6},{8,9},{9,8},{10,11... | collective-permute-start | bytes 196616 | tf_op jit(solution)/shard_map/ppermute | solution.py:59
  12.6 0.7 pad_add_fusion
  13.3 0.1 copy.8
  13.4 0.1 reshape.10.table.given
  13.6 0.7 copy-done.1
  14.3 2.2 %shard_map.65 = (f32[64,16,128]{2,1,0:T(8,128)S(1)}, bf16[16,48]{1,0:T(8,128)(2,1)S(1)}, bf16[128,128,128]{2,1,0:T(8,128)(2,1)S(1)}) custom-call(f32[64,16,128]{2,1,0:T(8,128)S(1)} %get-tuple-element.63.u.refs_0_, f32[16,16]{1,0:T(8,128)S(1)} %copy-done.1, bf16[128,128,128]{2,1,0:T(8,128)(2,1)} %coeffs.1), custom_call_target="tpu_custom_call" | custom-call | flops 4000000 | bytes 4000000 | tf_op jit(solution)/shard_map/pallas_call | solution.py:403
  16.5 1.3 %collective-permute-done.2.refs_2_ = bf16[16,16,128]{2,1,0:T(8,128)(2,1)S(1)} collective-permute-done((bf16[16,16,128]{2,1,0:T(8,128)(2,1)S(1)}, bf16[16,16,128]{2,1,0:T(8,128)(2,1)S(1)}, u32[]{:S(2)}, u32[]{:S(2)}) %collective-permute-start.2) | collective-permute-done | bytes 65568 | tf_op jit(solution)/shard_map/ppermute | solution.py:59
  17.8 3.2 %shard_map.66 = (f32[64,16,128]{2,1,0:T(8,128)S(1)}, bf16[64,16,128]{2,1,0:T(8,128)(2,1)S(1)}) custom-call(s32[77]{0:T(128)S(1)} %concatenate.6.flags, s32[960]{0:T(1024)S(1)} %reshape.10.table.given, bf16[65,16,128]{2,1,0:T(8,128)(2,1)S(1)} %get-tuple-element.62.vb, f32[64,16,128]{2,1,0:T(8,128)S(1)} %get-tuple-element.64.part, ...), custom_call_target="tpu_custom_call" | custom-call | flops 4000000 | bytes 4000000 | tf_op jit(solution)/shard_map/pallas_call | solution.py:364
  21.0 0.1 collective-permute-start.5
  21.1 3.3 %shard_map.67 = (s32[1025]{0:T(1024)S(1)}, f32[8,128]{1,0:T(8,128)S(1)}) custom-call(s32[960]{0:T(1024)S(1)} %reshape.10.table.given, f32[64,16,128]{2,1,0:T(8,128)S(1)} %get-tuple-element.70.after.refs_2_.refs_4_.refs_0_), custom_call_target="tpu_custom_call" | custom-call | flops 1000000 | bytes 1000000 | tf_op jit(solution)/shard_map/pallas_call | solution.py:413
  24.4 3.6 %collective-permute-done.5.refs_3_ = bf16[64,16,128]{2,1,0:T(8,128)(2,1)S(1)} collective-permute-done((bf16[64,16,128]{2,1,0:T(8,128)(2,1)S(1)}, bf16[64,16,128]{2,1,0:T(8,128)(2,1)S(1)}, u32[]{:S(2)}, u32[]{:S(2)}) %collective-permute-start.5) | collective-permute-done | bytes 262176 | tf_op jit(solution)/shard_map/ppermute | solution.py:64
  28.0 0.8 shard_map.69
  28.8 2.5 %collective-permute-start.6 = (bf16[16,16,128]{2,1,0:T(8,128)(2,1)S(1)}, bf16[16,16,128]{2,1,0:T(8,128)(2,1)S(1)}, u32[]{:S(2)}, u32[]{:S(2)}) collective-permute-start(bf16[16,16,128]{2,1,0:T(8,128)(2,1)S(1)} %get-tuple-element.77), channel_id=1, source_target_pairs={{0,32},{1,33},{2,4},{3,5},{4,2},{5,3},{6,8},{7,9},{8,6},{9,7},{10,... | collective-permute-start | bytes 196616 | tf_op jit(solution)/shard_map/ppermute | solution.py:59
  31.3 0.2 collective-permute-start.7
  31.5 1.3 %collective-permute-start.8 = (bf16[16,16,128]{2,1,0:T(8,128)(2,1)S(1)}, bf16[16,16,128]{2,1,0:T(8,128)(2,1)S(1)}, u32[]{:S(2)}, u32[]{:S(2)}) collective-permute-start(bf16[16,16,128]{2,1,0:T(8,128)(2,1)S(1)} %get-tuple-element.79), channel_id=1, source_target_pairs={{0,32},{1,2},{2,1},{3,4},{4,3},{5,6},{6,5},{7,8},{8,7},{9,10},{10,... | collective-permute-start | bytes 196616 | tf_op jit(solution)/shard_map/ppermute | solution.py:59
  32.8 2.0 %collective-permute-start.9 = (bf16[16,16,128]{2,1,0:T(8,128)(2,1)S(1)}, bf16[16,16,128]{2,1,0:T(8,128)(2,1)S(1)}, u32[]{:S(2)}, u32[]{:S(2)}) collective-permute-start(bf16[16,16,128]{2,1,0:T(8,128)(2,1)S(1)} %get-tuple-element.80), channel_id=1, source_target_pairs={{0,1},{1,0},{2,3},{3,2},{4,5},{5,4},{6,7},{7,6},{8,9},{9,8},{10,11... | collective-permute-start | bytes 196616 | tf_op jit(solution)/shard_map/ppermute | solution.py:59
  34.8 2.0 %shard_map.68 = (f32[64,16,128]{2,1,0:T(8,128)S(1)}, f32[64,16,128]{2,1,0:T(8,128)S(1)}, bf16[65,16,128]{2,1,0:T(8,128)(2,1)S(1)}, f32[64,16,128]{2,1,0:T(8,128)S(1)}) custom-call(s32[77]{0:T(128)S(1)} %concatenate.6.flags, s32[1025]{0:T(1024)S(1)} %get-tuple-element.71.table, bf16[16,48]{1,0:T(8,128)(2,1)S(1)} %get-tuple-element.72.mix, ...), custom_call_target="tpu_custom_call" | custom-call | flops 4000000 | bytes 4000000 | tf_op jit(solution)/shard_map/pallas_call | solution.py:364
  36.8 0.0 collective-permute-done.6.refs_0_
  36.8 0.5 collective-permute-done.7.refs_1_
  37.3 0.6 collective-permute-done.8.refs_2_
  37.9 2.8 %shard_map.70 = (f32[64,16,128]{2,1,0:T(8,128)S(1)}, f32[64,16,128]{2,1,0:T(8,128)S(1)}, bf16[65,16,128]{2,1,0:T(8,128)(2,1)S(1)}, bf16[16,16,128]{2,1,0:T(8,128...) custom-call(s32[77]{0:T(128)S(1)} %concatenate.6.flags, ...), custom_call_target="tpu_custom_call" | custom-call | flops 4000000 | bytes 4000000 | tf_op jit(solution)/shard_map/pallas_call | solution.py:364
  40.7 2.3 %collective-permute-start.10 = (bf16[16,16,128]{2,1,0:T(8,128)(2,1)S(1)}, bf16[16,16,128]{2,1,0:T(8,128)(2,1)S(1)}, u32[]{:S(2)}, u32[]{:S(2)}) collective-permute-start(bf16[16,16,128]{2,1,0:T(8,128)(2,1)S(1)} %get-tuple-element.85), channel_id=1, source_target_pairs={{0,32},{1,33},{2,4},{3,5},{4,2},{5,3},{6,8},{7,9},{8,6},{9,7},{10,... | collective-permute-start | bytes 196616 | tf_op jit(solution)/shard_map/ppermute | solution.py:59
  43.0 2.4 %collective-permute-start.11 = (bf16[16,16,128]{2,1,0:T(8,128)(2,1)S(1)}, bf16[16,16,128]{2,1,0:T(8,128)(2,1)S(1)}, u32[]{:S(2)}, u32[]{:S(2)}) collective-permute-start(bf16[16,16,128]{2,1,0:T(8,128)(2,1)S(1)} %get-tuple-element.86), channel_id=1, source_target_pairs={{0,2},{1,3},{2,0},{3,1},{4,6},{5,7},{6,4},{7,5},{8,10},{9,11},{10,... | collective-permute-start | bytes 196616 | tf_op jit(solution)/shard_map/ppermute | solution.py:59
  45.5 1.8 %collective-permute-start.12 = (bf16[16,16,128]{2,1,0:T(8,128)(2,1)S(1)}, bf16[16,16,128]{2,1,0:T(8,128)(2,1)S(1)}, u32[]{:S(2)}, u32[]{:S(2)}) collective-permute-start(bf16[16,16,128]{2,1,0:T(8,128)(2,1)S(1)} %get-tuple-element.87), channel_id=1, source_target_pairs={{0,32},{1,2},{2,1},{3,4},{4,3},{5,6},{6,5},{7,8},{8,7},{9,10},{10,... | collective-permute-start | bytes 196616 | tf_op jit(solution)/shard_map/ppermute | solution.py:59
  47.2 1.6 %shard_map.71 = (f32[64,16,128]{2,1,0:T(8,128)S(1)}, f32[64,16,128]{2,1,0:T(8,128)S(1)}) custom-call(s32[1025]{0:T(1024)S(1)} %get-tuple-element.71.table, f32[64,16,128]{2,1,0:T(8,128)S(1)} %get-tuple-element.83.u, bf16[65,16,128]{2,1,0:T(8,128)(2,1)S(1)} %get-tuple-element.82.vb, bf16[16,48]{1,0:T(8,128)(2,1)S(1)} %get-tuple-element.72.mix, ...), custom_call_target="tpu_custom_call" | custom-call | flops 4000000 | bytes 4000000 | tf_op jit(solution)/shard_map/pallas_call | solution.py:364
  48.9 3.0 %collective-permute-done.12.refs_2_ = bf16[16,16,128]{2,1,0:T(8,128)(2,1)S(1)} collective-permute-done((bf16[16,16,128]{2,1,0:T(8,128)(2,1)S(1)}, bf16[16,16,128]{2,1,0:T(8,128)(2,1)S(1)}, u32[]{:S(2)}, u32[]{:S(2)}) %collective-permute-start.12) | collective-permute-done | bytes 65568 | tf_op jit(solution)/shard_map/ppermute | solution.py:59
  51.8 2.8 %shard_map.72 = (f32[64,16,128]{2,1,0:T(8,128)S(1)}, f32[64,16,128]{2,1,0:T(8,128)S(1)}, bf16[65,16,128]{2,1,0:T(8,128)(2,1)S(1)}, bf16[16,16,128]{2,1,0:T(8,128...) custom-call(s32[77]{0:T(128)S(1)} %concatenate.6.flags, ...), custom_call_target="tpu_custom_call" | custom-call | flops 4000000 | bytes 4000000 | tf_op jit(solution)/shard_map/pallas_call | solution.py:364
  54.7 0.0 collective-permute-start.14
  54.7 1.7 %collective-permute-start.15 = (bf16[16,16,128]{2,1,0:T(8,128)(2,1)S(1)}, bf16[16,16,128]{2,1,0:T(8,128)(2,1)S(1)}, u32[]{:S(2)}, u32[]{:S(2)}) collective-permute-start(bf16[16,16,128]{2,1,0:T(8,128)(2,1)S(1)} %get-tuple-element.96), channel_id=1, source_target_pairs={{0,32},{1,33},{2,4},{3,5},{4,2},{5,3},{6,8},{7,9},{8,6},{9,7},{10,... | collective-permute-start | bytes 196616 | tf_op jit(solution)/shard_map/ppermute | solution.py:59
  56.4 1.2 %collective-permute-start.16 = (bf16[16,16,128]{2,1,0:T(8,128)(2,1)S(1)}, bf16[16,16,128]{2,1,0:T(8,128)(2,1)S(1)}, u32[]{:S(2)}, u32[]{:S(2)}) collective-permute-start(bf16[16,16,128]{2,1,0:T(8,128)(2,1)S(1)} %get-tuple-element.97), channel_id=1, source_target_pairs={{0,2},{1,3},{2,0},{3,1},{4,6},{5,7},{6,4},{7,5},{8,10},{9,11},{10,... | collective-permute-start | bytes 196616 | tf_op jit(solution)/shard_map/ppermute | solution.py:59
  57.6 1.6 %collective-permute-start.17 = (bf16[16,16,128]{2,1,0:T(8,128)(2,1)S(1)}, bf16[16,16,128]{2,1,0:T(8,128)(2,1)S(1)}, u32[]{:S(2)}, u32[]{:S(2)}) collective-permute-start(bf16[16,16,128]{2,1,0:T(8,128)(2,1)S(1)} %get-tuple-element.98), channel_id=1, source_target_pairs={{0,32},{1,2},{2,1},{3,4},{4,3},{5,6},{6,5},{7,8},{8,7},{9,10},{10,... | collective-permute-start | bytes 196616 | tf_op jit(solution)/shard_map/ppermute | solution.py:59
  59.2 0.7 collective-permute-start.18
  59.9 1.7 %shard_map.73 = (f32[64,16,128]{2,1,0:T(8,128)S(1)}, f32[64,16,128]{2,1,0:T(8,128)S(1)}) custom-call(s32[1025]{0:T(1024)S(1)} %get-tuple-element.71.table, f32[64,16,128]{2,1,0:T(8,128)S(1)} %get-tuple-element.90.u, bf16[65,16,128]{2,1,0:T(8,128)(2,1)S(1)} %get-tuple-element.92.vb, bf16[16,48]{1,0:T(8,128)(2,1)S(1)} %get-tuple-element.72.mix, ...), custom_call_target="tpu_custom_call" | custom-call | flops 4000000 | bytes 4000000 | tf_op jit(solution)/shard_map/pallas_call | solution.py:364
  61.5 1.6 %collective-permute-done.15.refs_0_ = bf16[16,16,128]{2,1,0:T(8,128)(2,1)S(1)} collective-permute-done((bf16[16,16,128]{2,1,0:T(8,128)(2,1)S(1)}, bf16[16,16,128]{2,1,0:T(8,128)(2,1)S(1)}, u32[]{:S(2)}, u32[]{:S(2)}) %collective-permute-start.15) | collective-permute-done | bytes 65568 | tf_op jit(solution)/shard_map/ppermute | solution.py:59
  63.1 0.4 collective-permute-done.16.refs_1_
  63.5 0.5 collective-permute-done.17.refs_2_
  64.0 2.7 %shard_map.74 = (f32[64,16,128]{2,1,0:T(8,128)S(1)}, bf16[64,16,128]{2,1,0:T(8,128)(2,1)S(1)}, f32[64,16,128]{2,1,0:T(8,128)S(1)}) custom-call(s32[77]{0:T(128)S(1)} %concatenate.6.flags, s32[1025]{0:T(1024)S(1)} %get-tuple-element.71.table, bf16[65,16,128]{2,1,0:T(8,128)(2,1)S(1)} %get-tuple-element.92.vb, f32[64,16,128]{2,1,0:T(8,128)S(1)} %get-tuple-element.95.part, ...), custom_call_target="tpu_custom_call" | custom-call | flops 4000000 | bytes 4000000 | tf_op jit(solution)/shard_map/pallas_call | solution.py:364
  66.8 0.0 collective-permute-start.19
  66.8 7.0 %collective-permute-done.19.refs_3_ = bf16[64,16,128]{2,1,0:T(8,128)(2,1)S(1)} collective-permute-done((bf16[64,16,128]{2,1,0:T(8,128)(2,1)S(1)}, bf16[64,16,128]{2,1,0:T(8,128)(2,1)S(1)}, u32[]{:S(2)}, u32[]{:S(2)}) %collective-permute-start.19) | collective-permute-done | bytes 262176 | tf_op jit(solution)/shard_map/ppermute | solution.py:64
  73.8 0.8 shard_map.76
  74.6 2.3 %collective-permute-start.20 = (bf16[16,16,128]{2,1,0:T(8,128)(2,1)S(1)}, bf16[16,16,128]{2,1,0:T(8,128)(2,1)S(1)}, u32[]{:S(2)}, u32[]{:S(2)}) collective-permute-start(bf16[16,16,128]{2,1,0:T(8,128)(2,1)S(1)} %get-tuple-element.106), channel_id=1, source_target_pairs={{0,32},{1,33},{2,4},{3,5},{4,2},{5,3},{6,8},{7,9},{8,6},{9,7},{10,... | collective-permute-start | bytes 196616 | tf_op jit(solution)/shard_map/ppermute | solution.py:59
  76.9 2.1 %collective-permute-start.21 = (bf16[16,16,128]{2,1,0:T(8,128)(2,1)S(1)}, bf16[16,16,128]{2,1,0:T(8,128)(2,1)S(1)}, u32[]{:S(2)}, u32[]{:S(2)}) collective-permute-start(bf16[16,16,128]{2,1,0:T(8,128)(2,1)S(1)} %get-tuple-element.107), channel_id=1, source_target_pairs={{0,2},{1,3},{2,0},{3,1},{4,6},{5,7},{6,4},{7,5},{8,10},{9,11},{10,... | collective-permute-start | bytes 196616 | tf_op jit(solution)/shard_map/ppermute | solution.py:59
  79.0 1.8 %collective-permute-start.22 = (bf16[16,16,128]{2,1,0:T(8,128)(2,1)S(1)}, bf16[16,16,128]{2,1,0:T(8,128)(2,1)S(1)}, u32[]{:S(2)}, u32[]{:S(2)}) collective-permute-start(bf16[16,16,128]{2,1,0:T(8,128)(2,1)S(1)} %get-tuple-element.108), channel_id=1, source_target_pairs={{0,32},{1,2},{2,1},{3,4},{4,3},{5,6},{6,5},{7,8},{8,7},{9,10},{10,... | collective-permute-start | bytes 196616 | tf_op jit(solution)/shard_map/ppermute | solution.py:59
  80.9 2.1 %shard_map.75 = (f32[64,16,128]{2,1,0:T(8,128)S(1)}, f32[64,16,128]{2,1,0:T(8,128)S(1)}, bf16[65,16,128]{2,1,0:T(8,128)(2,1)S(1)}) custom-call(s32[77]{0:T(128)S(1)} %concatenate.6.flags, s32[1025]{0:T(1024)S(1)} %get-tuple-element.71.table, bf16[16,48]{1,0:T(8,128)(2,1)S(1)} %get-tuple-element.72.mix, ...), custom_call_target="tpu_custom_call" | custom-call | flops 4000000 | bytes 4000000 | tf_op jit(solution)/shard_map/pallas_call | solution.py:364
  83.0 2.4 %collective-permute-done.22.refs_2_ = bf16[16,16,128]{2,1,0:T(8,128)(2,1)S(1)} collective-permute-done((bf16[16,16,128]{2,1,0:T(8,128)(2,1)S(1)}, bf16[16,16,128]{2,1,0:T(8,128)(2,1)S(1)}, u32[]{:S(2)}, u32[]{:S(2)}) %collective-permute-start.22) | collective-permute-done | bytes 65568 | tf_op jit(solution)/shard_map/ppermute | solution.py:59
  85.4 2.8 %shard_map.77 = (f32[64,16,128]{2,1,0:T(8,128)S(1)}, bf16[65,16,128]{2,1,0:T(8,128)(2,1)S(1)}, bf16[16,16,128]{2,1,0:T(8,128)(2,1)S(1)}, bf16[16,16,128]{2,1,0:T...) custom-call(s32[77]{0:T(128)S(1)} %concatenate.6.flags, ...), custom_call_target="tpu_custom_call" | custom-call | flops 4000000 | bytes 4000000 | tf_op jit(solution)/shard_map/pallas_call | solution.py:364
  88.2 1.7 %collective-permute-start.24 = (bf16[16,16,128]{2,1,0:T(8,128)(2,1)S(1)}, bf16[16,16,128]{2,1,0:T(8,128)(2,1)S(1)}, u32[]{:S(2)}, u32[]{:S(2)}) collective-permute-start(bf16[16,16,128]{2,1,0:T(8,128)(2,1)S(1)} %get-tuple-element.114), channel_id=1, source_target_pairs={{0,32},{1,33},{2,4},{3,5},{4,2},{5,3},{6,8},{7,9},{8,6},{9,7},{10,... | collective-permute-start | bytes 196616 | tf_op jit(solution)/shard_map/ppermute | solution.py:59
  89.9 1.5 %collective-permute-start.25 = (bf16[16,16,128]{2,1,0:T(8,128)(2,1)S(1)}, bf16[16,16,128]{2,1,0:T(8,128)(2,1)S(1)}, u32[]{:S(2)}, u32[]{:S(2)}) collective-permute-start(bf16[16,16,128]{2,1,0:T(8,128)(2,1)S(1)} %get-tuple-element.115), channel_id=1, source_target_pairs={{0,2},{1,3},{2,0},{3,1},{4,6},{5,7},{6,4},{7,5},{8,10},{9,11},{10,... | collective-permute-start | bytes 196616 | tf_op jit(solution)/shard_map/ppermute | solution.py:59
  91.4 1.6 %collective-permute-start.26 = (bf16[16,16,128]{2,1,0:T(8,128)(2,1)S(1)}, bf16[16,16,128]{2,1,0:T(8,128)(2,1)S(1)}, u32[]{:S(2)}, u32[]{:S(2)}) collective-permute-start(bf16[16,16,128]{2,1,0:T(8,128)(2,1)S(1)} %get-tuple-element.116), channel_id=1, source_target_pairs={{0,32},{1,2},{2,1},{3,4},{4,3},{5,6},{6,5},{7,8},{8,7},{9,10},{10,... | collective-permute-start | bytes 196616 | tf_op jit(solution)/shard_map/ppermute | solution.py:59
  93.0 0.3 collective-permute-start.27
  93.4 1.7 %shard_map.78 = (f32[64,16,128]{2,1,0:T(8,128)S(1)}, f32[64,16,128]{2,1,0:T(8,128)S(1)}) custom-call(s32[1025]{0:T(1024)S(1)} %get-tuple-element.71.table, f32[64,16,128]{2,1,0:T(8,128)S(1)} %get-tuple-element.112.u, bf16[65,16,128]{2,1,0:T(8,128)(2,1)S(1)} %get-tuple-element.111.vb, bf16[16,48]{1,0:T(8,128)(2,1)S(1)} %get-tuple-element.72.mix, ...), custom_call_target="tpu_custom_call" | custom-call | flops 4000000 | bytes 4000000 | tf_op jit(solution)/shard_map/pallas_call | solution.py:364
  95.1 0.5 collective-permute-done.24.refs_0_
  95.6 2.2 %collective-permute-done.26.refs_2_ = bf16[16,16,128]{2,1,0:T(8,128)(2,1)S(1)} collective-permute-done((bf16[16,16,128]{2,1,0:T(8,128)(2,1)S(1)}, bf16[16,16,128]{2,1,0:T(8,128)(2,1)S(1)}, u32[]{:S(2)}, u32[]{:S(2)}) %collective-permute-start.26) | collective-permute-done | bytes 65568 | tf_op jit(solution)/shard_map/ppermute | solution.py:59
  97.8 2.7 %shard_map.79 = f32[64,16,128]{2,1,0:T(8,128)S(1)} custom-call(s32[77]{0:T(128)S(1)} %concatenate.6.flags, s32[1025]{0:T(1024)S(1)} %get-tuple-element.71.table, bf16[65,16,128]{2,1,0:T(8,128)(2,1)S(1)} %get-tuple-element.111.vb, f32[64,16,128]{2,1,0:T(8,128)S(1)} %get-tuple-element.113.part, bf16[16,16,128]{2,1,0:T(8,128)(2,1)S(1)} %collective-permute-done.24.refs_0_, ...), custom_call_target="tpu_custom_call" | custom-call | flops 4000000 | bytes 4000000 | tf_op jit(solution)/shard_map/pallas_call | solution.py:364
  100.5 1.0 copy.9
  (19 shorter events, 0.1 us)
Async XLA Ops:
  0.9 1.0 %copy-start = (f32[1,16,64,128]{3,2,1,0:T(8,128)S(1)}, f32[1,16,64,128]{3,2,1,0:T(8,128)}, u32[]{:S(2)}) copy-start(f32[1,16,64,128]{3,2,1,0:T(8,128)} %param.6) | copy-start | bytes 1572868
  2.8 25.1 %collective-permute-start.4 = (f32[64,16,128]{2,1,0:T(8,128)S(1)}, f32[64,16,128]{2,1,0:T(8,128)S(1)}, u32[]{:S(2)}, u32[]{:S(2)}) collective-permute-start(f32[64,16,128]{2,1,0:T(8,128)S(1)} %get-tuple-element.63.u.refs_0_), channel_id=1, source_target_pairs={{0,32},{32,64},{64,96},{96,128},{128,160},{160,192},{192,224},{224... | collective-permute-start | bytes 1572872 | tf_op jit(solution)/shard_map/ppermute | solution.py:64
  2.9 13.6 %collective-permute-start = (bf16[16,16,128]{2,1,0:T(8,128)(2,1)S(1)}, bf16[16,16,128]{2,1,0:T(8,128)(2,1)S(1)}, u32[]{:S(2)}, u32[]{:S(2)}) collective-permute-start(bf16[16,16,128]{2,1,0:T(8,128)(2,1)S(1)} %get-tuple-element.65), channel_id=1, source_target_pairs={{0,32},{1,33},{2,4},{3,5},{4,2},{5,3},{6,8},{7,9},{8,6},{9,7},{10,... | collective-permute-start | bytes 196616 | tf_op jit(solution)/shard_map/ppermute | solution.py:59
  9.1 7.3 %collective-permute-start.1 = (bf16[16,16,128]{2,1,0:T(8,128)(2,1)S(1)}, bf16[16,16,128]{2,1,0:T(8,128)(2,1)S(1)}, u32[]{:S(2)}, u32[]{:S(2)}) collective-permute-start(bf16[16,16,128]{2,1,0:T(8,128)(2,1)S(1)} %get-tuple-element.66), channel_id=1, source_target_pairs={{0,2},{1,3},{2,0},{3,1},{4,6},{5,7},{6,4},{7,5},{8,10},{9,11},{10,... | collective-permute-start | bytes 196616 | tf_op jit(solution)/shard_map/ppermute | solution.py:59
  10.7 7.1 %collective-permute-start.2 = (bf16[16,16,128]{2,1,0:T(8,128)(2,1)S(1)}, bf16[16,16,128]{2,1,0:T(8,128)(2,1)S(1)}, u32[]{:S(2)}, u32[]{:S(2)}) collective-permute-start(bf16[16,16,128]{2,1,0:T(8,128)(2,1)S(1)} %get-tuple-element.67), channel_id=1, source_target_pairs={{0,32},{1,2},{2,1},{3,4},{4,3},{5,6},{6,5},{7,8},{8,7},{9,10},{10,... | collective-permute-start | bytes 196616 | tf_op jit(solution)/shard_map/ppermute | solution.py:59
  10.7 7.1 %collective-permute-start.3 = (bf16[16,16,128]{2,1,0:T(8,128)(2,1)S(1)}, bf16[16,16,128]{2,1,0:T(8,128)(2,1)S(1)}, u32[]{:S(2)}, u32[]{:S(2)}) collective-permute-start(bf16[16,16,128]{2,1,0:T(8,128)(2,1)S(1)} %get-tuple-element.68), channel_id=1, source_target_pairs={{0,1},{1,0},{2,3},{3,2},{4,5},{5,4},{6,7},{7,6},{8,9},{9,8},{10,11... | collective-permute-start | bytes 196616 | tf_op jit(solution)/shard_map/ppermute | solution.py:59
  13.6 0.7 copy-start.1
  21.0 7.0 %collective-permute-start.5 = (bf16[64,16,128]{2,1,0:T(8,128)(2,1)S(1)}, bf16[64,16,128]{2,1,0:T(8,128)(2,1)S(1)}, u32[]{:S(2)}, u32[]{:S(2)}) collective-permute-start(bf16[64,16,128]{2,1,0:T(8,128)(2,1)S(1)} %get-tuple-element.73), channel_id=1, source_target_pairs={{0,32},{32,64},{64,96},{96,128},{128,160},{160,192},{192,224},{224... | collective-permute-start | bytes 786440 | tf_op jit(solution)/shard_map/ppermute | solution.py:64
  28.8 8.0 %collective-permute-start.6 = (bf16[16,16,128]{2,1,0:T(8,128)(2,1)S(1)}, bf16[16,16,128]{2,1,0:T(8,128)(2,1)S(1)}, u32[]{:S(2)}, u32[]{:S(2)}) collective-permute-start(bf16[16,16,128]{2,1,0:T(8,128)(2,1)S(1)} %get-tuple-element.77), channel_id=1, source_target_pairs={{0,32},{1,33},{2,4},{3,5},{4,2},{5,3},{6,8},{7,9},{8,6},{9,7},{10,... | collective-permute-start | bytes 196616 | tf_op jit(solution)/shard_map/ppermute | solution.py:59
  31.3 6.0 %collective-permute-start.7 = (bf16[16,16,128]{2,1,0:T(8,128)(2,1)S(1)}, bf16[16,16,128]{2,1,0:T(8,128)(2,1)S(1)}, u32[]{:S(2)}, u32[]{:S(2)}) collective-permute-start(bf16[16,16,128]{2,1,0:T(8,128)(2,1)S(1)} %get-tuple-element.78), channel_id=1, source_target_pairs={{0,2},{1,3},{2,0},{3,1},{4,6},{5,7},{6,4},{7,5},{8,10},{9,11},{10,... | collective-permute-start | bytes 196616 | tf_op jit(solution)/shard_map/ppermute | solution.py:59
  31.5 6.4 %collective-permute-start.8 = (bf16[16,16,128]{2,1,0:T(8,128)(2,1)S(1)}, bf16[16,16,128]{2,1,0:T(8,128)(2,1)S(1)}, u32[]{:S(2)}, u32[]{:S(2)}) collective-permute-start(bf16[16,16,128]{2,1,0:T(8,128)(2,1)S(1)} %get-tuple-element.79), channel_id=1, source_target_pairs={{0,32},{1,2},{2,1},{3,4},{4,3},{5,6},{6,5},{7,8},{8,7},{9,10},{10,... | collective-permute-start | bytes 196616 | tf_op jit(solution)/shard_map/ppermute | solution.py:59
  32.8 5.1 %collective-permute-start.9 = (bf16[16,16,128]{2,1,0:T(8,128)(2,1)S(1)}, bf16[16,16,128]{2,1,0:T(8,128)(2,1)S(1)}, u32[]{:S(2)}, u32[]{:S(2)}) collective-permute-start(bf16[16,16,128]{2,1,0:T(8,128)(2,1)S(1)} %get-tuple-element.80), channel_id=1, source_target_pairs={{0,1},{1,0},{2,3},{3,2},{4,5},{5,4},{6,7},{7,6},{8,9},{9,8},{10,11... | collective-permute-start | bytes 196616 | tf_op jit(solution)/shard_map/ppermute | solution.py:59
  40.7 8.1 %collective-permute-start.10 = (bf16[16,16,128]{2,1,0:T(8,128)(2,1)S(1)}, bf16[16,16,128]{2,1,0:T(8,128)(2,1)S(1)}, u32[]{:S(2)}, u32[]{:S(2)}) collective-permute-start(bf16[16,16,128]{2,1,0:T(8,128)(2,1)S(1)} %get-tuple-element.85), channel_id=1, source_target_pairs={{0,32},{1,33},{2,4},{3,5},{4,2},{5,3},{6,8},{7,9},{8,6},{9,7},{10,... | collective-permute-start | bytes 196616 | tf_op jit(solution)/shard_map/ppermute | solution.py:59
  43.0 5.8 %collective-permute-start.11 = (bf16[16,16,128]{2,1,0:T(8,128)(2,1)S(1)}, bf16[16,16,128]{2,1,0:T(8,128)(2,1)S(1)}, u32[]{:S(2)}, u32[]{:S(2)}) collective-permute-start(bf16[16,16,128]{2,1,0:T(8,128)(2,1)S(1)} %get-tuple-element.86), channel_id=1, source_target_pairs={{0,2},{1,3},{2,0},{3,1},{4,6},{5,7},{6,4},{7,5},{8,10},{9,11},{10,... | collective-permute-start | bytes 196616 | tf_op jit(solution)/shard_map/ppermute | solution.py:59
  45.5 6.4 %collective-permute-start.12 = (bf16[16,16,128]{2,1,0:T(8,128)(2,1)S(1)}, bf16[16,16,128]{2,1,0:T(8,128)(2,1)S(1)}, u32[]{:S(2)}, u32[]{:S(2)}) collective-permute-start(bf16[16,16,128]{2,1,0:T(8,128)(2,1)S(1)} %get-tuple-element.87), channel_id=1, source_target_pairs={{0,32},{1,2},{2,1},{3,4},{4,3},{5,6},{6,5},{7,8},{8,7},{9,10},{10,... | collective-permute-start | bytes 196616 | tf_op jit(solution)/shard_map/ppermute | solution.py:59
  47.2 4.6 %collective-permute-start.13 = (bf16[16,16,128]{2,1,0:T(8,128)(2,1)S(1)}, bf16[16,16,128]{2,1,0:T(8,128)(2,1)S(1)}, u32[]{:S(2)}, u32[]{:S(2)}) collective-permute-start(bf16[16,16,128]{2,1,0:T(8,128)(2,1)S(1)} %get-tuple-element.88), channel_id=1, source_target_pairs={{0,1},{1,0},{2,3},{3,2},{4,5},{5,4},{6,7},{7,6},{8,9},{9,8},{10,11... | collective-permute-start | bytes 196616 | tf_op jit(solution)/shard_map/ppermute | solution.py:59
  54.7 19.1 %collective-permute-start.14 = (f32[64,16,128]{2,1,0:T(8,128)S(1)}, f32[64,16,128]{2,1,0:T(8,128)S(1)}, u32[]{:S(2)}, u32[]{:S(2)}) collective-permute-start(f32[64,16,128]{2,1,0:T(8,128)S(1)} %get-tuple-element.90.u), channel_id=1, source_target_pairs={{0,32},{32,64},{64,96},{96,128},{128,160},{160,192},{192,224},{224... | collective-permute-start | bytes 1572872 | tf_op jit(solution)/shard_map/ppermute | solution.py:64
  54.7 8.4 %collective-permute-start.15 = (bf16[16,16,128]{2,1,0:T(8,128)(2,1)S(1)}, bf16[16,16,128]{2,1,0:T(8,128)(2,1)S(1)}, u32[]{:S(2)}, u32[]{:S(2)}) collective-permute-start(bf16[16,16,128]{2,1,0:T(8,128)(2,1)S(1)} %get-tuple-element.96), channel_id=1, source_target_pairs={{0,32},{1,33},{2,4},{3,5},{4,2},{5,3},{6,8},{7,9},{8,6},{9,7},{10,... | collective-permute-start | bytes 196616 | tf_op jit(solution)/shard_map/ppermute | solution.py:59
  56.4 7.1 %collective-permute-start.16 = (bf16[16,16,128]{2,1,0:T(8,128)(2,1)S(1)}, bf16[16,16,128]{2,1,0:T(8,128)(2,1)S(1)}, u32[]{:S(2)}, u32[]{:S(2)}) collective-permute-start(bf16[16,16,128]{2,1,0:T(8,128)(2,1)S(1)} %get-tuple-element.97), channel_id=1, source_target_pairs={{0,2},{1,3},{2,0},{3,1},{4,6},{5,7},{6,4},{7,5},{8,10},{9,11},{10,... | collective-permute-start | bytes 196616 | tf_op jit(solution)/shard_map/ppermute | solution.py:59
  57.6 6.5 %collective-permute-start.17 = (bf16[16,16,128]{2,1,0:T(8,128)(2,1)S(1)}, bf16[16,16,128]{2,1,0:T(8,128)(2,1)S(1)}, u32[]{:S(2)}, u32[]{:S(2)}) collective-permute-start(bf16[16,16,128]{2,1,0:T(8,128)(2,1)S(1)} %get-tuple-element.98), channel_id=1, source_target_pairs={{0,32},{1,2},{2,1},{3,4},{4,3},{5,6},{6,5},{7,8},{8,7},{9,10},{10,... | collective-permute-start | bytes 196616 | tf_op jit(solution)/shard_map/ppermute | solution.py:59
  59.2 4.9 %collective-permute-start.18 = (bf16[16,16,128]{2,1,0:T(8,128)(2,1)S(1)}, bf16[16,16,128]{2,1,0:T(8,128)(2,1)S(1)}, u32[]{:S(2)}, u32[]{:S(2)}) collective-permute-start(bf16[16,16,128]{2,1,0:T(8,128)(2,1)S(1)} %get-tuple-element.99), channel_id=1, source_target_pairs={{0,1},{1,0},{2,3},{3,2},{4,5},{5,4},{6,7},{7,6},{8,9},{9,8},{10,11... | collective-permute-start | bytes 196616 | tf_op jit(solution)/shard_map/ppermute | solution.py:59
  66.8 7.0 %collective-permute-start.19 = (bf16[64,16,128]{2,1,0:T(8,128)(2,1)S(1)}, bf16[64,16,128]{2,1,0:T(8,128)(2,1)S(1)}, u32[]{:S(2)}, u32[]{:S(2)}) collective-permute-start(bf16[64,16,128]{2,1,0:T(8,128)(2,1)S(1)} %get-tuple-element.101), channel_id=1, source_target_pairs={{0,32},{32,64},{64,96},{96,128},{128,160},{160,192},{192,224},{224... | collective-permute-start | bytes 786440 | tf_op jit(solution)/shard_map/ppermute | solution.py:64
  74.6 8.4 %collective-permute-start.20 = (bf16[16,16,128]{2,1,0:T(8,128)(2,1)S(1)}, bf16[16,16,128]{2,1,0:T(8,128)(2,1)S(1)}, u32[]{:S(2)}, u32[]{:S(2)}) collective-permute-start(bf16[16,16,128]{2,1,0:T(8,128)(2,1)S(1)} %get-tuple-element.106), channel_id=1, source_target_pairs={{0,32},{1,33},{2,4},{3,5},{4,2},{5,3},{6,8},{7,9},{8,6},{9,7},{10,... | collective-permute-start | bytes 196616 | tf_op jit(solution)/shard_map/ppermute | solution.py:59
  76.9 6.0 %collective-permute-start.21 = (bf16[16,16,128]{2,1,0:T(8,128)(2,1)S(1)}, bf16[16,16,128]{2,1,0:T(8,128)(2,1)S(1)}, u32[]{:S(2)}, u32[]{:S(2)}) collective-permute-start(bf16[16,16,128]{2,1,0:T(8,128)(2,1)S(1)} %get-tuple-element.107), channel_id=1, source_target_pairs={{0,2},{1,3},{2,0},{3,1},{4,6},{5,7},{6,4},{7,5},{8,10},{9,11},{10,... | collective-permute-start | bytes 196616 | tf_op jit(solution)/shard_map/ppermute | solution.py:59
  79.0 6.4 %collective-permute-start.22 = (bf16[16,16,128]{2,1,0:T(8,128)(2,1)S(1)}, bf16[16,16,128]{2,1,0:T(8,128)(2,1)S(1)}, u32[]{:S(2)}, u32[]{:S(2)}) collective-permute-start(bf16[16,16,128]{2,1,0:T(8,128)(2,1)S(1)} %get-tuple-element.108), channel_id=1, source_target_pairs={{0,32},{1,2},{2,1},{3,4},{4,3},{5,6},{6,5},{7,8},{8,7},{9,10},{10,... | collective-permute-start | bytes 196616 | tf_op jit(solution)/shard_map/ppermute | solution.py:59
  80.9 4.5 %collective-permute-start.23 = (bf16[16,16,128]{2,1,0:T(8,128)(2,1)S(1)}, bf16[16,16,128]{2,1,0:T(8,128)(2,1)S(1)}, u32[]{:S(2)}, u32[]{:S(2)}) collective-permute-start(bf16[16,16,128]{2,1,0:T(8,128)(2,1)S(1)} %get-tuple-element.109), channel_id=1, source_target_pairs={{0,1},{1,0},{2,3},{3,2},{4,5},{5,4},{6,7},{7,6},{8,9},{9,8},{10,11... | collective-permute-start | bytes 196616 | tf_op jit(solution)/shard_map/ppermute | solution.py:59
  88.2 7.4 %collective-permute-start.24 = (bf16[16,16,128]{2,1,0:T(8,128)(2,1)S(1)}, bf16[16,16,128]{2,1,0:T(8,128)(2,1)S(1)}, u32[]{:S(2)}, u32[]{:S(2)}) collective-permute-start(bf16[16,16,128]{2,1,0:T(8,128)(2,1)S(1)} %get-tuple-element.114), channel_id=1, source_target_pairs={{0,32},{1,33},{2,4},{3,5},{4,2},{5,3},{6,8},{7,9},{8,6},{9,7},{10,... | collective-permute-start | bytes 196616 | tf_op jit(solution)/shard_map/ppermute | solution.py:59
  89.9 5.7 %collective-permute-start.25 = (bf16[16,16,128]{2,1,0:T(8,128)(2,1)S(1)}, bf16[16,16,128]{2,1,0:T(8,128)(2,1)S(1)}, u32[]{:S(2)}, u32[]{:S(2)}) collective-permute-start(bf16[16,16,128]{2,1,0:T(8,128)(2,1)S(1)} %get-tuple-element.115), channel_id=1, source_target_pairs={{0,2},{1,3},{2,0},{3,1},{4,6},{5,7},{6,4},{7,5},{8,10},{9,11},{10,... | collective-permute-start | bytes 196616 | tf_op jit(solution)/shard_map/ppermute | solution.py:59
  91.4 6.4 %collective-permute-start.26 = (bf16[16,16,128]{2,1,0:T(8,128)(2,1)S(1)}, bf16[16,16,128]{2,1,0:T(8,128)(2,1)S(1)}, u32[]{:S(2)}, u32[]{:S(2)}) collective-permute-start(bf16[16,16,128]{2,1,0:T(8,128)(2,1)S(1)} %get-tuple-element.116), channel_id=1, source_target_pairs={{0,32},{1,2},{2,1},{3,4},{4,3},{5,6},{6,5},{7,8},{8,7},{9,10},{10,... | collective-permute-start | bytes 196616 | tf_op jit(solution)/shard_map/ppermute | solution.py:59
  93.0 4.7 %collective-permute-start.27 = (bf16[16,16,128]{2,1,0:T(8,128)(2,1)S(1)}, bf16[16,16,128]{2,1,0:T(8,128)(2,1)S(1)}, u32[]{:S(2)}, u32[]{:S(2)}) collective-permute-start(bf16[16,16,128]{2,1,0:T(8,128)(2,1)S(1)} %get-tuple-element.117), channel_id=1, source_target_pairs={{0,1},{1,0},{2,3},{3,2},{4,5},{5,4},{6,7},{7,6},{8,9},{9,8},{10,11... | collective-permute-start | bytes 196616 | tf_op jit(solution)/shard_map/ppermute | solution.py:59
